TPU v7x, 32 devices: a whole 2x2x4 slice. The times are simulated.
32 devices in a mesh: bx: 4 (over y, x), by: 4 (over z), bz: 2 (over core).
Axes of the slice: x: 2, y: 2, z: 4, core: 2. Of those that a mesh axis runs over, the one named last changes fastest.
Arguments:
- position: float32 [3, 128, 128, 512], P(None, 'bx', 'by', 'bz'), may hold values from -2 to 2
- velocity: float32 [3, 128, 128, 512], P(None, 'bx', 'by', 'bz'), may hold values from -3 to 3
- density: float32 [128, 128, 512], P('bx', 'by', 'bz'), may hold values from 0.5 to 2
- energy: float32 [128, 128, 512], P('bx', 'by', 'bz'), may hold values from 0.1 to 10
- pinned: int32 [128, 128, 512], P('bx', 'by', 'bz'), may hold values 0 or 1
Outputs:
- velocity_new: float32 [3, 128, 128, 512], P(None, 'bx', 'by', 'bz')
- accel: float32 [3, 128, 128, 512], P(None, 'bx', 'by', 'bz')
- relaxed: float32 [3, 128, 128, 512], P(None, 'bx', 'by', 'bz')
- density_new: float32 [128, 128, 512], P('bx', 'by', 'bz')
- energy_new: float32 [128, 128, 512], P('bx', 'by', 'bz')
All inputs are finite; a program needn't handle non-finite values. No bound on the sum of `pinned` on one device may be relied on, other than what follows from the above.
Results may differ from a plain program's by a relative error of at most 0.0003.
Values sent between devices are 32-bit elements; how exact they have to be, the bound alone decides.
No kernel may reach another device: no remote copies, remote signals or barrier semaphores. Data moves between devices by JAX's collectives and lax.ppermute only.
A program may use at most 128 MiB of HBM per device.

v0:
```python
import jax
import jax.numpy as jnp
from jax import lax
from jax.sharding import PartitionSpec as P

CG_ITERS = 2
SWEEPS = 3


TIME_STEP = 0.6
RELAX_RATE = 0.8
CONSISTENT = 0.2


def from_behind(x, axis, by):
    length = lax.axis_size(axis)
    pairs = [(i, i + by) for i in range(length) if 0 <= i + by < length]
    return lax.ppermute(x, axis, pairs)


def padded(block, sides, width):
    for axis, dim in sides:
        count = lax.axis_size(axis)
        forward = [(i, i + 1) for i in range(count - 1)]
        backward = [(target, source) for source, target in forward]
        low = lax.ppermute(
            lax.slice_in_dim(block, block.shape[dim] - width, None, axis=dim), axis, forward
        )
        high = lax.ppermute(lax.slice_in_dim(block, 0, width, axis=dim), axis, backward)
        block = jnp.concatenate([low, block, high], axis=dim)
    return block


def shift_triple(along_dim, along, first, second):
    offsets = [0, 0, 0]
    offsets[along_dim] = along
    others = [d for d in range(3) if d != along_dim]
    offsets[others[0]] = first
    offsets[others[1]] = second
    return offsets


def select_at(extended, offsets):
    sizes = extended.shape[-3:]
    return extended[
        ...,
        1 + offsets[0] : sizes[0] - 1 + offsets[0],
        1 + offsets[1] : sizes[1] - 1 + offsets[1],
        1 + offsets[2] : sizes[2] - 1 + offsets[2],
    ]


def corner_force(pressure_ext):
    parts = []
    for along_dim in range(3):
        summed = 0.0
        for first in (0, -1):
            for second in (0, -1):
                summed = (
                    summed
                    + select_at(pressure_ext, shift_triple(along_dim, -1, first, second))
                    - select_at(pressure_ext, shift_triple(along_dim, 0, first, second))
                )
        parts.append(0.25 * summed)
    return jnp.stack(parts)


def node_mass(density_ext):
    summed = 0.0
    for first in (0, -1):
        for second in (0, -1):
            for third in (0, -1):
                summed = summed + select_at(density_ext, [first, second, third])
    return 0.125 * summed


def neighbours(extended):
    summed = 0.0
    for along_dim in range(3):
        for along in (-1, 1):
            summed = summed + select_at(extended, shift_triple(along_dim, along, 0, 0))
    return summed


def divergence(vel_ext):
    summed = 0.0
    for along_dim in range(3):
        for first in (0, 1):
            for second in (0, 1):
                summed = (
                    summed
                    + select_at(vel_ext[along_dim], shift_triple(along_dim, 1, first, second))
                    - select_at(vel_ext[along_dim], shift_triple(along_dim, 0, first, second))
                )
    return 0.25 * summed


def face_flux(packed, along_dim, along):
    speed = 0.0
    for first in (0, 1):
        for second in (0, 1):
            speed = speed + select_at(
                packed[along_dim], shift_triple(along_dim, along, first, second)
            )
    speed = 0.25 * speed
    upper = select_at(packed[3:5], shift_triple(along_dim, along, 0, 0))
    lower = select_at(packed[3:5], shift_triple(along_dim, along - 1, 0, 0))
    return speed * jnp.where(speed > 0, upper, lower)


def remap_cells(packed):
    result = select_at(packed[3:5], [0, 0, 0])
    for along_dim in range(3):
        result = result + face_flux(packed, along_dim, 1) - face_flux(packed, along_dim, 0)
    return result


def inner(first, second):
    return jnp.sum(first * second, axis=(1, 2, 3), keepdims=True)


def lower_cells(values):
    got = from_behind(values[..., -1:, :, :], "bx", 1)
    widened = jnp.concatenate([got, values], axis=-3)
    got = from_behind(widened[..., :, -1:, :], "by", 1)
    widened = jnp.concatenate([got, widened], axis=-2)
    got = from_behind(widened[..., :, :, -1:], "bz", 1)
    widened = jnp.concatenate([got, widened], axis=-1)
    return jnp.pad(widened, [(0, 0)] * (values.ndim - 3) + [(0, 1)] * 3)


def upper_nodes(values):
    got = from_behind(values[..., :1, :, :], "bx", -1)
    widened = jnp.concatenate([values, got], axis=-3)
    got = from_behind(widened[..., :, :1, :], "by", -1)
    widened = jnp.concatenate([widened, got], axis=-2)
    got = from_behind(widened[..., :, :, :1], "bz", -1)
    widened = jnp.concatenate([widened, got], axis=-1)
    return jnp.pad(widened, [(0, 0)] * (values.ndim - 3) + [(1, 0)] * 3)


def mass_apply(vector, masses):
    extended = padded(vector, (("bx", 1), ("by", 2), ("bz", 3)), 1)
    return masses * vector + CONSISTENT * (6.0 * vector + neighbours(extended))


def paired_sums(residual, image):
    return lax.psum((inner(residual, residual), inner(residual, image)), ("bx", "by", "bz"))


def one_sweep(relaxed, free):
    extended = padded(relaxed, (("bx", 1), ("by", 2), ("bz", 3)), 1)
    return relaxed + RELAX_RATE * free * (neighbours(extended) / 6.0 - relaxed)


def on_device(position, velocity, density, energy, pinned):
    cells = lower_cells(jnp.stack([density, energy]))
    force = corner_force(0.4 * cells[0] * cells[1])
    masses = node_mass(cells[0])
    solution = jnp.zeros_like(force)
    residual = force
    image = mass_apply(residual, masses)
    norm_now, product = paired_sums(residual, image)
    alpha = norm_now / product
    direction = residual
    along_image = image
    for step_index in range(CG_ITERS):
        solution = solution + alpha * direction
        residual = residual - alpha * along_image
        if step_index + 1 < CG_ITERS:
            image = mass_apply(residual, masses)
            norm_next, product = paired_sums(residual, image)
            ratio = norm_next / norm_now
            alpha = norm_next / (product - ratio * norm_next / alpha)
            direction = residual + ratio * direction
            along_image = image + ratio * along_image
            norm_now = norm_next
    velocity_new = velocity + TIME_STEP * solution
    vel_ext = upper_nodes(velocity_new)
    spread = divergence(vel_ext)
    pressure = 0.4 * density * energy
    energy_lag = energy - TIME_STEP * pressure * spread / density
    moved = position + TIME_STEP * velocity_new
    free = 1.0 - pinned.astype(jnp.float32)
    relaxed = moved
    for step_index in range(SWEEPS):
        relaxed = one_sweep(relaxed, free)
    packed = padded(
        jnp.concatenate([relaxed - moved, density[None], (density * energy_lag)[None]]),
        (("bx", 1), ("by", 2), ("bz", 3)),
        1,
    )
    remapped = remap_cells(packed)
    return (velocity_new, solution, relaxed, remapped[0], remapped[1])


def solution(mesh):
    in_specs = (
        P(None, "bx", "by", "bz"),
        P(None, "bx", "by", "bz"),
        P("bx", "by", "bz"),
        P("bx", "by", "bz"),
        P("bx", "by", "bz"),
    )
    out_specs = (
        P(None, "bx", "by", "bz"),
        P(None, "bx", "by", "bz"),
        P(None, "bx", "by", "bz"),
        P("bx", "by", "bz"),
        P("bx", "by", "bz"),
    )
    return jax.shard_map(
        on_device, mesh=mesh, in_specs=in_specs, out_specs=out_specs, check_vma=False
    )
```

profile of v0, /device:TPU:0, one launch (start us, length us, event | category | flops | bytes accessed | tf_op | source)
XLA Modules:
  0.0 517.6 jit_solution(7860723460517488252)
XLA Ops:
  1.6 4.8 collective-permute-start
  26.7 4.3 collective-permute-start.3
  33.6 5.0 collective-permute-done.4
  38.7 4.3 collective-permute-start.5
  45.2 4.3 collective-permute-done.6
  60.4 4.7 collective-permute-start.7
  73.3 16.0 %multiply_reduce_fusion.1 = (f32[3]{0:T(128)}, f32[3]{0:T(128)}, f32[3,32,32,256]{3,2,1,0:T(8,128)}) fusion(f32[1,32,32,256]{3,2,1,0:T(8,128)} %copy-done.11, f32[1,32,32,256]{3,2,1,0:T(8,128)S(1)} %copy-done.8, f32[1,32,32,256]{3,2,1,0:T(8,128)S(1)} %copy-done.10, f32[3,34,34,1]{3,2,1,0:T(8,128)} %copy.67, ...), kind=kLoop, calls=%fused_computation.194 | loop fusion | flops 36175864 | bytes 7773304 | tf_op jit(solution)/shard_map/reduce_sum | solution.py:119
  89.3 40.2 %all-reduce.3 = (f32[3,1,1,1]{0,3,2,1:T(1,128)S(1)}, f32[3,1,1,1]{0,3,2,1:T(1,128)S(1)}) all-reduce(f32[3,1,1,1]{0,3,2,1:T(1,128)} %bitcast.59, f32[3,1,1,1]{0,3,2,1:T(1,128)} %bitcast.58), channel_id=1, replica_groups=mesh['bx'=4,'by'=4,'bz'=2] {'bx','by','bz'}, use_global_device_ids=true, to_apply=%region_1.2 | all-reduce | flops 6 | bytes 48 | tf_op jit(solution)/shard_map/psum | solution.py:148
  139.6 4.3 collective-permute-done.10
  148.4 4.3 collective-permute-done.12
  171.4 15.8 %fusion.67 = f32[3]{0:T(128)} fusion(f32[3,32,32,256]{3,2,1,0:T(8,128)} %copy-done.3, f32[3,34,34,1]{3,2,1,0:T(8,128)} %copy.71, f32[3,34,1,256]{3,2,1,0:T(1,128)S(1)} %collective-permute-done.12, f32[3,34,1,256]{3,2,1,0:T(1,128)S(1)} %collective-permute-done.11, f32[3,1,32,256]{3,2,1,0:T(8,128)S(1)} %collective-permute-done.10, ...), kind=kLoop, calls=%fused_computation.147 | loop fusion | flops 23592956 | bytes 4627564 | tf_op jit(solution)/shard_map/reduce_sum | solution.py:119
  187.2 41.8 %all-reduce.2 = (f32[3,1,1,1]{0,3,2,1:T(1,128)S(1)}, f32[3,1,1,1]{0,3,2,1:T(1,128)S(1)}) all-reduce(f32[3,1,1,1]{0,3,2,1:T(1,128)} %bitcast.57, f32[3,1,1,1]{0,3,2,1:T(1,128)} %bitcast.60), channel_id=1, replica_groups=mesh['bx'=4,'by'=4,'bz'=2] {'bx','by','bz'}, use_global_device_ids=true, to_apply=%region_5.6 | all-reduce | flops 6 | bytes 48 | tf_op jit(solution)/shard_map/psum | solution.py:148
  229.6 6.7 %multiply_add_fusion = (f32[3,32,32,256]{3,2,1,0:T(8,128)S(1)}, f32[3,32,32,256]{3,2,1,0:T(8,128)}, f32[3,32,32,256]{3,2,1,0:T(8,128)}) fusion(f32[3,32,32,256]{3,2,1,0:T(8,128)} %param.5, f32[3,32,32,256]{3,2,1,0:T(8,128)} %param.6, f32[3,32,32,256]{3,2,1,0:T(8,128)} %copy-done.3, f32[3]{0:T(128)S(1)} %bitcast.56, f32[3]{0:T(128)S(1)} %get-tuple-element.33, ...), kind=kLoop, calls=%fused_computation.189 | loop fusion | flops 8650752 | bytes 22020132 | tf_op jit(solution)/shard_map/add | solution.py:183
  242.7 4.3 collective-permute-done.16
  248.5 4.6 collective-permute-start.17
  273.3 14.2 %fusion.57 = f32[3,32,32,256]{3,2,1,0:T(8,128)S(1)} fusion(f32[3,32,32,256]{3,2,1,0:T(8,128)} %copy-done.4, f32[3,34,34,1]{3,2,1,0:T(8,128)} %copy.81, f32[3,34,1,256]{3,2,1,0:T(1,128)S(1)} %copy.75, f32[3,34,1,256]{3,2,1,0:T(1,128)S(1)} %copy.73, f32[3,1,32,256]{3,2,1,0:T(8,128)S(1)} %collective-permute-done.16, ...), kind=kLoop, calls=%fused_computation.119 | loop fusion | flops 21233664 | bytes 7773280 | tf_op jit(solution)/shard_map/add | solution.py:153
  287.6 4.3 collective-permute-start.21
  294.5 4.5 collective-permute-done.22
  300.4 5.0 collective-permute-start.23
  306.8 5.5 %collective-permute-done.34 = f32[3,33,1,256]{3,1,2,0:T(8,128)S(1)} collective-permute-done((f32[3,33,1,256]{3,1,2,0:T(8,128)S(1)}, f32[3,33,1,256]{3,1,2,0:T(8,128)S(1)}, u32[]{:S(2)}, u32[]{:S(2)}) %collective-permute-start.34) | collective-permute-done | bytes 101408 | tf_op jit(solution)/shard_map/ppermute | solution.py:18
  340.5 14.4 %fusion.48 = f32[3,32,32,256]{3,2,1,0:T(8,128)S(1)} fusion(f32[3,32,32,256]{3,2,1,0:T(8,128)} %copy-done.5, f32[3,34,34,1]{3,2,1,0:T(8,128)} %copy.91, f32[3,34,1,256]{3,2,1,0:T(1,128)S(1)} %copy.85, f32[3,34,1,256]{3,2,1,0:T(1,128)S(1)} %copy.83, f32[3,1,32,256]{3,2,1,0:T(8,128)S(1)} %collective-permute-done.22, ...), kind=kLoop, calls=%fused_computation.92 | loop fusion | flops 21233664 | bytes 7773280 | tf_op jit(solution)/shard_map/add | solution.py:153
  358.5 4.7 select_maximum_fusion
  365.2 5.0 collective-permute-start.29
  383.8 4.3 collective-permute-start.31
  388.1 19.9 %fusion.121 = f32[1,32,32,256]{3,2,1,0:T(8,128)} fusion(f32[32,32,256]{2,1,0:T(8,128)S(1)} %copy-done, f32[32,32,256]{2,1,0:T(8,128)} %param.8, f32[34,34,258]{2,1,0:T(8,128)} %get-tuple-element.45, f32[34,34,258]{2,1,0:T(8,128)} %get-tuple-element.44, f32[34,34,258]{2,1,0:T(8,128)S(1)} %get-tuple-element.43), kind=kLoop, calls=%fused_computation.292 | loop fusion | flops 8126464 | bytes 28311552 | tf_op jit(solution)/shard_map/broadcast_in_dim | solution.py:189
  414.1 16.6 %fusion.130 = (f32[3,32,32,256]{3,2,1,0:T(8,128)S(1)}, f32[3,32,32,256]{3,2,1,0:T(8,128)}) fusion(f32[3,32,32,256]{3,2,1,0:T(8,128)} %copy-done.4, f32[3,32,32,256]{3,2,1,0:T(8,128)} %copy-done.6, f32[3,34,34,1]{3,2,1,0:T(8,128)} %copy.101, f32[3,34,1,256]{3,2,1,0:T(1,128)S(1)} %copy.95, f32[3,1,32,256]{3,2,1,0:T(8,128)S(1)} %collective-permute-done.28, ...), kind=kLoop, calls=%fused_computation.365 | loop fusion | flops 22020096 | bytes 14064736 | tf_op jit(solution)/shard_map/sub | solution.py:189
  437.8 5.9 %collective-permute-done.37 = f32[5,1,32,256]{3,2,1,0:T(8,128)S(1)} collective-permute-done((f32[5,1,32,256]{3,2,1,0:T(8,128)S(1)}, f32[5,1,32,256]{3,2,1,0:T(8,128)S(1)}, u32[]{:S(2)}, u32[]{:S(2)}) %collective-permute-start.37) | collective-permute-done | bytes 163872 | tf_op jit(solution)/shard_map/ppermute | solution.py:29
  450.7 4.4 collective-permute-done.39
  468.9 4.3 collective-permute-start.40
  480.1 16.1 %pad_maximum_fusion = f32[5,34,34,258]{3,2,1,0:T(8,128)S(1)} fusion(f32[5,34,34,1]{3,2,1,0:T(8,128)} %copy.109, f32[5,34,1,256]{3,2,1,0:T(1,128)} %copy-done.23, f32[5,1,32,256]{3,2,1,0:T(8,128)S(1)} %collective-permute-done.37, f32[1,32,32,256]{3,2,1,0:T(8,128)} %fusion.121, f32[1,32,32,256]{3,2,1,0:T(8,128)} %bitcast.45, ...), kind=kLoop, calls=%fused_computation | loop fusion | flops 11929920 | bytes 11929920 | tf_op jit(solution)/shard_map/concatenate | solution.py:30
  500.4 6.0 %broadcast_compare_fusion.1 = (pred[32,32,256]{2,1,0:T(8,128)(4,1)}, f32[32,32,256]{2,1,0:T(8,128)}, pred[32,32,256]{2,1,0:T(8,128)(4,1)}, f32[32,32,256]{2,1,0:...) fusion(f32[34,34,258]{2,1,0:T(8,128)S(1)} %get-tuple-element.39, ...), kind=kLoop, calls=%fused_computation.328 | loop fusion | flops 5242880 | bytes 22020096 | tf_op jit(solution)/shard_map/gt | solution.py:108
  506.5 9.3 %fusion.86 = f32[2,32,32,256]{3,2,1,0:T(8,128)S(1)} fusion(f32[3,32,32,256]{3,2,1,0:T(8,128)S(1)} %get-tuple-element.28, f32[1,32,32,256]{3,2,1,0:T(8,128)S(1)} %bitcast.51, f32[5,34,34,1]{3,2,1,0:T(8,128)S(1)} %copy-done.17, f32[5,34,1,256]{3,2,1,0:T(1,128)S(1)} %copy-done.24, f32[5,34,1,256]{3,2,1,0:T(1,128)S(1)} %copy-done.22, ...), kind=kLoop, calls=%fused_computation.206 | loop fusion | flops 25690112 | bytes 15926432 | tf_op jit(solution)/shard_map/sub | solution.py:114
  (210 shorter events, 206.0 us)
Async XLA Ops:
  1.6 6.7 %collective-permute-start = (f32[2,1,32,256]{3,2,1,0:T(8,128)S(1)}, f32[2,1,32,256]{3,2,1,0:T(8,128)S(1)}, u32[]{:S(2)}, u32[]{:S(2)}) collective-permute-start(f32[2,1,32,256]{3,2,1,0:T(8,128)S(1)} %pad_maximum_fusion.146), channel_id=1, source_target_pairs={{0,8},{8,16},{16,24},{1,9},{9,17},{17,25},{2,10},{10,18},{18,26},{... | collective-permute-start | bytes 196616 | tf_op jit(solution)/shard_map/ppermute | solution.py:18
  26.7 6.8 %collective-permute-start.3 = (f32[3,1,32,256]{3,2,1,0:T(8,128)S(1)}, f32[3,1,32,256]{3,2,1,0:T(8,128)S(1)}, u32[]{:S(2)}, u32[]{:S(2)}) collective-permute-start(f32[3,1,32,256]{3,2,1,0:T(8,128)S(1)} %get-tuple-element.78), channel_id=1, source_target_pairs={{0,8},{8,16},{16,24},{1,9},{9,17},{17,25},{2,10},{10,18},{18,26},{... | collective-permute-start | bytes 294920 | tf_op jit(solution)/shard_map/ppermute | solution.py:26
  31.0 7.5 %collective-permute-start.4 = (f32[3,1,32,256]{3,2,1,0:T(8,128)S(1)}, f32[3,1,32,256]{3,2,1,0:T(8,128)S(1)}, u32[]{:S(2)}, u32[]{:S(2)}) collective-permute-start(f32[3,1,32,256]{3,2,1,0:T(8,128)S(1)} %get-tuple-element.79), channel_id=1, source_target_pairs={{8,0},{16,8},{24,16},{9,1},{17,9},{25,17},{10,2},{18,10},{26,18},{... | collective-permute-start | bytes 294920 | tf_op jit(solution)/shard_map/ppermute | solution.py:29
  38.7 6.5 %collective-permute-start.5 = (f32[3,34,1,256]{3,2,1,0:T(1,128)S(1)}, f32[3,34,1,256]{3,2,1,0:T(1,128)S(1)}, u32[]{:S(2)}, u32[]{:S(2)}) collective-permute-start(f32[3,34,1,256]{3,2,1,0:T(1,128)S(1)} %get-tuple-element.68), channel_id=1, source_target_pairs={{0,2},{2,4},{4,6},{1,3},{3,5},{5,7},{8,10},{10,12},{12,14},{9,11},... | collective-permute-start | bytes 313352 | tf_op jit(solution)/shard_map/ppermute | solution.py:26
  42.9 6.6 %collective-permute-start.6 = (f32[3,34,1,256]{3,2,1,0:T(1,128)S(1)}, f32[3,34,1,256]{3,2,1,0:T(1,128)S(1)}, u32[]{:S(2)}, u32[]{:S(2)}) collective-permute-start(f32[3,34,1,256]{3,2,1,0:T(1,128)S(1)} %get-tuple-element.69), channel_id=1, source_target_pairs={{2,0},{4,2},{6,4},{3,1},{5,3},{7,5},{10,8},{12,10},{14,12},{11,9},... | collective-permute-start | bytes 313352 | tf_op jit(solution)/shard_map/ppermute | solution.py:29
  59.1 11.2 %collective-permute-start.8 = (f32[3,34,34,1]{2,3,1,0:T(1,128)}, f32[3,34,34,1]{2,3,1,0:T(1,128)}, u32[]{:S(2)}, u32[]{:S(2)}) collective-permute-start(f32[3,34,34,1]{2,3,1,0:T(1,128)} %copy.66), channel_id=1, source_target_pairs={{1,0},{3,2},{5,4},{7,6},{9,8},{11,10},{13,12},{15,14},{17,16},{19,... | collective-permute-start | bytes 41624 | tf_op jit(solution)/shard_map/ppermute | solution.py:29
  60.4 6.9 %collective-permute-start.7 = (f32[3,34,34,1]{2,3,1,0:T(1,128)}, f32[3,34,34,1]{2,3,1,0:T(1,128)}, u32[]{:S(2)}, u32[]{:S(2)}) collective-permute-start(f32[3,34,34,1]{2,3,1,0:T(1,128)} %copy.64), channel_id=1, source_target_pairs={{0,1},{2,3},{4,5},{6,7},{8,9},{10,11},{12,13},{14,15},{16,17},{18,... | collective-permute-start | bytes 41624 | tf_op jit(solution)/shard_map/ppermute | solution.py:26
  137.4 6.5 %collective-permute-start.10 = (f32[3,1,32,256]{3,2,1,0:T(8,128)S(1)}, f32[3,1,32,256]{3,2,1,0:T(8,128)S(1)}, u32[]{:S(2)}, u32[]{:S(2)}) collective-permute-start(f32[3,1,32,256]{3,2,1,0:T(8,128)S(1)} %get-tuple-element.77), channel_id=1, source_target_pairs={{8,0},{16,8},{24,16},{9,1},{17,9},{25,17},{10,2},{18,10},{26,18},{... | collective-permute-start | bytes 294920 | tf_op jit(solution)/shard_map/ppermute | solution.py:29
  146.2 6.6 %collective-permute-start.12 = (f32[3,34,1,256]{3,2,1,0:T(1,128)S(1)}, f32[3,34,1,256]{3,2,1,0:T(1,128)S(1)}, u32[]{:S(2)}, u32[]{:S(2)}) collective-permute-start(f32[3,34,1,256]{3,2,1,0:T(1,128)S(1)} %get-tuple-element.67), channel_id=1, source_target_pairs={{2,0},{4,2},{6,4},{3,1},{5,3},{7,5},{10,8},{12,10},{14,12},{11,9},... | collective-permute-start | bytes 313352 | tf_op jit(solution)/shard_map/ppermute | solution.py:29
  240.5 6.5 %collective-permute-start.16 = (f32[3,1,32,256]{3,2,1,0:T(8,128)S(1)}, f32[3,1,32,256]{3,2,1,0:T(8,128)S(1)}, u32[]{:S(2)}, u32[]{:S(2)}) collective-permute-start(f32[3,1,32,256]{3,2,1,0:T(8,128)S(1)} %get-tuple-element.75), channel_id=1, source_target_pairs={{8,0},{16,8},{24,16},{9,1},{17,9},{25,17},{10,2},{18,10},{26,18},{... | collective-permute-start | bytes 294920 | tf_op jit(solution)/shard_map/ppermute | solution.py:29
  247.2 6.8 %collective-permute-start.18 = (f32[3,34,1,256]{3,1,2,0:T(8,128)S(1)}, f32[3,34,1,256]{3,1,2,0:T(8,128)S(1)}, u32[]{:S(2)}, u32[]{:S(2)}) collective-permute-start(f32[3,34,1,256]{3,1,2,0:T(8,128)S(1)} %copy.74), channel_id=1, source_target_pairs={{2,0},{4,2},{6,4},{3,1},{5,3},{7,5},{10,8},{12,10},{14,12},{11,9},... | collective-permute-start | bytes 313352 | tf_op jit(solution)/shard_map/ppermute | solution.py:29
  248.5 7.0 %collective-permute-start.17 = (f32[3,34,1,256]{3,1,2,0:T(8,128)S(1)}, f32[3,34,1,256]{3,1,2,0:T(8,128)S(1)}, u32[]{:S(2)}, u32[]{:S(2)}) collective-permute-start(f32[3,34,1,256]{3,1,2,0:T(8,128)S(1)} %copy.72), channel_id=1, source_target_pairs={{0,2},{2,4},{4,6},{1,3},{3,5},{5,7},{8,10},{10,12},{12,14},{9,11},... | collective-permute-start | bytes 313352 | tf_op jit(solution)/shard_map/ppermute | solution.py:26
  263.0 8.1 %collective-permute-start.20 = (f32[3,34,34,1]{2,1,3,0:T(8,128)}, f32[3,34,34,1]{2,1,3,0:T(8,128)S(1)}, u32[]{:S(2)}, u32[]{:S(2)}) collective-permute-start(f32[3,34,34,1]{2,1,3,0:T(8,128)} %copy.80), channel_id=1, source_target_pairs={{1,0},{3,2},{5,4},{7,6},{9,8},{11,10},{13,12},{15,14},{17,16},{19,... | collective-permute-start | bytes 41624 | tf_op jit(solution)/shard_map/ppermute | solution.py:29
  287.6 6.9 %collective-permute-start.21 = (f32[3,1,32,256]{3,2,1,0:T(8,128)S(1)}, f32[3,1,32,256]{3,2,1,0:T(8,128)S(1)}, u32[]{:S(2)}, u32[]{:S(2)}) collective-permute-start(f32[3,1,32,256]{3,2,1,0:T(8,128)S(1)} %get-tuple-element.72), channel_id=1, source_target_pairs={{0,8},{8,16},{16,24},{1,9},{9,17},{17,25},{2,10},{10,18},{18,26},{... | collective-permute-start | bytes 294920 | tf_op jit(solution)/shard_map/ppermute | solution.py:26
  291.8 7.1 %collective-permute-start.22 = (f32[3,1,32,256]{3,2,1,0:T(8,128)S(1)}, f32[3,1,32,256]{3,2,1,0:T(8,128)S(1)}, u32[]{:S(2)}, u32[]{:S(2)}) collective-permute-start(f32[3,1,32,256]{3,2,1,0:T(8,128)S(1)} %get-tuple-element.73), channel_id=1, source_target_pairs={{8,0},{16,8},{24,16},{9,1},{17,9},{25,17},{10,2},{18,10},{26,18},{... | collective-permute-start | bytes 294920 | tf_op jit(solution)/shard_map/ppermute | solution.py:29
  293.2 12.2 %collective-permute-start.33 = (f32[3,1,32,256]{3,2,1,0:T(8,128)S(1)}, f32[3,1,32,256]{3,2,1,0:T(8,128)S(1)}, u32[]{:S(2)}, u32[]{:S(2)}) collective-permute-start(f32[3,1,32,256]{3,2,1,0:T(8,128)S(1)} %slice.782), channel_id=1, source_target_pairs={{8,0},{16,8},{24,16},{9,1},{17,9},{25,17},{10,2},{18,10},{26,18},{... | collective-permute-start | bytes 294920 | tf_op jit(solution)/shard_map/ppermute | solution.py:18
  299.1 13.3 %collective-permute-start.24 = (f32[3,34,1,256]{3,1,2,0:T(8,128)S(1)}, f32[3,34,1,256]{3,1,2,0:T(8,128)S(1)}, u32[]{:S(2)}, u32[]{:S(2)}) collective-permute-start(f32[3,34,1,256]{3,1,2,0:T(8,128)S(1)} %copy.84), channel_id=1, source_target_pairs={{2,0},{4,2},{6,4},{3,1},{5,3},{7,5},{10,8},{12,10},{14,12},{11,9},... | collective-permute-start | bytes 313352 | tf_op jit(solution)/shard_map/ppermute | solution.py:29
  300.4 12.1 %collective-permute-start.23 = (f32[3,34,1,256]{3,1,2,0:T(8,128)S(1)}, f32[3,34,1,256]{3,1,2,0:T(8,128)S(1)}, u32[]{:S(2)}, u32[]{:S(2)}) collective-permute-start(f32[3,34,1,256]{3,1,2,0:T(8,128)S(1)} %copy.82), channel_id=1, source_target_pairs={{0,2},{2,4},{4,6},{1,3},{3,5},{5,7},{8,10},{10,12},{12,14},{9,11},... | collective-permute-start | bytes 313352 | tf_op jit(solution)/shard_map/ppermute | solution.py:26
  305.5 6.8 %collective-permute-start.34 = (f32[3,33,1,256]{3,1,2,0:T(8,128)S(1)}, f32[3,33,1,256]{3,1,2,0:T(8,128)S(1)}, u32[]{:S(2)}, u32[]{:S(2)}) collective-permute-start(f32[3,33,1,256]{3,1,2,0:T(8,128)S(1)} %copy.102), channel_id=1, source_target_pairs={{2,0},{4,2},{6,4},{3,1},{5,3},{7,5},{10,8},{12,10},{14,12},{11,9},... | collective-permute-start | bytes 304136 | tf_op jit(solution)/shard_map/ppermute | solution.py:18
  321.0 17.3 %collective-permute-start.26 = (f32[3,34,34,1]{2,1,3,0:T(8,128)S(1)}, f32[3,34,34,1]{2,1,3,0:T(8,128)S(1)}, u32[]{:S(2)}, u32[]{:S(2)}) collective-permute-start(f32[3,34,34,1]{2,1,3,0:T(8,128)S(1)} %copy.90), channel_id=1, source_target_pairs={{1,0},{3,2},{5,4},{7,6},{9,8},{11,10},{13,12},{15,14},{17,16},{19,... | collective-permute-start | bytes 41624 | tf_op jit(solution)/shard_map/ppermute | solution.py:29
  322.3 13.7 %collective-permute-start.25 = (f32[3,34,34,1]{2,1,3,0:T(8,128)S(1)}, f32[3,34,34,1]{2,1,3,0:T(8,128)S(1)}, u32[]{:S(2)}, u32[]{:S(2)}) collective-permute-start(f32[3,34,34,1]{2,1,3,0:T(8,128)S(1)} %copy.88), channel_id=1, source_target_pairs={{0,1},{2,3},{4,5},{6,7},{8,9},{10,11},{12,13},{14,15},{16,17},{18,... | collective-permute-start | bytes 41624 | tf_op jit(solution)/shard_map/ppermute | solution.py:26
  355.0 8.3 %collective-permute-start.27 = (f32[3,1,32,256]{3,2,1,0:T(8,128)S(1)}, f32[3,1,32,256]{3,2,1,0:T(8,128)S(1)}, u32[]{:S(2)}, u32[]{:S(2)}) collective-permute-start(f32[3,1,32,256]{3,2,1,0:T(8,128)S(1)} %get-tuple-element.70), channel_id=1, source_target_pairs={{0,8},{8,16},{16,24},{1,9},{9,17},{17,25},{2,10},{10,18},{18,26},{... | collective-permute-start | bytes 294920 | tf_op jit(solution)/shard_map/ppermute | solution.py:26
  363.9 8.7 %collective-permute-start.30 = (f32[3,34,1,256]{3,1,2,0:T(8,128)S(1)}, f32[3,34,1,256]{3,1,2,0:T(8,128)S(1)}, u32[]{:S(2)}, u32[]{:S(2)}) collective-permute-start(f32[3,34,1,256]{3,1,2,0:T(8,128)S(1)} %copy.94), channel_id=1, source_target_pairs={{2,0},{4,2},{6,4},{3,1},{5,3},{7,5},{10,8},{12,10},{14,12},{11,9},... | collective-permute-start | bytes 313352 | tf_op jit(solution)/shard_map/ppermute | solution.py:29
  365.2 7.5 %collective-permute-start.29 = (f32[3,34,1,256]{3,1,2,0:T(8,128)S(1)}, f32[3,34,1,256]{3,1,2,0:T(8,128)S(1)}, u32[]{:S(2)}, u32[]{:S(2)}) collective-permute-start(f32[3,34,1,256]{3,1,2,0:T(8,128)S(1)} %copy.92), channel_id=1, source_target_pairs={{0,2},{2,4},{4,6},{1,3},{3,5},{5,7},{8,10},{10,12},{12,14},{9,11},... | collective-permute-start | bytes 313352 | tf_op jit(solution)/shard_map/ppermute | solution.py:26
  382.5 28.5 %collective-permute-start.32 = (f32[3,34,34,1]{2,1,3,0:T(8,128)}, f32[3,34,34,1]{2,1,3,0:T(8,128)}, u32[]{:S(2)}, u32[]{:S(2)}) collective-permute-start(f32[3,34,34,1]{2,1,3,0:T(8,128)} %copy.100), channel_id=1, source_target_pairs={{1,0},{3,2},{5,4},{7,6},{9,8},{11,10},{13,12},{15,14},{17,16},{19,... | collective-permute-start | bytes 41624 | tf_op jit(solution)/shard_map/ppermute | solution.py:29
  383.8 24.2 %collective-permute-start.31 = (f32[3,34,34,1]{2,1,3,0:T(8,128)}, f32[3,34,34,1]{2,1,3,0:T(8,128)}, u32[]{:S(2)}, u32[]{:S(2)}) collective-permute-start(f32[3,34,34,1]{2,1,3,0:T(8,128)} %copy.98), channel_id=1, source_target_pairs={{0,1},{2,3},{4,5},{6,7},{8,9},{10,11},{12,13},{14,15},{16,17},{18,... | collective-permute-start | bytes 41624 | tf_op jit(solution)/shard_map/ppermute | solution.py:26
  430.7 7.0 %collective-permute-start.36 = (f32[5,1,32,256]{3,2,1,0:T(8,128)S(1)}, f32[5,1,32,256]{3,2,1,0:T(8,128)S(1)}, u32[]{:S(2)}, u32[]{:S(2)}) collective-permute-start(f32[5,1,32,256]{3,2,1,0:T(8,128)S(1)} %get-tuple-element.48), channel_id=1, source_target_pairs={{0,8},{8,16},{16,24},{1,9},{9,17},{17,25},{2,10},{10,18},{18,26},{... | collective-permute-start | bytes 491528 | tf_op jit(solution)/shard_map/ppermute | solution.py:26
  435.0 8.7 %collective-permute-start.37 = (f32[5,1,32,256]{3,2,1,0:T(8,128)S(1)}, f32[5,1,32,256]{3,2,1,0:T(8,128)S(1)}, u32[]{:S(2)}, u32[]{:S(2)}) collective-permute-start(f32[5,1,32,256]{3,2,1,0:T(8,128)S(1)} %get-tuple-element.49), channel_id=1, source_target_pairs={{8,0},{16,8},{24,16},{9,1},{17,9},{25,17},{10,2},{18,10},{26,18},{... | collective-permute-start | bytes 491528 | tf_op jit(solution)/shard_map/ppermute | solution.py:29
  443.9 6.8 %collective-permute-start.38 = (f32[5,34,1,256]{3,2,1,0:T(1,128)S(1)}, f32[5,34,1,256]{3,2,1,0:T(1,128)S(1)}, u32[]{:S(2)}, u32[]{:S(2)}) collective-permute-start(f32[5,34,1,256]{3,2,1,0:T(1,128)S(1)} %get-tuple-element.46), channel_id=1, source_target_pairs={{0,2},{2,4},{4,6},{1,3},{3,5},{5,7},{8,10},{10,12},{12,14},{9,11},... | collective-permute-start | bytes 522248 | tf_op jit(solution)/shard_map/ppermute | solution.py:26
  447.8 7.3 %collective-permute-start.39 = (f32[5,34,1,256]{3,2,1,0:T(1,128)S(1)}, f32[5,34,1,256]{3,2,1,0:T(1,128)S(1)}, u32[]{:S(2)}, u32[]{:S(2)}) collective-permute-start(f32[5,34,1,256]{3,2,1,0:T(1,128)S(1)} %get-tuple-element.47), channel_id=1, source_target_pairs={{2,0},{4,2},{6,4},{3,1},{5,3},{7,5},{10,8},{12,10},{14,12},{11,9},... | collective-permute-start | bytes 522248 | tf_op jit(solution)/shard_map/ppermute | solution.py:29
  464.1 9.0 %collective-permute-start.41 = (f32[5,34,34,1]{2,3,1,0:T(1,128)}, f32[5,34,34,1]{2,3,1,0:T(1,128)}, u32[]{:S(2)}, u32[]{:S(2)}) collective-permute-start(f32[5,34,34,1]{2,3,1,0:T(1,128)} %copy.107), channel_id=1, source_target_pairs={{1,0},{3,2},{5,4},{7,6},{9,8},{11,10},{13,12},{15,14},{17,16},{19,... | collective-permute-start | bytes 69368 | tf_op jit(solution)/shard_map/ppermute | solution.py:29
  468.9 7.8 %collective-permute-start.40 = (f32[5,34,34,1]{2,3,1,0:T(1,128)}, f32[5,34,34,1]{2,3,1,0:T(1,128)}, u32[]{:S(2)}, u32[]{:S(2)}) collective-permute-start(f32[5,34,34,1]{2,3,1,0:T(1,128)} %copy.106), channel_id=1, source_target_pairs={{0,1},{2,3},{4,5},{6,7},{8,9},{10,11},{12,13},{14,15},{16,17},{18,... | collective-permute-start | bytes 69368 | tf_op jit(solution)/shard_map/ppermute | solution.py:26
  (39 other events, 466.0 us)
where the time goes:
time: 526 us; the launch traced here: 518 us
  other arithmetic  170 us (32%)
  starting transfers between devices  107 us (20%)
  local copies, waits for them, and re-layouts  97.8 us (19%)
  blocking collectives  82 us (16%)
  waiting for transfers between devices  59 us (11%)
    psum x2, blocking collectives, paired_sums(): lax.psum((inner(residual, residual), inner(residual, image)), ('bx', 'by'...  82 us
    ppermute x18, starting transfers between devices, padded(): lax.ppermute(lax.slice_in_dim(block, block.shape[dim] - width, None, axis...  69.7 us
    ppermute x18, waiting for transfers between devices, padded(): lax.ppermute(lax.slice_in_dim(block, 0, width, axis=dim), axis, backward)  38.4 us
    reduce_sum x3, other arithmetic, inner(): return jnp.sum(first * second, axis=(1, 2, 3), keepdims=True)  35.3 us
    slice x19, local copies, waits for them, and re-layouts, padded(): lax.slice_in_dim(block, block.shape[dim] - width, None, axis=dim)  30.9 us
    add x2, other arithmetic, one_sweep(): return relaxed + RELAX_RATE * free * (neighbours(extended) / 6.0 - relaxed)  28.7 us
    ppermute x18, starting transfers between devices, padded(): lax.ppermute(lax.slice_in_dim(block, 0, width, axis=dim), axis, backward)  23.6 us
    concatenate x7, other arithmetic, padded(): block = jnp.concatenate([low, block, high], axis=dim)  21.5 us
  transfers between devices with their start and end apart: 42, of which 23 were waited for; matrix products, arithmetic and copies ran while one was open for 12% of the time, Pallas kernels for 0%

commit v1 on v0

--- a/solution.py
+++ b/solution.py
@@ -3,7 +3,6 @@
 from jax import lax
 from jax.sharding import PartitionSpec as P
 
-CG_ITERS = 2
 SWEEPS = 3
 
 
@@ -144,8 +143,34 @@
     return masses * vector + CONSISTENT * (6.0 * vector + neighbours(extended))
 
 
-def paired_sums(residual, image):
-    return lax.psum((inner(residual, residual), inner(residual, image)), ("bx", "by", "bz"))
+def solve_weights(force, image, second):
+    square = inner(force, force)
+    shift = jnp.where(square > 0, inner(force, image) / jnp.where(square > 0, square, 1.0), 0.0)
+    rest = image - shift * force
+    rest_image = second - shift * image
+    sums = jnp.stack(
+        [
+            shift,
+            square,
+            inner(force, rest),
+            inner(rest, rest),
+            inner(force, rest_image),
+            inner(rest, rest_image),
+        ]
+    ).reshape(6, 3)
+    got = lax.all_gather(sums, ("bx", "by", "bz"))
+    c, p0, q1, q2, q3, q4 = [got[:, i, :] for i in range(6)]
+    total = lambda x: jnp.sum(x, axis=0)
+    norm_now = total(p0)
+    alpha = norm_now / total(q1 + c * p0)
+    a = 1.0 - alpha * c
+    norm_next = total(a * a * p0 - 2.0 * a * alpha * q1 + alpha * alpha * q2)
+    product = total(
+        a * a * (q1 + c * p0) - a * alpha * (q3 + q2 + c * q1) + alpha * alpha * q4
+    )
+    ratio = norm_next / norm_now
+    later = norm_next / (product - ratio * norm_next / alpha)
+    return (alpha + later * (1.0 + ratio)).reshape(3, 1, 1, 1), (-later * alpha).reshape(3, 1, 1, 1)
 
 
 def one_sweep(relaxed, free):
@@ -157,24 +182,10 @@
     cells = lower_cells(jnp.stack([density, energy]))
     force = corner_force(0.4 * cells[0] * cells[1])
     masses = node_mass(cells[0])
-    solution = jnp.zeros_like(force)
-    residual = force
-    image = mass_apply(residual, masses)
-    norm_now, product = paired_sums(residual, image)
-    alpha = norm_now / product
-    direction = residual
-    along_image = image
-    for step_index in range(CG_ITERS):
-        solution = solution + alpha * direction
-        residual = residual - alpha * along_image
-        if step_index + 1 < CG_ITERS:
-            image = mass_apply(residual, masses)
-            norm_next, product = paired_sums(residual, image)
-            ratio = norm_next / norm_now
-            alpha = norm_next / (product - ratio * norm_next / alpha)
-            direction = residual + ratio * direction
-            along_image = image + ratio * along_image
-            norm_now = norm_next
+    image = mass_apply(force, masses)
+    second = mass_apply(image, masses)
+    on_force, on_image = solve_weights(force, image, second)
+    solution = on_force * force + on_image * image
     velocity_new = velocity + TIME_STEP * solution
     vel_ext = upper_nodes(velocity_new)
     spread = divergence(vel_ext)

time: 526 us -> 482 us (0.916)
  blocking collectives: 82 us -> 38.7 us
    psum x2 -> x0, blocking collectives: 82 us -> none  [paired_sums(): lax.psum((inner(residual, residual), inner(residual, image)), ('bx', 'by'...]
    all_gather x0 -> x1, blocking collectives: none -> 38.7 us  [solve_weights(): got = lax.all_gather(sums, ('bx', 'by', 'bz'))]
    reduce_sum x3 -> x2, other arithmetic: 35.3 us -> 29.7 us  [inner(): return jnp.sum(first * second, axis=(1, 2, 3), keepdims=True)]
  transfers between devices with their start and end apart: 42 -> 42, of which waited for: 23 -> 23; matrix products, arithmetic and copies ran while one was open for 12% -> 13% of each run, Pallas kernels for 0% -> 0%
where the time goes in v1:
time: 482 us; the launch traced here: 474 us
  other arithmetic  167 us (35%)
  starting transfers between devices  108 us (22%)
  local copies, waits for them, and re-layouts  99 us (21%)
  waiting for transfers between devices  58.6 us (12%)
  blocking collectives  38.7 us (8%)
    ppermute x18, starting transfers between devices, padded(): lax.ppermute(lax.slice_in_dim(block, block.shape[dim] - width, None, axis...  70.6 us
    all_gather x1, blocking collectives, solve_weights(): got = lax.all_gather(sums, ('bx', 'by', 'bz'))  38.7 us
    ppermute x18, waiting for transfers between devices, padded(): lax.ppermute(lax.slice_in_dim(block, 0, width, axis=dim), axis, backward)  38.5 us
    slice x19, local copies, waits for them, and re-layouts, padded(): lax.slice_in_dim(block, block.shape[dim] - width, None, axis=dim)  30.9 us
    reduce_sum x2, other arithmetic, inner(): return jnp.sum(first * second, axis=(1, 2, 3), keepdims=True)  29.7 us
    add x2, other arithmetic, one_sweep(): return relaxed + RELAX_RATE * free * (neighbours(extended) / 6.0 - relaxed)  28.4 us
    ppermute x18, starting transfers between devices, padded(): lax.ppermute(lax.slice_in_dim(block, 0, width, axis=dim), axis, backward)  23.5 us
    concatenate x7, other arithmetic, padded(): block = jnp.concatenate([low, block, high], axis=dim)  21.5 us
  transfers between devices with their start and end apart: 42, of which 23 were waited for; matrix products, arithmetic and copies ran while one was open for 13% of the time, Pallas kernels for 0%

profile of v1, /device:TPU:0, one launch (start us, length us, event | category | flops | bytes accessed | tf_op | source)
XLA Modules:
  0.0 473.8 jit_solution(3328020007189394086)
XLA Ops:
  1.6 4.8 %collective-permute-start = (f32[2,1,32,256]{3,2,1,0:T(8,128)S(1)}, f32[2,1,32,256]{3,2,1,0:T(8,128)S(1)}, u32[]{:S(2)}, u32[]{:S(2)}) collective-permute-start(f32[2,1,32,256]{3,2,1,0:T(8,128)S(1)} %pad_maximum_fusion.146), channel_id=1, source_target_pairs={{0,8},{8,16},{16,24},{1,9},{9,17},{17,25},{2,10},{10,18},{18,26},{... | collective-permute-start | bytes 196616 | tf_op jit(solution)/shard_map/ppermute | solution.py:17
  26.7 4.3 collective-permute-start.3
  33.6 5.0 %collective-permute-done.4 = f32[3,1,32,256]{3,2,1,0:T(8,128)S(1)} collective-permute-done((f32[3,1,32,256]{3,2,1,0:T(8,128)S(1)}, f32[3,1,32,256]{3,2,1,0:T(8,128)S(1)}, u32[]{:S(2)}, u32[]{:S(2)}) %collective-permute-start.4) | collective-permute-done | bytes 98336 | tf_op jit(solution)/shard_map/ppermute | solution.py:28
  38.7 4.3 collective-permute-start.5
  45.2 4.3 collective-permute-done.6
  60.4 4.4 collective-permute-start.7
  73.1 14.8 %multiply_reduce_fusion.5 = (f32[3]{0:T(128)S(1)}, f32[3]{0:T(128)S(1)}, f32[3,32,32,256]{3,2,1,0:T(8,128)S(1)}) fusion(f32[1,32,32,256]{3,2,1,0:T(8,128)} %copy-done.11, f32[1,32,32,256]{3,2,1,0:T(8,128)S(1)} %copy-done.8, f32[1,32,32,256]{3,2,1,0:T(8,128)S(1)} %copy-done.10, f32[3,34,34,1]{3,2,1,0:T(8,128)} %copy.76, ...), kind=kLoop, calls=%fused_computation.197 | loop fusion | flops 36175864 | bytes 7773304 | tf_op jit(solution)/shard_map/reduce_sum | solution.py:118
  88.0 4.4 collective-permute-start.9
  94.5 4.3 collective-permute-done.10
  104.7 4.3 collective-permute-done.12
  131.0 14.8 %multiply_reduce_fusion = (f32[3]{0:T(128)S(1)}, f32[3]{0:T(128)S(1)}, f32[3]{0:T(128)S(1)}, f32[3]{0:T(128)S(1)}) fusion(f32[3,32,32,256]{3,2,1,0:T(8,128)} %copy-done.3, f32[1,32,32,256]{3,2,1,0:T(8,128)} %copy-done.11, f32[1,32,32,256]{3,2,1,0:T(8,128)S(1)} %copy-done.8, f32[1,32,32,256]{3,2,1,0:T(8,128)S(1)} %copy-done.10, f32[3]{0:T(128)} %compare_select_fusion, ...), kind=kLoop, calls=%fused_computation.191 | loop fusion | flops 33030128 | bytes 7773340 | tf_op jit(solution)/shard_map/reduce_sum | solution.py:118
  145.9 38.7 %all-gather = f32[192,3,1,1,1]{1,4,3,2,0:T(1,128)S(1)} all-gather(f32[6,3,1,1,1]{1,4,3,2,0:T(1,128)S(1)} %constant_dynamic-update-slice_fusion), channel_id=2, replica_groups=mesh['bx'=4,'by'=4,'bz'=2] {'bx','by','bz'}, dimensions={0}, use_global_device_ids=true | all-gather | bytes 2376 | tf_op jit(solution)/shard_map/all_gather | solution.py:161
  185.4 9.2 %multiply_add_fusion = (f32[3,32,32,256]{3,2,1,0:T(8,128)S(1)}, f32[3,32,32,256]{3,2,1,0:T(8,128)}, f32[3,32,32,256]{3,2,1,0:T(8,128)}) fusion(f32[3,32,32,256]{3,2,1,0:T(8,128)} %param.5, f32[3,32,32,256]{3,2,1,0:T(8,128)} %param.6, f32[3,32,32,256]{3,2,1,0:T(8,128)} %copy-done.3, f32[3]{0:T(128)S(1)} %negate_multiply_fusion, ...), kind=kLoop, calls=%fused_computation.188 | loop fusion | flops 7077888 | bytes 22020120 | tf_op jit(solution)/shard_map/add | solution.py:194
  198.8 4.7 collective-permute-done.16
  204.9 4.6 collective-permute-start.17
  229.5 14.1 %fusion.57 = f32[3,32,32,256]{3,2,1,0:T(8,128)S(1)} fusion(f32[3,32,32,256]{3,2,1,0:T(8,128)} %copy-done.4, f32[3,34,34,1]{3,2,1,0:T(8,128)} %copy.91, f32[3,34,1,256]{3,2,1,0:T(1,128)S(1)} %copy.85, f32[3,34,1,256]{3,2,1,0:T(1,128)S(1)} %copy.83, f32[3,1,32,256]{3,2,1,0:T(8,128)S(1)} %collective-permute-done.16, ...), kind=kLoop, calls=%fused_computation.119 | loop fusion | flops 21233664 | bytes 7773280 | tf_op jit(solution)/shard_map/add | solution.py:178
  243.7 4.4 collective-permute-start.21
  256.4 5.0 %collective-permute-start.23 = (f32[3,34,1,256]{3,1,2,0:T(8,128)S(1)}, f32[3,34,1,256]{3,1,2,0:T(8,128)S(1)}, u32[]{:S(2)}, u32[]{:S(2)}) collective-permute-start(f32[3,34,1,256]{3,1,2,0:T(8,128)S(1)} %copy.92), channel_id=1, source_target_pairs={{0,2},{2,4},{4,6},{1,3},{3,5},{5,7},{8,10},{10,12},{12,14},{9,11},... | collective-permute-start | bytes 313352 | tf_op jit(solution)/shard_map/ppermute | solution.py:25
  262.8 5.5 %collective-permute-done.34 = f32[3,33,1,256]{3,1,2,0:T(8,128)S(1)} collective-permute-done((f32[3,33,1,256]{3,1,2,0:T(8,128)S(1)}, f32[3,33,1,256]{3,1,2,0:T(8,128)S(1)}, u32[]{:S(2)}, u32[]{:S(2)}) %collective-permute-start.34) | collective-permute-done | bytes 101408 | tf_op jit(solution)/shard_map/ppermute | solution.py:17
  296.5 14.3 %fusion.48 = f32[3,32,32,256]{3,2,1,0:T(8,128)S(1)} fusion(f32[3,32,32,256]{3,2,1,0:T(8,128)} %copy-done.5, f32[3,34,34,1]{3,2,1,0:T(8,128)} %copy.101, f32[3,34,1,256]{3,2,1,0:T(1,128)S(1)} %copy.95, f32[3,34,1,256]{3,2,1,0:T(1,128)S(1)} %copy.93, f32[3,1,32,256]{3,2,1,0:T(8,128)S(1)} %collective-permute-done.22, ...), kind=kLoop, calls=%fused_computation.92 | loop fusion | flops 21233664 | bytes 7773280 | tf_op jit(solution)/shard_map/add | solution.py:178
  314.8 4.7 select_maximum_fusion
  321.4 4.6 collective-permute-start.29
  339.6 4.5 collective-permute-start.31
  344.0 19.8 %fusion.118 = f32[1,32,32,256]{3,2,1,0:T(8,128)} fusion(f32[32,32,256]{2,1,0:T(8,128)S(1)} %copy-done, f32[32,32,256]{2,1,0:T(8,128)} %param.8, f32[34,34,258]{2,1,0:T(8,128)} %get-tuple-element.54, f32[34,34,258]{2,1,0:T(8,128)} %get-tuple-element.53, f32[34,34,258]{2,1,0:T(8,128)S(1)} %get-tuple-element.52), kind=kLoop, calls=%fused_computation.293 | loop fusion | flops 8126464 | bytes 28311552 | tf_op jit(solution)/shard_map/broadcast_in_dim | solution.py:200
  369.8 16.3 %fusion.130 = (f32[3,32,32,256]{3,2,1,0:T(8,128)S(1)}, f32[3,32,32,256]{3,2,1,0:T(8,128)}) fusion(f32[3,32,32,256]{3,2,1,0:T(8,128)} %copy-done.4, f32[3,32,32,256]{3,2,1,0:T(8,128)} %copy-done.6, f32[3,34,34,1]{3,2,1,0:T(8,128)} %copy.111, f32[3,34,1,256]{3,2,1,0:T(1,128)S(1)} %copy.105, f32[3,1,32,256]{3,2,1,0:T(8,128)S(1)} %collective-permute-done.28, ...), kind=kLoop, calls=%fused_computation.392 | loop fusion | flops 22020096 | bytes 14064736 | tf_op jit(solution)/shard_map/sub | solution.py:200
  393.1 5.9 %collective-permute-done.37 = f32[5,1,32,256]{3,2,1,0:T(8,128)S(1)} collective-permute-done((f32[5,1,32,256]{3,2,1,0:T(8,128)S(1)}, f32[5,1,32,256]{3,2,1,0:T(8,128)S(1)}, u32[]{:S(2)}, u32[]{:S(2)}) %collective-permute-start.37) | collective-permute-done | bytes 163872 | tf_op jit(solution)/shard_map/ppermute | solution.py:28
  399.2 4.3 collective-permute-start.38
  406.5 4.4 collective-permute-done.39
  424.8 4.3 collective-permute-start.40
  436.0 16.1 %pad_maximum_fusion = f32[5,34,34,258]{3,2,1,0:T(8,128)S(1)} fusion(f32[5,34,34,1]{3,2,1,0:T(8,128)} %copy.119, f32[5,34,1,256]{3,2,1,0:T(1,128)} %copy-done.23, f32[5,1,32,256]{3,2,1,0:T(8,128)S(1)} %collective-permute-done.37, f32[1,32,32,256]{3,2,1,0:T(8,128)} %fusion.118, f32[1,32,32,256]{3,2,1,0:T(8,128)} %bitcast.51, ...), kind=kLoop, calls=%fused_computation | loop fusion | flops 11929920 | bytes 11929920 | tf_op jit(solution)/shard_map/concatenate | solution.py:29
  456.4 6.0 %broadcast_compare_fusion.1 = (pred[32,32,256]{2,1,0:T(8,128)(4,1)}, f32[32,32,256]{2,1,0:T(8,128)}, pred[32,32,256]{2,1,0:T(8,128)(4,1)}, f32[32,32,256]{2,1,0:...) fusion(f32[34,34,258]{2,1,0:T(8,128)S(1)} %get-tuple-element.48, ...), kind=kLoop, calls=%fused_computation.329 | loop fusion | flops 5242880 | bytes 22020096 | tf_op jit(solution)/shard_map/gt | solution.py:107
  462.5 9.3 %fusion.83 = f32[2,32,32,256]{3,2,1,0:T(8,128)S(1)} fusion(f32[3,32,32,256]{3,2,1,0:T(8,128)S(1)} %get-tuple-element.37, f32[1,32,32,256]{3,2,1,0:T(8,128)S(1)} %bitcast.57, f32[5,34,34,1]{3,2,1,0:T(8,128)S(1)} %copy-done.17, f32[5,34,1,256]{3,2,1,0:T(1,128)S(1)} %copy-done.24, f32[5,34,1,256]{3,2,1,0:T(1,128)S(1)} %copy-done.22, ...), kind=kLoop, calls=%fused_computation.207 | loop fusion | flops 25690112 | bytes 15926432 | tf_op jit(solution)/shard_map/sub | solution.py:113
  (220 shorter events, 201.5 us)
Async XLA Ops:
  1.6 6.7 %collective-permute-start = (f32[2,1,32,256]{3,2,1,0:T(8,128)S(1)}, f32[2,1,32,256]{3,2,1,0:T(8,128)S(1)}, u32[]{:S(2)}, u32[]{:S(2)}) collective-permute-start(f32[2,1,32,256]{3,2,1,0:T(8,128)S(1)} %pad_maximum_fusion.146), channel_id=1, source_target_pairs={{0,8},{8,16},{16,24},{1,9},{9,17},{17,25},{2,10},{10,18},{18,26},{... | collective-permute-start | bytes 196616 | tf_op jit(solution)/shard_map/ppermute | solution.py:17
  26.7 6.8 %collective-permute-start.3 = (f32[3,1,32,256]{3,2,1,0:T(8,128)S(1)}, f32[3,1,32,256]{3,2,1,0:T(8,128)S(1)}, u32[]{:S(2)}, u32[]{:S(2)}) collective-permute-start(f32[3,1,32,256]{3,2,1,0:T(8,128)S(1)} %get-tuple-element.87), channel_id=1, source_target_pairs={{0,8},{8,16},{16,24},{1,9},{9,17},{17,25},{2,10},{10,18},{18,26},{... | collective-permute-start | bytes 294920 | tf_op jit(solution)/shard_map/ppermute | solution.py:25
  31.0 7.5 %collective-permute-start.4 = (f32[3,1,32,256]{3,2,1,0:T(8,128)S(1)}, f32[3,1,32,256]{3,2,1,0:T(8,128)S(1)}, u32[]{:S(2)}, u32[]{:S(2)}) collective-permute-start(f32[3,1,32,256]{3,2,1,0:T(8,128)S(1)} %get-tuple-element.88), channel_id=1, source_target_pairs={{8,0},{16,8},{24,16},{9,1},{17,9},{25,17},{10,2},{18,10},{26,18},{... | collective-permute-start | bytes 294920 | tf_op jit(solution)/shard_map/ppermute | solution.py:28
  42.9 6.6 %collective-permute-start.6 = (f32[3,34,1,256]{3,2,1,0:T(1,128)S(1)}, f32[3,34,1,256]{3,2,1,0:T(1,128)S(1)}, u32[]{:S(2)}, u32[]{:S(2)}) collective-permute-start(f32[3,34,1,256]{3,2,1,0:T(1,128)S(1)} %get-tuple-element.78), channel_id=1, source_target_pairs={{2,0},{4,2},{6,4},{3,1},{5,3},{7,5},{10,8},{12,10},{14,12},{11,9},... | collective-permute-start | bytes 313352 | tf_op jit(solution)/shard_map/ppermute | solution.py:28
  59.1 11.0 %collective-permute-start.8 = (f32[3,34,34,1]{2,3,1,0:T(1,128)}, f32[3,34,34,1]{2,3,1,0:T(1,128)}, u32[]{:S(2)}, u32[]{:S(2)}) collective-permute-start(f32[3,34,34,1]{2,3,1,0:T(1,128)} %copy.75), channel_id=1, source_target_pairs={{1,0},{3,2},{5,4},{7,6},{9,8},{11,10},{13,12},{15,14},{17,16},{19,... | collective-permute-start | bytes 41624 | tf_op jit(solution)/shard_map/ppermute | solution.py:28
  60.4 6.6 %collective-permute-start.7 = (f32[3,34,34,1]{2,3,1,0:T(1,128)}, f32[3,34,34,1]{2,3,1,0:T(1,128)}, u32[]{:S(2)}, u32[]{:S(2)}) collective-permute-start(f32[3,34,34,1]{2,3,1,0:T(1,128)} %copy.73), channel_id=1, source_target_pairs={{0,1},{2,3},{4,5},{6,7},{8,9},{10,11},{12,13},{14,15},{16,17},{18,... | collective-permute-start | bytes 41624 | tf_op jit(solution)/shard_map/ppermute | solution.py:25
  88.0 6.6 %collective-permute-start.9 = (f32[3,1,32,256]{3,2,1,0:T(8,128)S(1)}, f32[3,1,32,256]{3,2,1,0:T(8,128)S(1)}, u32[]{:S(2)}, u32[]{:S(2)}) collective-permute-start(f32[3,1,32,256]{3,2,1,0:T(8,128)S(1)} %get-tuple-element.85), channel_id=1, source_target_pairs={{0,8},{8,16},{16,24},{1,9},{9,17},{17,25},{2,10},{10,18},{18,26},{... | collective-permute-start | bytes 294920 | tf_op jit(solution)/shard_map/ppermute | solution.py:25
  102.5 6.6 %collective-permute-start.12 = (f32[3,34,1,256]{3,2,1,0:T(1,128)S(1)}, f32[3,34,1,256]{3,2,1,0:T(1,128)S(1)}, u32[]{:S(2)}, u32[]{:S(2)}) collective-permute-start(f32[3,34,1,256]{3,2,1,0:T(1,128)S(1)} %get-tuple-element.76), channel_id=1, source_target_pairs={{2,0},{4,2},{6,4},{3,1},{5,3},{7,5},{10,8},{12,10},{14,12},{11,9},... | collective-permute-start | bytes 313352 | tf_op jit(solution)/shard_map/ppermute | solution.py:28
  118.5 9.6 %collective-permute-start.14 = (f32[3,34,34,1]{2,3,1,0:T(1,128)}, f32[3,34,34,1]{2,3,1,0:T(1,128)}, u32[]{:S(2)}, u32[]{:S(2)}) collective-permute-start(f32[3,34,34,1]{2,3,1,0:T(1,128)} %copy.79), channel_id=1, source_target_pairs={{1,0},{3,2},{5,4},{7,6},{9,8},{11,10},{13,12},{15,14},{17,16},{19,... | collective-permute-start | bytes 41624 | tf_op jit(solution)/shard_map/ppermute | solution.py:28
  195.9 7.5 %collective-permute-start.16 = (f32[3,1,32,256]{3,2,1,0:T(8,128)S(1)}, f32[3,1,32,256]{3,2,1,0:T(8,128)S(1)}, u32[]{:S(2)}, u32[]{:S(2)}) collective-permute-start(f32[3,1,32,256]{3,2,1,0:T(8,128)S(1)} %get-tuple-element.84), channel_id=1, source_target_pairs={{8,0},{16,8},{24,16},{9,1},{17,9},{25,17},{10,2},{18,10},{26,18},{... | collective-permute-start | bytes 294920 | tf_op jit(solution)/shard_map/ppermute | solution.py:28
  203.6 6.8 %collective-permute-start.18 = (f32[3,34,1,256]{3,1,2,0:T(8,128)S(1)}, f32[3,34,1,256]{3,1,2,0:T(8,128)S(1)}, u32[]{:S(2)}, u32[]{:S(2)}) collective-permute-start(f32[3,34,1,256]{3,1,2,0:T(8,128)S(1)} %copy.84), channel_id=1, source_target_pairs={{2,0},{4,2},{6,4},{3,1},{5,3},{7,5},{10,8},{12,10},{14,12},{11,9},... | collective-permute-start | bytes 313352 | tf_op jit(solution)/shard_map/ppermute | solution.py:28
  204.9 7.0 %collective-permute-start.17 = (f32[3,34,1,256]{3,1,2,0:T(8,128)S(1)}, f32[3,34,1,256]{3,1,2,0:T(8,128)S(1)}, u32[]{:S(2)}, u32[]{:S(2)}) collective-permute-start(f32[3,34,1,256]{3,1,2,0:T(8,128)S(1)} %copy.82), channel_id=1, source_target_pairs={{0,2},{2,4},{4,6},{1,3},{3,5},{5,7},{8,10},{10,12},{12,14},{9,11},... | collective-permute-start | bytes 313352 | tf_op jit(solution)/shard_map/ppermute | solution.py:25
  219.4 7.9 %collective-permute-start.20 = (f32[3,34,34,1]{2,1,3,0:T(8,128)}, f32[3,34,34,1]{2,1,3,0:T(8,128)S(1)}, u32[]{:S(2)}, u32[]{:S(2)}) collective-permute-start(f32[3,34,34,1]{2,1,3,0:T(8,128)} %copy.90), channel_id=1, source_target_pairs={{1,0},{3,2},{5,4},{7,6},{9,8},{11,10},{13,12},{15,14},{17,16},{19,... | collective-permute-start | bytes 41624 | tf_op jit(solution)/shard_map/ppermute | solution.py:28
  243.7 7.0 %collective-permute-start.21 = (f32[3,1,32,256]{3,2,1,0:T(8,128)S(1)}, f32[3,1,32,256]{3,2,1,0:T(8,128)S(1)}, u32[]{:S(2)}, u32[]{:S(2)}) collective-permute-start(f32[3,1,32,256]{3,2,1,0:T(8,128)S(1)} %get-tuple-element.81), channel_id=1, source_target_pairs={{0,8},{8,16},{16,24},{1,9},{9,17},{17,25},{2,10},{10,18},{18,26},{... | collective-permute-start | bytes 294920 | tf_op jit(solution)/shard_map/ppermute | solution.py:25
  248.1 6.8 %collective-permute-start.22 = (f32[3,1,32,256]{3,2,1,0:T(8,128)S(1)}, f32[3,1,32,256]{3,2,1,0:T(8,128)S(1)}, u32[]{:S(2)}, u32[]{:S(2)}) collective-permute-start(f32[3,1,32,256]{3,2,1,0:T(8,128)S(1)} %get-tuple-element.82), channel_id=1, source_target_pairs={{8,0},{16,8},{24,16},{9,1},{17,9},{25,17},{10,2},{18,10},{26,18},{... | collective-permute-start | bytes 294920 | tf_op jit(solution)/shard_map/ppermute | solution.py:28
  249.4 12.0 %collective-permute-start.33 = (f32[3,1,32,256]{3,2,1,0:T(8,128)S(1)}, f32[3,1,32,256]{3,2,1,0:T(8,128)S(1)}, u32[]{:S(2)}, u32[]{:S(2)}) collective-permute-start(f32[3,1,32,256]{3,2,1,0:T(8,128)S(1)} %slice.812), channel_id=1, source_target_pairs={{8,0},{16,8},{24,16},{9,1},{17,9},{25,17},{10,2},{18,10},{26,18},{... | collective-permute-start | bytes 294920 | tf_op jit(solution)/shard_map/ppermute | solution.py:17
  255.1 13.3 %collective-permute-start.24 = (f32[3,34,1,256]{3,1,2,0:T(8,128)S(1)}, f32[3,34,1,256]{3,1,2,0:T(8,128)S(1)}, u32[]{:S(2)}, u32[]{:S(2)}) collective-permute-start(f32[3,34,1,256]{3,1,2,0:T(8,128)S(1)} %copy.94), channel_id=1, source_target_pairs={{2,0},{4,2},{6,4},{3,1},{5,3},{7,5},{10,8},{12,10},{14,12},{11,9},... | collective-permute-start | bytes 313352 | tf_op jit(solution)/shard_map/ppermute | solution.py:28
  256.4 12.1 %collective-permute-start.23 = (f32[3,34,1,256]{3,1,2,0:T(8,128)S(1)}, f32[3,34,1,256]{3,1,2,0:T(8,128)S(1)}, u32[]{:S(2)}, u32[]{:S(2)}) collective-permute-start(f32[3,34,1,256]{3,1,2,0:T(8,128)S(1)} %copy.92), channel_id=1, source_target_pairs={{0,2},{2,4},{4,6},{1,3},{3,5},{5,7},{8,10},{10,12},{12,14},{9,11},... | collective-permute-start | bytes 313352 | tf_op jit(solution)/shard_map/ppermute | solution.py:25
  261.5 6.8 %collective-permute-start.34 = (f32[3,33,1,256]{3,1,2,0:T(8,128)S(1)}, f32[3,33,1,256]{3,1,2,0:T(8,128)S(1)}, u32[]{:S(2)}, u32[]{:S(2)}) collective-permute-start(f32[3,33,1,256]{3,1,2,0:T(8,128)S(1)} %copy.112), channel_id=1, source_target_pairs={{2,0},{4,2},{6,4},{3,1},{5,3},{7,5},{10,8},{12,10},{14,12},{11,9},... | collective-permute-start | bytes 304136 | tf_op jit(solution)/shard_map/ppermute | solution.py:17
  277.0 17.3 %collective-permute-start.26 = (f32[3,34,34,1]{2,1,3,0:T(8,128)S(1)}, f32[3,34,34,1]{2,1,3,0:T(8,128)S(1)}, u32[]{:S(2)}, u32[]{:S(2)}) collective-permute-start(f32[3,34,34,1]{2,1,3,0:T(8,128)S(1)} %copy.100), channel_id=1, source_target_pairs={{1,0},{3,2},{5,4},{7,6},{9,8},{11,10},{13,12},{15,14},{17,16},{19,... | collective-permute-start | bytes 41624 | tf_op jit(solution)/shard_map/ppermute | solution.py:28
  278.3 13.8 %collective-permute-start.25 = (f32[3,34,34,1]{2,1,3,0:T(8,128)S(1)}, f32[3,34,34,1]{2,1,3,0:T(8,128)S(1)}, u32[]{:S(2)}, u32[]{:S(2)}) collective-permute-start(f32[3,34,34,1]{2,1,3,0:T(8,128)S(1)} %copy.98), channel_id=1, source_target_pairs={{0,1},{2,3},{4,5},{6,7},{8,9},{10,11},{12,13},{14,15},{16,17},{18,... | collective-permute-start | bytes 41624 | tf_op jit(solution)/shard_map/ppermute | solution.py:25
  310.8 8.7 %collective-permute-start.27 = (f32[3,1,32,256]{3,2,1,0:T(8,128)S(1)}, f32[3,1,32,256]{3,2,1,0:T(8,128)S(1)}, u32[]{:S(2)}, u32[]{:S(2)}) collective-permute-start(f32[3,1,32,256]{3,2,1,0:T(8,128)S(1)} %get-tuple-element.79), channel_id=1, source_target_pairs={{0,8},{8,16},{16,24},{1,9},{9,17},{17,25},{2,10},{10,18},{18,26},{... | collective-permute-start | bytes 294920 | tf_op jit(solution)/shard_map/ppermute | solution.py:25
  320.1 8.2 %collective-permute-start.30 = (f32[3,34,1,256]{3,1,2,0:T(8,128)S(1)}, f32[3,34,1,256]{3,1,2,0:T(8,128)S(1)}, u32[]{:S(2)}, u32[]{:S(2)}) collective-permute-start(f32[3,34,1,256]{3,1,2,0:T(8,128)S(1)} %copy.104), channel_id=1, source_target_pairs={{2,0},{4,2},{6,4},{3,1},{5,3},{7,5},{10,8},{12,10},{14,12},{11,9},... | collective-permute-start | bytes 313352 | tf_op jit(solution)/shard_map/ppermute | solution.py:28
  321.4 7.0 %collective-permute-start.29 = (f32[3,34,1,256]{3,1,2,0:T(8,128)S(1)}, f32[3,34,1,256]{3,1,2,0:T(8,128)S(1)}, u32[]{:S(2)}, u32[]{:S(2)}) collective-permute-start(f32[3,34,1,256]{3,1,2,0:T(8,128)S(1)} %copy.102), channel_id=1, source_target_pairs={{0,2},{2,4},{4,6},{1,3},{3,5},{5,7},{8,10},{10,12},{12,14},{9,11},... | collective-permute-start | bytes 313352 | tf_op jit(solution)/shard_map/ppermute | solution.py:25
  338.3 28.6 %collective-permute-start.32 = (f32[3,34,34,1]{2,1,3,0:T(8,128)}, f32[3,34,34,1]{2,1,3,0:T(8,128)}, u32[]{:S(2)}, u32[]{:S(2)}) collective-permute-start(f32[3,34,34,1]{2,1,3,0:T(8,128)} %copy.110), channel_id=1, source_target_pairs={{1,0},{3,2},{5,4},{7,6},{9,8},{11,10},{13,12},{15,14},{17,16},{19,... | collective-permute-start | bytes 41624 | tf_op jit(solution)/shard_map/ppermute | solution.py:28
  339.6 24.3 %collective-permute-start.31 = (f32[3,34,34,1]{2,1,3,0:T(8,128)}, f32[3,34,34,1]{2,1,3,0:T(8,128)}, u32[]{:S(2)}, u32[]{:S(2)}) collective-permute-start(f32[3,34,34,1]{2,1,3,0:T(8,128)} %copy.108), channel_id=1, source_target_pairs={{0,1},{2,3},{4,5},{6,7},{8,9},{10,11},{12,13},{14,15},{16,17},{18,... | collective-permute-start | bytes 41624 | tf_op jit(solution)/shard_map/ppermute | solution.py:25
  386.2 6.9 %collective-permute-start.36 = (f32[5,1,32,256]{3,2,1,0:T(8,128)S(1)}, f32[5,1,32,256]{3,2,1,0:T(8,128)S(1)}, u32[]{:S(2)}, u32[]{:S(2)}) collective-permute-start(f32[5,1,32,256]{3,2,1,0:T(8,128)S(1)} %get-tuple-element.57), channel_id=1, source_target_pairs={{0,8},{8,16},{16,24},{1,9},{9,17},{17,25},{2,10},{10,18},{18,26},{... | collective-permute-start | bytes 491528 | tf_op jit(solution)/shard_map/ppermute | solution.py:25
  390.3 8.7 %collective-permute-start.37 = (f32[5,1,32,256]{3,2,1,0:T(8,128)S(1)}, f32[5,1,32,256]{3,2,1,0:T(8,128)S(1)}, u32[]{:S(2)}, u32[]{:S(2)}) collective-permute-start(f32[5,1,32,256]{3,2,1,0:T(8,128)S(1)} %get-tuple-element.58), channel_id=1, source_target_pairs={{8,0},{16,8},{24,16},{9,1},{17,9},{25,17},{10,2},{18,10},{26,18},{... | collective-permute-start | bytes 491528 | tf_op jit(solution)/shard_map/ppermute | solution.py:28
  399.2 7.2 %collective-permute-start.38 = (f32[5,34,1,256]{3,2,1,0:T(1,128)S(1)}, f32[5,34,1,256]{3,2,1,0:T(1,128)S(1)}, u32[]{:S(2)}, u32[]{:S(2)}) collective-permute-start(f32[5,34,1,256]{3,2,1,0:T(1,128)S(1)} %get-tuple-element.55), channel_id=1, source_target_pairs={{0,2},{2,4},{4,6},{1,3},{3,5},{5,7},{8,10},{10,12},{12,14},{9,11},... | collective-permute-start | bytes 522248 | tf_op jit(solution)/shard_map/ppermute | solution.py:25
  403.5 7.3 %collective-permute-start.39 = (f32[5,34,1,256]{3,2,1,0:T(1,128)S(1)}, f32[5,34,1,256]{3,2,1,0:T(1,128)S(1)}, u32[]{:S(2)}, u32[]{:S(2)}) collective-permute-start(f32[5,34,1,256]{3,2,1,0:T(1,128)S(1)} %get-tuple-element.56), channel_id=1, source_target_pairs={{2,0},{4,2},{6,4},{3,1},{5,3},{7,5},{10,8},{12,10},{14,12},{11,9},... | collective-permute-start | bytes 522248 | tf_op jit(solution)/shard_map/ppermute | solution.py:28
  419.8 9.3 %collective-permute-start.41 = (f32[5,34,34,1]{2,3,1,0:T(1,128)}, f32[5,34,34,1]{2,3,1,0:T(1,128)}, u32[]{:S(2)}, u32[]{:S(2)}) collective-permute-start(f32[5,34,34,1]{2,3,1,0:T(1,128)} %copy.117), channel_id=1, source_target_pairs={{1,0},{3,2},{5,4},{7,6},{9,8},{11,10},{13,12},{15,14},{17,16},{19,... | collective-permute-start | bytes 69368 | tf_op jit(solution)/shard_map/ppermute | solution.py:28
  424.8 7.7 %collective-permute-start.40 = (f32[5,34,34,1]{2,3,1,0:T(1,128)}, f32[5,34,34,1]{2,3,1,0:T(1,128)}, u32[]{:S(2)}, u32[]{:S(2)}) collective-permute-start(f32[5,34,34,1]{2,3,1,0:T(1,128)} %copy.116), channel_id=1, source_target_pairs={{0,1},{2,3},{4,5},{6,7},{8,9},{10,11},{12,13},{14,15},{16,17},{18,... | collective-permute-start | bytes 69368 | tf_op jit(solution)/shard_map/ppermute | solution.py:25
  (38 other events, 486.1 us)

commit v2 on v1

v2 whole, which is shorter than its diff:
```python
import functools

import jax
import jax.numpy as jnp
from jax import lax
from jax.experimental import pallas as pl
from jax.experimental.pallas import tpu as pltpu
from jax.sharding import PartitionSpec as P

SWEEPS = 3
TIME_STEP = 0.6
RELAX_RATE = 0.8
CONSISTENT = 0.2

LANES = 128
ROWS = 8
MOMENTS = 6
NARROW = 2
WIDE = SWEEPS + 2
VMEM_BYTES = 62 * 2**20


class Plan:
    def __init__(self, groups, shape):
        self.groups = groups
        self.x, self.y, self.z = shape
        self.tiles = self.z // LANES
        self.low = max(low for _, low, _ in groups)
        self.high = max(high for _, _, high in groups)
        self.planes = self.low + self.x + self.high
        self.rows = self.y + 2 * ROWS
        self.fields = []
        low_at = high_at = lane_at = 0
        for group, (count, low, high) in enumerate(groups):
            for component in range(count):
                self.fields.append(
                    (group, component, low, high, low_at, high_at, lane_at + low)
                )
                low_at += low
                high_at += high
                lane_at += low + high
        assert lane_at <= LANES
        self.packed_low_at, self.packed_high_at = low_at, high_at
        self.low_rows = low_at + -(-self.low // self.tiles)
        self.high_rows = high_at + -(-self.high // self.tiles)

    def folded(self, k, at):
        return at + k // self.tiles, (k % self.tiles) * LANES


def round_up(value, step):
    return -(-value // step) * step


def from_behind(x, axis):
    count = lax.axis_size(axis)
    return lax.ppermute(x, axis, [(i, i + 1) for i in range(count - 1)])


def from_ahead(x, axis):
    count = lax.axis_size(axis)
    return lax.ppermute(x, axis, [(i + 1, i) for i in range(count - 1)])


def lane_index(shape):
    return lax.broadcasted_iota(jnp.int32, shape, len(shape) - 1)


def pack_lanes(plan, arrays):
    half = LANES // 2

    def kernel(*refs):
        out = refs[-1]
        lane = lane_index((plan.y, LANES))
        in_low_half = lane < half

        def plane(x, _):
            packed = jnp.zeros((plan.y, LANES), jnp.float32)
            for group, component, low, high, _, _, start in plan.fields:
                first, last = refs[2 * group], refs[2 * group + 1]
                edge = jnp.where(in_low_half, first[component, x], last[component, x])
                moved = pltpu.roll(edge, start, 1)
                packed = jnp.where((lane >= start - low) & (lane < start + high), moved, packed)
            out[x] = packed
            return 0

        lax.fori_loop(0, plan.x, plane, 0)

    specs, operands = [], []
    for (count, _, _), array in zip(plan.groups, arrays):
        block = (count, plan.x, plan.y, LANES)
        specs.append(pl.BlockSpec(block, lambda i: (0, 0, 0, 0)))
        specs.append(pl.BlockSpec(block, lambda i: (0, 0, 0, plan.tiles - 1)))
        operands += [array, array]
    return pl.pallas_call(
        kernel,
        grid=(1,),
        in_specs=specs,
        out_specs=pl.BlockSpec((plan.x, plan.y, LANES), lambda i: (0, 0, 0)),
        out_shape=jax.ShapeDtypeStruct((plan.x, plan.y, LANES), jnp.float32),
        compiler_params=pltpu.CompilerParams(vmem_limit_bytes=VMEM_BYTES),
        name="pack_lanes",
    )(*operands)


def exchange_lanes(plan, packed):
    lane = lane_index((1, 1, LANES))
    is_low = functools.reduce(
        jnp.logical_or,
        [(lane >= start - low) & (lane < start) for _, _, low, _, _, _, start in plan.fields],
    )
    count = lax.axis_size("bz")
    if count == 2:
        got = lax.ppermute(packed, "bz", [(0, 1), (1, 0)])
        return jnp.where(is_low == (lax.axis_index("bz") == 1), got, 0.0)
    return jnp.where(is_low, from_behind(packed, "bz"), from_ahead(packed, "bz"))


def fold_planes(plan, planes):
    count = round_up(planes.shape[0], plan.tiles)
    planes = jnp.pad(planes, ((0, count - planes.shape[0]), (0, 0), (0, 0)))
    return jnp.concatenate([planes[t :: plan.tiles] for t in range(plan.tiles)], axis=-1)


def exchange_planes(plan, arrays, packed):
    up, down = [], []
    for (count, low, high), array in zip(plan.groups, arrays):
        up.append(array[:, plan.x - low :].reshape(count * low, plan.y, plan.z))
        down.append(array[:, :high].reshape(count * high, plan.y, plan.z))
    up.append(fold_planes(plan, packed[plan.x - plan.low :]))
    down.append(fold_planes(plan, packed[: plan.high]))
    return (
        from_behind(jnp.concatenate(up, axis=0), "bx"),
        from_ahead(jnp.concatenate(down, axis=0), "bx"),
    )


def pack_rows(plan, arrays, packed, below, above):
    groups = len(plan.groups)

    def kernel(*refs):
        own = refs[: 2 * groups]
        packed_first, packed_last, below_first, below_last, above_first, above_last = refs[
            2 * groups : 2 * groups + 6
        ]
        up, down = refs[-2:]
        up[...] = jnp.zeros(up.shape, jnp.float32)
        down[...] = jnp.zeros(down.shape, jnp.float32)

        def put(plane, field, first, last):
            _, _, low, high, low_at, high_at, _ = field
            up[plane, low_at : low_at + low, :] = last[ROWS - low : ROWS, :]
            down[plane, high_at : high_at + high, :] = first[0:high, :]

        def put_packed(plane, first, last, at):
            for k in range(plan.low):
                row, lanes = plan.folded(k, plan.packed_low_at)
                source = ROWS - plan.low + k
                up[plane, row : row + 1, lanes : lanes + LANES] = last[
                    source : source + 1, at : at + LANES
                ]
            for k in range(plan.high):
                row, lanes = plan.folded(k, plan.packed_high_at)
                down[plane, row : row + 1, lanes : lanes + LANES] = first[
                    k : k + 1, at : at + LANES
                ]

        def own_plane(x, _):
            for field in plan.fields:
                group, component = field[:2]
                put(plan.low + x, field, own[2 * group].at[component, x], own[2 * group + 1].at[component, x])
            put_packed(plan.low + x, packed_first.at[x], packed_last.at[x], 0)
            return 0

        lax.fori_loop(0, plan.x, own_plane, 0)
        for k in range(plan.low):
            for field in plan.fields:
                _, _, low, _, low_at, _, _ = field
                skipped = plan.low - low
                if k >= skipped:
                    source = low_at + k - skipped
                    put(k, field, below_first.at[source], below_last.at[source])
            source, lanes = plan.folded(k, plan.packed_low_at)
            put_packed(k, below_first.at[source], below_last.at[source], lanes)
        for k in range(plan.high):
            for field in plan.fields:
                _, _, _, high, _, high_at, _ = field
                if k < high:
                    source = high_at + k
                    put(plan.low + plan.x + k, field, above_first.at[source], above_last.at[source])
            source, lanes = plan.folded(k, plan.packed_high_at)
            put_packed(plan.low + plan.x + k, above_first.at[source], above_last.at[source], lanes)

    last = plan.y // ROWS - 1
    specs, operands = [], []
    for (count, _, _), array in zip(plan.groups, arrays):
        block = (count, plan.x, ROWS, plan.z)
        specs.append(pl.BlockSpec(block, lambda i: (0, 0, 0, 0)))
        specs.append(pl.BlockSpec(block, lambda i: (0, 0, last, 0)))
        operands += [array, array]
    for array in (packed, below, above):
        block = (array.shape[0], ROWS, array.shape[2])
        specs.append(pl.BlockSpec(block, lambda i: (0, 0, 0)))
        specs.append(pl.BlockSpec(block, lambda i: (0, last, 0)))
        operands += [array, array]
    shapes = [
        (plan.planes, round_up(rows, ROWS), plan.z) for rows in (plan.low_rows, plan.high_rows)
    ]
    return pl.pallas_call(
        kernel,
        grid=(1,),
        in_specs=specs,
        out_specs=[pl.BlockSpec(shape, lambda i: (0, 0, 0)) for shape in shapes],
        out_shape=[jax.ShapeDtypeStruct(shape, jnp.float32) for shape in shapes],
        compiler_params=pltpu.CompilerParams(vmem_limit_bytes=VMEM_BYTES),
        name="pack_rows",
    )(*operands)


def exchange(plan, arrays):
    packed = exchange_lanes(plan, pack_lanes(plan, arrays))
    below, above = exchange_planes(plan, arrays, packed)
    up, down = pack_rows(plan, arrays, packed, below, above)
    return packed, below, above, from_behind(up, "by"), from_ahead(down, "by")


def assemble(plan, arrays, messages, extended, packed_ext, semaphores):
    packed, below, above, left, right = messages
    copies = []

    def copy(source, target):
        copies.append(
            pltpu.make_async_copy(source, target, semaphores.at[len(copies)])
        )
        copies[-1].start()

    own_rows = pl.ds(ROWS, plan.y)
    own_planes = pl.ds(plan.low, plan.x)
    for group, component, low, high, low_at, high_at, _ in plan.fields:
        target = extended[group].at[component]
        for t in range(plan.tiles):
            lanes = pl.ds(t * LANES, LANES)
            copy(arrays[group].at[component, :, :, lanes], target.at[own_planes, t, own_rows, :])
            copy(
                below.at[pl.ds(low_at, low), :, lanes],
                target.at[pl.ds(plan.low - low, low), t, own_rows, :],
            )
            copy(
                above.at[pl.ds(high_at, high), :, lanes],
                target.at[pl.ds(plan.low + plan.x, high), t, own_rows, :],
            )
    copy(packed, packed_ext.at[own_planes, own_rows, :])
    for k in range(plan.low):
        source, lanes = plan.folded(k, plan.packed_low_at)
        copy(below.at[source, :, pl.ds(lanes, LANES)], packed_ext.at[k, own_rows, :])
    for k in range(plan.high):
        source, lanes = plan.folded(k, plan.packed_high_at)
        copy(
            above.at[source, :, pl.ds(lanes, LANES)],
            packed_ext.at[plan.low + plan.x + k, own_rows, :],
        )
    for one in copies:
        one.wait()

    top = ROWS + plan.y

    def plane(i, _):
        for group, component, low, high, low_at, high_at, _ in plan.fields:
            target = extended[group]
            for t in range(plan.tiles):
                lanes = slice(t * LANES, (t + 1) * LANES)
                target[component, i, t, ROWS - low : ROWS, :] = left[i, low_at : low_at + low, lanes]
                target[component, i, t, top : top + high, :] = right[
                    i, high_at : high_at + high, lanes
                ]
        for k in range(plan.low):
            row, lanes = plan.folded(k, plan.packed_low_at)
            to = ROWS - plan.low + k
            packed_ext[i, to : to + 1, :] = left[i, row : row + 1, lanes : lanes + LANES]
        for k in range(plan.high):
            row, lanes = plan.folded(k, plan.packed_high_at)
            packed_ext[i, top + k : top + k + 1, :] = right[i, row : row + 1, lanes : lanes + LANES]
        tile = packed_ext[i]
        for group, component, _, _, _, _, start in plan.fields:
            extended[group][component, i, plan.tiles] = pltpu.roll(tile, (LANES - start) % LANES, 1)
        return 0

    lax.fori_loop(0, plan.planes, plane, 0)


def assemble_copies(plan):
    return len(plan.fields) * plan.tiles * 3 + 1 + plan.low + plan.high


def load(ref, index, row):
    return [ref[(*index, t, pl.ds(row, ROWS), slice(None))] for t in range(ref.shape[-3])]


def store(ref, index, row, tiles):
    for t, tile in enumerate(tiles):
        ref[(*index, t, pl.ds(row, ROWS), slice(None))] = tile


def each(function, *tiles):
    return [function(*one) for one in zip(*tiles)]


def add(first, second):
    return each(lambda a, b: a + b, first, second)


def subtract(first, second):
    return each(lambda a, b: a - b, first, second)


def lane_below(tiles):
    lane = lane_index((ROWS, LANES))
    rolled = [pltpu.roll(tile, 1, 1) for tile in tiles]
    return [jnp.where(lane == 0, rolled[t - 1], rolled[t]) for t in range(len(tiles))]


def lane_above(tiles):
    lane = lane_index((ROWS, LANES))
    rolled = [pltpu.roll(tile, LANES - 1, 1) for tile in tiles]
    count = len(tiles)
    return [
        jnp.where(lane == LANES - 1, rolled[(t + 1) % count], rolled[t]) for t in range(count)
    ]


def chunks(first, last, body):
    count = -(-(last - first + 1) // ROWS)

    def one(j, _):
        body(jnp.minimum(first + j * ROWS, last - ROWS + 1))
        return 0

    lax.fori_loop(0, count, one, 0)


class Inside:
    def __init__(self, plan, flags):
        self.plan = plan
        self.flags = flags

    def tiles(self, row, scale):
        plan, flags = self.plan, self.flags
        rows = row + lax.broadcasted_iota(jnp.int32, (ROWS, LANES), 0)
        keep = jnp.where(rows < ROWS, flags[2], jnp.where(rows >= ROWS + plan.y, flags[3], 1.0))
        lane = lane_index((ROWS, LANES))
        edge = jnp.where(lane < LANES // 2, flags[5], flags[4])
        keep = scale * keep
        return [keep] * plan.tiles + [keep * edge]

    def plane(self, i):
        plan, flags = self.plan, self.flags
        return jnp.where(
            i < plan.low, flags[0], jnp.where(i >= plan.low + plan.x, flags[1], 1.0)
        )


def force_pass(density, energy, force, mass, inside, planes, rows):
    def chunk(row):
        keep = inside.tiles(row, 0.4 * 0.25)

        def slab(i):
            here, under = load(density, (0, i), row), load(density, (0, i), row - 1)
            p = each(lambda a, b: a * b, here, load(energy, (0, i), row))
            p_under = each(lambda a, b: a * b, under, load(energy, (0, i), row - 1))
            summed, stepped = add(p, p_under), subtract(p_under, p)
            weight = add(here, under)
            summed_z, stepped_z = lane_below(summed), lane_below(stepped)
            return (
                add(summed, summed_z),
                add(stepped, stepped_z),
                subtract(summed_z, summed),
                add(weight, lane_below(weight)),
            )

        def plane(i, before):
            now = slab(i)
            here = inside.plane(i)
            scale = [tile * here for tile in keep]
            for component in range(3):
                across = (subtract if component == 0 else add)(before[component], now[component])
                store(force, (component, i), row, each(lambda a, b: a * b, scale, across))
            store(
                mass,
                (0, i),
                row,
                each(lambda a, b: 0.125 * (a + b) + 6.0 * CONSISTENT, before[3], now[3]),
            )
            return now

        lax.fori_loop(planes[0], planes[1] + 1, plane, slab(planes[0] - 1))

    chunks(*rows, chunk)


def face_sum(ref, component, i, row, before, here, after):
    total = add(add(before, after), add(lane_below(here), lane_above(here)))
    return add(total, add(load(ref, (component, i), row - 1), load(ref, (component, i), row + 1)))


def stencil_pass(ref, planes, rows, setup, use):
    def chunk(row):
        given = setup(row)

        def plane(i, carried):
            before, here = carried
            after = [load(ref, (component, i + 1), row) for component in range(3)]
            sums = [
                face_sum(ref, component, i, row, before[component], here[component], after[component])
                for component in range(3)
            ]
            use(i, row, here, sums, given)
            return here, after

        first = [load(ref, (component, planes[0] - 1), row) for component in range(3)]
        second = [load(ref, (component, planes[0]), row) for component in range(3)]
        lax.fori_loop(planes[0], planes[1] + 1, plane, (first, second))

    chunks(*rows, chunk)


def whole_sum(tile):
    return jnp.sum(jnp.sum(tile, axis=0, keepdims=True), axis=1, keepdims=True)


def moments_kernel(plan, *refs):
    flags, density, energy, packed, below, above, left, right, out = refs[:9]
    density_ext, energy_ext, packed_ext, force, image, mass, semaphores = refs[9:]
    assemble(
        plan,
        [density, energy],
        (packed, below, above, left, right),
        [density_ext, energy_ext],
        packed_ext,
        semaphores,
    )
    inside = Inside(plan, flags)
    low, x, y = plan.low, plan.x, plan.y
    force_pass(
        density_ext,
        energy_ext,
        force,
        mass,
        inside,
        (low - 1, low + x + 1),
        (ROWS - 1, ROWS + y + 1),
    )

    def multiply(i, row, here, sums, keep):
        weight = load(mass, (0, i), row)
        scale = [tile * inside.plane(i) for tile in keep]
        for component in range(3):
            result = each(
                lambda m, a, k, s: m * a + k * s, weight, here[component], scale, sums[component]
            )
            store(image, (component, i), row, result)

    stencil_pass(
        force,
        (low, low + x),
        (ROWS, ROWS + y),
        lambda row: inside.tiles(row, CONSISTENT),
        multiply,
    )

    own = range(plan.tiles)
    nothing = jnp.zeros((ROWS, LANES), jnp.float32)

    def first_plane(n, sums):
        i, row = low + n // (y // ROWS), ROWS + (n % (y // ROWS)) * ROWS
        sums = list(sums)
        for component in range(3):
            f = load(force, (component, i), row)
            v = load(image, (component, i), row)
            for t in own:
                sums[component] = sums[component] + f[t] * f[t]
                sums[3 + component] = sums[3 + component] + f[t] * v[t]
        return tuple(sums)

    sums = lax.fori_loop(0, x * (y // ROWS), first_plane, (nothing,) * 6)
    sums = [whole_sum(one) for one in sums]
    square = sums[:3]
    shift = [
        jnp.where(square[c] > 0, sums[3 + c] / jnp.where(square[c] > 0, square[c], 1.0), 0.0)
        for c in range(3)
    ]

    def pair(component, i, row):
        f = load(force, (component, i), row)
        v = load(image, (component, i), row)
        return f, each(lambda a, b: a - shift[component] * b, v, f)

    def second_chunk(j, sums):
        row = ROWS + j * ROWS

        def plane(i, carried):
            here, sums = carried
            sums = list(sums)
            ahead = [pair(component, i + 1, row) for component in range(3)]
            weight = load(mass, (0, i), row)
            for component in range(3):
                f, w = here[component]
                f_next, w_next = ahead[component]
                f_up, w_up = pair(component, i, row + 1)
                f_high = add(add(f_next, f_up), lane_above(f))
                w_high = add(add(w_next, w_up), lane_above(w))
                for t in own:
                    at = 4 * component
                    heavy = weight[t] * w[t]
                    sums[at] = sums[at] + f[t] * w[t]
                    sums[at + 1] = sums[at + 1] + w[t] * w[t]
                    sums[at + 2] = sums[at + 2] + (
                        f[t] * heavy + CONSISTENT * (f[t] * w_high[t] + w[t] * f_high[t])
                    )
                    sums[at + 3] = sums[at + 3] + w[t] * (
                        heavy + (2.0 * CONSISTENT) * w_high[t]
                    )
            return ahead, tuple(sums)

        start = [pair(component, low, row) for component in range(3)]
        return lax.fori_loop(low, low + x, plane, (start, sums))[1]

    rest = lax.fori_loop(0, y // ROWS, second_chunk, (nothing,) * 12)
    lane = lane_index((1, LANES))
    line = jnp.zeros((1, LANES), jnp.float32)
    for c in range(3):
        values = [shift[c], square[c]] + [whole_sum(one) for one in rest[4 * c : 4 * c + 4]]
        for k, value in enumerate(values):
            line = jnp.where(lane == 3 * k + c, value, line)
    out[...] = line


def solve_weights(sums):
    rows = sums.shape[0]
    got = [sums if k == 0 else pltpu.roll(sums, LANES - 3 * k, 1) for k in range(MOMENTS)]
    c, p0, q1, q2, q3, q4 = got

    def total(value):
        return jnp.sum(value, axis=0, keepdims=True)

    norm_now = total(p0)
    alpha = norm_now / total(q1 + c * p0)
    a = 1.0 - alpha * c
    norm_next = total(a * a * p0 - 2.0 * a * alpha * q1 + alpha * alpha * q2)
    product = total(a * a * (q1 + c * p0) - a * alpha * (q3 + q2 + c * q1) + alpha * alpha * q4)
    ratio = norm_next / norm_now
    later = norm_next / (product - ratio * norm_next / alpha)
    lane = lane_index((1, LANES))

    def pick(value, component):
        return jnp.sum(jnp.where(lane == component, value, 0.0), axis=1, keepdims=True)

    on_force, on_image = alpha + later * (1.0 + ratio), -later * alpha
    return [(pick(on_force, k), pick(on_image, k)) for k in range(3)]


def step_kernel(plan, *refs):
    flags, sums, density, energy, base, velocity, free = refs[:7]
    messages = refs[7:12]
    velocity_new, accel, relaxed, density_new, energy_new = refs[12:17]
    (
        density_ext,
        energy_ext,
        moved,
        speed,
        free_ext,
        packed_ext,
        force,
        mass,
        other,
        semaphores,
        out_semaphores,
    ) = refs[17:]
    assemble(
        plan,
        [density, energy, base, velocity, free],
        messages,
        [density_ext, energy_ext, moved, speed, free_ext],
        packed_ext,
        semaphores,
    )
    inside = Inside(plan, flags)
    low, x, y = plan.low, plan.x, plan.y
    weights = solve_weights(sums[...])
    reach = SWEEPS + 1
    force_pass(
        density_ext,
        energy_ext,
        force,
        mass,
        inside,
        (low - reach, low + x + reach),
        (ROWS - reach, ROWS + y + reach),
    )

    def advance(i, row, here, sums, keep):
        weight = load(mass, (0, i), row)
        scale = [tile * inside.plane(i) for tile in keep]
        for component in range(3):
            on_force, on_image = weights[component]
            result = each(
                lambda m, a, k, s: on_force * a + on_image * (m * a + k * s),
                weight,
                here[component],
                scale,
                sums[component],
            )
            store(other, (component, i), row, result)
            at = (component, i)
            store(speed, at, row, each(lambda v, a: v + TIME_STEP * a, load(speed, at, row), result))
            store(
                moved,
                at,
                row,
                each(lambda b, a: b + (TIME_STEP * TIME_STEP) * a, load(moved, at, row), result),
            )

    reach -= 1
    advanced = round_up(y + 2 * reach + 1, ROWS)
    stencil_pass(
        force,
        (low - reach, low + x + reach),
        (ROWS - reach, ROWS - reach + advanced - 1),
        lambda row: inside.tiles(row, CONSISTENT),
        advance,
    )

    out_copies = []

    def write(source, target, component, result=None):
        for t in range(plan.tiles):
            place = target if result is None else target.at[result]
            out_copies.append(
                pltpu.make_async_copy(
                    source.at[component, pl.ds(low, x), t, pl.ds(ROWS, y), :],
                    place.at[:, :, pl.ds(t * LANES, LANES)],
                    out_semaphores.at[len(out_copies)],
                )
            )
            out_copies[-1].start()

    for component in range(3):
        write(other, accel, component, component)
    accel_copies = len(out_copies)
    for component in range(3):
        write(speed, velocity_new, component, component)

    content = mass

    def content_chunk(row):
        def slab(i):
            under = [load(speed, (component, i), row) for component in range(3)]
            over = [load(speed, (component, i), row + 1) for component in range(3)]
            along_x = add(under[0], over[0])
            along_y = subtract(over[1], under[1])
            along_z = add(under[2], over[2])
            along_x = add(along_x, lane_above(along_x))
            along_y = add(along_y, lane_above(along_y))
            along_z = subtract(lane_above(along_z), along_z)
            return along_x, add(along_y, along_z)

        def plane(i, before):
            now = slab(i + 1)
            spread = add(subtract(now[0], before[0]), add(now[1], before[1]))
            held = load(energy_ext, (0, i), row)
            lagged = each(lambda e, s: e - (0.25 * 0.4 * TIME_STEP) * (e * s), held, spread)
            store(
                content, (0, i), row, each(lambda d, e: d * e, load(density_ext, (0, i), row), lagged)
            )
            return now

        lax.fori_loop(low - 1, low + x + 1, plane, slab(low - 1))

    chunks(ROWS - 1, ROWS + y, content_chunk)

    for one in out_copies[:accel_copies]:
        one.wait()
    source, target = moved, other
    for _ in range(SWEEPS):
        reach -= 1

        def relax(i, row, here, sums, given, target=target):
            rate = load(free_ext, (0, i), row)
            for component in range(3):
                result = each(
                    lambda r, s, f: r + f * (s * (1.0 / 6.0) - r),
                    here[component],
                    sums[component],
                    rate,
                )
                store(target, (component, i), row, result)

        stencil_pass(
            source,
            (low - reach, low + x + reach),
            (ROWS - reach, ROWS + y + reach),
            lambda row: None,
            relax,
        )
        source, target = target, (force if target is other else other)
    settled, free_buffer = source, target
    for component in range(3):
        write(settled, relaxed, component, component)

    quantities = (density_ext, content)

    def remap_chunk(row):
        def shift(component, i, at):
            return subtract(
                load(settled, (component, i), at), load(moved, (component, i), at)
            )

        def slab(i):
            x_here = add(shift(0, i, row), shift(0, i, row + 1))
            y_here, y_over = shift(1, i, row), shift(1, i, row + 1)
            z_here = add(shift(2, i, row), shift(2, i, row + 1))
            return (
                add(x_here, lane_above(x_here)),
                add(y_here, lane_above(y_here)),
                add(y_over, lane_above(y_over)),
                z_here,
                [load(one, (0, i), row) for one in quantities],
            )

        def flux(speeds, upper, lower):
            return each(lambda s, u, l: s * jnp.where(s > 0, u, l), speeds, upper, lower)

        def x_flux(speeds, upper, lower):
            return [flux(speeds, u, l) for u, l in zip(upper, lower)]

        def plane(i, carried):
            now, entering = carried
            ahead = slab(i + 1)
            leaving = x_flux(ahead[0], ahead[4], now[4])
            y_here, y_over, z_here = [add(now[k], ahead[k]) for k in (1, 2, 3)]
            for k, one in enumerate(quantities):
                held = now[4][k]
                under, over = load(one, (0, i), row - 1), load(one, (0, i), row + 1)
                through_z = flux(z_here, held, lane_below(held))
                change = subtract(leaving[k], entering[k])
                change = add(change, flux(y_over, over, held))
                change = subtract(change, flux(y_here, held, under))
                change = add(change, subtract(lane_above(through_z), through_z))
                result = each(lambda q, c: q + 0.25 * c, held, change)
                store(free_buffer, (k, i), row, result[: plan.tiles])
            return ahead, leaving

        start = slab(low)
        before = [load(one, (0, low - 1), row) for one in quantities]
        lax.fori_loop(low, low + x, plane, (start, x_flux(start[0], start[4], before)))

    chunks(ROWS, ROWS + y - 1, remap_chunk)
    write(free_buffer, density_new, 0)
    write(free_buffer, energy_new, 1)
    for one in out_copies[accel_copies:]:
        one.wait()


def gather_lines(line):
    for axis in ("bz", "by", "bx"):
        count = lax.axis_size(axis)
        if count & (count - 1):
            line = lax.all_gather(line, axis, axis=0, tiled=True)
            continue
        step = 1
        while step < count:
            got = lax.ppermute(line, axis, [(i, i ^ step) for i in range(count)])
            later = (lax.axis_index(axis) // step) % 2 == 1
            line = jnp.concatenate([jnp.where(later, got, line), jnp.where(later, line, got)])
            step *= 2
    return line


def any_space():
    return pl.BlockSpec(memory_space=pl.ANY)


def in_vmem():
    return pl.BlockSpec(memory_space=pltpu.VMEM)


def in_smem():
    return pl.BlockSpec(memory_space=pltpu.SMEM)


def extended_scratch(plan, count):
    return pltpu.VMEM((count, plan.planes, plan.tiles + 1, plan.rows, LANES), jnp.float32)


def message_specs():
    return [any_space()] * 3 + [in_vmem()] * 2


def on_device(position, velocity, density, energy, pinned):
    shape = density.shape
    density, energy = density[None], energy[None]
    flags = jnp.stack(
        [
            jnp.float32(limit)
            for axis in ("bx", "by", "bz")
            for limit in (
                lax.axis_index(axis) > 0,
                lax.axis_index(axis) < lax.axis_size(axis) - 1,
            )
        ]
    )

    narrow = Plan([(1, NARROW, NARROW)] * 2, shape)
    line = pl.pallas_call(
        functools.partial(moments_kernel, narrow),
        in_specs=[in_smem()] + [any_space()] * 2 + message_specs(),
        out_specs=in_vmem(),
        out_shape=jax.ShapeDtypeStruct((1, LANES), jnp.float32),
        scratch_shapes=[
            extended_scratch(narrow, 1),
            extended_scratch(narrow, 1),
            pltpu.VMEM((narrow.planes, narrow.rows, LANES), jnp.float32),
            extended_scratch(narrow, 3),
            extended_scratch(narrow, 3),
            extended_scratch(narrow, 1),
            pltpu.SemaphoreType.DMA((assemble_copies(narrow),)),
        ],
        compiler_params=pltpu.CompilerParams(vmem_limit_bytes=VMEM_BYTES),
        name="moments",
    )(flags, density, energy, *exchange(narrow, [density, energy]))

    base = position + TIME_STEP * velocity
    free = (RELAX_RATE * (1.0 - pinned.astype(jnp.float32)))[None]
    wide = Plan(
        [
            (1, WIDE, WIDE),
            (1, WIDE, WIDE),
            (3, SWEEPS, SWEEPS + 1),
            (3, 1, 2),
            (1, SWEEPS - 1, SWEEPS),
        ],
        shape,
    )
    arrays = [density, energy, base, velocity, free]
    messages = exchange(wide, arrays)
    nodes = jax.ShapeDtypeStruct((3, *shape), jnp.float32)
    cells = jax.ShapeDtypeStruct(shape, jnp.float32)
    return pl.pallas_call(
        functools.partial(step_kernel, wide),
        in_specs=[in_smem(), in_vmem()] + [any_space()] * 5 + message_specs(),
        out_specs=[any_space()] * 5,
        out_shape=[nodes, nodes, nodes, cells, cells],
        scratch_shapes=[
            extended_scratch(wide, 1),
            extended_scratch(wide, 1),
            extended_scratch(wide, 3),
            extended_scratch(wide, 3),
            extended_scratch(wide, 1),
            pltpu.VMEM((wide.planes, wide.rows, LANES), jnp.float32),
            extended_scratch(wide, 3),
            extended_scratch(wide, 1),
            extended_scratch(wide, 3),
            pltpu.SemaphoreType.DMA((assemble_copies(wide),)),
            pltpu.SemaphoreType.DMA((11 * wide.tiles,)),
        ],
        compiler_params=pltpu.CompilerParams(vmem_limit_bytes=VMEM_BYTES),
        name="step",
    )(flags, gather_lines(line), *arrays, *messages)


def solution(mesh):
    in_specs = (
        P(None, "bx", "by", "bz"),
        P(None, "bx", "by", "bz"),
        P("bx", "by", "bz"),
        P("bx", "by", "bz"),
        P("bx", "by", "bz"),
    )
    out_specs = (
        P(None, "bx", "by", "bz"),
        P(None, "bx", "by", "bz"),
        P(None, "bx", "by", "bz"),
        P("bx", "by", "bz"),
        P("bx", "by", "bz"),
    )
    return jax.shard_map(
        on_device, mesh=mesh, in_specs=in_specs, out_specs=out_specs, check_vma=False
    )
```

time: 482 us -> 349 us (0.72); the launches traced: 474 us -> 348 us
  Pallas kernels: 0 us -> 210 us
  other arithmetic: 167 us -> 11.3 us
  local copies, waits for them, and re-layouts: 99 us -> 15.5 us
  starting transfers between devices: 108 us -> 31.6 us
  blocking collectives: 38.7 us -> 0 us
  waiting for transfers between devices: 58.6 us -> 78.1 us
    pallas_call x0 -> x6, Pallas kernels: none -> 210 us  [the longest x1 139 us: on_device(): pl.pallas_call(functools.partial(step_kernel, wide), in_specs=[in_smem(),...]
    ppermute x42 -> x15, starting transfers between devices: 108 us -> 31.6 us  [the longest x4 20.1 us: from_behind(): return lax.ppermute(x, axis, [(i, i + 1) for i in range(count - 1)])]
    slice x33 -> x10, local copies, waits for them, and re-layouts: 54.6 us -> 0.05 us  [the longest x3 0.02 us: fold_planes(): planes[t::plan.tiles]]
    all_gather x1 -> x0, blocking collectives: 38.7 us -> none  [solve_weights(): got = lax.all_gather(sums, ('bx', 'by', 'bz'))]
    ppermute x21 -> x0, local copies, waits for them, and re-layouts: 37.8 us -> none  [the longest x9 17.3 us: padded(): lax.ppermute(lax.slice_in_dim(block, block.shape[dim] - width, None, axis...]
    concatenate x13 -> x9, other arithmetic: 34.4 us -> 2.04 us  [the longest x2 0.73 us: exchange_planes(): jnp.concatenate(up, axis=0)]
    add x4 -> x1, other arithmetic: 37.6 us -> 5.51 us  [on_device(): base = position + TIME_STEP * velocity]
    reduce_sum x4 -> x0, other arithmetic: 30 us -> none  [the longest x2 29.7 us: inner(): return jnp.sum(first * second, axis=(1, 2, 3), keepdims=True)]
  transfers between devices with their start and end apart: 42 -> 15, of which waited for: 23 -> 8; matrix products, arithmetic and copies ran while one was open for 13% -> 7% of each run, Pallas kernels for 0% -> 19%
where the time goes in v2:
time: 349 us; the launch traced here: 348 us
  Pallas kernels  210 us (60%)
  waiting for transfers between devices  78.1 us (22%)
  starting transfers between devices  31.6 us (9%)
  local copies, waits for them, and re-layouts  15.5 us (4%)
  other arithmetic  11.3 us (3%)
    pallas_call x1, Pallas kernels, on_device(): pl.pallas_call(functools.partial(step_kernel, wide), in_specs=[in_smem(),...  139 us
    pallas_call x1, Pallas kernels, on_device(): pl.pallas_call(functools.partial(moments_kernel, narrow), in_specs=[in_sm...  51 us
    ppermute x5, waiting for transfers between devices, gather_lines(): got = lax.ppermute(line, axis, [(i, i ^ step) for i in range(count)])  36.5 us
    ppermute x4, waiting for transfers between devices, from_ahead(): return lax.ppermute(x, axis, [(i + 1, i) for i in range(count - 1)])  29.6 us
    ppermute x4, starting transfers between devices, from_behind(): return lax.ppermute(x, axis, [(i, i + 1) for i in range(count - 1)])  20.1 us
    unnamed x26, local copies, waits for them, and re-layouts  14.4 us
    pallas_call x2, Pallas kernels, pack_lanes(): pl.pallas_call(kernel, grid=(1,), in_specs=specs, out_specs=pl.BlockSpec(...  12.8 us
    ppermute x4, waiting for transfers between devices, from_behind(): return lax.ppermute(x, axis, [(i, i + 1) for i in range(count - 1)])  12 us
  transfers between devices with their start and end apart: 15, of which 8 were waited for; matrix products, arithmetic and copies ran while one was open for 7% of the time, Pallas kernels for 19%

profile of v2, /device:TPU:0, one launch (start us, length us, event | category | flops | bytes accessed | tf_op | source)
XLA Modules:
  0.0 348.0 jit_solution(11680588141864599358)
XLA Ops:
  0.6 4.9 %pack_lanes.2 = f32[32,32,128]{2,1,0:T(8,128)} custom-call(f32[1,32,32,256]{3,2,1,0:T(8,128)} %bitcast.52, f32[1,32,32,256]{3,2,1,0:T(8,128)} %bitcast.53, f32[1,32,32,256]{3,2,1,0:T(8,128)} %bitcast.64, f32[1,32,32,256]{3,2,1,0:T(8,128)} %bitcast.65), custom_call_target="tpu_custom_call" | custom-call | tf_op jit(solution)/shard_map/pack_lanes/pallas_call | solution.py:95
  6.0 1.3 multiply_bitcast_fusion.refs_8_.refs_9_.refs_6_
  7.2 5.5 %multiply_add_fusion.refs_4_.refs_5_ = f32[3,32,32,256]{3,2,1,0:T(8,128)} fusion(f32[3,32,32,256]{3,2,1,0:T(8,128)} %param.5, f32[3,32,32,256]{3,2,1,0:T(8,128)} %refs_5_.1), kind=kLoop, calls=%fused_computation | loop fusion | flops 1572864 | bytes 9437184 | tf_op jit(solution)/shard_map/add | solution.py:831
  12.7 7.9 %pack_lanes.3 = f32[32,32,128]{2,1,0:T(8,128)} custom-call(f32[1,32,32,256]{3,2,1,0:T(8,128)} %bitcast.54, f32[1,32,32,256]{3,2,1,0:T(8,128)} %bitcast.55, f32[1,32,32,256]{3,2,1,0:T(8,128)} %bitcast.66, f32[1,32,32,256]{3,2,1,0:T(8,128)} %bitcast.67, f32[3,32,32,256]{3,2,1,0:T(8,128)} %multiply_add_fusion.refs_4_.refs_5_, ...), custom_call_target="tpu_custom_call" | custom-call | tf_op jit(solution)/shard_map/pack_lanes/pallas_call | solution.py:95
  20.7 1.7 fusion.1
  22.4 1.8 fusion
  25.0 1.5 bitcast_dynamic-update-slice_fusion
  26.5 1.5 fusion.5
  29.5 1.6 fusion.4
  32.8 5.8 %collective-permute-start.11 = (f32[27,32,256]{2,1,0:T(8,128)}, f32[27,32,256]{2,1,0:T(8,128)}, u32[]{:S(2)}, u32[]{:S(2)}) collective-permute-start(f32[27,32,256]{2,1,0:T(8,128)} %maximum_dynamic-update-slice_fusion), channel_id=1, source_target_pairs={{0,8},{8,16},{16,24},{1,9},{9,17},{17,25},{2,10},{10,18},{18,26},{... | collective-permute-start | bytes 2654216 | tf_op jit(solution)/shard_map/ppermute | solution.py:57
  39.3 1.3 collective-permute-start.12
  40.6 1.1 broadcast_select_fusion.1.refs_4_.refs_5_.refs_3_
  42.5 4.6 %collective-permute-start.1 = (f32[5,32,256]{2,1,0:T(8,128)S(1)}, f32[5,32,256]{2,1,0:T(8,128)S(1)}, u32[]{:S(2)}, u32[]{:S(2)}) collective-permute-start(f32[5,32,256]{2,1,0:T(8,128)S(1)} %maximum_maximum_fusion), channel_id=1, source_target_pairs={{0,8},{8,16},{16,24},{1,9},{9,17},{17,25},{2,10},{10,18},{18,26},{... | collective-permute-start | bytes 491528 | tf_op jit(solution)/shard_map/ppermute | solution.py:57
  47.1 1.3 collective-permute-start.2
  48.4 12.0 %collective-permute-done.1.refs_6_.refs_7_.refs_4_ = f32[5,32,256]{2,1,0:T(8,128)S(1)} collective-permute-done((f32[5,32,256]{2,1,0:T(8,128)S(1)}, f32[5,32,256]{2,1,0:T(8,128)S(1)}, u32[]{:S(2)}, u32[]{:S(2)}) %collective-permute-start.1) | collective-permute-done | bytes 163872 | tf_op jit(solution)/shard_map/ppermute | solution.py:57
  60.4 29.3 %collective-permute-done.2.refs_8_.refs_9_.refs_5_ = f32[5,32,256]{2,1,0:T(8,128)S(1)} collective-permute-done((f32[5,32,256]{2,1,0:T(8,128)S(1)}, f32[5,32,256]{2,1,0:T(8,128)S(1)}, u32[]{:S(2)}, u32[]{:S(2)}) %collective-permute-start.2) | collective-permute-done | bytes 163872 | tf_op jit(solution)/shard_map/ppermute | solution.py:62
  90.4 2.5 pack_rows.2
  92.9 3.5 %collective-permute-start.3 = (f32[36,8,256]{2,1,0:T(8,128)}, f32[36,8,256]{2,1,0:T(8,128)S(1)}, u32[]{:S(2)}, u32[]{:S(2)}) collective-permute-start(f32[36,8,256]{2,1,0:T(8,128)} %get-tuple-element.9), channel_id=1, source_target_pairs={{0,2},{2,4},{4,6},{1,3},{3,5},{5,7},{8,10},{10,12},{12,14},{9,11},... | collective-permute-start | bytes 884744 | tf_op jit(solution)/shard_map/ppermute | solution.py:57
  96.4 1.3 collective-permute-start.4
  98.8 5.5 %pack_rows.3 = (f32[42,32,256]{2,1,0:T(8,128)}, f32[42,40,256]{2,1,0:T(8,128)}) custom-call(f32[1,32,32,256]{3,2,1,0:T(8,128)} %bitcast.60, f32[1,32,32,256]{3,2,1,0:T(8,128)} %bitcast.61, f32[1,32,32,256]{3,2,1,0:T(8,128)} %bitcast.72, f32[1,32,32,256]{3,2,1,0:T(8,128)} %bitcast.73, f32[3,32,32,256]{3,2,1,0:T(8,128)} %multiply_add_fusion.refs_4_.refs_5_, ...), custom_call_target="tpu_custom_call" | custom-call | tf_op jit(solution)/shard_map/pack_rows/pallas_call | solution.py:209
  104.2 1.3 collective-permute-start.14
  106.9 51.0 %moments.1 = f32[1,128]{1,0:T(1,128)} custom-call(f32[6]{0:T(128)} %stack.36.refs_0_, f32[1,32,32,256]{3,2,1,0:T(8,128)} %bitcast.62, f32[1,32,32,256]{3,2,1,0:T(8,128)} %bitcast.74, f32[32,32,128]{2,1,0:T(8,128)} %copy-done.2, f32[5,32,256]{2,1,0:T(8,128)} %copy-done.4, f32[5,32,256]{2,1,0:T(8,128)} %copy-done.5, f32[36,8,256]{2,1,0:T(8,128)} %copy-done.7, ...), custom_call_target="tpu_custom_call" | custom-call | tf_op jit(solution)/shard_map/moments/pallas_call | solution.py:813
  158.0 1.2 collective-permute-done.5
  159.9 6.3 %collective-permute-start.13 = (f32[42,32,256]{2,1,0:T(8,128)}, f32[42,32,256]{2,1,0:T(8,128)}, u32[]{:S(2)}, u32[]{:S(2)}) collective-permute-start(f32[42,32,256]{2,1,0:T(8,128)} %get-tuple-element.11), channel_id=1, source_target_pairs={{0,2},{2,4},{4,6},{1,3},{3,5},{5,7},{8,10},{10,12},{12,14},{9,11},... | collective-permute-start | bytes 4128776 | tf_op jit(solution)/shard_map/ppermute | solution.py:57
  167.2 28.0 %collective-permute-done.6 = f32[2,128]{1,0:T(2,128)S(1)} collective-permute-done((f32[2,128]{1,0:T(2,128)S(1)}, f32[2,128]{1,0:T(2,128)S(1)}, u32[]{:S(2)}, u32[]{:S(2)}) %collective-permute-start.6) | collective-permute-done | bytes 1056 | tf_op jit(solution)/shard_map/ppermute | solution.py:771
  195.2 3.2 collective-permute-start.7
  198.4 1.6 collective-permute-done.7
  200.0 1.6 collective-permute-start.8
  201.5 2.1 collective-permute-done.8
  203.8 3.6 %collective-permute-done.9 = f32[16,128]{1,0:T(8,128)S(1)} collective-permute-done((f32[16,128]{1,0:T(8,128)S(1)}, f32[16,128]{1,0:T(8,128)S(1)}, u32[]{:S(2)}, u32[]{:S(2)}) %collective-permute-start.9) | collective-permute-done | bytes 8224 | tf_op jit(solution)/shard_map/ppermute | solution.py:771
  208.0 1.2 copy-done.3
  209.2 138.8 %step.1 = (f32[3,32,32,256]{3,2,1,0:T(8,128)}, f32[3,32,32,256]{3,2,1,0:T(8,128)}, f32[3,32,32,256]{3,2,1,0:T(8,128)}, f32[32,32,256]{2,1,0:T(8,128)}, f32[32,32,256]{2,1,0:T(8,128)}) custom-call(f32[6]{0:T(128)} %stack.36.refs_0_, f32[32,128]{1,0:T(8,128)} %pad_maximum_fusion.refs_1_, f32[1,32,32,256]{3,2,1,0:T(8,128)} %bitcast.63, ...), custom_call_target="tpu_custom_call" | custom-call | tf_op jit(solution)/shard_map/step/pallas_call | solution.py:847
  (64 shorter events, 11.5 us)
Async XLA Ops:
  0.6 5.3 %copy-start.6 = (s32[32,32,256]{2,1,0:T(8,128)S(1)}, s32[32,32,256]{2,1,0:T(8,128)}, u32[]{:S(2)}) copy-start(s32[32,32,256]{2,1,0:T(8,128)} %param.9) | copy-start | bytes 3145732
  5.5 35.1 %collective-permute-start = (f32[32,32,128]{2,1,0:T(8,128)}, f32[32,32,128]{2,1,0:T(8,128)}, u32[]{:S(2)}, u32[]{:S(2)}) collective-permute-start(f32[32,32,128]{2,1,0:T(8,128)} %pack_lanes.2), channel_id=1, source_target_pairs={{0,1},{1,0},{2,3},{3,2},{4,5},{5,4},{6,7},{7,6},{8,9},{9,8},{10,11... | collective-permute-start | bytes 1572872 | tf_op jit(solution)/shard_map/ppermute | solution.py:114
  20.6 11.4 %collective-permute-start.10 = (f32[32,32,128]{2,1,0:T(8,128)}, f32[32,32,128]{2,1,0:T(8,128)S(1)}, u32[]{:S(2)}, u32[]{:S(2)}) collective-permute-start(f32[32,32,128]{2,1,0:T(8,128)} %pack_lanes.3), channel_id=1, source_target_pairs={{0,1},{1,0},{2,3},{3,2},{4,5},{5,4},{6,7},{7,6},{8,9},{9,8},{10,11... | collective-permute-start | bytes 1572872 | tf_op jit(solution)/shard_map/ppermute | solution.py:114
  22.4 1.8 slice-start
  22.4 5.6 %slice-start.1 = ((f32[3,32,32,256]{3,2,1,0:T(8,128)}), f32[3,4,32,256]{3,2,1,0:T(8,128)S(1)}, s32[]{:S(2)}) async-start(f32[3,32,32,256]{3,2,1,0:T(8,128)} %multiply_add_fusion.refs_4_.refs_5_), calls=%async_computation.1 | async-start | bytes 786432 | tf_op jit(solution)/shard_map/slice | solution.py:129
  22.4 6.4 %slice-start.2 = ((f32[3,32,32,256]{3,2,1,0:T(8,128)}), f32[3,2,32,256]{3,2,1,0:T(8,128)S(1)}, s32[]{:S(2)}) async-start(f32[3,32,32,256]{3,2,1,0:T(8,128)} %refs_5_.1), calls=%async_computation.2 | async-start | bytes 393216 | tf_op jit(solution)/shard_map/slice | solution.py:129
  29.5 9.1 %copy-start.8 = (pred[6]{0:T(512)(128)(4,1)S(1)}, pred[6]{0:T(512)(128)(4,1)}, u32[]{:S(2)}) copy-start(pred[6]{0:T(512)(128)(4,1)} %constant.135.clone.1) | copy-start | bytes 22
  32.1 9.7 %copy-start.1 = (f32[32,32,128]{2,1,0:T(8,128)}, f32[32,32,128]{2,1,0:T(8,128)S(1)}, u32[]{:S(2)}) copy-start(f32[32,32,128]{2,1,0:T(8,128)S(1)} %broadcast_select_fusion.refs_10_.refs_11_.refs_7_) | copy-start | bytes 1572868
  32.8 64.9 %collective-permute-start.11 = (f32[27,32,256]{2,1,0:T(8,128)}, f32[27,32,256]{2,1,0:T(8,128)}, u32[]{:S(2)}, u32[]{:S(2)}) collective-permute-start(f32[27,32,256]{2,1,0:T(8,128)} %maximum_dynamic-update-slice_fusion), channel_id=1, source_target_pairs={{0,8},{8,16},{16,24},{1,9},{9,17},{17,25},{2,10},{10,18},{18,26},{... | collective-permute-start | bytes 2654216 | tf_op jit(solution)/shard_map/ppermute | solution.py:57
  39.3 58.4 %collective-permute-start.12 = (f32[34,32,256]{2,1,0:T(8,128)}, f32[34,32,256]{2,1,0:T(8,128)S(1)}, u32[]{:S(2)}, u32[]{:S(2)}) collective-permute-start(f32[34,32,256]{2,1,0:T(8,128)} %maximum_dynamic-update-slice_fusion.1), channel_id=1, source_target_pairs={{8,0},{16,8},{24,16},{9,1},{17,9},{25,17},{10,2},{18,10},{26,18},{... | collective-permute-start | bytes 3342344 | tf_op jit(solution)/shard_map/ppermute | solution.py:62
  41.7 0.8 copy-start.2
  42.5 17.9 %collective-permute-start.1 = (f32[5,32,256]{2,1,0:T(8,128)S(1)}, f32[5,32,256]{2,1,0:T(8,128)S(1)}, u32[]{:S(2)}, u32[]{:S(2)}) collective-permute-start(f32[5,32,256]{2,1,0:T(8,128)S(1)} %maximum_maximum_fusion), channel_id=1, source_target_pairs={{0,8},{8,16},{16,24},{1,9},{9,17},{17,25},{2,10},{10,18},{18,26},{... | collective-permute-start | bytes 491528 | tf_op jit(solution)/shard_map/ppermute | solution.py:57
  47.1 42.6 %collective-permute-start.2 = (f32[5,32,256]{2,1,0:T(8,128)S(1)}, f32[5,32,256]{2,1,0:T(8,128)S(1)}, u32[]{:S(2)}, u32[]{:S(2)}) collective-permute-start(f32[5,32,256]{2,1,0:T(8,128)S(1)} %maximum_maximum_fusion.1), channel_id=1, source_target_pairs={{8,0},{16,8},{24,16},{9,1},{17,9},{25,17},{10,2},{18,10},{26,18},{... | collective-permute-start | bytes 491528 | tf_op jit(solution)/shard_map/ppermute | solution.py:62
  60.4 29.3 %copy-start.4 = (f32[5,32,256]{2,1,0:T(8,128)}, f32[5,32,256]{2,1,0:T(8,128)S(1)}, u32[]{:S(2)}) copy-start(f32[5,32,256]{2,1,0:T(8,128)S(1)} %collective-permute-done.1.refs_6_.refs_7_.refs_4_) | copy-start | bytes 491524
  89.8 0.7 copy-start.5
  92.9 13.3 %collective-permute-start.3 = (f32[36,8,256]{2,1,0:T(8,128)}, f32[36,8,256]{2,1,0:T(8,128)S(1)}, u32[]{:S(2)}, u32[]{:S(2)}) collective-permute-start(f32[36,8,256]{2,1,0:T(8,128)} %get-tuple-element.9), channel_id=1, source_target_pairs={{0,2},{2,4},{4,6},{1,3},{3,5},{5,7},{8,10},{10,12},{12,14},{9,11},... | collective-permute-start | bytes 884744 | tf_op jit(solution)/shard_map/ppermute | solution.py:57
  96.4 10.0 %collective-permute-start.4 = (f32[36,8,256]{2,1,0:T(8,128)}, f32[36,8,256]{2,1,0:T(8,128)}, u32[]{:S(2)}, u32[]{:S(2)}) collective-permute-start(f32[36,8,256]{2,1,0:T(8,128)} %get-tuple-element.10), channel_id=1, source_target_pairs={{2,0},{4,2},{6,4},{3,1},{5,3},{7,5},{10,8},{12,10},{14,12},{11,9},... | collective-permute-start | bytes 884744 | tf_op jit(solution)/shard_map/ppermute | solution.py:62
  97.8 1.0 copy-start
  104.2 103.8 %collective-permute-start.14 = (f32[42,40,256]{2,1,0:T(8,128)}, f32[42,40,256]{2,1,0:T(8,128)S(1)}, u32[]{:S(2)}, u32[]{:S(2)}) collective-permute-start(f32[42,40,256]{2,1,0:T(8,128)} %get-tuple-element.12), channel_id=1, source_target_pairs={{2,0},{4,2},{6,4},{3,1},{5,3},{7,5},{10,8},{12,10},{14,12},{11,9},... | collective-permute-start | bytes 5160968 | tf_op jit(solution)/shard_map/ppermute | solution.py:62
  106.2 0.7 copy-start.7
  157.9 1.3 collective-permute-start.5
  159.9 48.1 %collective-permute-start.13 = (f32[42,32,256]{2,1,0:T(8,128)}, f32[42,32,256]{2,1,0:T(8,128)}, u32[]{:S(2)}, u32[]{:S(2)}) collective-permute-start(f32[42,32,256]{2,1,0:T(8,128)} %get-tuple-element.11), channel_id=1, source_target_pairs={{0,2},{2,4},{4,6},{1,3},{3,5},{5,7},{8,10},{10,12},{12,14},{9,11},... | collective-permute-start | bytes 4128776 | tf_op jit(solution)/shard_map/ppermute | solution.py:57
  166.2 29.0 %collective-permute-start.6 = (f32[2,128]{1,0:T(2,128)S(1)}, f32[2,128]{1,0:T(2,128)S(1)}, u32[]{:S(2)}, u32[]{:S(2)}) collective-permute-start(f32[2,128]{1,0:T(2,128)S(1)} %pad_maximum_fusion.4), channel_id=1, source_target_pairs={{0,2},{2,0},{4,6},{6,4},{1,3},{3,1},{5,7},{7,5},{8,10},{10,8},{12,... | collective-permute-start | bytes 3080 | tf_op jit(solution)/shard_map/ppermute | solution.py:771
  195.2 4.7 %collective-permute-start.7 = (f32[4,128]{1,0:T(4,128)S(1)}, f32[4,128]{1,0:T(4,128)S(1)}, u32[]{:S(2)}, u32[]{:S(2)}) collective-permute-start(f32[4,128]{1,0:T(4,128)S(1)} %pad_maximum_fusion.3), channel_id=1, source_target_pairs={{0,4},{2,6},{4,0},{6,2},{1,5},{3,7},{5,1},{7,3},{8,12},{10,14},{12... | collective-permute-start | bytes 6152 | tf_op jit(solution)/shard_map/ppermute | solution.py:771
  200.0 3.7 %collective-permute-start.8 = (f32[8,128]{1,0:T(8,128)S(1)}, f32[8,128]{1,0:T(8,128)S(1)}, u32[]{:S(2)}, u32[]{:S(2)}) collective-permute-start(f32[8,128]{1,0:T(8,128)S(1)} %pad_maximum_fusion.2), channel_id=1, source_target_pairs={{0,8},{8,0},{16,24},{24,16},{1,9},{9,1},{17,25},{25,17},{2,10},{10... | collective-permute-start | bytes 12296 | tf_op jit(solution)/shard_map/ppermute | solution.py:771
  203.7 3.7 %collective-permute-start.9 = (f32[16,128]{1,0:T(8,128)S(1)}, f32[16,128]{1,0:T(8,128)S(1)}, u32[]{:S(2)}, u32[]{:S(2)}) collective-permute-start(f32[16,128]{1,0:T(8,128)S(1)} %pad_maximum_fusion.1), channel_id=1, source_target_pairs={{0,16},{8,24},{16,0},{24,8},{1,17},{9,25},{17,1},{25,9},{2,18},{10... | collective-permute-start | bytes 24584 | tf_op jit(solution)/shard_map/ppermute | solution.py:771
  208.0 1.2 copy-start.3

commit v3 on v2

--- a/solution.py
+++ b/solution.py
@@ -14,14 +14,16 @@
 
 LANES = 128
 ROWS = 8
-MOMENTS = 6
+MOMENTS = 7
+UNROLL = 4
+POSITION, VELOCITY, PINNED = 2, 3, 4
 NARROW = 2
 WIDE = SWEEPS + 2
 VMEM_BYTES = 62 * 2**20
 
 
 class Plan:
-    def __init__(self, groups, shape):
+    def __init__(self, groups, shape, starts=None):
         self.groups = groups
         self.x, self.y, self.z = shape
         self.tiles = self.z // LANES
@@ -33,17 +35,24 @@
         low_at = high_at = lane_at = 0
         for group, (count, low, high) in enumerate(groups):
             for component in range(count):
-                self.fields.append(
-                    (group, component, low, high, low_at, high_at, lane_at + low)
-                )
+                start = lane_at + low if starts is None else starts[len(self.fields)]
+                self.fields.append((group, component, low, high, low_at, high_at, start))
                 low_at += low
                 high_at += high
                 lane_at += low + high
         assert lane_at <= LANES
+        self.starts = [field[-1] for field in self.fields]
         self.packed_low_at, self.packed_high_at = low_at, high_at
         self.low_rows = low_at + -(-self.low // self.tiles)
         self.high_rows = high_at + -(-self.high // self.tiles)
 
+    def value(self, group, component, get):
+        if group == POSITION:
+            return get(POSITION, component) + TIME_STEP * get(VELOCITY, component)
+        if group == PINNED:
+            return RELAX_RATE * (1.0 - get(PINNED, component).astype(jnp.float32))
+        return get(group, component)
+
     def folded(self, k, at):
         return at + k // self.tiles, (k % self.tiles) * LANES
 
@@ -60,6 +69,24 @@
 def from_ahead(x, axis):
     count = lax.axis_size(axis)
     return lax.ppermute(x, axis, [(i + 1, i) for i in range(count - 1)])
+
+
+def any_space():
+    return pl.BlockSpec(memory_space=pl.ANY)
+
+
+def in_vmem():
+    return pl.BlockSpec(memory_space=pltpu.VMEM)
+
+
+def in_smem():
+    return pl.BlockSpec(memory_space=pltpu.SMEM)
+
+
+def cost(microseconds):
+    return pl.CostEstimate(
+        flops=0, bytes_accessed=int(microseconds * 3.0e6), transcendentals=0
+    )
 
 
 def lane_index(shape):
@@ -75,11 +102,13 @@
         in_low_half = lane < half
 
         def plane(x, _):
+            def edge(group, component):
+                first, last = refs[2 * group], refs[2 * group + 1]
+                return jnp.where(in_low_half, first[component, x], last[component, x])
+
             packed = jnp.zeros((plan.y, LANES), jnp.float32)
             for group, component, low, high, _, _, start in plan.fields:
-                first, last = refs[2 * group], refs[2 * group + 1]
-                edge = jnp.where(in_low_half, first[component, x], last[component, x])
-                moved = pltpu.roll(edge, start, 1)
+                moved = pltpu.roll(plan.value(group, component, edge), start, 1)
                 packed = jnp.where((lane >= start - low) & (lane < start + high), moved, packed)
             out[x] = packed
             return 0
@@ -99,6 +128,7 @@
         out_specs=pl.BlockSpec((plan.x, plan.y, LANES), lambda i: (0, 0, 0)),
         out_shape=jax.ShapeDtypeStruct((plan.x, plan.y, LANES), jnp.float32),
         compiler_params=pltpu.CompilerParams(vmem_limit_bytes=VMEM_BYTES),
+        cost_estimate=cost(6),
         name="pack_lanes",
     )(*operands)
 
@@ -116,33 +146,77 @@
     return jnp.where(is_low, from_behind(packed, "bz"), from_ahead(packed, "bz"))
 
 
-def fold_planes(plan, planes):
-    count = round_up(planes.shape[0], plan.tiles)
-    planes = jnp.pad(planes, ((0, count - planes.shape[0]), (0, 0), (0, 0)))
-    return jnp.concatenate([planes[t :: plan.tiles] for t in range(plan.tiles)], axis=-1)
-
-
-def exchange_planes(plan, arrays, packed):
-    up, down = [], []
-    for (count, low, high), array in zip(plan.groups, arrays):
-        up.append(array[:, plan.x - low :].reshape(count * low, plan.y, plan.z))
-        down.append(array[:, :high].reshape(count * high, plan.y, plan.z))
-    up.append(fold_planes(plan, packed[plan.x - plan.low :]))
-    down.append(fold_planes(plan, packed[: plan.high]))
-    return (
-        from_behind(jnp.concatenate(up, axis=0), "bx"),
-        from_ahead(jnp.concatenate(down, axis=0), "bx"),
-    )
-
-
-def pack_rows(plan, arrays, packed, below, above):
+def pack_planes(plan, arrays, packed):
+    sizes = [plan.low_rows, plan.high_rows]
+    needed = [
+        max(low if to_low else high for _, low, high in plan.groups) for to_low in (True, False)
+    ]
+    depths = [(low, high) for _, low, high in plan.groups]
+    if len(depths) > VELOCITY:
+        depths[VELOCITY] = depths[POSITION]
+
+    def kernel(*refs):
+        groups = len(plan.groups)
+        own, packed_ref, outs = refs[:groups], refs[groups], refs[groups + 1 : groups + 3]
+        edges, semaphores = refs[groups + 3 : -1], refs[-1]
+        copies = []
+
+        def copy(source, target):
+            copies.append(pltpu.make_async_copy(source, target, semaphores.at[len(copies)]))
+            copies[-1].start()
+
+        for side, out in enumerate(outs):
+            for group, array in enumerate(own):
+                depth = depths[group][side]
+                planes = pl.ds(plan.x - depth, depth) if side == 0 else pl.ds(0, depth)
+                copy(array.at[:, planes], edges[2 * group + side])
+            first = plan.x - needed[0] if side == 0 else 0
+            at = (plan.packed_low_at, plan.packed_high_at)[side]
+            for k in range(needed[side]):
+                row, lanes = plan.folded(k, at)
+                copy(packed_ref.at[first + k], out.at[row, :, pl.ds(lanes, LANES)])
+        for one in copies:
+            one.wait()
+        for side, out in enumerate(outs):
+            for field in plan.fields:
+                group, component = field[:2]
+                depth, at = field[2 + side], field[4 + side]
+
+                def get(argument, part):
+                    held = edges[2 * argument + side]
+                    skip = depths[argument][0] - depth if side == 0 else 0
+                    return held[part, skip : skip + depth]
+
+                out[at : at + depth] = plan.value(group, component, get)
+
+    shapes = [(size, plan.y, plan.z) for size in sizes]
+    scratch = [
+        pltpu.VMEM((array.shape[0], depth, plan.y, plan.z), array.dtype)
+        for array, pair in zip(arrays, depths)
+        for depth in pair
+    ]
+    count = 2 * len(arrays) + sum(needed)
+    return pl.pallas_call(
+        kernel,
+        in_specs=[any_space()] * (len(arrays) + 1),
+        out_specs=[in_vmem()] * 2,
+        out_shape=[jax.ShapeDtypeStruct(shape, jnp.float32) for shape in shapes],
+        scratch_shapes=scratch + [pltpu.SemaphoreType.DMA((count,))],
+        compiler_params=pltpu.CompilerParams(vmem_limit_bytes=VMEM_BYTES),
+        cost_estimate=cost(3),
+        name="pack_planes",
+    )(*arrays, packed)
+
+
+def row_shapes(plan, planes):
+    return [(planes, round_up(rows, ROWS), plan.z) for rows in (plan.low_rows, plan.high_rows)]
+
+
+def pack_rows(plan, arrays, packed, below, above, own, halo):
     groups = len(plan.groups)
 
     def kernel(*refs):
-        own = refs[: 2 * groups]
-        packed_first, packed_last, below_first, below_last, above_first, above_last = refs[
-            2 * groups : 2 * groups + 6
-        ]
+        refs = list(refs)
         up, down = refs[-2:]
         up[...] = jnp.zeros(up.shape, jnp.float32)
         down[...] = jnp.zeros(down.shape, jnp.float32)
@@ -165,47 +239,61 @@
                     k : k + 1, at : at + LANES
                 ]
 
-        def own_plane(x, _):
-            for field in plan.fields:
-                group, component = field[:2]
-                put(plan.low + x, field, own[2 * group].at[component, x], own[2 * group + 1].at[component, x])
-            put_packed(plan.low + x, packed_first.at[x], packed_last.at[x], 0)
-            return 0
-
-        lax.fori_loop(0, plan.x, own_plane, 0)
-        for k in range(plan.low):
-            for field in plan.fields:
-                _, _, low, _, low_at, _, _ = field
-                skipped = plan.low - low
-                if k >= skipped:
-                    source = low_at + k - skipped
-                    put(k, field, below_first.at[source], below_last.at[source])
-            source, lanes = plan.folded(k, plan.packed_low_at)
-            put_packed(k, below_first.at[source], below_last.at[source], lanes)
-        for k in range(plan.high):
-            for field in plan.fields:
-                _, _, _, high, _, high_at, _ = field
-                if k < high:
-                    source = high_at + k
-                    put(plan.low + plan.x + k, field, above_first.at[source], above_last.at[source])
-            source, lanes = plan.folded(k, plan.packed_high_at)
-            put_packed(plan.low + plan.x + k, above_first.at[source], above_last.at[source], lanes)
+        base = 0
+        if own:
+            blocks = refs[: 2 * groups + 2]
+            del refs[: 2 * groups + 2]
+            base = plan.x
+
+            def own_plane(x, _):
+                for field in plan.fields:
+                    first, last = [
+                        plan.value(
+                            *field[:2],
+                            lambda argument, part: blocks[2 * argument + side][part, x],
+                        )
+                        for side in range(2)
+                    ]
+                    put(x, field, first, last)
+                put_packed(x, blocks[-2].at[x], blocks[-1].at[x], 0)
+                return 0
+
+            lax.fori_loop(0, plan.x, own_plane, 0)
+        if halo:
+            below_first, below_last, above_first, above_last = refs[:4]
+            for k in range(plan.low):
+                for field in plan.fields:
+                    _, _, low, _, low_at, _, _ = field
+                    skipped = plan.low - low
+                    if k >= skipped:
+                        source = low_at + k - skipped
+                        put(base + k, field, below_first.at[source], below_last.at[source])
+                source, lanes = plan.folded(k, plan.packed_low_at)
+                put_packed(base + k, below_first.at[source], below_last.at[source], lanes)
+            base += plan.low
+            for k in range(plan.high):
+                for field in plan.fields:
+                    _, _, _, high, _, high_at, _ = field
+                    if k < high:
+                        source = high_at + k
+                        put(base + k, field, above_first.at[source], above_last.at[source])
+                source, lanes = plan.folded(k, plan.packed_high_at)
+                put_packed(base + k, above_first.at[source], above_last.at[source], lanes)
 
     last = plan.y // ROWS - 1
     specs, operands = [], []
-    for (count, _, _), array in zip(plan.groups, arrays):
-        block = (count, plan.x, ROWS, plan.z)
-        specs.append(pl.BlockSpec(block, lambda i: (0, 0, 0, 0)))
-        specs.append(pl.BlockSpec(block, lambda i: (0, 0, last, 0)))
-        operands += [array, array]
-    for array in (packed, below, above):
+    if own:
+        for array in arrays:
+            block = (array.shape[0], plan.x, ROWS, plan.z)
+            specs.append(pl.BlockSpec(block, lambda i: (0, 0, 0, 0)))
+            specs.append(pl.BlockSpec(block, lambda i: (0, 0, last, 0)))
+            operands += [array, array]
+    for array in ([packed] if own else []) + ([below, above] if halo else []):
         block = (array.shape[0], ROWS, array.shape[2])
         specs.append(pl.BlockSpec(block, lambda i: (0, 0, 0)))
         specs.append(pl.BlockSpec(block, lambda i: (0, last, 0)))
         operands += [array, array]
-    shapes = [
-        (plan.planes, round_up(rows, ROWS), plan.z) for rows in (plan.low_rows, plan.high_rows)
-    ]
+    shapes = row_shapes(plan, plan.x * own + (plan.low + plan.high) * halo)
     return pl.pallas_call(
         kernel,
         grid=(1,),
@@ -213,19 +301,21 @@
         out_specs=[pl.BlockSpec(shape, lambda i: (0, 0, 0)) for shape in shapes],
         out_shape=[jax.ShapeDtypeStruct(shape, jnp.float32) for shape in shapes],
         compiler_params=pltpu.CompilerParams(vmem_limit_bytes=VMEM_BYTES),
+        cost_estimate=cost(4),
         name="pack_rows",
     )(*operands)
 
 
-def exchange(plan, arrays):
-    packed = exchange_lanes(plan, pack_lanes(plan, arrays))
-    below, above = exchange_planes(plan, arrays, packed)
-    up, down = pack_rows(plan, arrays, packed, below, above)
-    return packed, below, above, from_behind(up, "by"), from_ahead(down, "by")
-
-
-def assemble(plan, arrays, messages, extended, packed_ext, semaphores):
-    packed, below, above, left, right = messages
+def exchange(axis, pair):
+    return [from_behind(pair[0], axis), from_ahead(pair[1], axis)]
+
+
+def assemble(plan, arrays, messages, extended, packed_ext, pinned_own, semaphores):
+    packed, below, above = messages[:3]
+    if len(messages) == 5:
+        sides = [(messages[3], messages[3], plan.x), (messages[4], messages[4], plan.x)]
+    else:
+        sides = [(messages[3], messages[5], 0), (messages[4], messages[6], 0)]
     copies = []
 
     def copy(source, target):
@@ -240,7 +330,10 @@
         target = extended[group].at[component]
         for t in range(plan.tiles):
             lanes = pl.ds(t * LANES, LANES)
-            copy(arrays[group].at[component, :, :, lanes], target.at[own_planes, t, own_rows, :])
+            place = target.at[own_planes, t, own_rows, :]
+            if group == PINNED:
+                place = pinned_own.at[:, t]
+            copy(arrays[group].at[component, :, :, lanes], place)
             copy(
                 below.at[pl.ds(low_at, low), :, lanes],
                 target.at[pl.ds(plan.low - low, low), t, own_rows, :],
@@ -264,32 +357,76 @@
 
     top = ROWS + plan.y
 
-    def plane(i, _):
+    def fill(i, left, right, at):
         for group, component, low, high, low_at, high_at, _ in plan.fields:
             target = extended[group]
             for t in range(plan.tiles):
                 lanes = slice(t * LANES, (t + 1) * LANES)
-                target[component, i, t, ROWS - low : ROWS, :] = left[i, low_at : low_at + low, lanes]
+                target[component, i, t, ROWS - low : ROWS, :] = left[at, low_at : low_at + low, lanes]
                 target[component, i, t, top : top + high, :] = right[
-                    i, high_at : high_at + high, lanes
+                    at, high_at : high_at + high, lanes
                 ]
         for k in range(plan.low):
             row, lanes = plan.folded(k, plan.packed_low_at)
             to = ROWS - plan.low + k
-            packed_ext[i, to : to + 1, :] = left[i, row : row + 1, lanes : lanes + LANES]
+            packed_ext[i, to : to + 1, :] = left[at, row : row + 1, lanes : lanes + LANES]
         for k in range(plan.high):
             row, lanes = plan.folded(k, plan.packed_high_at)
-            packed_ext[i, top + k : top + k + 1, :] = right[i, row : row + 1, lanes : lanes + LANES]
+            packed_ext[i, top + k : top + k + 1, :] = right[at, row : row + 1, lanes : lanes + LANES]
         tile = packed_ext[i]
         for group, component, _, _, _, _, start in plan.fields:
             extended[group][component, i, plan.tiles] = pltpu.roll(tile, (LANES - start) % LANES, 1)
+
+    def own_plane(x, _):
+        i = plan.low + x
+        if pinned_own is not None:
+            for t in range(plan.tiles):
+                at = (i, t, slice(ROWS, top))
+
+                def get(argument, component):
+                    if argument == PINNED:
+                        return pinned_own[x, t]
+                    return extended[argument][(component, *at)]
+
+                for group, component in [(POSITION, c) for c in range(3)] + [(PINNED, 0)]:
+                    extended[group][(component, *at)] = plan.value(group, component, get)
+        fill(i, sides[0][0], sides[1][0], x)
         return 0
 
-    lax.fori_loop(0, plan.planes, plane, 0)
+    def low_plane(k, _):
+        fill(k, sides[0][1], sides[1][1], sides[0][2] + k)
+        return 0
+
+    def high_plane(k, _):
+        at = sides[0][2] + plan.low + k
+        fill(plan.low + plan.x + k, sides[0][1], sides[1][1], at)
+        return 0
+
+    lax.fori_loop(0, plan.x, own_plane, 0)
+    lax.fori_loop(0, plan.low, low_plane, 0)
+    lax.fori_loop(0, plan.high, high_plane, 0)
 
 
 def assemble_copies(plan):
     return len(plan.fields) * plan.tiles * 3 + 1 + plan.low + plan.high
+
+
+def plane_loop(first, last, body, carried):
+    def turn(i, carried, count):
+        pending = []
+        for k in range(count):
+            carried, stores = body(i + k, carried)
+            pending += stores
+        for one in pending:
+            store(*one)
+        return carried
+
+    count = last - first + 1
+    carried = lax.fori_loop(
+        0, count // UNROLL, lambda j, c: turn(first + j * UNROLL, c, UNROLL), carried
+    )
+    rest = count % UNROLL
+    return turn(last + 1 - rest, carried, rest) if rest else carried
 
 
 def load(ref, index, row):
@@ -381,18 +518,16 @@
             now = slab(i)
             here = inside.plane(i)
             scale = [tile * here for tile in keep]
+            stores = []
             for component in range(3):
                 across = (subtract if component == 0 else add)(before[component], now[component])
-                store(force, (component, i), row, each(lambda a, b: a * b, scale, across))
-            store(
-                mass,
-                (0, i),
-                row,
-                each(lambda a, b: 0.125 * (a + b) + 6.0 * CONSISTENT, before[3], now[3]),
-            )
-            return now
-
-        lax.fori_loop(planes[0], planes[1] + 1, plane, slab(planes[0] - 1))
+                result = each(lambda a, b: a * b, scale, across)
+                stores.append((force, (component, i), row, result))
+            result = each(lambda a, b: 0.125 * (a + b) + 6.0 * CONSISTENT, before[3], now[3])
+            stores.append((mass, (0, i), row, result))
+            return now, stores
+
+        plane_loop(*planes, plane, slab(planes[0] - 1))
 
     chunks(*rows, chunk)
 
@@ -413,12 +548,11 @@
                 face_sum(ref, component, i, row, before[component], here[component], after[component])
                 for component in range(3)
             ]
-            use(i, row, here, sums, given)
-            return here, after
+            return (here, after), use(i, row, here, sums, given)
 
         first = [load(ref, (component, planes[0] - 1), row) for component in range(3)]
         second = [load(ref, (component, planes[0]), row) for component in range(3)]
-        lax.fori_loop(planes[0], planes[1] + 1, plane, (first, second))
+        plane_loop(*planes, plane, (first, second))
 
     chunks(*rows, chunk)
 
@@ -428,14 +562,16 @@
 
 
 def moments_kernel(plan, *refs):
-    flags, density, energy, packed, below, above, left, right, out = refs[:9]
+    flags, density, energy = refs[:3]
+    messages, out = refs[3:8], refs[8]
     density_ext, energy_ext, packed_ext, force, image, mass, semaphores = refs[9:]
     assemble(
         plan,
         [density, energy],
-        (packed, below, above, left, right),
+        messages,
         [density_ext, energy_ext],
         packed_ext,
+        None,
         semaphores,
     )
     inside = Inside(plan, flags)
@@ -453,11 +589,13 @@
     def multiply(i, row, here, sums, keep):
         weight = load(mass, (0, i), row)
         scale = [tile * inside.plane(i) for tile in keep]
+        stores = []
         for component in range(3):
             result = each(
                 lambda m, a, k, s: m * a + k * s, weight, here[component], scale, sums[component]
             )
-            store(image, (component, i), row, result)
+            stores.append((image, (component, i), row, result))
+        return stores
 
     stencil_pass(
         force,
@@ -470,18 +608,22 @@
     own = range(plan.tiles)
     nothing = jnp.zeros((ROWS, LANES), jnp.float32)
 
-    def first_plane(n, sums):
-        i, row = low + n // (y // ROWS), ROWS + (n % (y // ROWS)) * ROWS
-        sums = list(sums)
-        for component in range(3):
-            f = load(force, (component, i), row)
-            v = load(image, (component, i), row)
-            for t in own:
-                sums[component] = sums[component] + f[t] * f[t]
-                sums[3 + component] = sums[3 + component] + f[t] * v[t]
-        return tuple(sums)
-
-    sums = lax.fori_loop(0, x * (y // ROWS), first_plane, (nothing,) * 6)
+    def first_chunk(j, sums):
+        row = ROWS + j * ROWS
+
+        def plane(i, sums):
+            sums = list(sums)
+            for component in range(3):
+                f = load(force, (component, i), row)
+                v = load(image, (component, i), row)
+                for t in own:
+                    sums[component] = sums[component] + f[t] * f[t]
+                    sums[3 + component] = sums[3 + component] + f[t] * v[t]
+            return tuple(sums), []
+
+        return plane_loop(low, low + x - 1, plane, sums)
+
+    sums = lax.fori_loop(0, y // ROWS, first_chunk, (nothing,) * 6)
     sums = [whole_sum(one) for one in sums]
     square = sums[:3]
     shift = [
@@ -509,7 +651,7 @@
                 f_high = add(add(f_next, f_up), lane_above(f))
                 w_high = add(add(w_next, w_up), lane_above(w))
                 for t in own:
-                    at = 4 * component
+                    at = 5 * component
                     heavy = weight[t] * w[t]
                     sums[at] = sums[at] + f[t] * w[t]
                     sums[at + 1] = sums[at + 1] + w[t] * w[t]
@@ -519,25 +661,27 @@
                     sums[at + 3] = sums[at + 3] + w[t] * (
                         heavy + (2.0 * CONSISTENT) * w_high[t]
                     )
-            return ahead, tuple(sums)
+                    sums[at + 4] = sums[at + 4] + f[t] * (
+                        weight[t] * f[t] + (2.0 * CONSISTENT) * f_high[t]
+                    )
+            return (ahead, tuple(sums)), []
 
         start = [pair(component, low, row) for component in range(3)]
-        return lax.fori_loop(low, low + x, plane, (start, sums))[1]
-
-    rest = lax.fori_loop(0, y // ROWS, second_chunk, (nothing,) * 12)
+        return plane_loop(low, low + x - 1, plane, (start, sums))[1]
+
+    rest = lax.fori_loop(0, y // ROWS, second_chunk, (nothing,) * 15)
     lane = lane_index((1, LANES))
     line = jnp.zeros((1, LANES), jnp.float32)
     for c in range(3):
-        values = [shift[c], square[c]] + [whole_sum(one) for one in rest[4 * c : 4 * c + 4]]
+        values = [shift[c], square[c]] + [whole_sum(one) for one in rest[5 * c : 5 * c + 5]]
         for k, value in enumerate(values):
             line = jnp.where(lane == 3 * k + c, value, line)
     out[...] = line
 
 
 def solve_weights(sums):
-    rows = sums.shape[0]
     got = [sums if k == 0 else pltpu.roll(sums, LANES - 3 * k, 1) for k in range(MOMENTS)]
-    c, p0, q1, q2, q3, q4 = got
+    c, p0, q1, q2, q3, q4, q5 = got
 
     def total(value):
         return jnp.sum(value, axis=0, keepdims=True)
@@ -546,7 +690,7 @@
     alpha = norm_now / total(q1 + c * p0)
     a = 1.0 - alpha * c
     norm_next = total(a * a * p0 - 2.0 * a * alpha * q1 + alpha * alpha * q2)
-    product = total(a * a * (q1 + c * p0) - a * alpha * (q3 + q2 + c * q1) + alpha * alpha * q4)
+    product = total(a * a * q5 - 2.0 * a * alpha * q3 + alpha * alpha * q4)
     ratio = norm_next / norm_now
     later = norm_next / (product - ratio * norm_next / alpha)
     lane = lane_index((1, LANES))
@@ -559,9 +703,9 @@
 
 
 def step_kernel(plan, *refs):
-    flags, sums, density, energy, base, velocity, free = refs[:7]
-    messages = refs[7:12]
-    velocity_new, accel, relaxed, density_new, energy_new = refs[12:17]
+    flags, sums, density, energy, position, velocity, pinned = refs[:7]
+    messages = refs[7:14]
+    velocity_new, accel, relaxed, density_new, energy_new = refs[14:19]
     (
         density_ext,
         energy_ext,
@@ -569,18 +713,20 @@
         speed,
         free_ext,
         packed_ext,
+        pinned_own,
         force,
         mass,
         other,
         semaphores,
         out_semaphores,
-    ) = refs[17:]
+    ) = refs[19:]
     assemble(
         plan,
-        [density, energy, base, velocity, free],
+        [density, energy, position, velocity, pinned],
         messages,
         [density_ext, energy_ext, moved, speed, free_ext],
         packed_ext,
+        pinned_own,
         semaphores,
     )
     inside = Inside(plan, flags)
@@ -600,6 +746,7 @@
     def advance(i, row, here, sums, keep):
         weight = load(mass, (0, i), row)
         scale = [tile * inside.plane(i) for tile in keep]
+        stores = []
         for component in range(3):
             on_force, on_image = weights[component]
             result = each(
@@ -609,15 +756,17 @@
                 scale,
                 sums[component],
             )
-            store(other, (component, i), row, result)
             at = (component, i)
-            store(speed, at, row, each(lambda v, a: v + TIME_STEP * a, load(speed, at, row), result))
-            store(
-                moved,
-                at,
-                row,
-                each(lambda b, a: b + (TIME_STEP * TIME_STEP) * a, load(moved, at, row), result),
+            faster = each(lambda v, a: v + TIME_STEP * a, load(speed, at, row), result)
+            further = each(
+                lambda b, a: b + (TIME_STEP * TIME_STEP) * a, load(moved, at, row), result
             )
+            stores += [
+                (other, at, row, result),
+                (speed, at, row, faster),
+                (moved, at, row, further),
+            ]
+        return stores
 
     reach -= 1
     advanced = round_up(y + 2 * reach + 1, ROWS)
@@ -668,12 +817,10 @@
             spread = add(subtract(now[0], before[0]), add(now[1], before[1]))
             held = load(energy_ext, (0, i), row)
             lagged = each(lambda e, s: e - (0.25 * 0.4 * TIME_STEP) * (e * s), held, spread)
-            store(
-                content, (0, i), row, each(lambda d, e: d * e, load(density_ext, (0, i), row), lagged)
-            )
-            return now
-
-        lax.fori_loop(low - 1, low + x + 1, plane, slab(low - 1))
+            result = each(lambda d, e: d * e, load(density_ext, (0, i), row), lagged)
+            return now, [(content, (0, i), row, result)]
+
+        plane_loop(low - 1, low + x, plane, slab(low - 1))
 
     chunks(ROWS - 1, ROWS + y, content_chunk)
 
@@ -685,6 +832,7 @@
 
         def relax(i, row, here, sums, given, target=target):
             rate = load(free_ext, (0, i), row)
+            stores = []
             for component in range(3):
                 result = each(
                     lambda r, s, f: r + f * (s * (1.0 / 6.0) - r),
@@ -692,7 +840,8 @@
                     sums[component],
                     rate,
                 )
-                store(target, (component, i), row, result)
+                stores.append((target, (component, i), row, result))
+            return stores
 
         stencil_pass(
             source,
@@ -737,6 +886,7 @@
             ahead = slab(i + 1)
             leaving = x_flux(ahead[0], ahead[4], now[4])
             y_here, y_over, z_here = [add(now[k], ahead[k]) for k in (1, 2, 3)]
+            stores = []
             for k, one in enumerate(quantities):
                 held = now[4][k]
                 under, over = load(one, (0, i), row - 1), load(one, (0, i), row + 1)
@@ -746,12 +896,12 @@
                 change = subtract(change, flux(y_here, held, under))
                 change = add(change, subtract(lane_above(through_z), through_z))
                 result = each(lambda q, c: q + 0.25 * c, held, change)
-                store(free_buffer, (k, i), row, result[: plan.tiles])
-            return ahead, leaving
+                stores.append((free_buffer, (k, i), row, result[: plan.tiles]))
+            return (ahead, leaving), stores
 
         start = slab(low)
         before = [load(one, (0, low - 1), row) for one in quantities]
-        lax.fori_loop(low, low + x, plane, (start, x_flux(start[0], start[4], before)))
+        plane_loop(low, low + x - 1, plane, (start, x_flux(start[0], start[4], before)))
 
     chunks(ROWS, ROWS + y - 1, remap_chunk)
     write(free_buffer, density_new, 0)
@@ -760,8 +910,8 @@
         one.wait()
 
 
-def gather_lines(line):
-    for axis in ("bz", "by", "bx"):
+def gather_lines(line, axes):
+    for axis in axes:
         count = lax.axis_size(axis)
         if count & (count - 1):
             line = lax.all_gather(line, axis, axis=0, tiled=True)
@@ -775,29 +925,17 @@
     return line
 
 
-def any_space():
-    return pl.BlockSpec(memory_space=pl.ANY)
-
-
-def in_vmem():
-    return pl.BlockSpec(memory_space=pltpu.VMEM)
-
-
-def in_smem():
-    return pl.BlockSpec(memory_space=pltpu.SMEM)
-
-
 def extended_scratch(plan, count):
     return pltpu.VMEM((count, plan.planes, plan.tiles + 1, plan.rows, LANES), jnp.float32)
 
 
-def message_specs():
-    return [any_space()] * 3 + [in_vmem()] * 2
+def message_specs(rows):
+    return [any_space()] * 3 + [in_vmem()] * rows
 
 
 def on_device(position, velocity, density, energy, pinned):
     shape = density.shape
-    density, energy = density[None], energy[None]
+    arrays = [density[None], energy[None], position, velocity, pinned[None]]
     flags = jnp.stack(
         [
             jnp.float32(limit)
@@ -808,11 +946,31 @@
             )
         ]
     )
-
-    narrow = Plan([(1, NARROW, NARROW)] * 2, shape)
+    wide = Plan(
+        [
+            (1, WIDE, WIDE),
+            (1, WIDE, WIDE),
+            (3, SWEEPS, SWEEPS + 1),
+            (3, 1, 2),
+            (1, SWEEPS - 1, SWEEPS),
+        ],
+        shape,
+    )
+    narrow = Plan([(1, NARROW, NARROW)] * 2, shape, wide.starts)
+
+    packed = exchange_lanes(wide, pack_lanes(wide, arrays))
+    planes = exchange("bx", pack_planes(narrow, arrays[:2], packed))
+    wide_planes = pack_planes(wide, arrays, packed)
+    wide_rows = pack_rows(wide, arrays, packed, None, None, True, False)
+    planes, wide_planes = lax.optimization_barrier((planes, wide_planes))
+    rows = exchange("by", pack_rows(narrow, arrays[:2], packed, *planes, True, True))
+    wide_planes = exchange("bx", wide_planes)
+    rows, wide_rows = lax.optimization_barrier((rows, wide_rows))
+    wide_rows = exchange("by", wide_rows)
+
     line = pl.pallas_call(
         functools.partial(moments_kernel, narrow),
-        in_specs=[in_smem()] + [any_space()] * 2 + message_specs(),
+        in_specs=[in_smem()] + [any_space()] * 2 + message_specs(2),
         out_specs=in_vmem(),
         out_shape=jax.ShapeDtypeStruct((1, LANES), jnp.float32),
         scratch_shapes=[
@@ -825,28 +983,20 @@
             pltpu.SemaphoreType.DMA((assemble_copies(narrow),)),
         ],
         compiler_params=pltpu.CompilerParams(vmem_limit_bytes=VMEM_BYTES),
+        cost_estimate=cost(30),
         name="moments",
-    )(flags, density, energy, *exchange(narrow, [density, energy]))
-
-    base = position + TIME_STEP * velocity
-    free = (RELAX_RATE * (1.0 - pinned.astype(jnp.float32)))[None]
-    wide = Plan(
-        [
-            (1, WIDE, WIDE),
-            (1, WIDE, WIDE),
-            (3, SWEEPS, SWEEPS + 1),
-            (3, 1, 2),
-            (1, SWEEPS - 1, SWEEPS),
-        ],
-        shape,
-    )
-    arrays = [density, energy, base, velocity, free]
-    messages = exchange(wide, arrays)
+    )(flags, *arrays[:2], packed, *planes, *rows)
+
+    line, wide_rows = lax.optimization_barrier((line, wide_rows))
+    lines = gather_lines(line, ("bz", "by"))
+    lines, wide_planes = lax.optimization_barrier((lines, wide_planes))
+    corners = exchange("by", pack_rows(wide, None, None, *wide_planes, False, True))
+    messages = [packed, *wide_planes, *wide_rows, *corners]
     nodes = jax.ShapeDtypeStruct((3, *shape), jnp.float32)
     cells = jax.ShapeDtypeStruct(shape, jnp.float32)
     return pl.pallas_call(
         functools.partial(step_kernel, wide),
-        in_specs=[in_smem(), in_vmem()] + [any_space()] * 5 + message_specs(),
+        in_specs=[in_smem(), in_vmem()] + [any_space()] * 5 + message_specs(4),
         out_specs=[any_space()] * 5,
         out_shape=[nodes, nodes, nodes, cells, cells],
         scratch_shapes=[
@@ -856,6 +1006,7 @@
             extended_scratch(wide, 3),
             extended_scratch(wide, 1),
             pltpu.VMEM((wide.planes, wide.rows, LANES), jnp.float32),
+            pltpu.VMEM((wide.x, wide.tiles, wide.y, LANES), jnp.int32),
             extended_scratch(wide, 3),
             extended_scratch(wide, 1),
             extended_scratch(wide, 3),
@@ -863,8 +1014,9 @@
             pltpu.SemaphoreType.DMA((11 * wide.tiles,)),
         ],
         compiler_params=pltpu.CompilerParams(vmem_limit_bytes=VMEM_BYTES),
+        cost_estimate=cost(60),
         name="step",
-    )(flags, gather_lines(line), *arrays, *messages)
+    )(flags, gather_lines(lines, ("bx",)), *arrays, *messages)
 
 
 def solution(mesh):

time: 349 us -> 187 us (0.54)
  Pallas kernels: 210 us -> 109 us
  waiting for transfers between devices: 78.1 us -> 32.2 us
  local copies, waits for them, and re-layouts: 15.5 us -> 2.28 us
  other arithmetic: 11.3 us -> 2.67 us
  starting transfers between devices: 31.6 us -> 39 us
    pallas_call x1, Pallas kernels: 139 us -> 62.5 us  [on_device(): pl.pallas_call(functools.partial(step_kernel, wide), in_specs=[in_smem(),...]
    ppermute x5, waiting for transfers between devices: 36.5 us -> 4.76 us  [gather_lines(): got = lax.ppermute(line, axis, [(i, i ^ step) for i in range(count)])]
    pallas_call x1, Pallas kernels: 51 us -> 24.2 us  [on_device(): pl.pallas_call(functools.partial(moments_kernel, narrow), in_specs=[in_sm...]
    ppermute x4 -> x5, waiting for transfers between devices: 29.6 us -> 8.91 us  [from_ahead(): return lax.ppermute(x, axis, [(i + 1, i) for i in range(count - 1)])]
    unnamed x26 -> x16, local copies, waits for them, and re-layouts: 14.4 us -> 2.18 us
    add x1 -> x0, other arithmetic: 5.51 us -> none  [on_device(): base = position + TIME_STEP * velocity]
    pallas_call x0 -> x2, Pallas kernels: none -> 4.96 us  [pack_planes(): pl.pallas_call(kernel, in_specs=[any_space()] * (len(arrays) + 1), out_sp...]
    pallas_call x2 -> x1, Pallas kernels: 12.8 us -> 7.9 us  [pack_lanes(): pl.pallas_call(kernel, grid=(1,), in_specs=specs, out_specs=pl.BlockSpec(...]
  transfers between devices with their start and end apart: 15 -> 16, of which waited for: 8 -> 7; matrix products, arithmetic and copies ran while one was open for 7% -> 1% of each run, Pallas kernels for 19% -> 19%
where the time goes in v3:
time: 187 us; the launch traced here: 186 us
  Pallas kernels  109 us (58%)
  starting transfers between devices  39 us (21%)
  waiting for transfers between devices  32.2 us (17%)
  other arithmetic  2.67 us (1%)
  local copies, waits for them, and re-layouts  2.28 us (1%)
    pallas_call x1, Pallas kernels, on_device(): pl.pallas_call(functools.partial(step_kernel, wide), in_specs=[in_smem(),...  62.5 us
    pallas_call x1, Pallas kernels, on_device(): pl.pallas_call(functools.partial(moments_kernel, narrow), in_specs=[in_sm...  24.2 us
    ppermute x5, starting transfers between devices, from_behind(): return lax.ppermute(x, axis, [(i, i + 1) for i in range(count - 1)])  22.9 us
    ppermute x5, waiting for transfers between devices, from_behind(): return lax.ppermute(x, axis, [(i, i + 1) for i in range(count - 1)])  16.8 us
    pallas_call x3, Pallas kernels, pack_rows(): pl.pallas_call(kernel, grid=(1,), in_specs=specs, out_specs=[pl.BlockSpec...  9.45 us
    ppermute x5, starting transfers between devices, gather_lines(): got = lax.ppermute(line, axis, [(i, i ^ step) for i in range(count)])  9.17 us
    ppermute x5, waiting for transfers between devices, from_ahead(): return lax.ppermute(x, axis, [(i + 1, i) for i in range(count - 1)])  8.91 us
    pallas_call x1, Pallas kernels, pack_lanes(): pl.pallas_call(kernel, grid=(1,), in_specs=specs, out_specs=pl.BlockSpec(...  7.9 us
  transfers between devices with their start and end apart: 16, of which 7 were waited for; matrix products, arithmetic and copies ran while one was open for 1% of the time, Pallas kernels for 19%

profile of v3, /device:TPU:0, one launch (start us, length us, event | category | flops | bytes accessed | tf_op | source)
XLA Modules:
  0.0 186.1 jit_solution(18196929674021848148)
XLA Ops:
  0.6 7.9 %pack_lanes.1 = f32[32,32,128]{2,1,0:T(8,128)} custom-call(f32[1,32,32,256]{3,2,1,0:T(8,128)} %bitcast.9, f32[1,32,32,256]{3,2,1,0:T(8,128)} %bitcast.10, f32[1,32,32,256]{3,2,1,0:T(8,128)} %bitcast.19, f32[1,32,32,256]{3,2,1,0:T(8,128)} %bitcast.20, f32[3,32,32,256]{3,2,1,0:T(8,128)} %refs_4_.5, f32[3,32,32,256]{3,2,1,0:T(8,128)} %refs_4_.5, ...), custom_call_target="tpu_custom_call" | custom-call | bytes 18000000 | tf_op jit(solution)/shard_map/pack_lanes/pallas_call | solution.py:124
  9.0 1.7 collective-permute-done
  10.7 0.8 broadcast_select_fusion.refs_2_.refs_5_.refs_4_.refs_10_.refs_11_.refs_3_.refs_7_
  11.6 1.8 pack_planes.2
  13.3 4.8 %collective-permute-start.1 = (f32[5,32,256]{2,1,0:T(8,128)}, f32[5,32,256]{2,1,0:T(8,128)S(1)}, u32[]{:S(2)}, u32[]{:S(2)}) collective-permute-start(f32[5,32,256]{2,1,0:T(8,128)} %get-tuple-element.29), channel_id=1, source_target_pairs={{0,8},{8,16},{16,24},{1,9},{9,17},{17,25},{2,10},{10,18},{18,26},{... | collective-permute-start | bytes 491528 | tf_op jit(solution)/shard_map/ppermute | solution.py:66
  18.1 1.3 collective-permute-start.2
  19.4 3.2 %pack_planes.3 = (f32[27,32,256]{2,1,0:T(8,128)}, f32[34,32,256]{2,1,0:T(8,128)}) custom-call(f32[1,32,32,256]{3,2,1,0:T(8,128)} %bitcast.12, f32[1,32,32,256]{3,2,1,0:T(8,128)} %bitcast.22, f32[3,32,32,256]{3,2,1,0:T(8,128)} %refs_4_.5, f32[3,32,32,256]{3,2,1,0:T(8,128)} %refs_5_.5, s32[1,32,32,256]{3,2,1,0:T(8,128)} %bitcast.31, ...), custom_call_target="tpu_custom_call" | custom-call | bytes 9000000 | tf_op jit(solution)/shard_map/pack_planes/pallas_call | solution.py:199
  22.6 4.9 %collective-permute-done.2.refs_8_.refs_9_.refs_5_ = f32[5,32,256]{2,1,0:T(8,128)S(1)} collective-permute-done((f32[5,32,256]{2,1,0:T(8,128)}, f32[5,32,256]{2,1,0:T(8,128)S(1)}, u32[]{:S(2)}, u32[]{:S(2)}) %collective-permute-start.2) | collective-permute-done | bytes 163872 | tf_op jit(solution)/shard_map/ppermute | solution.py:71
  28.2 2.4 %pack_rows.3 = (f32[36,8,256]{2,1,0:T(8,128)}, f32[36,8,256]{2,1,0:T(8,128)}) custom-call(f32[1,32,32,256]{3,2,1,0:T(8,128)} %bitcast.13, f32[1,32,32,256]{3,2,1,0:T(8,128)} %bitcast.14, f32[1,32,32,256]{3,2,1,0:T(8,128)} %bitcast.23, f32[1,32,32,256]{3,2,1,0:T(8,128)} %bitcast.24, ...), custom_call_target="tpu_custom_call" | custom-call | bytes 12000000 | tf_op jit(solution)/shard_map/pack_rows/pallas_call | solution.py:297
  30.6 3.5 %collective-permute-start.3 = (f32[36,8,256]{2,1,0:T(8,128)}, f32[36,8,256]{2,1,0:T(8,128)S(1)}, u32[]{:S(2)}, u32[]{:S(2)}) collective-permute-start(f32[36,8,256]{2,1,0:T(8,128)} %get-tuple-element.35), channel_id=1, source_target_pairs={{0,2},{2,4},{4,6},{1,3},{3,5},{5,7},{8,10},{10,12},{12,14},{9,11},... | collective-permute-start | bytes 884744 | tf_op jit(solution)/shard_map/ppermute | solution.py:66
  34.1 1.3 collective-permute-start.4
  35.4 4.7 %pack_rows.4 = (f32[32,32,256]{2,1,0:T(8,128)}, f32[32,40,256]{2,1,0:T(8,128)}) custom-call(f32[1,32,32,256]{3,2,1,0:T(8,128)} %bitcast.15, f32[1,32,32,256]{3,2,1,0:T(8,128)} %bitcast.16, f32[1,32,32,256]{3,2,1,0:T(8,128)} %bitcast.25, f32[1,32,32,256]{3,2,1,0:T(8,128)} %bitcast.26, f32[3,32,32,256]{3,2,1,0:T(8,128)} %refs_4_.5, ...), custom_call_target="tpu_custom_call" | custom-call | bytes 12000000 | tf_op jit(solution)/shard_map/pack_rows/pallas_call | solution.py:297
  40.1 4.0 %collective-permute-done.4.refs_7_ = f32[36,8,256]{2,1,0:T(8,128)S(1)} collective-permute-done((f32[36,8,256]{2,1,0:T(8,128)}, f32[36,8,256]{2,1,0:T(8,128)S(1)}, u32[]{:S(2)}, u32[]{:S(2)}) %collective-permute-start.4) | collective-permute-done | bytes 294944 | tf_op jit(solution)/shard_map/ppermute | solution.py:71
  44.2 1.3 collective-permute-start.6
  45.5 5.5 %collective-permute-start.5 = (f32[32,32,256]{2,1,0:T(8,128)}, f32[32,32,256]{2,1,0:T(8,128)}, u32[]{:S(2)}, u32[]{:S(2)}) collective-permute-start(f32[32,32,256]{2,1,0:T(8,128)} %get-tuple-element.41), channel_id=1, source_target_pairs={{0,2},{2,4},{4,6},{1,3},{3,5},{5,7},{8,10},{10,12},{12,14},{9,11},... | collective-permute-start | bytes 3145736 | tf_op jit(solution)/shard_map/ppermute | solution.py:66
  51.0 1.3 collective-permute-start.11
  52.9 24.2 %moments.1 = f32[1,128]{1,0:T(1,128)} custom-call(f32[6]{0:T(128)} %stack.36.refs_0_, f32[1,32,32,256]{3,2,1,0:T(8,128)} %bitcast.17, f32[1,32,32,256]{3,2,1,0:T(8,128)} %bitcast.27, f32[32,32,128]{2,1,0:T(8,128)} %broadcast_select_fusion.refs_2_.refs_5_.refs_4_.refs_10_.refs_11_.refs_3_.refs_7_, f32[5,32,256]{2,1,0:T(8,128)} %copy-done.2, ...), custom_call_target="tpu_custom_call" | custom-call | bytes 90000000 | tf_op jit(solution)/shard_map/moments/pallas_call | solution.py:971
  77.2 4.6 %collective-permute-start.10 = (f32[27,32,256]{2,1,0:T(8,128)}, f32[27,32,256]{2,1,0:T(8,128)S(1)}, u32[]{:S(2)}, u32[]{:S(2)}) collective-permute-start(f32[27,32,256]{2,1,0:T(8,128)} %get-tuple-element.44), channel_id=1, source_target_pairs={{0,8},{8,16},{16,24},{1,9},{9,17},{17,25},{2,10},{10,18},{18,26},{... | collective-permute-start | bytes 2654216 | tf_op jit(solution)/shard_map/ppermute | solution.py:66
  82.5 0.7 collective-permute-start.8
  83.2 3.0 %collective-permute-done.8 = f32[2,128]{1,0:T(2,128)S(1)} collective-permute-done((f32[2,128]{1,0:T(2,128)S(1)}, f32[2,128]{1,0:T(2,128)S(1)}, u32[]{:S(2)}, u32[]{:S(2)}) %collective-permute-start.8) | collective-permute-done | bytes 1056 | tf_op jit(solution)/shard_map/ppermute | solution.py:921
  86.2 2.8 %collective-permute-start.9 = (f32[4,128]{1,0:T(4,128)S(1)}, f32[4,128]{1,0:T(4,128)S(1)}, u32[]{:S(2)}, u32[]{:S(2)}) collective-permute-start(f32[4,128]{1,0:T(4,128)S(1)} %pad_maximum_fusion.3), channel_id=1, source_target_pairs={{0,4},{2,6},{4,0},{6,2},{1,5},{3,7},{5,1},{7,3},{8,12},{10,14},{12... | collective-permute-start | bytes 6152 | tf_op jit(solution)/shard_map/ppermute | solution.py:921
  89.0 1.8 collective-permute-done.9
  90.8 10.9 %collective-permute-done.10.refs_0_.refs_1_.refs_8_ = f32[27,32,256]{2,1,0:T(8,128)S(1)} collective-permute-done((f32[27,32,256]{2,1,0:T(8,128)}, f32[27,32,256]{2,1,0:T(8,128)S(1)}, u32[]{:S(2)}, u32[]{:S(2)}) %collective-permute-start.10) | collective-permute-done | bytes 884768 | tf_op jit(solution)/shard_map/ppermute | solution.py:66
  101.6 2.5 %collective-permute-start.12 = (f32[8,128]{1,0:T(8,128)S(1)}, f32[8,128]{1,0:T(8,128)S(1)}, u32[]{:S(2)}, u32[]{:S(2)}) collective-permute-start(f32[8,128]{1,0:T(8,128)S(1)} %pad_maximum_fusion.2), channel_id=1, source_target_pairs={{0,8},{8,0},{16,24},{24,16},{1,9},{9,1},{17,25},{25,17},{2,10},{10... | collective-permute-start | bytes 12296 | tf_op jit(solution)/shard_map/ppermute | solution.py:921
  104.2 2.3 %pack_rows.5 = (f32[10,32,256]{2,1,0:T(8,128)}, f32[10,40,256]{2,1,0:T(8,128)}) custom-call(f32[27,32,256]{2,1,0:T(8,128)} %copy-done.1, f32[27,32,256]{2,1,0:T(8,128)} %copy-done.1, f32[34,32,256]{2,1,0:T(8,128)} %copy-done, f32[34,32,256]{2,1,0:T(8,128)} %copy-done), custom_call_target="tpu_custom_call" | custom-call | bytes 12000000 | tf_op jit(solution)/shard_map/pack_rows/pallas_call | solution.py:297
  106.5 1.3 collective-permute-start.15
  107.8 3.2 %collective-permute-start.13 = (f32[16,128]{1,0:T(8,128)S(1)}, f32[16,128]{1,0:T(8,128)S(1)}, u32[]{:S(2)}, u32[]{:S(2)}) collective-permute-start(f32[16,128]{1,0:T(8,128)S(1)} %pad_maximum_fusion.1), channel_id=1, source_target_pairs={{0,16},{8,24},{16,0},{24,8},{1,17},{9,25},{17,1},{25,9},{2,18},{10... | collective-permute-start | bytes 24584 | tf_op jit(solution)/shard_map/ppermute | solution.py:921
  110.9 4.6 %collective-permute-start.14 = (f32[10,32,256]{2,1,0:T(8,128)}, f32[10,32,256]{2,1,0:T(8,128)S(1)}, u32[]{:S(2)}, u32[]{:S(2)}) collective-permute-start(f32[10,32,256]{2,1,0:T(8,128)} %get-tuple-element.51), channel_id=1, source_target_pairs={{0,2},{2,4},{4,6},{1,3},{3,5},{5,7},{8,10},{10,12},{12,14},{9,11},... | collective-permute-start | bytes 983048 | tf_op jit(solution)/shard_map/ppermute | solution.py:66
  116.1 5.9 %collective-permute-done.14.refs_12_ = f32[10,32,256]{2,1,0:T(8,128)S(1)} collective-permute-done((f32[10,32,256]{2,1,0:T(8,128)}, f32[10,32,256]{2,1,0:T(8,128)S(1)}, u32[]{:S(2)}, u32[]{:S(2)}) %collective-permute-start.14) | collective-permute-done | bytes 327712 | tf_op jit(solution)/shard_map/ppermute | solution.py:66
  122.0 0.7 copy-done.5
  122.8 0.8 copy-done.4
  123.5 62.5 %step.1 = (f32[3,32,32,256]{3,2,1,0:T(8,128)}, f32[3,32,32,256]{3,2,1,0:T(8,128)}, f32[3,32,32,256]{3,2,1,0:T(8,128)}, f32[32,32,256]{2,1,0:T(8,128)}, f32[32,32,256]{2,1,0:T(8,128)}) custom-call(f32[6]{0:T(128)} %stack.36.refs_0_, f32[32,128]{1,0:T(8,128)} %pad_maximum_fusion.refs_1_, f32[1,32,32,256]{3,2,1,0:T(8,128)} %bitcast.18, ...), custom_call_target="tpu_custom_call" | custom-call | bytes 180000000 | tf_op jit(solution)/shard_map/step/pallas_call | solution.py:997
  (38 shorter events, 3.2 us)
Async XLA Ops:
  8.5 2.2 %collective-permute-start = (f32[32,32,128]{2,1,0:T(8,128)}, f32[32,32,128]{2,1,0:T(8,128)S(1)}, u32[]{:S(2)}, u32[]{:S(2)}) collective-permute-start(f32[32,32,128]{2,1,0:T(8,128)} %pack_lanes.1), channel_id=1, source_target_pairs={{0,1},{1,0},{2,3},{3,2},{4,5},{5,4},{6,7},{7,6},{8,9},{9,8},{10,11... | collective-permute-start | bytes 1572872 | tf_op jit(solution)/shard_map/ppermute | solution.py:144
  13.3 9.3 %collective-permute-start.1 = (f32[5,32,256]{2,1,0:T(8,128)}, f32[5,32,256]{2,1,0:T(8,128)S(1)}, u32[]{:S(2)}, u32[]{:S(2)}) collective-permute-start(f32[5,32,256]{2,1,0:T(8,128)} %get-tuple-element.29), channel_id=1, source_target_pairs={{0,8},{8,16},{16,24},{1,9},{9,17},{17,25},{2,10},{10,18},{18,26},{... | collective-permute-start | bytes 491528 | tf_op jit(solution)/shard_map/ppermute | solution.py:66
  18.1 9.4 %collective-permute-start.2 = (f32[5,32,256]{2,1,0:T(8,128)}, f32[5,32,256]{2,1,0:T(8,128)S(1)}, u32[]{:S(2)}, u32[]{:S(2)}) collective-permute-start(f32[5,32,256]{2,1,0:T(8,128)} %get-tuple-element.30), channel_id=1, source_target_pairs={{8,0},{16,8},{24,16},{9,1},{17,9},{25,17},{10,2},{18,10},{26,18},{... | collective-permute-start | bytes 491528 | tf_op jit(solution)/shard_map/ppermute | solution.py:71
  22.6 4.9 %copy-start.2 = (f32[5,32,256]{2,1,0:T(8,128)}, f32[5,32,256]{2,1,0:T(8,128)S(1)}, u32[]{:S(2)}) copy-start(f32[5,32,256]{2,1,0:T(8,128)S(1)} %collective-permute-done.1.refs_6_.refs_7_.refs_4_) | copy-start | bytes 491524
  27.5 0.7 copy-start.3
  30.6 9.5 %collective-permute-start.3 = (f32[36,8,256]{2,1,0:T(8,128)}, f32[36,8,256]{2,1,0:T(8,128)S(1)}, u32[]{:S(2)}, u32[]{:S(2)}) collective-permute-start(f32[36,8,256]{2,1,0:T(8,128)} %get-tuple-element.35), channel_id=1, source_target_pairs={{0,2},{2,4},{4,6},{1,3},{3,5},{5,7},{8,10},{10,12},{12,14},{9,11},... | collective-permute-start | bytes 884744 | tf_op jit(solution)/shard_map/ppermute | solution.py:66
  34.1 10.0 %collective-permute-start.4 = (f32[36,8,256]{2,1,0:T(8,128)}, f32[36,8,256]{2,1,0:T(8,128)S(1)}, u32[]{:S(2)}, u32[]{:S(2)}) collective-permute-start(f32[36,8,256]{2,1,0:T(8,128)} %get-tuple-element.36), channel_id=1, source_target_pairs={{2,0},{4,2},{6,4},{3,1},{5,3},{7,5},{10,8},{12,10},{14,12},{11,9},... | collective-permute-start | bytes 884744 | tf_op jit(solution)/shard_map/ppermute | solution.py:71
  40.1 12.7 %copy-start.6 = (f32[36,8,256]{2,1,0:T(8,128)}, f32[36,8,256]{2,1,0:T(8,128)S(1)}, u32[]{:S(2)}) copy-start(f32[36,8,256]{2,1,0:T(8,128)S(1)} %collective-permute-done.3.refs_6_) | copy-start | bytes 884740
  44.2 8.7 %copy-start.7 = (f32[36,8,256]{2,1,0:T(8,128)}, f32[36,8,256]{2,1,0:T(8,128)S(1)}, u32[]{:S(2)}) copy-start(f32[36,8,256]{2,1,0:T(8,128)S(1)} %collective-permute-done.4.refs_7_) | copy-start | bytes 884740
  44.2 33.0 %collective-permute-start.6 = (f32[32,40,256]{2,1,0:T(8,128)}, f32[32,40,256]{2,1,0:T(8,128)}, u32[]{:S(2)}, u32[]{:S(2)}) collective-permute-start(f32[32,40,256]{2,1,0:T(8,128)} %get-tuple-element.42), channel_id=1, source_target_pairs={{2,0},{4,2},{6,4},{3,1},{5,3},{7,5},{10,8},{12,10},{14,12},{11,9},... | collective-permute-start | bytes 3932168 | tf_op jit(solution)/shard_map/ppermute | solution.py:71
  45.5 31.7 %collective-permute-start.5 = (f32[32,32,256]{2,1,0:T(8,128)}, f32[32,32,256]{2,1,0:T(8,128)}, u32[]{:S(2)}, u32[]{:S(2)}) collective-permute-start(f32[32,32,256]{2,1,0:T(8,128)} %get-tuple-element.41), channel_id=1, source_target_pairs={{0,2},{2,4},{4,6},{1,3},{3,5},{5,7},{8,10},{10,12},{12,14},{9,11},... | collective-permute-start | bytes 3145736 | tf_op jit(solution)/shard_map/ppermute | solution.py:66
  51.0 50.7 %collective-permute-start.11 = (f32[34,32,256]{2,1,0:T(8,128)}, f32[34,32,256]{2,1,0:T(8,128)S(1)}, u32[]{:S(2)}, u32[]{:S(2)}) collective-permute-start(f32[34,32,256]{2,1,0:T(8,128)} %get-tuple-element.45), channel_id=1, source_target_pairs={{8,0},{16,8},{24,16},{9,1},{17,9},{25,17},{10,2},{18,10},{26,18},{... | collective-permute-start | bytes 3342344 | tf_op jit(solution)/shard_map/ppermute | solution.py:71
  77.2 4.7 %collective-permute-start.7 = (f32[1,128]{1,0:T(1,128)}, f32[1,128]{1,0:T(1,128)S(1)}, u32[]{:S(2)}, u32[]{:S(2)}) collective-permute-start(f32[1,128]{1,0:T(1,128)} %moments.1), channel_id=1, source_target_pairs={{0,1},{1,0},{2,3},{3,2},{4,5},{5,4},{6,7},{7,6},{8,9},{9,8},{10,11... | collective-permute-start | bytes 1544 | tf_op jit(solution)/shard_map/ppermute | solution.py:921
  77.2 24.4 %collective-permute-start.10 = (f32[27,32,256]{2,1,0:T(8,128)}, f32[27,32,256]{2,1,0:T(8,128)S(1)}, u32[]{:S(2)}, u32[]{:S(2)}) collective-permute-start(f32[27,32,256]{2,1,0:T(8,128)} %get-tuple-element.44), channel_id=1, source_target_pairs={{0,8},{8,16},{16,24},{1,9},{9,17},{17,25},{2,10},{10,18},{18,26},{... | collective-permute-start | bytes 2654216 | tf_op jit(solution)/shard_map/ppermute | solution.py:66
  82.5 3.6 %collective-permute-start.8 = (f32[2,128]{1,0:T(2,128)S(1)}, f32[2,128]{1,0:T(2,128)S(1)}, u32[]{:S(2)}, u32[]{:S(2)}) collective-permute-start(f32[2,128]{1,0:T(2,128)S(1)} %pad_maximum_fusion.4), channel_id=1, source_target_pairs={{0,2},{2,0},{4,6},{6,4},{1,3},{3,1},{5,7},{7,5},{8,10},{10,8},{12,... | collective-permute-start | bytes 3080 | tf_op jit(solution)/shard_map/ppermute | solution.py:921
  86.2 4.5 %collective-permute-start.9 = (f32[4,128]{1,0:T(4,128)S(1)}, f32[4,128]{1,0:T(4,128)S(1)}, u32[]{:S(2)}, u32[]{:S(2)}) collective-permute-start(f32[4,128]{1,0:T(4,128)S(1)} %pad_maximum_fusion.3), channel_id=1, source_target_pairs={{0,4},{2,6},{4,0},{6,2},{1,5},{3,7},{5,1},{7,3},{8,12},{10,14},{12... | collective-permute-start | bytes 6152 | tf_op jit(solution)/shard_map/ppermute | solution.py:921
  101.6 2.5 %copy-start.1 = (f32[27,32,256]{2,1,0:T(8,128)}, f32[27,32,256]{2,1,0:T(8,128)S(1)}, u32[]{:S(2)}) copy-start(f32[27,32,256]{2,1,0:T(8,128)S(1)} %collective-permute-done.10.refs_0_.refs_1_.refs_8_) | copy-start | bytes 2654212
  101.6 2.5 %copy-start = (f32[34,32,256]{2,1,0:T(8,128)}, f32[34,32,256]{2,1,0:T(8,128)S(1)}, u32[]{:S(2)}) copy-start(f32[34,32,256]{2,1,0:T(8,128)S(1)} %collective-permute-done.11.refs_2_.refs_3_.refs_9_) | copy-start | bytes 3342340
  101.6 6.1 %collective-permute-start.12 = (f32[8,128]{1,0:T(8,128)S(1)}, f32[8,128]{1,0:T(8,128)S(1)}, u32[]{:S(2)}, u32[]{:S(2)}) collective-permute-start(f32[8,128]{1,0:T(8,128)S(1)} %pad_maximum_fusion.2), channel_id=1, source_target_pairs={{0,8},{8,0},{16,24},{24,16},{1,9},{9,1},{17,25},{25,17},{2,10},{10... | collective-permute-start | bytes 12296 | tf_op jit(solution)/shard_map/ppermute | solution.py:921
  106.5 15.6 %collective-permute-start.15 = (f32[10,40,256]{2,1,0:T(8,128)}, f32[10,40,256]{2,1,0:T(8,128)S(1)}, u32[]{:S(2)}, u32[]{:S(2)}) collective-permute-start(f32[10,40,256]{2,1,0:T(8,128)} %get-tuple-element.52), channel_id=1, source_target_pairs={{2,0},{4,2},{6,4},{3,1},{5,3},{7,5},{10,8},{12,10},{14,12},{11,9},... | collective-permute-start | bytes 1228808 | tf_op jit(solution)/shard_map/ppermute | solution.py:71
  107.8 7.7 %collective-permute-start.13 = (f32[16,128]{1,0:T(8,128)S(1)}, f32[16,128]{1,0:T(8,128)S(1)}, u32[]{:S(2)}, u32[]{:S(2)}) collective-permute-start(f32[16,128]{1,0:T(8,128)S(1)} %pad_maximum_fusion.1), channel_id=1, source_target_pairs={{0,16},{8,24},{16,0},{24,8},{1,17},{9,25},{17,1},{25,9},{2,18},{10... | collective-permute-start | bytes 24584 | tf_op jit(solution)/shard_map/ppermute | solution.py:921
  110.9 11.1 %collective-permute-start.14 = (f32[10,32,256]{2,1,0:T(8,128)}, f32[10,32,256]{2,1,0:T(8,128)S(1)}, u32[]{:S(2)}, u32[]{:S(2)}) collective-permute-start(f32[10,32,256]{2,1,0:T(8,128)} %get-tuple-element.51), channel_id=1, source_target_pairs={{0,2},{2,4},{4,6},{1,3},{3,5},{5,7},{8,10},{10,12},{12,14},{9,11},... | collective-permute-start | bytes 983048 | tf_op jit(solution)/shard_map/ppermute | solution.py:66
  122.0 0.7 copy-start.5
  122.8 0.8 copy-start.4

commit v4 on v3

--- a/solution.py
+++ b/solution.py
@@ -1,4 +1,5 @@
 import functools
+from typing import NamedTuple
 
 import jax
 import jax.numpy as jnp
@@ -15,16 +16,30 @@
 LANES = 128
 ROWS = 8
 MOMENTS = 7
-UNROLL = 4
+UNROLL = 6
 POSITION, VELOCITY, PINNED = 2, 3, 4
 NARROW = 2
 WIDE = SWEEPS + 2
 VMEM_BYTES = 62 * 2**20
 
 
+class Field(NamedTuple):
+    group: int
+    component: int
+    low: int
+    high: int
+    skip: int
+    low_at: int
+    high_at: int
+    full_low_at: int
+    full_high_at: int
+    start: int
+
+
 class Plan:
-    def __init__(self, groups, shape, starts=None):
+    def __init__(self, groups, shape, inner=None, starts=None, cut=None):
         self.groups = groups
+        self.inner = inner
         self.x, self.y, self.z = shape
         self.tiles = self.z // LANES
         self.low = max(low for _, low, _ in groups)
@@ -32,19 +47,26 @@
         self.planes = self.low + self.x + self.high
         self.rows = self.y + 2 * ROWS
         self.fields = []
-        low_at = high_at = lane_at = 0
+        at = [0] * 4
+        lane_at = 0
         for group, (count, low, high) in enumerate(groups):
+            skip = 0 if inner is None or group >= len(inner.groups) else inner.low
             for component in range(count):
                 start = lane_at + low if starts is None else starts[len(self.fields)]
-                self.fields.append((group, component, low, high, low_at, high_at, start))
-                low_at += low
-                high_at += high
+                self.fields.append(Field(group, component, low, high, skip, *at, start))
+                for k, size in enumerate((low - skip, high - skip, low, high)):
+                    at[k] += size
                 lane_at += low + high
         assert lane_at <= LANES
-        self.starts = [field[-1] for field in self.fields]
-        self.packed_low_at, self.packed_high_at = low_at, high_at
-        self.low_rows = low_at + -(-self.low // self.tiles)
-        self.high_rows = high_at + -(-self.high // self.tiles)
+        self.starts = [field.start for field in self.fields]
+        self.packed_at = at
+        depths = (self.low, self.high) * 2
+        self.sizes = [one + -(-depth // self.tiles) for one, depth in zip(at, depths)]
+        cuts = [] if cut is None else [(self.fields[cut].low_at, self.fields[cut].high_at)]
+        self.parts = []
+        for side in range(2):
+            ends = [0, *(one[side] for one in cuts), self.sizes[side]]
+            self.parts.append([b - a for a, b in zip(ends, ends[1:])])
 
     def value(self, group, component, get):
         if group == POSITION:
@@ -107,28 +129,30 @@
                 return jnp.where(in_low_half, first[component, x], last[component, x])
 
             packed = jnp.zeros((plan.y, LANES), jnp.float32)
-            for group, component, low, high, _, _, start in plan.fields:
+            for group, component, low, high, *_, start in plan.fields:
                 moved = pltpu.roll(plan.value(group, component, edge), start, 1)
                 packed = jnp.where((lane >= start - low) & (lane < start + high), moved, packed)
             out[x] = packed
             return 0
 
-        lax.fori_loop(0, plan.x, plane, 0)
-
+        for x in range(planes):
+            plane(x, 0)
+
+    planes = 4 if plan.x % 4 == 0 else 1
     specs, operands = [], []
     for (count, _, _), array in zip(plan.groups, arrays):
-        block = (count, plan.x, plan.y, LANES)
-        specs.append(pl.BlockSpec(block, lambda i: (0, 0, 0, 0)))
-        specs.append(pl.BlockSpec(block, lambda i: (0, 0, 0, plan.tiles - 1)))
+        block = (count, planes, plan.y, LANES)
+        specs.append(pl.BlockSpec(block, lambda i: (0, i, 0, 0)))
+        specs.append(pl.BlockSpec(block, lambda i: (0, i, 0, plan.tiles - 1)))
         operands += [array, array]
     return pl.pallas_call(
         kernel,
-        grid=(1,),
+        grid=(plan.x // planes,),
         in_specs=specs,
-        out_specs=pl.BlockSpec((plan.x, plan.y, LANES), lambda i: (0, 0, 0)),
+        out_specs=pl.BlockSpec((planes, plan.y, LANES), lambda i: (i, 0, 0)),
         out_shape=jax.ShapeDtypeStruct((plan.x, plan.y, LANES), jnp.float32),
         compiler_params=pltpu.CompilerParams(vmem_limit_bytes=VMEM_BYTES),
-        cost_estimate=cost(6),
+        cost_estimate=cost(0.5),
         name="pack_lanes",
     )(*operands)
 
@@ -137,7 +161,7 @@
     lane = lane_index((1, 1, LANES))
     is_low = functools.reduce(
         jnp.logical_or,
-        [(lane >= start - low) & (lane < start) for _, _, low, _, _, _, start in plan.fields],
+        [(lane >= start - low) & (lane < start) for _, _, low, *_, start in plan.fields],
     )
     count = lax.axis_size("bz")
     if count == 2:
@@ -146,8 +170,14 @@
     return jnp.where(is_low, from_behind(packed, "bz"), from_ahead(packed, "bz"))
 
 
+def part_of(parts, at):
+    for part in parts:
+        if at < part.shape[0]:
+            return part, at
+        at -= part.shape[0]
+
+
 def pack_planes(plan, arrays, packed):
-    sizes = [plan.low_rows, plan.high_rows]
     needed = [
         max(low if to_low else high for _, low, high in plan.groups) for to_low in (True, False)
     ]
@@ -157,8 +187,10 @@
 
     def kernel(*refs):
         groups = len(plan.groups)
-        own, packed_ref, outs = refs[:groups], refs[groups], refs[groups + 1 : groups + 3]
-        edges, semaphores = refs[groups + 3 : -1], refs[-1]
+        own, packed_ref = refs[:groups], refs[groups]
+        count = len(plan.parts[0])
+        outs = refs[groups + 1 : groups + 1 + count], refs[groups + 1 + count : groups + 1 + 2 * count]
+        edges, semaphores = refs[groups + 1 + 2 * count : -1], refs[-1]
         copies = []
 
         def copy(source, target):
@@ -171,49 +203,51 @@
                 planes = pl.ds(plan.x - depth, depth) if side == 0 else pl.ds(0, depth)
                 copy(array.at[:, planes], edges[2 * group + side])
             first = plan.x - needed[0] if side == 0 else 0
-            at = (plan.packed_low_at, plan.packed_high_at)[side]
+            at = plan.packed_at[side]
             for k in range(needed[side]):
                 row, lanes = plan.folded(k, at)
-                copy(packed_ref.at[first + k], out.at[row, :, pl.ds(lanes, LANES)])
+                part, row = part_of(out, row)
+                copy(packed_ref.at[first + k], part.at[row, :, pl.ds(lanes, LANES)])
         for one in copies:
             one.wait()
         for side, out in enumerate(outs):
             for field in plan.fields:
-                group, component = field[:2]
-                depth, at = field[2 + side], field[4 + side]
+                at = (field.low_at, field.high_at)[side]
+                depth = (field.low, field.high)[side] - field.skip
 
                 def get(argument, part):
                     held = edges[2 * argument + side]
-                    skip = depths[argument][0] - depth if side == 0 else 0
-                    return held[part, skip : skip + depth]
-
-                out[at : at + depth] = plan.value(group, component, get)
-
-    shapes = [(size, plan.y, plan.z) for size in sizes]
+                    first = depths[argument][0] - field.low if side == 0 else field.skip
+                    return held[part, first : first + depth]
+
+                part, at = part_of(out, at)
+                part[at : at + depth] = plan.value(field.group, field.component, get)
+
+    shapes = [(size, plan.y, plan.z) for side in plan.parts for size in side]
     scratch = [
         pltpu.VMEM((array.shape[0], depth, plan.y, plan.z), array.dtype)
         for array, pair in zip(arrays, depths)
         for depth in pair
     ]
     count = 2 * len(arrays) + sum(needed)
-    return pl.pallas_call(
+    outs = pl.pallas_call(
         kernel,
         in_specs=[any_space()] * (len(arrays) + 1),
-        out_specs=[in_vmem()] * 2,
+        out_specs=[in_vmem()] * len(shapes),
         out_shape=[jax.ShapeDtypeStruct(shape, jnp.float32) for shape in shapes],
         scratch_shapes=scratch + [pltpu.SemaphoreType.DMA((count,))],
         compiler_params=pltpu.CompilerParams(vmem_limit_bytes=VMEM_BYTES),
-        cost_estimate=cost(3),
+        cost_estimate=cost(0.5),
         name="pack_planes",
     )(*arrays, packed)
-
-
-def row_shapes(plan, planes):
-    return [(planes, round_up(rows, ROWS), plan.z) for rows in (plan.low_rows, plan.high_rows)]
-
-
-def pack_rows(plan, arrays, packed, below, above, own, halo):
+    return list(zip(outs[: len(plan.parts[0])], outs[len(plan.parts[0]) :]))
+
+
+def pack_rows(plan, arrays, packed, own, planes=(), inner_planes=()):
     groups = len(plan.groups)
+    sizes, packed_at = plan.sizes[2:], plan.packed_at[2:]
+    if own:
+        sizes, packed_at = plan.sizes[:2], plan.packed_at[:2]
 
     def kernel(*refs):
         refs = list(refs)
@@ -222,19 +256,22 @@
         down[...] = jnp.zeros(down.shape, jnp.float32)
 
         def put(plane, field, first, last):
-            _, _, low, high, low_at, high_at, _ = field
-            up[plane, low_at : low_at + low, :] = last[ROWS - low : ROWS, :]
-            down[plane, high_at : high_at + high, :] = first[0:high, :]
+            low_at, high_at, skip = field.full_low_at, field.full_high_at, 0
+            if own:
+                low_at, high_at, skip = field.low_at, field.high_at, field.skip
+            low, high = field.low - skip, field.high - skip
+            up[plane, low_at : low_at + low, :] = last[ROWS - field.low : ROWS - skip, :]
+            down[plane, high_at : high_at + high, :] = first[skip : field.high, :]
 
         def put_packed(plane, first, last, at):
             for k in range(plan.low):
-                row, lanes = plan.folded(k, plan.packed_low_at)
+                row, lanes = plan.folded(k, packed_at[0])
                 source = ROWS - plan.low + k
                 up[plane, row : row + 1, lanes : lanes + LANES] = last[
                     source : source + 1, at : at + LANES
                 ]
             for k in range(plan.high):
-                row, lanes = plan.folded(k, plan.packed_high_at)
+                row, lanes = plan.folded(k, packed_at[1])
                 down[plane, row : row + 1, lanes : lanes + LANES] = first[
                     k : k + 1, at : at + LANES
                 ]
@@ -259,26 +296,37 @@
                 return 0
 
             lax.fori_loop(0, plan.x, own_plane, 0)
-        if halo:
-            below_first, below_last, above_first, above_last = refs[:4]
-            for k in range(plan.low):
-                for field in plan.fields:
-                    _, _, low, _, low_at, _, _ = field
-                    skipped = plan.low - low
-                    if k >= skipped:
-                        source = low_at + k - skipped
-                        put(base + k, field, below_first.at[source], below_last.at[source])
-                source, lanes = plan.folded(k, plan.packed_low_at)
-                put_packed(base + k, below_first.at[source], below_last.at[source], lanes)
-            base += plan.low
-            for k in range(plan.high):
-                for field in plan.fields:
-                    _, _, _, high, _, high_at, _ = field
-                    if k < high:
-                        source = high_at + k
-                        put(base + k, field, above_first.at[source], above_last.at[source])
-                source, lanes = plan.folded(k, plan.packed_high_at)
-                put_packed(base + k, above_first.at[source], above_last.at[source], lanes)
+        if planes:
+            count = len(plan.parts[0])
+            pairs = [tuple(refs[2 * k : 2 * k + 2]) for k in range(2 * count + 2)]
+            if plan.inner is None:
+                pairs = pairs[: 2 * count]
+            sides = [pairs[:count], pairs[count : 2 * count]]
+            inner_sides = [pairs[2 * count : 2 * count + 1], pairs[2 * count + 1 :]]
+
+            def find(parts, at):
+                part, at = part_of([first for first, _ in parts], at)
+                pair = next(pair for pair in parts if pair[0] is part)
+                return [ref.at[at] for ref in pair]
+
+            for side in range(2):
+                for k in range((plan.low, plan.high)[side]):
+                    for field in plan.fields:
+                        depth, at = (field.low, field.low_at) if side == 0 else (field.high, field.high_at)
+                        j = plan.low - k if side == 0 else k + 1
+                        if j > depth:
+                            continue
+                        if j > field.skip:
+                            source = at + (depth - j if side == 0 else j - 1 - field.skip)
+                            parts = sides[side]
+                        else:
+                            other = plan.inner.fields[field.group]
+                            source = other.low_at + other.low - j if side == 0 else other.high_at + j - 1
+                            parts = inner_sides[side]
+                        put(base + k, field, *find(parts, source))
+                    source, lanes = plan.folded(k, plan.packed_at[side])
+                    put_packed(base + k, *find(sides[side], source), lanes)
+                base += plan.low
 
     last = plan.y // ROWS - 1
     specs, operands = [], []
@@ -288,12 +336,13 @@
             specs.append(pl.BlockSpec(block, lambda i: (0, 0, 0, 0)))
             specs.append(pl.BlockSpec(block, lambda i: (0, 0, last, 0)))
             operands += [array, array]
-    for array in ([packed] if own else []) + ([below, above] if halo else []):
+    for array in ([packed] if own else []) + [*planes, *inner_planes]:
         block = (array.shape[0], ROWS, array.shape[2])
         specs.append(pl.BlockSpec(block, lambda i: (0, 0, 0)))
         specs.append(pl.BlockSpec(block, lambda i: (0, last, 0)))
         operands += [array, array]
-    shapes = row_shapes(plan, plan.x * own + (plan.low + plan.high) * halo)
+    count = plan.x * own + (plan.low + plan.high) * bool(planes)
+    shapes = [(count, round_up(size, ROWS), plan.z) for size in sizes]
     return pl.pallas_call(
         kernel,
         grid=(1,),
@@ -301,7 +350,7 @@
         out_specs=[pl.BlockSpec(shape, lambda i: (0, 0, 0)) for shape in shapes],
         out_shape=[jax.ShapeDtypeStruct(shape, jnp.float32) for shape in shapes],
         compiler_params=pltpu.CompilerParams(vmem_limit_bytes=VMEM_BYTES),
-        cost_estimate=cost(4),
+        cost_estimate=cost(0.5),
         name="pack_rows",
     )(*operands)
 
@@ -310,12 +359,14 @@
     return [from_behind(pair[0], axis), from_ahead(pair[1], axis)]
 
 
-def assemble(plan, arrays, messages, extended, packed_ext, pinned_own, semaphores):
-    packed, below, above = messages[:3]
-    if len(messages) == 5:
-        sides = [(messages[3], messages[3], plan.x), (messages[4], messages[4], plan.x)]
+def assemble(plan, arrays, messages, inner, extended, packed_ext, pinned_own, semaphores):
+    count = len(plan.parts[0])
+    packed, below, above = messages[0], messages[1 : 1 + count], messages[1 + count : 1 + 2 * count]
+    rest = messages[1 + 2 * count :]
+    if len(rest) == 2:
+        sides = [(rest[0], rest[0], plan.x), (rest[1], rest[1], plan.x)]
     else:
-        sides = [(messages[3], messages[5], 0), (messages[4], messages[6], 0)]
+        sides = [(rest[0], rest[2], 0), (rest[1], rest[3], 0)]
     copies = []
 
     def copy(source, target):
@@ -326,89 +377,122 @@
 
     own_rows = pl.ds(ROWS, plan.y)
     own_planes = pl.ds(plan.low, plan.x)
-    for group, component, low, high, low_at, high_at, _ in plan.fields:
+    for field in plan.fields:
+        group, component, low, high, skip = field[:5]
         target = extended[group].at[component]
+        after = plan.low + plan.x
         for t in range(plan.tiles):
             lanes = pl.ds(t * LANES, LANES)
+
+            def planes(source, at, first, count):
+                if count:
+                    source, at = part_of(source, at)
+                    copy(
+                        source.at[pl.ds(at, count), :, lanes],
+                        target.at[pl.ds(first, count), t, own_rows, :],
+                    )
+
             place = target.at[own_planes, t, own_rows, :]
             if group == PINNED:
                 place = pinned_own.at[:, t]
             copy(arrays[group].at[component, :, :, lanes], place)
-            copy(
-                below.at[pl.ds(low_at, low), :, lanes],
-                target.at[pl.ds(plan.low - low, low), t, own_rows, :],
-            )
-            copy(
-                above.at[pl.ds(high_at, high), :, lanes],
-                target.at[pl.ds(plan.low + plan.x, high), t, own_rows, :],
-            )
+            planes(below, field.low_at, plan.low - low, low - skip)
+            planes(above, field.high_at, after + skip, high - skip)
+            if skip:
+                other = plan.inner.fields[group]
+                planes(inner[:1], other.low_at, plan.low - skip, skip)
+                planes(inner[1:2], other.high_at, after, skip)
+    large = len(copies)
     copy(packed, packed_ext.at[own_planes, own_rows, :])
     for k in range(plan.low):
-        source, lanes = plan.folded(k, plan.packed_low_at)
-        copy(below.at[source, :, pl.ds(lanes, LANES)], packed_ext.at[k, own_rows, :])
+        source, lanes = plan.folded(k, plan.packed_at[0])
+        part, source = part_of(below, source)
+        copy(part.at[source, :, pl.ds(lanes, LANES)], packed_ext.at[k, own_rows, :])
     for k in range(plan.high):
-        source, lanes = plan.folded(k, plan.packed_high_at)
+        source, lanes = plan.folded(k, plan.packed_at[1])
+        part, source = part_of(above, source)
         copy(
-            above.at[source, :, pl.ds(lanes, LANES)],
+            part.at[source, :, pl.ds(lanes, LANES)],
             packed_ext.at[plan.low + plan.x + k, own_rows, :],
         )
-    for one in copies:
+    for one in copies[large:]:
         one.wait()
 
     top = ROWS + plan.y
 
-    def fill(i, left, right, at):
-        for group, component, low, high, low_at, high_at, _ in plan.fields:
-            target = extended[group]
-            for t in range(plan.tiles):
-                lanes = slice(t * LANES, (t + 1) * LANES)
-                target[component, i, t, ROWS - low : ROWS, :] = left[at, low_at : low_at + low, lanes]
-                target[component, i, t, top : top + high, :] = right[
-                    at, high_at : high_at + high, lanes
-                ]
+    def fill(i, left, right, at, own):
+        def rows(field, first, source, source_at, count):
+            if count:
+                for t in range(plan.tiles):
+                    extended[field.group][field.component, i, t, first : first + count, :] = source[
+                        at, source_at : source_at + count, t * LANES : (t + 1) * LANES
+                    ]
+
+        packed_at = plan.packed_at[:2] if own else plan.packed_at[2:]
+        for field in plan.fields:
+            low, high, skip = field.low, field.high, field.skip
+            if own:
+                rows(field, ROWS - low, left, field.low_at, low - skip)
+                rows(field, top + skip, right, field.high_at, high - skip)
+                if skip:
+                    other = plan.inner.fields[field.group]
+                    rows(field, ROWS - skip, inner[2], other.low_at, skip)
+                    rows(field, top, inner[3], other.high_at, skip)
+            else:
+                rows(field, ROWS - low, left, field.full_low_at, low)
+                rows(field, top, right, field.full_high_at, high)
         for k in range(plan.low):
-            row, lanes = plan.folded(k, plan.packed_low_at)
+            row, lanes = plan.folded(k, packed_at[0])
             to = ROWS - plan.low + k
             packed_ext[i, to : to + 1, :] = left[at, row : row + 1, lanes : lanes + LANES]
         for k in range(plan.high):
-            row, lanes = plan.folded(k, plan.packed_high_at)
+            row, lanes = plan.folded(k, packed_at[1])
             packed_ext[i, top + k : top + k + 1, :] = right[at, row : row + 1, lanes : lanes + LANES]
         tile = packed_ext[i]
-        for group, component, _, _, _, _, start in plan.fields:
-            extended[group][component, i, plan.tiles] = pltpu.roll(tile, (LANES - start) % LANES, 1)
+        for field in plan.fields:
+            extended[field.group][field.component, i, plan.tiles] = pltpu.roll(
+                tile, (LANES - field.start) % LANES, 1
+            )
 
     def own_plane(x, _):
+        fill(plan.low + x, sides[0][0], sides[1][0], x, True)
+        return 0
+
+    def finish_plane(x, _):
         i = plan.low + x
-        if pinned_own is not None:
-            for t in range(plan.tiles):
-                at = (i, t, slice(ROWS, top))
-
-                def get(argument, component):
-                    if argument == PINNED:
-                        return pinned_own[x, t]
-                    return extended[argument][(component, *at)]
-
-                for group, component in [(POSITION, c) for c in range(3)] + [(PINNED, 0)]:
-                    extended[group][(component, *at)] = plan.value(group, component, get)
-        fill(i, sides[0][0], sides[1][0], x)
+        for t in range(plan.tiles):
+            at = (i, t, slice(ROWS, top))
+
+            def get(argument, component):
+                if argument == PINNED:
+                    return pinned_own[x, t]
+                return extended[argument][(component, *at)]
+
+            for group, component in [(POSITION, c) for c in range(3)] + [(PINNED, 0)]:
+                extended[group][(component, *at)] = plan.value(group, component, get)
         return 0
 
     def low_plane(k, _):
-        fill(k, sides[0][1], sides[1][1], sides[0][2] + k)
+        fill(k, sides[0][1], sides[1][1], sides[0][2] + k, False)
         return 0
 
     def high_plane(k, _):
         at = sides[0][2] + plan.low + k
-        fill(plan.low + plan.x + k, sides[0][1], sides[1][1], at)
+        fill(plan.low + plan.x + k, sides[0][1], sides[1][1], at, False)
         return 0
 
     lax.fori_loop(0, plan.x, own_plane, 0)
     lax.fori_loop(0, plan.low, low_plane, 0)
     lax.fori_loop(0, plan.high, high_plane, 0)
+    for one in copies[:large]:
+        one.wait()
+    if pinned_own is not None:
+        lax.fori_loop(0, plan.x, finish_plane, 0)
 
 
 def assemble_copies(plan):
-    return len(plan.fields) * plan.tiles * 3 + 1 + plan.low + plan.high
+    skipping = sum(field.skip > 0 for field in plan.fields)
+    return (3 * len(plan.fields) + 2 * skipping) * plan.tiles + 1 + plan.low + plan.high
 
 
 def plane_loop(first, last, body, carried):
@@ -569,6 +653,7 @@
         plan,
         [density, energy],
         messages,
+        None,
         [density_ext, energy_ext],
         packed_ext,
         None,
@@ -704,8 +789,8 @@
 
 def step_kernel(plan, *refs):
     flags, sums, density, energy, position, velocity, pinned = refs[:7]
-    messages = refs[7:14]
-    velocity_new, accel, relaxed, density_new, energy_new = refs[14:19]
+    messages, inner = refs[7:16], refs[16:20]
+    velocity_new, accel, relaxed, density_new, energy_new = refs[20:25]
     (
         density_ext,
         energy_ext,
@@ -719,11 +804,12 @@
         other,
         semaphores,
         out_semaphores,
-    ) = refs[19:]
+    ) = refs[25:]
     assemble(
         plan,
         [density, energy, position, velocity, pinned],
         messages,
+        inner,
         [density_ext, energy_ext, moved, speed, free_ext],
         packed_ext,
         pinned_own,
@@ -929,8 +1015,8 @@
     return pltpu.VMEM((count, plan.planes, plan.tiles + 1, plan.rows, LANES), jnp.float32)
 
 
-def message_specs(rows):
-    return [any_space()] * 3 + [in_vmem()] * rows
+def message_specs(planes, rows):
+    return [any_space()] * planes + [in_vmem()] * rows
 
 
 def on_device(position, velocity, density, energy, pinned):
@@ -946,31 +1032,33 @@
             )
         ]
     )
-    wide = Plan(
-        [
-            (1, WIDE, WIDE),
-            (1, WIDE, WIDE),
-            (3, SWEEPS, SWEEPS + 1),
-            (3, 1, 2),
-            (1, SWEEPS - 1, SWEEPS),
-        ],
-        shape,
-    )
-    narrow = Plan([(1, NARROW, NARROW)] * 2, shape, wide.starts)
+    groups = [
+        (1, WIDE, WIDE),
+        (1, WIDE, WIDE),
+        (3, SWEEPS, SWEEPS + 1),
+        (3, 1, 2),
+        (1, SWEEPS - 1, SWEEPS),
+    ]
+    starts = Plan(groups, shape).starts
+    narrow = Plan([(1, NARROW, NARROW)] * 2, shape, None, starts)
+    wide = Plan(groups, shape, narrow, cut=3)
 
     packed = exchange_lanes(wide, pack_lanes(wide, arrays))
-    planes = exchange("bx", pack_planes(narrow, arrays[:2], packed))
-    wide_planes = pack_planes(wide, arrays, packed)
-    wide_rows = pack_rows(wide, arrays, packed, None, None, True, False)
-    planes, wide_planes = lax.optimization_barrier((planes, wide_planes))
-    rows = exchange("by", pack_rows(narrow, arrays[:2], packed, *planes, True, True))
-    wide_planes = exchange("bx", wide_planes)
-    rows, wide_rows = lax.optimization_barrier((rows, wide_rows))
+    planes = exchange("bx", *pack_planes(narrow, arrays[:2], packed))
+    first_planes, last_planes = pack_planes(wide, arrays, packed)
+    wide_rows = pack_rows(wide, arrays, packed, True)
+    planes, first_planes = lax.optimization_barrier((planes, first_planes))
+    rows = exchange("by", pack_rows(narrow, arrays[:2], packed, True, planes))
+    first_planes = exchange("bx", first_planes)
+    rows, first_planes, last_planes, wide_rows = lax.optimization_barrier(
+        (rows, first_planes, last_planes, wide_rows)
+    )
+    last_planes = exchange("bx", last_planes)
     wide_rows = exchange("by", wide_rows)
 
     line = pl.pallas_call(
         functools.partial(moments_kernel, narrow),
-        in_specs=[in_smem()] + [any_space()] * 2 + message_specs(2),
+        in_specs=[in_smem()] + [any_space()] * 2 + message_specs(3, 2),
         out_specs=in_vmem(),
         out_shape=jax.ShapeDtypeStruct((1, LANES), jnp.float32),
         scratch_shapes=[
@@ -983,20 +1071,21 @@
             pltpu.SemaphoreType.DMA((assemble_copies(narrow),)),
         ],
         compiler_params=pltpu.CompilerParams(vmem_limit_bytes=VMEM_BYTES),
-        cost_estimate=cost(30),
+        cost_estimate=cost(1),
         name="moments",
     )(flags, *arrays[:2], packed, *planes, *rows)
 
-    line, wide_rows = lax.optimization_barrier((line, wide_rows))
-    lines = gather_lines(line, ("bz", "by"))
-    lines, wide_planes = lax.optimization_barrier((lines, wide_planes))
-    corners = exchange("by", pack_rows(wide, None, None, *wide_planes, False, True))
+    line, wide_rows, last_planes = lax.optimization_barrier((line, wide_rows, last_planes))
+    wide_planes = [pair[side] for side in range(2) for pair in (first_planes, last_planes)]
+    corners = exchange("by", pack_rows(wide, None, None, False, wide_planes, planes))
+    lines = gather_lines(line, ("bz", "bx"))
+    lines, corners = lax.optimization_barrier((lines, corners))
     messages = [packed, *wide_planes, *wide_rows, *corners]
     nodes = jax.ShapeDtypeStruct((3, *shape), jnp.float32)
     cells = jax.ShapeDtypeStruct(shape, jnp.float32)
     return pl.pallas_call(
         functools.partial(step_kernel, wide),
-        in_specs=[in_smem(), in_vmem()] + [any_space()] * 5 + message_specs(4),
+        in_specs=[in_smem(), in_vmem()] + [any_space()] * 5 + message_specs(5, 4) + message_specs(2, 2),
         out_specs=[any_space()] * 5,
         out_shape=[nodes, nodes, nodes, cells, cells],
         scratch_shapes=[
@@ -1014,9 +1103,9 @@
             pltpu.SemaphoreType.DMA((11 * wide.tiles,)),
         ],
         compiler_params=pltpu.CompilerParams(vmem_limit_bytes=VMEM_BYTES),
-        cost_estimate=cost(60),
+        cost_estimate=cost(1),
         name="step",
-    )(flags, gather_lines(lines, ("bx",)), *arrays, *messages)
+    )(flags, gather_lines(lines, ("by",)), *arrays, *messages, *planes, *rows)
 
 
 def solution(mesh):

time: 187 us -> 171 us (0.914)
  waiting for transfers between devices: 32.2 us -> 22.2 us
  Pallas kernels: 109 us -> 99.6 us
  starting transfers between devices: 39 us -> 44.2 us
  local copies, waits for them, and re-layouts: 2.28 us -> 0.14 us
    ppermute x5 -> x6, waiting for transfers between devices: 16.8 us -> 7.03 us  [from_behind(): return lax.ppermute(x, axis, [(i, i + 1) for i in range(count - 1)])]
    pallas_call x1, Pallas kernels: 62.5 us -> 56.4 us  [on_device(): pl.pallas_call(functools.partial(step_kernel, wide), in_specs=[in_smem(),...]
    ppermute x5 -> x6, starting transfers between devices: 22.9 us -> 27.9 us  [from_behind(): return lax.ppermute(x, axis, [(i, i + 1) for i in range(count - 1)])]
    pallas_call x1, Pallas kernels: 24.2 us -> 21.6 us  [on_device(): pl.pallas_call(functools.partial(moments_kernel, narrow), in_specs=[in_sm...]
    unnamed x16 -> x20, local copies, waits for them, and re-layouts: 2.18 us -> 0.04 us
    ppermute x5 -> x6, starting transfers between devices: 6.42 us -> 7.71 us  [from_ahead(): return lax.ppermute(x, axis, [(i + 1, i) for i in range(count - 1)])]
    ppermute x5 -> x6, waiting for transfers between devices: 8.91 us -> 8.94 us  [from_ahead(): return lax.ppermute(x, axis, [(i + 1, i) for i in range(count - 1)])]
  transfers between devices with their start and end apart: 16 -> 18, of which waited for: 7 -> 8; matrix products, arithmetic and copies ran while one was open for 1% -> 0% of each run, Pallas kernels for 19% -> 20%
where the time goes in v4:
time: 171 us; the launch traced here: 170 us
  Pallas kernels  99.6 us (58%)
  starting transfers between devices  44.2 us (26%)
  waiting for transfers between devices  22.2 us (13%)
  other arithmetic  2.75 us (2%)
    pallas_call x1, Pallas kernels, on_device(): pl.pallas_call(functools.partial(step_kernel, wide), in_specs=[in_smem(),...  56.4 us
    ppermute x6, starting transfers between devices, from_behind(): return lax.ppermute(x, axis, [(i, i + 1) for i in range(count - 1)])  27.9 us
    pallas_call x1, Pallas kernels, on_device(): pl.pallas_call(functools.partial(moments_kernel, narrow), in_specs=[in_sm...  21.6 us
    pallas_call x3, Pallas kernels, pack_rows(): pl.pallas_call(kernel, grid=(1,), in_specs=specs, out_specs=[pl.BlockSpec...  9.31 us
    ppermute x6, waiting for transfers between devices, from_ahead(): return lax.ppermute(x, axis, [(i + 1, i) for i in range(count - 1)])  8.94 us
    ppermute x5, starting transfers between devices, gather_lines(): got = lax.ppermute(line, axis, [(i, i ^ step) for i in range(count)])  8.15 us
    ppermute x6, starting transfers between devices, from_ahead(): return lax.ppermute(x, axis, [(i + 1, i) for i in range(count - 1)])  7.71 us
    pallas_call x1, Pallas kernels, pack_lanes(): pl.pallas_call(kernel, grid=(plan.x // planes,), in_specs=specs, out_spec...  7.45 us
  transfers between devices with their start and end apart: 18, of which 8 were waited for; matrix products, arithmetic and copies ran while one was open for 0% of the time, Pallas kernels for 20%

profile of v4, /device:TPU:0, one launch (start us, length us, event | category | flops | bytes accessed | tf_op | source)
XLA Modules:
  0.0 169.9 jit_solution(11672941955176199145)
XLA Ops:
  0.6 7.5 %pack_lanes.1 = f32[32,32,128]{2,1,0:T(8,128)} custom-call(f32[1,32,32,256]{3,2,1,0:T(8,128)} %bitcast.9, f32[1,32,32,256]{3,2,1,0:T(8,128)} %bitcast.10, f32[1,32,32,256]{3,2,1,0:T(8,128)} %bitcast.19, f32[1,32,32,256]{3,2,1,0:T(8,128)} %bitcast.20, f32[3,32,32,256]{3,2,1,0:T(8,128)} %refs_4_.5, f32[3,32,32,256]{3,2,1,0:T(8,128)} %refs_4_.5, ...), custom_call_target="tpu_custom_call" | custom-call | bytes 1500000 | tf_op jit(solution)/shard_map/pack_lanes/pallas_call | solution.py:148
  8.6 1.7 %collective-permute-done = f32[32,32,128]{2,1,0:T(8,128)S(1)} collective-permute-done((f32[32,32,128]{2,1,0:T(8,128)}, f32[32,32,128]{2,1,0:T(8,128)S(1)}, u32[]{:S(2)}, u32[]{:S(2)}) %collective-permute-start) | collective-permute-done | bytes 524320 | tf_op jit(solution)/shard_map/ppermute | solution.py:168
  10.3 0.8 broadcast_select_fusion.refs_2_.refs_5_.refs_4_.refs_10_.refs_11_.refs_3_.refs_7_
  11.1 1.8 %pack_planes.2 = (f32[5,32,256]{2,1,0:T(8,128)}, f32[5,32,256]{2,1,0:T(8,128)}) custom-call(f32[1,32,32,256]{3,2,1,0:T(8,128)} %bitcast.11, f32[1,32,32,256]{3,2,1,0:T(8,128)} %bitcast.21, f32[32,32,128]{2,1,0:T(8,128)} %broadcast_select_fusion.refs_2_.refs_5_.refs_4_.refs_10_.refs_11_.refs_3_.refs_7_), custom_call_target="tpu_custom_call" | custom-call | bytes 1500000 | tf_op jit(solution)/shard_map/pack_planes/pallas_call | solution.py:233
  12.9 4.8 %collective-permute-start.1 = (f32[5,32,256]{2,1,0:T(8,128)}, f32[5,32,256]{2,1,0:T(8,128)S(1)}, u32[]{:S(2)}, u32[]{:S(2)}) collective-permute-start(f32[5,32,256]{2,1,0:T(8,128)} %get-tuple-element.37), channel_id=1, source_target_pairs={{0,8},{8,16},{16,24},{1,9},{9,17},{17,25},{2,10},{10,18},{18,26},{... | collective-permute-start | bytes 491528 | tf_op jit(solution)/shard_map/ppermute | solution.py:88
  17.7 1.3 collective-permute-start.2
  19.0 3.1 %pack_planes.3 = (f32[9,32,256]{2,1,0:T(8,128)}, f32[14,32,256]{2,1,0:T(8,128)}, f32[10,32,256]{2,1,0:T(8,128)}, f32[20,32,256]{2,1,0:T(8,128)}) custom-call(f32[1,32,32,256]{3,2,1,0:T(8,128)} %bitcast.12, f32[1,32,32,256]{3,2,1,0:T(8,128)} %bitcast.22, f32[3,32,32,256]{3,2,1,0:T(8,128)} %refs_4_.5, f32[3,32,32,256]{3,2,1,0:T(8,128)} %refs_5_.5, ...), custom_call_target="tpu_custom_call" | custom-call | bytes 1500000 | tf_op jit(solution)/shard_map/pack_planes/pallas_call | solution.py:233
  22.1 5.0 %collective-permute-done.2.refs_8_.refs_9_.refs_5_.refs_10_.refs_11_.refs_17_ = f32[5,32,256]{2,1,0:T(8,128)S(1)} collective-permute-done((f32[5,32,256]{2,1,0:T(8,128)}, f32[5,32,256]{2,1,0:T(8,128)S(1)}, u32[]{:S(2)}, u32[]{:S(2)}) %collective-permute-start.2) | collective-permute-done | bytes 163872 | tf_op jit(solution)/shard_map/ppermute | solution.py:93
  27.1 1.3 collective-permute-start.6
  28.4 4.6 %collective-permute-start.5 = (f32[9,32,256]{2,1,0:T(8,128)}, f32[9,32,256]{2,1,0:T(8,128)S(1)}, u32[]{:S(2)}, u32[]{:S(2)}) collective-permute-start(f32[9,32,256]{2,1,0:T(8,128)} %get-tuple-element.45), channel_id=1, source_target_pairs={{0,8},{8,16},{16,24},{1,9},{9,17},{17,25},{2,10},{10,18},{18,26},{... | collective-permute-start | bytes 884744 | tf_op jit(solution)/shard_map/ppermute | solution.py:88
  33.0 2.5 %pack_rows.3 = (f32[36,8,256]{2,1,0:T(8,128)}, f32[36,8,256]{2,1,0:T(8,128)}) custom-call(f32[1,32,32,256]{3,2,1,0:T(8,128)} %bitcast.13, f32[1,32,32,256]{3,2,1,0:T(8,128)} %bitcast.14, f32[1,32,32,256]{3,2,1,0:T(8,128)} %bitcast.23, f32[1,32,32,256]{3,2,1,0:T(8,128)} %bitcast.24, ...), custom_call_target="tpu_custom_call" | custom-call | bytes 1500000 | tf_op jit(solution)/shard_map/pack_rows/pallas_call | solution.py:346
  35.4 3.5 %collective-permute-start.3 = (f32[36,8,256]{2,1,0:T(8,128)}, f32[36,8,256]{2,1,0:T(8,128)S(1)}, u32[]{:S(2)}, u32[]{:S(2)}) collective-permute-start(f32[36,8,256]{2,1,0:T(8,128)} %get-tuple-element.43), channel_id=1, source_target_pairs={{0,2},{2,4},{4,6},{1,3},{3,5},{5,7},{8,10},{10,12},{12,14},{9,11},... | collective-permute-start | bytes 884744 | tf_op jit(solution)/shard_map/ppermute | solution.py:88
  38.9 1.3 collective-permute-start.4
  40.2 4.5 %pack_rows.4 = (f32[32,24,256]{2,1,0:T(8,128)}, f32[32,32,256]{2,1,0:T(8,128)}) custom-call(f32[1,32,32,256]{3,2,1,0:T(8,128)} %bitcast.15, f32[1,32,32,256]{3,2,1,0:T(8,128)} %bitcast.16, f32[1,32,32,256]{3,2,1,0:T(8,128)} %bitcast.25, f32[1,32,32,256]{3,2,1,0:T(8,128)} %bitcast.26, f32[3,32,32,256]{3,2,1,0:T(8,128)} %refs_4_.5, ...), custom_call_target="tpu_custom_call" | custom-call | bytes 1500000 | tf_op jit(solution)/shard_map/pack_rows/pallas_call | solution.py:346
  44.8 3.6 %collective-permute-done.4.refs_7_.refs_19_ = f32[36,8,256]{2,1,0:T(8,128)S(1)} collective-permute-done((f32[36,8,256]{2,1,0:T(8,128)}, f32[36,8,256]{2,1,0:T(8,128)S(1)}, u32[]{:S(2)}, u32[]{:S(2)}) %collective-permute-start.4) | collective-permute-done | bytes 294944 | tf_op jit(solution)/shard_map/ppermute | solution.py:93
  48.4 1.3 collective-permute-start.8
  49.7 5.5 %collective-permute-start.7 = (f32[32,24,256]{2,1,0:T(8,128)}, f32[32,24,256]{2,1,0:T(8,128)}, u32[]{:S(2)}, u32[]{:S(2)}) collective-permute-start(f32[32,24,256]{2,1,0:T(8,128)} %get-tuple-element.53), channel_id=1, source_target_pairs={{0,2},{2,4},{4,6},{1,3},{3,5},{5,7},{8,10},{10,12},{12,14},{9,11},... | collective-permute-start | bytes 2359304 | tf_op jit(solution)/shard_map/ppermute | solution.py:88
  55.2 1.3 collective-permute-start.10
  56.5 5.1 %collective-permute-start.9 = (f32[14,32,256]{2,1,0:T(8,128)}, f32[14,32,256]{2,1,0:T(8,128)S(1)}, u32[]{:S(2)}, u32[]{:S(2)}) collective-permute-start(f32[14,32,256]{2,1,0:T(8,128)} %get-tuple-element.55), channel_id=1, source_target_pairs={{0,8},{8,16},{16,24},{1,9},{9,17},{17,25},{2,10},{10,18},{18,26},{... | collective-permute-start | bytes 1376264 | tf_op jit(solution)/shard_map/ppermute | solution.py:88
  62.2 21.6 %moments.1 = f32[1,128]{1,0:T(1,128)} custom-call(f32[6]{0:T(128)} %stack.36.refs_0_, f32[1,32,32,256]{3,2,1,0:T(8,128)} %bitcast.17, f32[1,32,32,256]{3,2,1,0:T(8,128)} %bitcast.27, f32[32,32,128]{2,1,0:T(8,128)} %broadcast_select_fusion.refs_2_.refs_5_.refs_4_.refs_10_.refs_11_.refs_3_.refs_7_, f32[5,32,256]{2,1,0:T(8,128)} %copy-done, ...), custom_call_target="tpu_custom_call" | custom-call | bytes 3000000 | tf_op jit(solution)/shard_map/moments/pallas_call | solution.py:1059
  84.0 1.2 collective-permute-done.11
  85.3 0.7 broadcast_select_fusion.6
  85.9 3.0 %collective-permute-start.12 = (f32[2,128]{1,0:T(2,128)S(1)}, f32[2,128]{1,0:T(2,128)S(1)}, u32[]{:S(2)}, u32[]{:S(2)}) collective-permute-start(f32[2,128]{1,0:T(2,128)S(1)} %pad_maximum_fusion.4), channel_id=1, source_target_pairs={{0,8},{8,0},{16,24},{24,16},{1,9},{9,1},{17,25},{25,17},{2,10},{10... | collective-permute-start | bytes 3080 | tf_op jit(solution)/shard_map/ppermute | solution.py:1007
  88.9 2.3 %pack_rows.5 = (f32[10,32,256]{2,1,0:T(8,128)}, f32[10,40,256]{2,1,0:T(8,128)}) custom-call(f32[9,32,256]{2,1,0:T(8,128)} %copy-done.5, f32[9,32,256]{2,1,0:T(8,128)} %copy-done.5, f32[14,32,256]{2,1,0:T(8,128)} %copy-done.3, f32[14,32,256]{2,1,0:T(8,128)} %copy-done.3, f32[10,32,256]{2,1,0:T(8,128)} %copy-done.4, f32[10,32,256]{2,1,0:T(8,128)} %copy-done.4, ...), custom_call_target="tpu_custom_call" | custom-call | bytes 1500000 | tf_op jit(solution)/shard_map/pack_rows/pallas_call | solution.py:346
  91.2 1.3 collective-permute-start.15
  92.6 4.6 %collective-permute-start.14 = (f32[10,32,256]{2,1,0:T(8,128)}, f32[10,32,256]{2,1,0:T(8,128)S(1)}, u32[]{:S(2)}, u32[]{:S(2)}) collective-permute-start(f32[10,32,256]{2,1,0:T(8,128)} %get-tuple-element.62), channel_id=1, source_target_pairs={{0,2},{2,4},{4,6},{1,3},{3,5},{5,7},{8,10},{10,12},{12,14},{9,11},... | collective-permute-start | bytes 983048 | tf_op jit(solution)/shard_map/ppermute | solution.py:88
  97.2 7.0 %collective-permute-done.14.refs_14_ = f32[10,32,256]{2,1,0:T(8,128)S(1)} collective-permute-done((f32[10,32,256]{2,1,0:T(8,128)}, f32[10,32,256]{2,1,0:T(8,128)S(1)}, u32[]{:S(2)}, u32[]{:S(2)}) %collective-permute-start.14) | collective-permute-done | bytes 327712 | tf_op jit(solution)/shard_map/ppermute | solution.py:88
  104.6 2.1 %collective-permute-start.16 = (f32[8,128]{1,0:T(8,128)S(1)}, f32[8,128]{1,0:T(8,128)S(1)}, u32[]{:S(2)}, u32[]{:S(2)}) collective-permute-start(f32[8,128]{1,0:T(8,128)S(1)} %pad_maximum_fusion.2), channel_id=1, source_target_pairs={{0,2},{2,0},{4,6},{6,4},{1,3},{3,1},{5,7},{7,5},{8,10},{10,8},{12,... | collective-permute-start | bytes 12296 | tf_op jit(solution)/shard_map/ppermute | solution.py:1007
  106.7 1.6 collective-permute-done.16
  108.3 2.9 %collective-permute-start.17 = (f32[16,128]{1,0:T(8,128)S(1)}, f32[16,128]{1,0:T(8,128)S(1)}, u32[]{:S(2)}, u32[]{:S(2)}) collective-permute-start(f32[16,128]{1,0:T(8,128)S(1)} %pad_maximum_fusion.1), channel_id=1, source_target_pairs={{0,4},{2,6},{4,0},{6,2},{1,5},{3,7},{5,1},{7,3},{8,12},{10,14},{12... | collective-permute-start | bytes 24584 | tf_op jit(solution)/shard_map/ppermute | solution.py:1007
  111.2 1.6 collective-permute-done.17
  113.5 56.4 %step.1 = (f32[3,32,32,256]{3,2,1,0:T(8,128)}, f32[3,32,32,256]{3,2,1,0:T(8,128)}, f32[3,32,32,256]{3,2,1,0:T(8,128)}, f32[32,32,256]{2,1,0:T(8,128)}, f32[32,32,256]{2,1,0:T(8,128)}) custom-call(f32[6]{0:T(128)} %stack.36.refs_0_, f32[32,128]{1,0:T(8,128)} %pad_maximum_fusion.refs_1_, f32[1,32,32,256]{3,2,1,0:T(8,128)} %bitcast.18, ...), custom_call_target="tpu_custom_call" | custom-call | bytes 3000000 | tf_op jit(solution)/shard_map/step/pallas_call | solution.py:1086
  (46 shorter events, 2.3 us)
Async XLA Ops:
  8.1 2.2 %collective-permute-start = (f32[32,32,128]{2,1,0:T(8,128)}, f32[32,32,128]{2,1,0:T(8,128)S(1)}, u32[]{:S(2)}, u32[]{:S(2)}) collective-permute-start(f32[32,32,128]{2,1,0:T(8,128)} %pack_lanes.1), channel_id=1, source_target_pairs={{0,1},{1,0},{2,3},{3,2},{4,5},{5,4},{6,7},{7,6},{8,9},{9,8},{10,11... | collective-permute-start | bytes 1572872 | tf_op jit(solution)/shard_map/ppermute | solution.py:168
  12.9 9.2 %collective-permute-start.1 = (f32[5,32,256]{2,1,0:T(8,128)}, f32[5,32,256]{2,1,0:T(8,128)S(1)}, u32[]{:S(2)}, u32[]{:S(2)}) collective-permute-start(f32[5,32,256]{2,1,0:T(8,128)} %get-tuple-element.37), channel_id=1, source_target_pairs={{0,8},{8,16},{16,24},{1,9},{9,17},{17,25},{2,10},{10,18},{18,26},{... | collective-permute-start | bytes 491528 | tf_op jit(solution)/shard_map/ppermute | solution.py:88
  17.7 9.4 %collective-permute-start.2 = (f32[5,32,256]{2,1,0:T(8,128)}, f32[5,32,256]{2,1,0:T(8,128)S(1)}, u32[]{:S(2)}, u32[]{:S(2)}) collective-permute-start(f32[5,32,256]{2,1,0:T(8,128)} %get-tuple-element.38), channel_id=1, source_target_pairs={{8,0},{16,8},{24,16},{9,1},{17,9},{25,17},{10,2},{18,10},{26,18},{... | collective-permute-start | bytes 491528 | tf_op jit(solution)/shard_map/ppermute | solution.py:93
  22.1 10.9 %copy-start = (f32[5,32,256]{2,1,0:T(8,128)}, f32[5,32,256]{2,1,0:T(8,128)S(1)}, u32[]{:S(2)}) copy-start(f32[5,32,256]{2,1,0:T(8,128)S(1)} %collective-permute-done.1.refs_6_.refs_7_.refs_4_.refs_8_.refs_9_.refs_16_) | copy-start | bytes 491524
  27.1 5.9 %copy-start.1 = (f32[5,32,256]{2,1,0:T(8,128)}, f32[5,32,256]{2,1,0:T(8,128)S(1)}, u32[]{:S(2)}) copy-start(f32[5,32,256]{2,1,0:T(8,128)S(1)} %collective-permute-done.2.refs_8_.refs_9_.refs_5_.refs_10_.refs_11_.refs_17_) | copy-start | bytes 491524
  27.1 21.3 %collective-permute-start.6 = (f32[10,32,256]{2,1,0:T(8,128)}, f32[10,32,256]{2,1,0:T(8,128)S(1)}, u32[]{:S(2)}, u32[]{:S(2)}) collective-permute-start(f32[10,32,256]{2,1,0:T(8,128)} %get-tuple-element.46), channel_id=1, source_target_pairs={{8,0},{16,8},{24,16},{9,1},{17,9},{25,17},{10,2},{18,10},{26,18},{... | collective-permute-start | bytes 983048 | tf_op jit(solution)/shard_map/ppermute | solution.py:93
  28.4 16.4 %collective-permute-start.5 = (f32[9,32,256]{2,1,0:T(8,128)}, f32[9,32,256]{2,1,0:T(8,128)S(1)}, u32[]{:S(2)}, u32[]{:S(2)}) collective-permute-start(f32[9,32,256]{2,1,0:T(8,128)} %get-tuple-element.45), channel_id=1, source_target_pairs={{0,8},{8,16},{16,24},{1,9},{9,17},{17,25},{2,10},{10,18},{18,26},{... | collective-permute-start | bytes 884744 | tf_op jit(solution)/shard_map/ppermute | solution.py:88
  35.4 9.3 %collective-permute-start.3 = (f32[36,8,256]{2,1,0:T(8,128)}, f32[36,8,256]{2,1,0:T(8,128)S(1)}, u32[]{:S(2)}, u32[]{:S(2)}) collective-permute-start(f32[36,8,256]{2,1,0:T(8,128)} %get-tuple-element.43), channel_id=1, source_target_pairs={{0,2},{2,4},{4,6},{1,3},{3,5},{5,7},{8,10},{10,12},{12,14},{9,11},... | collective-permute-start | bytes 884744 | tf_op jit(solution)/shard_map/ppermute | solution.py:88
  38.9 9.5 %collective-permute-start.4 = (f32[36,8,256]{2,1,0:T(8,128)}, f32[36,8,256]{2,1,0:T(8,128)S(1)}, u32[]{:S(2)}, u32[]{:S(2)}) collective-permute-start(f32[36,8,256]{2,1,0:T(8,128)} %get-tuple-element.44), channel_id=1, source_target_pairs={{2,0},{4,2},{6,4},{3,1},{5,3},{7,5},{10,8},{12,10},{14,12},{11,9},... | collective-permute-start | bytes 884744 | tf_op jit(solution)/shard_map/ppermute | solution.py:93
  44.8 44.1 %copy-start.5 = (f32[9,32,256]{2,1,0:T(8,128)}, f32[9,32,256]{2,1,0:T(8,128)S(1)}, u32[]{:S(2)}) copy-start(f32[9,32,256]{2,1,0:T(8,128)S(1)} %collective-permute-done.5.refs_0_.refs_1_.refs_8_) | copy-start | bytes 884740
  44.8 17.5 %copy-start.6 = (f32[36,8,256]{2,1,0:T(8,128)}, f32[36,8,256]{2,1,0:T(8,128)S(1)}, u32[]{:S(2)}) copy-start(f32[36,8,256]{2,1,0:T(8,128)S(1)} %collective-permute-done.3.refs_6_.refs_18_) | copy-start | bytes 884740
  48.4 1.3 copy-start.7
  48.4 40.5 %copy-start.4 = (f32[10,32,256]{2,1,0:T(8,128)}, f32[10,32,256]{2,1,0:T(8,128)S(1)}, u32[]{:S(2)}) copy-start(f32[10,32,256]{2,1,0:T(8,128)S(1)} %collective-permute-done.6.refs_4_.refs_5_.refs_10_) | copy-start | bytes 983044
  48.4 35.5 %collective-permute-start.8 = (f32[32,32,256]{2,1,0:T(8,128)}, f32[32,32,256]{2,1,0:T(8,128)}, u32[]{:S(2)}, u32[]{:S(2)}) collective-permute-start(f32[32,32,256]{2,1,0:T(8,128)} %get-tuple-element.54), channel_id=1, source_target_pairs={{2,0},{4,2},{6,4},{3,1},{5,3},{7,5},{10,8},{12,10},{14,12},{11,9},... | collective-permute-start | bytes 3145736 | tf_op jit(solution)/shard_map/ppermute | solution.py:93
  49.7 34.2 %collective-permute-start.7 = (f32[32,24,256]{2,1,0:T(8,128)}, f32[32,24,256]{2,1,0:T(8,128)}, u32[]{:S(2)}, u32[]{:S(2)}) collective-permute-start(f32[32,24,256]{2,1,0:T(8,128)} %get-tuple-element.53), channel_id=1, source_target_pairs={{0,2},{2,4},{4,6},{1,3},{3,5},{5,7},{8,10},{10,12},{12,14},{9,11},... | collective-permute-start | bytes 2359304 | tf_op jit(solution)/shard_map/ppermute | solution.py:88
  55.2 28.7 %collective-permute-start.10 = (f32[20,32,256]{2,1,0:T(8,128)}, f32[20,32,256]{2,1,0:T(8,128)S(1)}, u32[]{:S(2)}, u32[]{:S(2)}) collective-permute-start(f32[20,32,256]{2,1,0:T(8,128)} %get-tuple-element.56), channel_id=1, source_target_pairs={{8,0},{16,8},{24,16},{9,1},{17,9},{25,17},{10,2},{18,10},{26,18},{... | collective-permute-start | bytes 1966088 | tf_op jit(solution)/shard_map/ppermute | solution.py:93
  56.5 27.4 %collective-permute-start.9 = (f32[14,32,256]{2,1,0:T(8,128)}, f32[14,32,256]{2,1,0:T(8,128)S(1)}, u32[]{:S(2)}, u32[]{:S(2)}) collective-permute-start(f32[14,32,256]{2,1,0:T(8,128)} %get-tuple-element.55), channel_id=1, source_target_pairs={{0,8},{8,16},{16,24},{1,9},{9,17},{17,25},{2,10},{10,18},{18,26},{... | collective-permute-start | bytes 1376264 | tf_op jit(solution)/shard_map/ppermute | solution.py:88
  83.9 5.0 %copy-start.3 = (f32[14,32,256]{2,1,0:T(8,128)}, f32[14,32,256]{2,1,0:T(8,128)S(1)}, u32[]{:S(2)}) copy-start(f32[14,32,256]{2,1,0:T(8,128)S(1)} %collective-permute-done.9.refs_2_.refs_3_.refs_9_) | copy-start | bytes 1376260
  83.9 5.0 %copy-start.2 = (f32[20,32,256]{2,1,0:T(8,128)}, f32[20,32,256]{2,1,0:T(8,128)S(1)}, u32[]{:S(2)}) copy-start(f32[20,32,256]{2,1,0:T(8,128)S(1)} %collective-permute-done.10.refs_6_.refs_7_.refs_11_) | copy-start | bytes 1966084
  83.9 1.3 collective-permute-start.11
  85.9 6.6 %collective-permute-start.12 = (f32[2,128]{1,0:T(2,128)S(1)}, f32[2,128]{1,0:T(2,128)S(1)}, u32[]{:S(2)}, u32[]{:S(2)}) collective-permute-start(f32[2,128]{1,0:T(2,128)S(1)} %pad_maximum_fusion.4), channel_id=1, source_target_pairs={{0,8},{8,0},{16,24},{24,16},{1,9},{9,1},{17,25},{25,17},{2,10},{10... | collective-permute-start | bytes 3080 | tf_op jit(solution)/shard_map/ppermute | solution.py:1007
  91.2 13.4 %collective-permute-start.15 = (f32[10,40,256]{2,1,0:T(8,128)}, f32[10,40,256]{2,1,0:T(8,128)S(1)}, u32[]{:S(2)}, u32[]{:S(2)}) collective-permute-start(f32[10,40,256]{2,1,0:T(8,128)} %get-tuple-element.63), channel_id=1, source_target_pairs={{2,0},{4,2},{6,4},{3,1},{5,3},{7,5},{10,8},{12,10},{14,12},{11,9},... | collective-permute-start | bytes 1228808 | tf_op jit(solution)/shard_map/ppermute | solution.py:93
  92.5 4.7 %collective-permute-start.13 = (f32[4,128]{1,0:T(4,128)S(1)}, f32[4,128]{1,0:T(4,128)S(1)}, u32[]{:S(2)}, u32[]{:S(2)}) collective-permute-start(f32[4,128]{1,0:T(4,128)S(1)} %pad_maximum_fusion.3), channel_id=1, source_target_pairs={{0,16},{8,24},{16,0},{24,8},{1,17},{9,25},{17,1},{25,9},{2,18},{10... | collective-permute-start | bytes 6152 | tf_op jit(solution)/shard_map/ppermute | solution.py:1007
  92.6 11.6 %collective-permute-start.14 = (f32[10,32,256]{2,1,0:T(8,128)}, f32[10,32,256]{2,1,0:T(8,128)S(1)}, u32[]{:S(2)}, u32[]{:S(2)}) collective-permute-start(f32[10,32,256]{2,1,0:T(8,128)} %get-tuple-element.62), channel_id=1, source_target_pairs={{0,2},{2,4},{4,6},{1,3},{3,5},{5,7},{8,10},{10,12},{12,14},{9,11},... | collective-permute-start | bytes 983048 | tf_op jit(solution)/shard_map/ppermute | solution.py:88
  104.3 9.2 %copy-start.9 = (f32[10,32,256]{2,1,0:T(8,128)}, f32[10,32,256]{2,1,0:T(8,128)S(1)}, u32[]{:S(2)}) copy-start(f32[10,32,256]{2,1,0:T(8,128)S(1)} %collective-permute-done.14.refs_14_) | copy-start | bytes 983044
  104.6 8.9 %copy-start.8 = (f32[10,40,256]{2,1,0:T(8,128)}, f32[10,40,256]{2,1,0:T(8,128)S(1)}, u32[]{:S(2)}) copy-start(f32[10,40,256]{2,1,0:T(8,128)S(1)} %collective-permute-done.15.refs_15_) | copy-start | bytes 1228804
  104.6 3.7 %collective-permute-start.16 = (f32[8,128]{1,0:T(8,128)S(1)}, f32[8,128]{1,0:T(8,128)S(1)}, u32[]{:S(2)}, u32[]{:S(2)}) collective-permute-start(f32[8,128]{1,0:T(8,128)S(1)} %pad_maximum_fusion.2), channel_id=1, source_target_pairs={{0,2},{2,0},{4,6},{6,4},{1,3},{3,1},{5,7},{7,5},{8,10},{10,8},{12,... | collective-permute-start | bytes 12296 | tf_op jit(solution)/shard_map/ppermute | solution.py:1007
  108.3 4.6 %collective-permute-start.17 = (f32[16,128]{1,0:T(8,128)S(1)}, f32[16,128]{1,0:T(8,128)S(1)}, u32[]{:S(2)}, u32[]{:S(2)}) collective-permute-start(f32[16,128]{1,0:T(8,128)S(1)} %pad_maximum_fusion.1), channel_id=1, source_target_pairs={{0,4},{2,6},{4,0},{6,2},{1,5},{3,7},{5,1},{7,3},{8,12},{10,14},{12... | collective-permute-start | bytes 24584 | tf_op jit(solution)/shard_map/ppermute | solution.py:1007

commit v5 on v4

--- a/solution.py
+++ b/solution.py
@@ -177,7 +177,7 @@
         at -= part.shape[0]
 
 
-def pack_planes(plan, arrays, packed):
+def pack_planes(plan, flags, arrays, packed):
     needed = [
         max(low if to_low else high for _, low, high in plan.groups) for to_low in (True, False)
     ]
@@ -187,6 +187,7 @@
 
     def kernel(*refs):
         groups = len(plan.groups)
+        edge, refs = refs[0], refs[1:]
         own, packed_ref = refs[:groups], refs[groups]
         count = len(plan.parts[0])
         outs = refs[groups + 1 : groups + 1 + count], refs[groups + 1 + count : groups + 1 + 2 * count]
@@ -223,6 +224,13 @@
                 part, at = part_of(out, at)
                 part[at : at + depth] = plan.value(field.group, field.component, get)
 
+        for side, parts in enumerate(outs):
+
+            @pl.when(edge[1 - side] == 0.0)
+            def _(parts=parts):
+                for part in parts:
+                    part[...] = jnp.zeros(part.shape, jnp.float32)
+
     shapes = [(size, plan.y, plan.z) for side in plan.parts for size in side]
     scratch = [
         pltpu.VMEM((array.shape[0], depth, plan.y, plan.z), array.dtype)
@@ -232,26 +240,29 @@
     count = 2 * len(arrays) + sum(needed)
     outs = pl.pallas_call(
         kernel,
-        in_specs=[any_space()] * (len(arrays) + 1),
+        in_specs=[in_smem()] + [any_space()] * (len(arrays) + 1),
         out_specs=[in_vmem()] * len(shapes),
         out_shape=[jax.ShapeDtypeStruct(shape, jnp.float32) for shape in shapes],
         scratch_shapes=scratch + [pltpu.SemaphoreType.DMA((count,))],
         compiler_params=pltpu.CompilerParams(vmem_limit_bytes=VMEM_BYTES),
         cost_estimate=cost(0.5),
         name="pack_planes",
-    )(*arrays, packed)
+    )(flags, *arrays, packed)
     return list(zip(outs[: len(plan.parts[0])], outs[len(plan.parts[0]) :]))
 
 
-def pack_rows(plan, arrays, packed, own, planes=(), inner_planes=()):
+def pack_rows(plan, flags, arrays, packed, own, planes=(), inner_planes=()):
     groups = len(plan.groups)
     sizes, packed_at = plan.sizes[2:], plan.packed_at[2:]
     if own:
         sizes, packed_at = plan.sizes[:2], plan.packed_at[:2]
 
-    def kernel(*refs):
-        refs = list(refs)
-        up, down = refs[-2:]
+    def kernel(flags, *refs):
+        for parity in range(2):
+            up, down = refs[-2:] if parity == 0 else refs[:-3:-1]
+            pl.when(flags[6] == parity)(functools.partial(pack, flags, list(refs[:-2]), up, down))
+
+    def pack(flags, refs, up, down):
         up[...] = jnp.zeros(up.shape, jnp.float32)
         down[...] = jnp.zeros(down.shape, jnp.float32)
 
@@ -328,8 +339,16 @@
                     put_packed(base + k, *find(sides[side], source), lanes)
                 base += plan.low
 
+        @pl.when(flags[3] == 0.0)
+        def _():
+            up[...] = jnp.zeros(up.shape, jnp.float32)
+
+        @pl.when(flags[2] == 0.0)
+        def _():
+            down[...] = jnp.zeros(down.shape, jnp.float32)
+
     last = plan.y // ROWS - 1
-    specs, operands = [], []
+    specs, operands = [in_smem()], [flags]
     if own:
         for array in arrays:
             block = (array.shape[0], plan.x, ROWS, plan.z)
@@ -342,7 +361,7 @@
         specs.append(pl.BlockSpec(block, lambda i: (0, last, 0)))
         operands += [array, array]
     count = plan.x * own + (plan.low + plan.high) * bool(planes)
-    shapes = [(count, round_up(size, ROWS), plan.z) for size in sizes]
+    shapes = [(count, round_up(max(sizes), ROWS), plan.z)] * 2
     return pl.pallas_call(
         kernel,
         grid=(1,),
@@ -355,18 +374,30 @@
     )(*operands)
 
 
-def exchange(axis, pair):
-    return [from_behind(pair[0], axis), from_ahead(pair[1], axis)]
-
-
-def assemble(plan, arrays, messages, inner, extended, packed_ext, pinned_own, semaphores):
+def exchange_planes(pair):
+    count = lax.axis_size("bx")
+    return [
+        lax.ppermute(one, "bx", [(i, (i + step) % count) for i in range(count)])
+        for one, step in zip(pair, (1, -1))
+    ]
+
+
+def exchange_rows(pair):
+    count = lax.axis_size("by")
+    got = []
+    for parity, one in enumerate(pair):
+        partner = list(range(count))
+        for i in range(parity, count - 1, 2):
+            partner[i], partner[i + 1] = i + 1, i
+        got.append(lax.ppermute(one, "by", list(enumerate(partner))))
+    return got
+
+
+def assemble(plan, flags, arrays, messages, inner, extended, packed_ext, pinned_own, semaphores):
     count = len(plan.parts[0])
     packed, below, above = messages[0], messages[1 : 1 + count], messages[1 + count : 1 + 2 * count]
     rest = messages[1 + 2 * count :]
-    if len(rest) == 2:
-        sides = [(rest[0], rest[0], plan.x), (rest[1], rest[1], plan.x)]
-    else:
-        sides = [(rest[0], rest[2], 0), (rest[1], rest[3], 0)]
+    own_messages, halo_messages, halo_at = rest[:2], rest[-2:], plan.x if len(rest) == 2 else 0
     copies = []
 
     def copy(source, target):
@@ -420,7 +451,7 @@
 
     top = ROWS + plan.y
 
-    def fill(i, left, right, at, own):
+    def fill(i, left, right, inner_left, inner_right, at, own):
         def rows(field, first, source, source_at, count):
             if count:
                 for t in range(plan.tiles):
@@ -436,8 +467,8 @@
                 rows(field, top + skip, right, field.high_at, high - skip)
                 if skip:
                     other = plan.inner.fields[field.group]
-                    rows(field, ROWS - skip, inner[2], other.low_at, skip)
-                    rows(field, top, inner[3], other.high_at, skip)
+                    rows(field, ROWS - skip, inner_left, other.low_at, skip)
+                    rows(field, top, inner_right, other.high_at, skip)
             else:
                 rows(field, ROWS - low, left, field.full_low_at, low)
                 rows(field, top, right, field.full_high_at, high)
@@ -454,9 +485,28 @@
                 tile, (LANES - field.start) % LANES, 1
             )
 
-    def own_plane(x, _):
-        fill(plan.low + x, sides[0][0], sides[1][0], x, True)
-        return 0
+    def fill_all(parity):
+        def ordered(pair):
+            return pair[::-1] if parity == 0 else pair
+
+        own, halo = ordered(own_messages), ordered(halo_messages)
+        inner_rows = (None, None) if inner is None else ordered(inner[2:4])
+
+        def own_plane(x, _):
+            fill(plan.low + x, *own, *inner_rows, x, True)
+            return 0
+
+        def low_plane(k, _):
+            fill(k, *halo, None, None, halo_at + k, False)
+            return 0
+
+        def high_plane(k, _):
+            fill(plan.low + plan.x + k, *halo, None, None, halo_at + plan.low + k, False)
+            return 0
+
+        lax.fori_loop(0, plan.x, own_plane, 0)
+        lax.fori_loop(0, plan.low, low_plane, 0)
+        lax.fori_loop(0, plan.high, high_plane, 0)
 
     def finish_plane(x, _):
         i = plan.low + x
@@ -472,18 +522,8 @@
                 extended[group][(component, *at)] = plan.value(group, component, get)
         return 0
 
-    def low_plane(k, _):
-        fill(k, sides[0][1], sides[1][1], sides[0][2] + k, False)
-        return 0
-
-    def high_plane(k, _):
-        at = sides[0][2] + plan.low + k
-        fill(plan.low + plan.x + k, sides[0][1], sides[1][1], at, False)
-        return 0
-
-    lax.fori_loop(0, plan.x, own_plane, 0)
-    lax.fori_loop(0, plan.low, low_plane, 0)
-    lax.fori_loop(0, plan.high, high_plane, 0)
+    for parity in range(2):
+        pl.when(flags[6] == parity)(functools.partial(fill_all, parity))
     for one in copies[:large]:
         one.wait()
     if pinned_own is not None:
@@ -651,6 +691,7 @@
     density_ext, energy_ext, packed_ext, force, image, mass, semaphores = refs[9:]
     assemble(
         plan,
+        flags,
         [density, energy],
         messages,
         None,
@@ -807,6 +848,7 @@
     ) = refs[25:]
     assemble(
         plan,
+        flags,
         [density, energy, position, velocity, pinned],
         messages,
         inner,
@@ -1031,6 +1073,7 @@
                 lax.axis_index(axis) < lax.axis_size(axis) - 1,
             )
         ]
+        + [(lax.axis_index("by") % 2).astype(jnp.float32)]
     )
     groups = [
         (1, WIDE, WIDE),
@@ -1039,22 +1082,25 @@
         (3, 1, 2),
         (1, SWEEPS - 1, SWEEPS),
     ]
-    starts = Plan(groups, shape).starts
-    narrow = Plan([(1, NARROW, NARROW)] * 2, shape, None, starts)
-    wide = Plan(groups, shape, narrow, cut=3)
-
-    packed = exchange_lanes(wide, pack_lanes(wide, arrays))
-    planes = exchange("bx", *pack_planes(narrow, arrays[:2], packed))
-    first_planes, last_planes = pack_planes(wide, arrays, packed)
-    wide_rows = pack_rows(wide, arrays, packed, True)
-    planes, first_planes = lax.optimization_barrier((planes, first_planes))
-    rows = exchange("by", pack_rows(narrow, arrays[:2], packed, True, planes))
-    first_planes = exchange("bx", first_planes)
+    narrow = Plan([(1, NARROW, NARROW)] * 2, shape)
+    wide = Plan(groups, shape, narrow, cut=5)
+    cells = arrays[:2]
+
+    packed = exchange_lanes(narrow, pack_lanes(narrow, cells))
+    planes = exchange_planes(*pack_planes(narrow, flags, cells, packed))
+    wide_lanes = pack_lanes(wide, arrays)
+    planes, wide_lanes = lax.optimization_barrier((planes, wide_lanes))
+    wide_packed = exchange_lanes(wide, wide_lanes)
+    rows = exchange_rows(pack_rows(narrow, flags, cells, packed, True, planes))
+
+    first_planes, last_planes = pack_planes(wide, flags, arrays, wide_packed)
+    wide_rows = pack_rows(wide, flags, arrays, wide_packed, True)
     rows, first_planes, last_planes, wide_rows = lax.optimization_barrier(
         (rows, first_planes, last_planes, wide_rows)
     )
-    last_planes = exchange("bx", last_planes)
-    wide_rows = exchange("by", wide_rows)
+    first_planes = exchange_planes(first_planes)
+    last_planes = exchange_planes(last_planes)
+    wide_rows = exchange_rows(wide_rows)
 
     line = pl.pallas_call(
         functools.partial(moments_kernel, narrow),
@@ -1073,21 +1119,21 @@
         compiler_params=pltpu.CompilerParams(vmem_limit_bytes=VMEM_BYTES),
         cost_estimate=cost(1),
         name="moments",
-    )(flags, *arrays[:2], packed, *planes, *rows)
-
-    line, wide_rows, last_planes = lax.optimization_barrier((line, wide_rows, last_planes))
+    )(flags, *cells, packed, *planes, *rows)
+
+    line, wide_rows, first_planes = lax.optimization_barrier((line, wide_rows, first_planes))
+    lines = gather_lines(line, ("bz", "by"))
+    lines, last_planes = lax.optimization_barrier((lines, last_planes))
     wide_planes = [pair[side] for side in range(2) for pair in (first_planes, last_planes)]
-    corners = exchange("by", pack_rows(wide, None, None, False, wide_planes, planes))
-    lines = gather_lines(line, ("bz", "bx"))
-    lines, corners = lax.optimization_barrier((lines, corners))
-    messages = [packed, *wide_planes, *wide_rows, *corners]
+    corners = exchange_rows(pack_rows(wide, flags, None, None, False, wide_planes, planes))
+    messages = [wide_packed, *wide_planes, *wide_rows, *corners]
     nodes = jax.ShapeDtypeStruct((3, *shape), jnp.float32)
-    cells = jax.ShapeDtypeStruct(shape, jnp.float32)
+    cell = jax.ShapeDtypeStruct(shape, jnp.float32)
     return pl.pallas_call(
         functools.partial(step_kernel, wide),
         in_specs=[in_smem(), in_vmem()] + [any_space()] * 5 + message_specs(5, 4) + message_specs(2, 2),
         out_specs=[any_space()] * 5,
-        out_shape=[nodes, nodes, nodes, cells, cells],
+        out_shape=[nodes, nodes, nodes, cell, cell],
         scratch_shapes=[
             extended_scratch(wide, 1),
             extended_scratch(wide, 1),
@@ -1105,7 +1151,7 @@
         compiler_params=pltpu.CompilerParams(vmem_limit_bytes=VMEM_BYTES),
         cost_estimate=cost(1),
         name="step",
-    )(flags, gather_lines(lines, ("by",)), *arrays, *messages, *planes, *rows)
+    )(flags, gather_lines(lines, ("bx",)), *arrays, *messages, *planes, *rows)
 
 
 def solution(mesh):

time: 171 us -> 172 us (level)
  starting transfers between devices: 44.2 us -> 31.2 us
  Pallas kernels: 99.6 us -> 107 us
  waiting for transfers between devices: 22.2 us -> 25.7 us
  local copies, waits for them, and re-layouts: 0.14 us -> 2.86 us
    ppermute x12, starting transfers between devices: 35.6 us -> 28.3 us  [the longest x6 19.4 us: exchange_rows(): got.append(lax.ppermute(one, 'by', list(enumerate(partner))))]
    ppermute x5, starting transfers between devices: 8.15 us -> 2.42 us  [gather_lines(): got = lax.ppermute(line, axis, [(i, i ^ step) for i in range(count)])]
    pallas_call x1 -> x2, Pallas kernels: 7.45 us -> 13 us  [pack_lanes(): pl.pallas_call(kernel, grid=(plan.x // planes,), in_specs=specs, out_spec...]
    ppermute x5, waiting for transfers between devices: 4.45 us -> 9.37 us  [gather_lines(): got = lax.ppermute(line, axis, [(i, i ^ step) for i in range(count)])]
    unnamed x20 -> x22, local copies, waits for them, and re-layouts: 0.04 us -> 2.2 us
  transfers between devices with their start and end apart: 18 -> 19, of which waited for: 8 -> 9; matrix products, arithmetic and copies ran while one was open for 0% -> 1% of each run, Pallas kernels for 20% -> 25%
where the time goes in v5:
time: 172 us; the launch traced here: 171 us
  Pallas kernels  107 us (62%)
  starting transfers between devices  31.2 us (18%)
  waiting for transfers between devices  25.7 us (15%)
  other arithmetic  3 us (2%)
  local copies, waits for them, and re-layouts  2.86 us (2%)
    pallas_call x1, Pallas kernels, on_device(): pl.pallas_call(functools.partial(step_kernel, wide), in_specs=[in_smem(),...  56.5 us
    pallas_call x1, Pallas kernels, on_device(): pl.pallas_call(functools.partial(moments_kernel, narrow), in_specs=[in_sm...  21.6 us
    ppermute x6, starting transfers between devices, exchange_rows(): got.append(lax.ppermute(one, 'by', list(enumerate(partner))))  19.4 us
    pallas_call x2, Pallas kernels, pack_lanes(): pl.pallas_call(kernel, grid=(plan.x // planes,), in_specs=specs, out_spec...  13 us
    ppermute x6, waiting for transfers between devices, exchange_planes(): lax.ppermute(one, 'bx', [(i, (i + step) % count) for i in range(count)])  12.1 us
    pallas_call x3, Pallas kernels, pack_rows(): pl.pallas_call(kernel, grid=(1,), in_specs=specs, out_specs=[pl.BlockSpec...  9.67 us
    ppermute x5, waiting for transfers between devices, gather_lines(): got = lax.ppermute(line, axis, [(i, i ^ step) for i in range(count)])  9.37 us
    ppermute x6, starting transfers between devices, exchange_planes(): lax.ppermute(one, 'bx', [(i, (i + step) % count) for i in range(count)])  8.93 us
  transfers between devices with their start and end apart: 19, of which 9 were waited for; matrix products, arithmetic and copies ran while one was open for 1% of the time, Pallas kernels for 25%

profile of v5, /device:TPU:0, one launch (start us, length us, event | category | flops | bytes accessed | tf_op | source)
XLA Modules:
  0.0 170.7 jit_solution(9024030390781956954)
XLA Ops:
  0.6 5.6 %pack_lanes.2 = f32[32,32,128]{2,1,0:T(8,128)} custom-call(f32[1,32,32,256]{3,2,1,0:T(8,128)} %bitcast.10, f32[1,32,32,256]{3,2,1,0:T(8,128)} %bitcast.11, f32[1,32,32,256]{3,2,1,0:T(8,128)} %bitcast.22, f32[1,32,32,256]{3,2,1,0:T(8,128)} %bitcast.23), custom_call_target="tpu_custom_call" | custom-call | bytes 1500000 | tf_op jit(solution)/shard_map/pack_lanes/pallas_call | solution.py:148
  7.4 1.1 collective-permute-done
  8.4 0.8 broadcast_select_fusion.1.refs_3_.refs_4_.refs_5_
  9.3 2.5 %pack_planes.2 = (f32[5,32,256]{2,1,0:T(8,128)}, f32[5,32,256]{2,1,0:T(8,128)}) custom-call(f32[7]{0:T(128)} %stack.55.refs_0_.flags, f32[1,32,32,256]{3,2,1,0:T(8,128)} %bitcast.12, f32[1,32,32,256]{3,2,1,0:T(8,128)} %bitcast.24, f32[32,32,128]{2,1,0:T(8,128)} %broadcast_select_fusion.1.refs_3_.refs_4_.refs_5_), custom_call_target="tpu_custom_call" | custom-call | bytes 1500000 | tf_op jit(solution)/shard_map/pack_planes/pallas_call | solution.py:241
  11.7 2.9 %collective-permute-start.1 = (f32[5,32,256]{2,1,0:T(8,128)}, f32[5,32,256]{2,1,0:T(8,128)S(1)}, u32[]{:S(2)}, u32[]{:S(2)}) collective-permute-start(f32[5,32,256]{2,1,0:T(8,128)} %get-tuple-element.36), channel_id=1, source_target_pairs={{0,8},{8,16},{16,24},{24,0},{1,9},{9,17},{17,25},{25,1},{2,10},{10... | collective-permute-start | bytes 491528 | tf_op jit(solution)/shard_map/ppermute | solution.py:380
  14.6 1.0 collective-permute-start.2
  15.7 7.4 %pack_lanes.3 = f32[32,32,128]{2,1,0:T(8,128)} custom-call(f32[1,32,32,256]{3,2,1,0:T(8,128)} %bitcast.13, f32[1,32,32,256]{3,2,1,0:T(8,128)} %bitcast.14, f32[1,32,32,256]{3,2,1,0:T(8,128)} %bitcast.25, f32[1,32,32,256]{3,2,1,0:T(8,128)} %bitcast.26, f32[3,32,32,256]{3,2,1,0:T(8,128)} %refs_4_.7, f32[3,32,32,256]{3,2,1,0:T(8,128)} %refs_4_.7, ...), custom_call_target="tpu_custom_call" | custom-call | bytes 1500000 | tf_op jit(solution)/shard_map/pack_lanes/pallas_call | solution.py:148
  23.1 1.0 collective-permute-done.2.refs_8_.refs_9_.refs_5_.refs_10_.refs_11_.refs_17_
  24.7 2.5 %pack_rows.3 = (f32[36,8,256]{2,1,0:T(8,128)}, f32[36,8,256]{2,1,0:T(8,128)}) custom-call(f32[7]{0:T(128)} %stack.55.refs_0_.flags, f32[1,32,32,256]{3,2,1,0:T(8,128)} %bitcast.15, f32[1,32,32,256]{3,2,1,0:T(8,128)} %bitcast.16, f32[1,32,32,256]{3,2,1,0:T(8,128)} %bitcast.27, f32[1,32,32,256]{3,2,1,0:T(8,128)} %bitcast.28, ...), custom_call_target="tpu_custom_call" | custom-call | bytes 1500000 | tf_op jit(solution)/shard_map/pack_rows/pallas_call | solution.py:365
  27.2 1.6 collective-permute-start.3
  28.8 1.6 collective-permute-start.4
  30.4 0.9 broadcast_select_fusion.refs_6_.refs_10_.refs_11_.refs_7_
  31.3 3.9 %pack_planes.3 = (f32[15,32,256]{2,1,0:T(8,128)}, f32[8,32,256]{2,1,0:T(8,128)}, f32[18,32,256]{2,1,0:T(8,128)}, f32[12,32,256]{2,1,0:T(8,128)}) custom-call(f32[7]{0:T(128)} %stack.55.refs_0_.flags, f32[1,32,32,256]{3,2,1,0:T(8,128)} %bitcast.17, f32[1,32,32,256]{3,2,1,0:T(8,128)} %bitcast.29, f32[3,32,32,256]{3,2,1,0:T(8,128)} %refs_4_.7, ...), custom_call_target="tpu_custom_call" | custom-call | bytes 1500000 | tf_op jit(solution)/shard_map/pack_planes/pallas_call | solution.py:241
  35.2 4.8 %pack_rows.4 = (f32[32,32,256]{2,1,0:T(8,128)}, f32[32,32,256]{2,1,0:T(8,128)}) custom-call(f32[7]{0:T(128)} %stack.55.refs_0_.flags, f32[1,32,32,256]{3,2,1,0:T(8,128)} %bitcast.18, f32[1,32,32,256]{3,2,1,0:T(8,128)} %bitcast.19, f32[1,32,32,256]{3,2,1,0:T(8,128)} %bitcast.30, f32[1,32,32,256]{3,2,1,0:T(8,128)} %bitcast.31, f32[3,32,32,256]{3,2,1,0:T(8,128)} %refs_4_.7, ...), custom_call_target="tpu_custom_call" | custom-call | bytes 1500000 | tf_op jit(solution)/shard_map/pack_rows/pallas_call | solution.py:365
  40.0 3.5 %collective-permute-start.6 = (f32[32,32,256]{2,1,0:T(8,128)}, f32[32,32,256]{2,1,0:T(8,128)}, u32[]{:S(2)}, u32[]{:S(2)}) collective-permute-start(f32[32,32,256]{2,1,0:T(8,128)} %get-tuple-element.51), channel_id=1, source_target_pairs={{0,2},{2,0},{4,6},{6,4},{1,3},{3,1},{5,7},{7,5},{8,10},{10,8},{12,... | collective-permute-start | bytes 3145736 | tf_op jit(solution)/shard_map/ppermute | solution.py:392
  43.5 9.4 %collective-permute-start.7 = (f32[32,32,256]{2,1,0:T(8,128)}, f32[32,32,256]{2,1,0:T(8,128)}, u32[]{:S(2)}, u32[]{:S(2)}) collective-permute-start(f32[32,32,256]{2,1,0:T(8,128)} %get-tuple-element.52), channel_id=1, source_target_pairs={{0,0},{2,4},{4,2},{6,6},{1,1},{3,5},{5,3},{7,7},{8,8},{10,12},{12,... | collective-permute-start | bytes 3145736 | tf_op jit(solution)/shard_map/ppermute | solution.py:392
  52.9 1.4 collective-permute-start.9
  54.9 21.6 %moments.1 = f32[1,128]{1,0:T(1,128)} custom-call(f32[7]{0:T(128)} %stack.55.refs_0_.flags, f32[1,32,32,256]{3,2,1,0:T(8,128)} %bitcast.20, f32[1,32,32,256]{3,2,1,0:T(8,128)} %bitcast.32, f32[32,32,128]{2,1,0:T(8,128)} %broadcast_select_fusion.1.refs_3_.refs_4_.refs_5_, f32[5,32,256]{2,1,0:T(8,128)} %copy-done, f32[5,32,256]{2,1,0:T(8,128)} %copy-done.1, ...), custom_call_target="tpu_custom_call" | custom-call | bytes 3000000 | tf_op jit(solution)/shard_map/moments/pallas_call | solution.py:1105
  76.6 1.7 %collective-permute-done.8.refs_0_.refs_1_.refs_8_ = f32[15,32,256]{2,1,0:T(8,128)S(1)} collective-permute-done((f32[15,32,256]{2,1,0:T(8,128)}, f32[15,32,256]{2,1,0:T(8,128)S(1)}, u32[]{:S(2)}, u32[]{:S(2)}) %collective-permute-start.8) | collective-permute-done | bytes 491552 | tf_op jit(solution)/shard_map/ppermute | solution.py:380
  78.4 1.3 collective-permute-done.10
  80.4 2.0 %collective-permute-start.14 = (f32[12,32,256]{2,1,0:T(8,128)}, f32[12,32,256]{2,1,0:T(8,128)S(1)}, u32[]{:S(2)}, u32[]{:S(2)}) collective-permute-start(f32[12,32,256]{2,1,0:T(8,128)} %get-tuple-element.57), channel_id=1, source_target_pairs={{0,24},{8,0},{16,8},{24,16},{1,25},{9,1},{17,9},{25,17},{2,26},{10... | collective-permute-start | bytes 1179656 | tf_op jit(solution)/shard_map/ppermute | solution.py:380
  82.4 1.6 collective-permute-done.11
  84.2 1.0 collective-permute-start.13
  85.2 3.4 %collective-permute-done.12 = f32[4,128]{1,0:T(4,128)S(1)} collective-permute-done((f32[4,128]{1,0:T(4,128)S(1)}, f32[4,128]{1,0:T(4,128)S(1)}, u32[]{:S(2)}, u32[]{:S(2)}) %collective-permute-start.12) | collective-permute-done | bytes 2080 | tf_op jit(solution)/shard_map/ppermute | solution.py:1049
  88.6 9.4 %collective-permute-done.13.refs_2_.refs_3_.refs_9_ = f32[8,32,256]{2,1,0:T(8,128)S(1)} collective-permute-done((f32[8,32,256]{2,1,0:T(8,128)S(1)}, f32[8,32,256]{2,1,0:T(8,128)S(1)}, u32[]{:S(2)}, u32[]{:S(2)}) %collective-permute-start.13) | collective-permute-done | bytes 262176 | tf_op jit(solution)/shard_map/ppermute | solution.py:380
  98.0 1.5 collective-permute-start.15
  99.6 2.4 %pack_rows.5 = (f32[10,40,256]{2,1,0:T(8,128)}, f32[10,40,256]{2,1,0:T(8,128)}) custom-call(f32[7]{0:T(128)} %stack.55.refs_0_.flags, f32[15,32,256]{2,1,0:T(8,128)} %copy-done.3, f32[15,32,256]{2,1,0:T(8,128)} %copy-done.3, f32[8,32,256]{2,1,0:T(8,128)} %copy-done.5, f32[8,32,256]{2,1,0:T(8,128)} %copy-done.5, f32[18,32,256]{2,1,0:T(8,128)} %copy-done.2, ...), custom_call_target="tpu_custom_call" | custom-call | bytes 1500000 | tf_op jit(solution)/shard_map/pack_rows/pallas_call | solution.py:365
  101.9 1.7 collective-permute-start.17
  103.6 1.6 collective-permute-start.18
  105.9 3.1 %collective-permute-done.16 = f32[16,128]{1,0:T(8,128)S(1)} collective-permute-done((f32[16,128]{1,0:T(8,128)S(1)}, f32[16,128]{1,0:T(8,128)S(1)}, u32[]{:S(2)}, u32[]{:S(2)}) %collective-permute-start.16) | collective-permute-done | bytes 8224 | tf_op jit(solution)/shard_map/ppermute | solution.py:1049
  109.6 3.0 %collective-permute-done.17.refs_14_ = f32[10,40,256]{2,1,0:T(8,128)S(1)} collective-permute-done((f32[10,40,256]{2,1,0:T(8,128)}, f32[10,40,256]{2,1,0:T(8,128)S(1)}, u32[]{:S(2)}, u32[]{:S(2)}) %collective-permute-start.17) | collective-permute-done | bytes 409632 | tf_op jit(solution)/shard_map/ppermute | solution.py:392
  114.1 56.5 %step.1 = (f32[3,32,32,256]{3,2,1,0:T(8,128)}, f32[3,32,32,256]{3,2,1,0:T(8,128)}, f32[3,32,32,256]{3,2,1,0:T(8,128)}, f32[32,32,256]{2,1,0:T(8,128)}, f32[32,32,256]{2,1,0:T(8,128)}) custom-call(f32[7]{0:T(128)} %stack.55.refs_0_.flags, f32[32,128]{1,0:T(8,128)} %pad_maximum_fusion.refs_1_, f32[1,32,32,256]{3,2,1,0:T(8,128)} %bitcast.21, ...), custom_call_target="tpu_custom_call" | custom-call | bytes 3000000 | tf_op jit(solution)/shard_map/step/pallas_call | solution.py:1132
  (52 shorter events, 6.2 us)
Async XLA Ops:
  6.2 2.2 %collective-permute-start = (f32[32,32,128]{2,1,0:T(8,128)}, f32[32,32,128]{2,1,0:T(8,128)S(1)}, u32[]{:S(2)}, u32[]{:S(2)}) collective-permute-start(f32[32,32,128]{2,1,0:T(8,128)} %pack_lanes.2), channel_id=1, source_target_pairs={{0,1},{1,0},{2,3},{3,2},{4,5},{5,4},{6,7},{7,6},{8,9},{9,8},{10,11... | collective-permute-start | bytes 1572872 | tf_op jit(solution)/shard_map/ppermute | solution.py:168
  11.7 11.4 %collective-permute-start.1 = (f32[5,32,256]{2,1,0:T(8,128)}, f32[5,32,256]{2,1,0:T(8,128)S(1)}, u32[]{:S(2)}, u32[]{:S(2)}) collective-permute-start(f32[5,32,256]{2,1,0:T(8,128)} %get-tuple-element.36), channel_id=1, source_target_pairs={{0,8},{8,16},{16,24},{24,0},{1,9},{9,17},{17,25},{25,1},{2,10},{10... | collective-permute-start | bytes 491528 | tf_op jit(solution)/shard_map/ppermute | solution.py:380
  14.6 9.4 %collective-permute-start.2 = (f32[5,32,256]{2,1,0:T(8,128)}, f32[5,32,256]{2,1,0:T(8,128)S(1)}, u32[]{:S(2)}, u32[]{:S(2)}) collective-permute-start(f32[5,32,256]{2,1,0:T(8,128)} %get-tuple-element.37), channel_id=1, source_target_pairs={{0,24},{8,0},{16,8},{24,16},{1,25},{9,1},{17,9},{25,17},{2,26},{10... | collective-permute-start | bytes 491528 | tf_op jit(solution)/shard_map/ppermute | solution.py:380
  23.1 1.0 copy-start
  24.1 0.7 copy-start.1
  24.1 6.3 %collective-permute-start.5 = (f32[32,32,128]{2,1,0:T(8,128)}, f32[32,32,128]{2,1,0:T(8,128)S(1)}, u32[]{:S(2)}, u32[]{:S(2)}) collective-permute-start(f32[32,32,128]{2,1,0:T(8,128)} %pack_lanes.3), channel_id=1, source_target_pairs={{0,1},{1,0},{2,3},{3,2},{4,5},{5,4},{6,7},{7,6},{8,9},{9,8},{10,11... | collective-permute-start | bytes 1572872 | tf_op jit(solution)/shard_map/ppermute | solution.py:168
  27.2 12.7 %collective-permute-start.3 = (f32[36,8,256]{2,1,0:T(8,128)}, f32[36,8,256]{2,1,0:T(8,128)S(1)}, u32[]{:S(2)}, u32[]{:S(2)}) collective-permute-start(f32[36,8,256]{2,1,0:T(8,128)} %get-tuple-element.40), channel_id=1, source_target_pairs={{0,2},{2,0},{4,6},{6,4},{1,3},{3,1},{5,7},{7,5},{8,10},{10,8},{12,... | collective-permute-start | bytes 884744 | tf_op jit(solution)/shard_map/ppermute | solution.py:392
  28.8 11.2 %collective-permute-start.4 = (f32[36,8,256]{2,1,0:T(8,128)}, f32[36,8,256]{2,1,0:T(8,128)S(1)}, u32[]{:S(2)}, u32[]{:S(2)}) collective-permute-start(f32[36,8,256]{2,1,0:T(8,128)} %get-tuple-element.41), channel_id=1, source_target_pairs={{0,0},{2,4},{4,2},{6,6},{1,1},{3,5},{5,3},{7,7},{8,8},{10,12},{12,... | collective-permute-start | bytes 884744 | tf_op jit(solution)/shard_map/ppermute | solution.py:392
  40.0 44.2 %copy-start.10 = (f32[8,32,256]{2,1,0:T(8,128)S(1)}, f32[8,32,256]{2,1,0:T(8,128)}, u32[]{:S(2)}) copy-start(f32[8,32,256]{2,1,0:T(8,128)} %get-tuple-element.56) | copy-start | bytes 786436
  40.0 15.0 %copy-start.6 = (f32[36,8,256]{2,1,0:T(8,128)}, f32[36,8,256]{2,1,0:T(8,128)S(1)}, u32[]{:S(2)}) copy-start(f32[36,8,256]{2,1,0:T(8,128)S(1)} %collective-permute-done.3.refs_6_.refs_18_) | copy-start | bytes 884740
  40.0 14.9 %copy-start.7 = (f32[36,8,256]{2,1,0:T(8,128)}, f32[36,8,256]{2,1,0:T(8,128)S(1)}, u32[]{:S(2)}) copy-start(f32[36,8,256]{2,1,0:T(8,128)S(1)} %collective-permute-done.4.refs_7_.refs_19_) | copy-start | bytes 884740
  40.0 38.3 %collective-permute-start.6 = (f32[32,32,256]{2,1,0:T(8,128)}, f32[32,32,256]{2,1,0:T(8,128)}, u32[]{:S(2)}, u32[]{:S(2)}) collective-permute-start(f32[32,32,256]{2,1,0:T(8,128)} %get-tuple-element.51), channel_id=1, source_target_pairs={{0,2},{2,0},{4,6},{6,4},{1,3},{3,1},{5,7},{7,5},{8,10},{10,8},{12,... | collective-permute-start | bytes 3145736 | tf_op jit(solution)/shard_map/ppermute | solution.py:392
  43.5 34.9 %collective-permute-start.7 = (f32[32,32,256]{2,1,0:T(8,128)}, f32[32,32,256]{2,1,0:T(8,128)}, u32[]{:S(2)}, u32[]{:S(2)}) collective-permute-start(f32[32,32,256]{2,1,0:T(8,128)} %get-tuple-element.52), channel_id=1, source_target_pairs={{0,0},{2,4},{4,2},{6,6},{1,1},{3,5},{5,3},{7,7},{8,8},{10,12},{12,... | collective-permute-start | bytes 3145736 | tf_op jit(solution)/shard_map/ppermute | solution.py:392
  52.9 25.4 %collective-permute-start.9 = (f32[18,32,256]{2,1,0:T(8,128)}, f32[18,32,256]{2,1,0:T(8,128)S(1)}, u32[]{:S(2)}, u32[]{:S(2)}) collective-permute-start(f32[18,32,256]{2,1,0:T(8,128)} %get-tuple-element.54), channel_id=1, source_target_pairs={{0,24},{8,0},{16,8},{24,16},{1,25},{9,1},{17,9},{25,17},{2,26},{10... | collective-permute-start | bytes 1769480 | tf_op jit(solution)/shard_map/ppermute | solution.py:380
  54.3 24.0 %collective-permute-start.8 = (f32[15,32,256]{2,1,0:T(8,128)}, f32[15,32,256]{2,1,0:T(8,128)S(1)}, u32[]{:S(2)}, u32[]{:S(2)}) collective-permute-start(f32[15,32,256]{2,1,0:T(8,128)} %get-tuple-element.53), channel_id=1, source_target_pairs={{0,8},{8,16},{16,24},{24,0},{1,9},{9,17},{17,25},{25,1},{2,10},{10... | collective-permute-start | bytes 1474568 | tf_op jit(solution)/shard_map/ppermute | solution.py:380
  78.3 21.2 %copy-start.3 = (f32[15,32,256]{2,1,0:T(8,128)}, f32[15,32,256]{2,1,0:T(8,128)S(1)}, u32[]{:S(2)}) copy-start(f32[15,32,256]{2,1,0:T(8,128)S(1)} %collective-permute-done.8.refs_0_.refs_1_.refs_8_) | copy-start | bytes 1474564
  78.3 21.2 %copy-start.2 = (f32[18,32,256]{2,1,0:T(8,128)}, f32[18,32,256]{2,1,0:T(8,128)S(1)}, u32[]{:S(2)}) copy-start(f32[18,32,256]{2,1,0:T(8,128)S(1)} %collective-permute-done.9.refs_4_.refs_5_.refs_10_) | copy-start | bytes 1769476
  78.3 1.4 collective-permute-start.10
  80.4 3.6 %collective-permute-start.11 = (f32[2,128]{1,0:T(2,128)S(1)}, f32[2,128]{1,0:T(2,128)S(1)}, u32[]{:S(2)}, u32[]{:S(2)}) collective-permute-start(f32[2,128]{1,0:T(2,128)S(1)} %pad_maximum_fusion.4), channel_id=1, source_target_pairs={{0,2},{2,0},{4,6},{6,4},{1,3},{3,1},{5,7},{7,5},{8,10},{10,8},{12,... | collective-permute-start | bytes 3080 | tf_op jit(solution)/shard_map/ppermute | solution.py:1049
  80.4 17.6 %collective-permute-start.14 = (f32[12,32,256]{2,1,0:T(8,128)}, f32[12,32,256]{2,1,0:T(8,128)S(1)}, u32[]{:S(2)}, u32[]{:S(2)}) collective-permute-start(f32[12,32,256]{2,1,0:T(8,128)} %get-tuple-element.57), channel_id=1, source_target_pairs={{0,24},{8,0},{16,8},{24,16},{1,25},{9,1},{17,9},{25,17},{2,26},{10... | collective-permute-start | bytes 1179656 | tf_op jit(solution)/shard_map/ppermute | solution.py:380
  84.0 4.5 %collective-permute-start.12 = (f32[4,128]{1,0:T(4,128)S(1)}, f32[4,128]{1,0:T(4,128)S(1)}, u32[]{:S(2)}, u32[]{:S(2)}) collective-permute-start(f32[4,128]{1,0:T(4,128)S(1)} %pad_maximum_fusion.3), channel_id=1, source_target_pairs={{0,4},{2,6},{4,0},{6,2},{1,5},{3,7},{5,1},{7,3},{8,12},{10,14},{12... | collective-permute-start | bytes 6152 | tf_op jit(solution)/shard_map/ppermute | solution.py:1049
  84.2 13.8 %collective-permute-start.13 = (f32[8,32,256]{2,1,0:T(8,128)S(1)}, f32[8,32,256]{2,1,0:T(8,128)S(1)}, u32[]{:S(2)}, u32[]{:S(2)}) collective-permute-start(f32[8,32,256]{2,1,0:T(8,128)S(1)} %copy-done.10), channel_id=1, source_target_pairs={{0,8},{8,16},{16,24},{24,0},{1,9},{9,17},{17,25},{25,1},{2,10},{10... | collective-permute-start | bytes 786440 | tf_op jit(solution)/shard_map/ppermute | solution.py:380
  98.0 1.5 copy-start.5
  98.0 1.5 copy-start.4
  98.0 7.2 %collective-permute-start.15 = (f32[8,128]{1,0:T(8,128)S(1)}, f32[8,128]{1,0:T(8,128)S(1)}, u32[]{:S(2)}, u32[]{:S(2)}) collective-permute-start(f32[8,128]{1,0:T(8,128)S(1)} %pad_maximum_fusion.2), channel_id=1, source_target_pairs={{0,8},{8,0},{16,24},{24,16},{1,9},{9,1},{17,25},{25,17},{2,10},{10... | collective-permute-start | bytes 12296 | tf_op jit(solution)/shard_map/ppermute | solution.py:1049
  101.9 10.7 %collective-permute-start.17 = (f32[10,40,256]{2,1,0:T(8,128)}, f32[10,40,256]{2,1,0:T(8,128)S(1)}, u32[]{:S(2)}, u32[]{:S(2)}) collective-permute-start(f32[10,40,256]{2,1,0:T(8,128)} %get-tuple-element.65), channel_id=1, source_target_pairs={{0,2},{2,0},{4,6},{6,4},{1,3},{3,1},{5,7},{7,5},{8,10},{10,8},{12,... | collective-permute-start | bytes 1228808 | tf_op jit(solution)/shard_map/ppermute | solution.py:392
  103.6 9.0 %collective-permute-start.18 = (f32[10,40,256]{2,1,0:T(8,128)}, f32[10,40,256]{2,1,0:T(8,128)S(1)}, u32[]{:S(2)}, u32[]{:S(2)}) collective-permute-start(f32[10,40,256]{2,1,0:T(8,128)} %get-tuple-element.66), channel_id=1, source_target_pairs={{0,0},{2,4},{4,2},{6,6},{1,1},{3,5},{5,3},{7,7},{8,8},{10,12},{12,... | collective-permute-start | bytes 1228808 | tf_op jit(solution)/shard_map/ppermute | solution.py:392
  105.3 3.7 %collective-permute-start.16 = (f32[16,128]{1,0:T(8,128)S(1)}, f32[16,128]{1,0:T(8,128)S(1)}, u32[]{:S(2)}, u32[]{:S(2)}) collective-permute-start(f32[16,128]{1,0:T(8,128)S(1)} %pad_maximum_fusion.1), channel_id=1, source_target_pairs={{0,16},{8,24},{16,0},{24,8},{1,17},{9,25},{17,1},{25,9},{2,18},{10... | collective-permute-start | bytes 24584 | tf_op jit(solution)/shard_map/ppermute | solution.py:1049
  112.6 0.8 copy-start.8
  113.4 0.8 copy-start.9

commit v6 on v5

--- a/solution.py
+++ b/solution.py
@@ -1,4 +1,5 @@
 import functools
+import math
 from typing import NamedTuple
 
 import jax
@@ -138,7 +139,7 @@
         for x in range(planes):
             plane(x, 0)
 
-    planes = 4 if plan.x % 4 == 0 else 1
+    planes = next(n for n in (16 if len(arrays) == 2 else 8, 4, 1) if plan.x % n == 0)
     specs, operands = [], []
     for (count, _, _), array in zip(plan.groups, arrays):
         block = (count, planes, plan.y, LANES)
@@ -535,11 +536,12 @@
     return (3 * len(plan.fields) + 2 * skipping) * plan.tiles + 1 + plan.low + plan.high
 
 
-def plane_loop(first, last, body, carried):
-    def turn(i, carried, count):
+def plane_loop(ref, first, last, row, body, carried):
+    def turn(plane, carried, count):
+        here = spot(ref, plane, row)
         pending = []
         for k in range(count):
-            carried, stores = body(i + k, carried)
+            carried, stores = body(here.at_plane(k), carried)
             pending += stores
         for one in pending:
             store(*one)
@@ -553,13 +555,39 @@
     return turn(last + 1 - rest, carried, rest) if rest else carried
 
 
-def load(ref, index, row):
-    return [ref[(*index, t, pl.ds(row, ROWS), slice(None))] for t in range(ref.shape[-3])]
-
-
-def store(ref, index, row, tiles):
-    for t, tile in enumerate(tiles):
-        ref[(*index, t, pl.ds(row, ROWS), slice(None))] = tile
+class Spot(NamedTuple):
+    base: jax.Array
+    plane: jax.Array
+    planes: int = 0
+    rows: int = 0
+
+    def at_plane(self, step):
+        return self._replace(planes=self.planes + step)
+
+    def at_row(self, step):
+        return self._replace(rows=self.rows + step)
+
+
+def spot(ref, plane, row):
+    return Spot(plane * (ref.shape[-3] * ref.shape[-2]) + row, plane)
+
+
+def tile_rows(ref, component, at):
+    planes, tiles, rows, lanes = ref.shape[-4:]
+    first = (component * planes + at.planes) * tiles * rows + at.rows
+    flat = ref.reshape(math.prod(ref.shape[:-1]), lanes)
+    return flat, [at.base + (first + t * rows) for t in range(tiles)]
+
+
+def load(ref, component, at):
+    flat, starts = tile_rows(ref, component, at)
+    return [flat[pl.ds(start, ROWS), :] for start in starts]
+
+
+def store(ref, component, at, tiles):
+    flat, starts = tile_rows(ref, component, at)
+    for start, tile in zip(starts, tiles):
+        flat[pl.ds(start, ROWS), :] = tile
 
 
 def each(function, *tiles):
@@ -613,8 +641,9 @@
         keep = scale * keep
         return [keep] * plan.tiles + [keep * edge]
 
-    def plane(self, i):
+    def plane(self, at):
         plan, flags = self.plan, self.flags
+        i = at.plane + at.planes
         return jnp.where(
             i < plan.low, flags[0], jnp.where(i >= plan.low + plan.x, flags[1], 1.0)
         )
@@ -624,10 +653,10 @@
     def chunk(row):
         keep = inside.tiles(row, 0.4 * 0.25)
 
-        def slab(i):
-            here, under = load(density, (0, i), row), load(density, (0, i), row - 1)
-            p = each(lambda a, b: a * b, here, load(energy, (0, i), row))
-            p_under = each(lambda a, b: a * b, under, load(energy, (0, i), row - 1))
+        def slab(at):
+            here, under = load(density, 0, at), load(density, 0, at.at_row(-1))
+            p = each(lambda a, b: a * b, here, load(energy, 0, at))
+            p_under = each(lambda a, b: a * b, under, load(energy, 0, at.at_row(-1)))
             summed, stepped = add(p, p_under), subtract(p_under, p)
             weight = add(here, under)
             summed_z, stepped_z = lane_below(summed), lane_below(stepped)
@@ -638,45 +667,47 @@
                 add(weight, lane_below(weight)),
             )
 
-        def plane(i, before):
-            now = slab(i)
-            here = inside.plane(i)
+        def plane(at, before):
+            now = slab(at)
+            here = inside.plane(at)
             scale = [tile * here for tile in keep]
             stores = []
             for component in range(3):
                 across = (subtract if component == 0 else add)(before[component], now[component])
                 result = each(lambda a, b: a * b, scale, across)
-                stores.append((force, (component, i), row, result))
+                stores.append((force, component, at, result))
             result = each(lambda a, b: 0.125 * (a + b) + 6.0 * CONSISTENT, before[3], now[3])
-            stores.append((mass, (0, i), row, result))
+            stores.append((mass, 0, at, result))
             return now, stores
 
-        plane_loop(*planes, plane, slab(planes[0] - 1))
+        plane_loop(density, *planes, row, plane, slab(spot(density, planes[0] - 1, row)))
 
     chunks(*rows, chunk)
 
 
-def face_sum(ref, component, i, row, before, here, after):
+def face_sum(ref, component, at, before, here, after):
     total = add(add(before, after), add(lane_below(here), lane_above(here)))
-    return add(total, add(load(ref, (component, i), row - 1), load(ref, (component, i), row + 1)))
+    sides = add(load(ref, component, at.at_row(-1)), load(ref, component, at.at_row(1)))
+    return add(total, sides)
 
 
 def stencil_pass(ref, planes, rows, setup, use):
     def chunk(row):
         given = setup(row)
 
-        def plane(i, carried):
+        def plane(at, carried):
             before, here = carried
-            after = [load(ref, (component, i + 1), row) for component in range(3)]
+            after = [load(ref, component, at.at_plane(1)) for component in range(3)]
             sums = [
-                face_sum(ref, component, i, row, before[component], here[component], after[component])
+                face_sum(ref, component, at, before[component], here[component], after[component])
                 for component in range(3)
             ]
-            return (here, after), use(i, row, here, sums, given)
-
-        first = [load(ref, (component, planes[0] - 1), row) for component in range(3)]
-        second = [load(ref, (component, planes[0]), row) for component in range(3)]
-        plane_loop(*planes, plane, (first, second))
+            return (here, after), use(at, here, sums, given)
+
+        start = spot(ref, planes[0], row)
+        first = [load(ref, component, start.at_plane(-1)) for component in range(3)]
+        second = [load(ref, component, start) for component in range(3)]
+        plane_loop(ref, *planes, row, plane, (first, second))
 
     chunks(*rows, chunk)
 
@@ -712,15 +743,15 @@
         (ROWS - 1, ROWS + y + 1),
     )
 
-    def multiply(i, row, here, sums, keep):
-        weight = load(mass, (0, i), row)
-        scale = [tile * inside.plane(i) for tile in keep]
+    def multiply(at, here, sums, keep):
+        weight = load(mass, 0, at)
+        scale = [tile * inside.plane(at) for tile in keep]
         stores = []
         for component in range(3):
             result = each(
                 lambda m, a, k, s: m * a + k * s, weight, here[component], scale, sums[component]
             )
-            stores.append((image, (component, i), row, result))
+            stores.append((image, component, at, result))
         return stores
 
     stencil_pass(
@@ -737,17 +768,17 @@
     def first_chunk(j, sums):
         row = ROWS + j * ROWS
 
-        def plane(i, sums):
+        def plane(at, sums):
             sums = list(sums)
             for component in range(3):
-                f = load(force, (component, i), row)
-                v = load(image, (component, i), row)
+                f = load(force, component, at)
+                v = load(image, component, at)
                 for t in own:
                     sums[component] = sums[component] + f[t] * f[t]
                     sums[3 + component] = sums[3 + component] + f[t] * v[t]
             return tuple(sums), []
 
-        return plane_loop(low, low + x - 1, plane, sums)
+        return plane_loop(force, low, low + x - 1, row, plane, sums)
 
     sums = lax.fori_loop(0, y // ROWS, first_chunk, (nothing,) * 6)
     sums = [whole_sum(one) for one in sums]
@@ -757,43 +788,43 @@
         for c in range(3)
     ]
 
-    def pair(component, i, row):
-        f = load(force, (component, i), row)
-        v = load(image, (component, i), row)
+    def pair(component, at):
+        f = load(force, component, at)
+        v = load(image, component, at)
         return f, each(lambda a, b: a - shift[component] * b, v, f)
 
     def second_chunk(j, sums):
         row = ROWS + j * ROWS
 
-        def plane(i, carried):
+        def plane(at, carried):
             here, sums = carried
             sums = list(sums)
-            ahead = [pair(component, i + 1, row) for component in range(3)]
-            weight = load(mass, (0, i), row)
+            ahead = [pair(component, at.at_plane(1)) for component in range(3)]
+            weight = load(mass, 0, at)
             for component in range(3):
                 f, w = here[component]
                 f_next, w_next = ahead[component]
-                f_up, w_up = pair(component, i, row + 1)
+                f_up, w_up = pair(component, at.at_row(1))
                 f_high = add(add(f_next, f_up), lane_above(f))
                 w_high = add(add(w_next, w_up), lane_above(w))
                 for t in own:
-                    at = 5 * component
+                    k = 5 * component
                     heavy = weight[t] * w[t]
-                    sums[at] = sums[at] + f[t] * w[t]
-                    sums[at + 1] = sums[at + 1] + w[t] * w[t]
-                    sums[at + 2] = sums[at + 2] + (
+                    sums[k] = sums[k] + f[t] * w[t]
+                    sums[k + 1] = sums[k + 1] + w[t] * w[t]
+                    sums[k + 2] = sums[k + 2] + (
                         f[t] * heavy + CONSISTENT * (f[t] * w_high[t] + w[t] * f_high[t])
                     )
-                    sums[at + 3] = sums[at + 3] + w[t] * (
+                    sums[k + 3] = sums[k + 3] + w[t] * (
                         heavy + (2.0 * CONSISTENT) * w_high[t]
                     )
-                    sums[at + 4] = sums[at + 4] + f[t] * (
+                    sums[k + 4] = sums[k + 4] + f[t] * (
                         weight[t] * f[t] + (2.0 * CONSISTENT) * f_high[t]
                     )
             return (ahead, tuple(sums)), []
 
-        start = [pair(component, low, row) for component in range(3)]
-        return plane_loop(low, low + x - 1, plane, (start, sums))[1]
+        start = [pair(component, spot(force, low, row)) for component in range(3)]
+        return plane_loop(force, low, low + x - 1, row, plane, (start, sums))[1]
 
     rest = lax.fori_loop(0, y // ROWS, second_chunk, (nothing,) * 15)
     lane = lane_index((1, LANES))
@@ -871,9 +902,9 @@
         (ROWS - reach, ROWS + y + reach),
     )
 
-    def advance(i, row, here, sums, keep):
-        weight = load(mass, (0, i), row)
-        scale = [tile * inside.plane(i) for tile in keep]
+    def advance(at, here, sums, keep):
+        weight = load(mass, 0, at)
+        scale = [tile * inside.plane(at) for tile in keep]
         stores = []
         for component in range(3):
             on_force, on_image = weights[component]
@@ -884,15 +915,14 @@
                 scale,
                 sums[component],
             )
-            at = (component, i)
-            faster = each(lambda v, a: v + TIME_STEP * a, load(speed, at, row), result)
+            faster = each(lambda v, a: v + TIME_STEP * a, load(speed, component, at), result)
             further = each(
-                lambda b, a: b + (TIME_STEP * TIME_STEP) * a, load(moved, at, row), result
+                lambda b, a: b + (TIME_STEP * TIME_STEP) * a, load(moved, component, at), result
             )
             stores += [
-                (other, at, row, result),
-                (speed, at, row, faster),
-                (moved, at, row, further),
+                (other, component, at, result),
+                (speed, component, at, faster),
+                (moved, component, at, further),
             ]
         return stores
 
@@ -929,9 +959,9 @@
     content = mass
 
     def content_chunk(row):
-        def slab(i):
-            under = [load(speed, (component, i), row) for component in range(3)]
-            over = [load(speed, (component, i), row + 1) for component in range(3)]
+        def slab(at):
+            under = [load(speed, component, at) for component in range(3)]
+            over = [load(speed, component, at.at_row(1)) for component in range(3)]
             along_x = add(under[0], over[0])
             along_y = subtract(over[1], under[1])
             along_z = add(under[2], over[2])
@@ -940,15 +970,15 @@
             along_z = subtract(lane_above(along_z), along_z)
             return along_x, add(along_y, along_z)
 
-        def plane(i, before):
-            now = slab(i + 1)
+        def plane(at, before):
+            now = slab(at.at_plane(1))
             spread = add(subtract(now[0], before[0]), add(now[1], before[1]))
-            held = load(energy_ext, (0, i), row)
+            held = load(energy_ext, 0, at)
             lagged = each(lambda e, s: e - (0.25 * 0.4 * TIME_STEP) * (e * s), held, spread)
-            result = each(lambda d, e: d * e, load(density_ext, (0, i), row), lagged)
-            return now, [(content, (0, i), row, result)]
-
-        plane_loop(low - 1, low + x, plane, slab(low - 1))
+            result = each(lambda d, e: d * e, load(density_ext, 0, at), lagged)
+            return now, [(content, 0, at, result)]
+
+        plane_loop(speed, low - 1, low + x, row, plane, slab(spot(speed, low - 1, row)))
 
     chunks(ROWS - 1, ROWS + y, content_chunk)
 
@@ -958,8 +988,8 @@
     for _ in range(SWEEPS):
         reach -= 1
 
-        def relax(i, row, here, sums, given, target=target):
-            rate = load(free_ext, (0, i), row)
+        def relax(at, here, sums, given, target=target):
+            rate = load(free_ext, 0, at)
             stores = []
             for component in range(3):
                 result = each(
@@ -968,7 +998,7 @@
                     sums[component],
                     rate,
                 )
-                stores.append((target, (component, i), row, result))
+                stores.append((target, component, at, result))
             return stores
 
         stencil_pass(
@@ -986,21 +1016,20 @@
     quantities = (density_ext, content)
 
     def remap_chunk(row):
-        def shift(component, i, at):
-            return subtract(
-                load(settled, (component, i), at), load(moved, (component, i), at)
-            )
-
-        def slab(i):
-            x_here = add(shift(0, i, row), shift(0, i, row + 1))
-            y_here, y_over = shift(1, i, row), shift(1, i, row + 1)
-            z_here = add(shift(2, i, row), shift(2, i, row + 1))
+        def shift(component, at):
+            return subtract(load(settled, component, at), load(moved, component, at))
+
+        def slab(at):
+            over = at.at_row(1)
+            x_here = add(shift(0, at), shift(0, over))
+            y_here, y_over = shift(1, at), shift(1, over)
+            z_here = add(shift(2, at), shift(2, over))
             return (
                 add(x_here, lane_above(x_here)),
                 add(y_here, lane_above(y_here)),
                 add(y_over, lane_above(y_over)),
                 z_here,
-                [load(one, (0, i), row) for one in quantities],
+                [load(one, 0, at) for one in quantities],
             )
 
         def flux(speeds, upper, lower):
@@ -1009,27 +1038,28 @@
         def x_flux(speeds, upper, lower):
             return [flux(speeds, u, l) for u, l in zip(upper, lower)]
 
-        def plane(i, carried):
+        def plane(at, carried):
             now, entering = carried
-            ahead = slab(i + 1)
+            ahead = slab(at.at_plane(1))
             leaving = x_flux(ahead[0], ahead[4], now[4])
             y_here, y_over, z_here = [add(now[k], ahead[k]) for k in (1, 2, 3)]
             stores = []
             for k, one in enumerate(quantities):
                 held = now[4][k]
-                under, over = load(one, (0, i), row - 1), load(one, (0, i), row + 1)
+                under, over = [load(one, 0, at.at_row(step)) for step in (-1, 1)]
                 through_z = flux(z_here, held, lane_below(held))
                 change = subtract(leaving[k], entering[k])
                 change = add(change, flux(y_over, over, held))
                 change = subtract(change, flux(y_here, held, under))
                 change = add(change, subtract(lane_above(through_z), through_z))
                 result = each(lambda q, c: q + 0.25 * c, held, change)
-                stores.append((free_buffer, (k, i), row, result[: plan.tiles]))
+                stores.append((free_buffer, k, at, result[: plan.tiles]))
             return (ahead, leaving), stores
 
-        start = slab(low)
-        before = [load(one, (0, low - 1), row) for one in quantities]
-        plane_loop(low, low + x - 1, plane, (start, x_flux(start[0], start[4], before)))
+        first = spot(settled, low, row)
+        start = slab(first)
+        before = [load(one, 0, first.at_plane(-1)) for one in quantities]
+        plane_loop(settled, low, low + x - 1, row, plane, (start, x_flux(start[0], start[4], before)))
 
     chunks(ROWS, ROWS + y - 1, remap_chunk)
     write(free_buffer, density_new, 0)
@@ -1083,7 +1113,7 @@
         (1, SWEEPS - 1, SWEEPS),
     ]
     narrow = Plan([(1, NARROW, NARROW)] * 2, shape)
-    wide = Plan(groups, shape, narrow, cut=5)
+    wide = Plan(groups, shape, narrow, cut=8)
     cells = arrays[:2]
 
     packed = exchange_lanes(narrow, pack_lanes(narrow, cells))
@@ -1122,7 +1152,7 @@
     )(flags, *cells, packed, *planes, *rows)
 
     line, wide_rows, first_planes = lax.optimization_barrier((line, wide_rows, first_planes))
-    lines = gather_lines(line, ("bz", "by"))
+    lines = gather_lines(line, ("bz",))
     lines, last_planes = lax.optimization_barrier((lines, last_planes))
     wide_planes = [pair[side] for side in range(2) for pair in (first_planes, last_planes)]
     corners = exchange_rows(pack_rows(wide, flags, None, None, False, wide_planes, planes))
@@ -1151,7 +1181,7 @@
         compiler_params=pltpu.CompilerParams(vmem_limit_bytes=VMEM_BYTES),
         cost_estimate=cost(1),
         name="step",
-    )(flags, gather_lines(lines, ("bx",)), *arrays, *messages, *planes, *rows)
+    )(flags, gather_lines(lines, ("bx", "by")), *arrays, *messages, *planes, *rows)
 
 
 def solution(mesh):

time: 172 us -> 175 us (1.017)
  waiting for transfers between devices: 25.7 us -> 31.8 us
  Pallas kernels: 107 us -> 102 us
  starting transfers between devices: 31.2 us -> 33.1 us
    ppermute x6, waiting for transfers between devices: 12.1 us -> 18.5 us  [exchange_planes(): lax.ppermute(one, 'bx', [(i, (i + step) % count) for i in range(count)])]
    pallas_call x2, Pallas kernels: 13 us -> 8.14 us  [pack_lanes(): pl.pallas_call(kernel, grid=(plan.x // planes,), in_specs=specs, out_spec...]
    ppermute x6, waiting for transfers between devices: 3.05 us -> 0.02 us  [exchange_rows(): got.append(lax.ppermute(one, 'by', list(enumerate(partner))))]
    ppermute x5, waiting for transfers between devices: 9.37 us -> 12.1 us  [gather_lines(): got = lax.ppermute(line, axis, [(i, i ^ step) for i in range(count)])]
  transfers between devices with their start and end apart: 19 -> 19, of which waited for: 9 -> 8; matrix products, arithmetic and copies ran while one was open for 1% -> 2% of each run, Pallas kernels for 25% -> 24%
where the time goes in v6:
time: 175 us; the launch traced here: 174 us
  Pallas kernels  102 us (58%)
  starting transfers between devices  33.1 us (19%)
  waiting for transfers between devices  31.8 us (18%)
  other arithmetic  3.01 us (2%)
  local copies, waits for them, and re-layouts  2.8 us (2%)
    pallas_call x1, Pallas kernels, on_device(): pl.pallas_call(functools.partial(step_kernel, wide), in_specs=[in_smem(),...  56.5 us
    pallas_call x1, Pallas kernels, on_device(): pl.pallas_call(functools.partial(moments_kernel, narrow), in_specs=[in_sm...  21.7 us
    ppermute x6, starting transfers between devices, exchange_rows(): got.append(lax.ppermute(one, 'by', list(enumerate(partner))))  19.7 us
    ppermute x6, waiting for transfers between devices, exchange_planes(): lax.ppermute(one, 'bx', [(i, (i + step) % count) for i in range(count)])  18.5 us
    ppermute x5, waiting for transfers between devices, gather_lines(): got = lax.ppermute(line, axis, [(i, i ^ step) for i in range(count)])  12.1 us
    pallas_call x3, Pallas kernels, pack_rows(): pl.pallas_call(kernel, grid=(1,), in_specs=specs, out_specs=[pl.BlockSpec...  9.67 us
    ppermute x6, starting transfers between devices, exchange_planes(): lax.ppermute(one, 'bx', [(i, (i + step) % count) for i in range(count)])  8.94 us
    pallas_call x2, Pallas kernels, pack_lanes(): pl.pallas_call(kernel, grid=(plan.x // planes,), in_specs=specs, out_spec...  8.14 us
  transfers between devices with their start and end apart: 19, of which 8 were waited for; matrix products, arithmetic and copies ran while one was open for 2% of the time, Pallas kernels for 24%

profile of v6, /device:TPU:0, one launch (start us, length us, event | category | flops | bytes accessed | tf_op | source)
XLA Modules:
  0.0 173.8 jit_solution(15838248335744308542)
XLA Ops:
  0.6 2.4 %pack_lanes.2 = f32[32,32,128]{2,1,0:T(8,128)} custom-call(f32[1,32,32,256]{3,2,1,0:T(8,128)} %bitcast.10, f32[1,32,32,256]{3,2,1,0:T(8,128)} %bitcast.11, f32[1,32,32,256]{3,2,1,0:T(8,128)} %bitcast.22, f32[1,32,32,256]{3,2,1,0:T(8,128)} %bitcast.23), custom_call_target="tpu_custom_call" | custom-call | bytes 1500000 | tf_op jit(solution)/shard_map/pack_lanes/pallas_call | solution.py:149
  4.1 1.1 collective-permute-done
  5.3 0.8 broadcast_select_fusion.1.refs_3_.refs_4_.refs_5_
  6.1 2.5 %pack_planes.2 = (f32[5,32,256]{2,1,0:T(8,128)}, f32[5,32,256]{2,1,0:T(8,128)}) custom-call(f32[7]{0:T(128)} %stack.55.refs_0_.flags, f32[1,32,32,256]{3,2,1,0:T(8,128)} %bitcast.12, f32[1,32,32,256]{3,2,1,0:T(8,128)} %bitcast.24, f32[32,32,128]{2,1,0:T(8,128)} %broadcast_select_fusion.1.refs_3_.refs_4_.refs_5_), custom_call_target="tpu_custom_call" | custom-call | bytes 1500000 | tf_op jit(solution)/shard_map/pack_planes/pallas_call | solution.py:242
  8.6 2.9 %collective-permute-start.1 = (f32[5,32,256]{2,1,0:T(8,128)}, f32[5,32,256]{2,1,0:T(8,128)S(1)}, u32[]{:S(2)}, u32[]{:S(2)}) collective-permute-start(f32[5,32,256]{2,1,0:T(8,128)} %get-tuple-element.36), channel_id=1, source_target_pairs={{0,8},{8,16},{16,24},{24,0},{1,9},{9,17},{17,25},{25,1},{2,10},{10... | collective-permute-start | bytes 491528 | tf_op jit(solution)/shard_map/ppermute | solution.py:381
  11.5 1.0 collective-permute-start.2
  12.5 5.7 %pack_lanes.3 = f32[32,32,128]{2,1,0:T(8,128)} custom-call(f32[1,32,32,256]{3,2,1,0:T(8,128)} %bitcast.13, f32[1,32,32,256]{3,2,1,0:T(8,128)} %bitcast.14, f32[1,32,32,256]{3,2,1,0:T(8,128)} %bitcast.25, f32[1,32,32,256]{3,2,1,0:T(8,128)} %bitcast.26, f32[3,32,32,256]{3,2,1,0:T(8,128)} %refs_4_.7, f32[3,32,32,256]{3,2,1,0:T(8,128)} %refs_4_.7, ...), custom_call_target="tpu_custom_call" | custom-call | bytes 1500000 | tf_op jit(solution)/shard_map/pack_lanes/pallas_call | solution.py:149
  18.2 2.7 %collective-permute-done.2.refs_8_.refs_9_.refs_5_.refs_10_.refs_11_.refs_17_ = f32[5,32,256]{2,1,0:T(8,128)S(1)} collective-permute-done((f32[5,32,256]{2,1,0:T(8,128)}, f32[5,32,256]{2,1,0:T(8,128)S(1)}, u32[]{:S(2)}, u32[]{:S(2)}) %collective-permute-start.2) | collective-permute-done | bytes 163872 | tf_op jit(solution)/shard_map/ppermute | solution.py:381
  21.6 2.5 %pack_rows.3 = (f32[36,8,256]{2,1,0:T(8,128)}, f32[36,8,256]{2,1,0:T(8,128)}) custom-call(f32[7]{0:T(128)} %stack.55.refs_0_.flags, f32[1,32,32,256]{3,2,1,0:T(8,128)} %bitcast.15, f32[1,32,32,256]{3,2,1,0:T(8,128)} %bitcast.16, f32[1,32,32,256]{3,2,1,0:T(8,128)} %bitcast.27, f32[1,32,32,256]{3,2,1,0:T(8,128)} %bitcast.28, ...), custom_call_target="tpu_custom_call" | custom-call | bytes 1500000 | tf_op jit(solution)/shard_map/pack_rows/pallas_call | solution.py:366
  24.1 1.6 collective-permute-start.3
  25.6 1.6 collective-permute-start.4
  27.3 0.8 broadcast_select_fusion.refs_6_.refs_10_.refs_11_.refs_7_
  28.1 3.9 %pack_planes.3 = (f32[18,32,256]{2,1,0:T(8,128)}, f32[5,32,256]{2,1,0:T(8,128)}, f32[24,32,256]{2,1,0:T(8,128)}, f32[6,32,256]{2,1,0:T(8,128)}) custom-call(f32[7]{0:T(128)} %stack.55.refs_0_.flags, f32[1,32,32,256]{3,2,1,0:T(8,128)} %bitcast.17, f32[1,32,32,256]{3,2,1,0:T(8,128)} %bitcast.29, f32[3,32,32,256]{3,2,1,0:T(8,128)} %refs_4_.7, ...), custom_call_target="tpu_custom_call" | custom-call | bytes 1500000 | tf_op jit(solution)/shard_map/pack_planes/pallas_call | solution.py:242
  32.0 4.8 %pack_rows.4 = (f32[32,32,256]{2,1,0:T(8,128)}, f32[32,32,256]{2,1,0:T(8,128)}) custom-call(f32[7]{0:T(128)} %stack.55.refs_0_.flags, f32[1,32,32,256]{3,2,1,0:T(8,128)} %bitcast.18, f32[1,32,32,256]{3,2,1,0:T(8,128)} %bitcast.19, f32[1,32,32,256]{3,2,1,0:T(8,128)} %bitcast.30, f32[1,32,32,256]{3,2,1,0:T(8,128)} %bitcast.31, f32[3,32,32,256]{3,2,1,0:T(8,128)} %refs_4_.7, ...), custom_call_target="tpu_custom_call" | custom-call | bytes 1500000 | tf_op jit(solution)/shard_map/pack_rows/pallas_call | solution.py:366
  36.8 3.5 %collective-permute-start.6 = (f32[32,32,256]{2,1,0:T(8,128)}, f32[32,32,256]{2,1,0:T(8,128)}, u32[]{:S(2)}, u32[]{:S(2)}) collective-permute-start(f32[32,32,256]{2,1,0:T(8,128)} %get-tuple-element.51), channel_id=1, source_target_pairs={{0,2},{2,0},{4,6},{6,4},{1,3},{3,1},{5,7},{7,5},{8,10},{10,8},{12,... | collective-permute-start | bytes 3145736 | tf_op jit(solution)/shard_map/ppermute | solution.py:393
  40.3 9.5 %collective-permute-start.7 = (f32[32,32,256]{2,1,0:T(8,128)}, f32[32,32,256]{2,1,0:T(8,128)}, u32[]{:S(2)}, u32[]{:S(2)}) collective-permute-start(f32[32,32,256]{2,1,0:T(8,128)} %get-tuple-element.52), channel_id=1, source_target_pairs={{0,0},{2,4},{4,2},{6,6},{1,1},{3,5},{5,3},{7,7},{8,8},{10,12},{12,... | collective-permute-start | bytes 3145736 | tf_op jit(solution)/shard_map/ppermute | solution.py:393
  49.7 1.4 collective-permute-start.9
  51.8 21.7 %moments.1 = f32[1,128]{1,0:T(1,128)} custom-call(f32[7]{0:T(128)} %stack.55.refs_0_.flags, f32[1,32,32,256]{3,2,1,0:T(8,128)} %bitcast.20, f32[1,32,32,256]{3,2,1,0:T(8,128)} %bitcast.32, f32[32,32,128]{2,1,0:T(8,128)} %broadcast_select_fusion.1.refs_3_.refs_4_.refs_5_, f32[5,32,256]{2,1,0:T(8,128)} %copy-done.1, f32[5,32,256]{2,1,0:T(8,128)} %copy-done.2, ...), custom_call_target="tpu_custom_call" | custom-call | bytes 3000000 | tf_op jit(solution)/shard_map/moments/pallas_call | solution.py:1135
  73.4 7.5 %collective-permute-done.8.refs_0_.refs_1_.refs_8_ = f32[18,32,256]{2,1,0:T(8,128)S(1)} collective-permute-done((f32[18,32,256]{2,1,0:T(8,128)}, f32[18,32,256]{2,1,0:T(8,128)S(1)}, u32[]{:S(2)}, u32[]{:S(2)}) %collective-permute-start.8) | collective-permute-done | bytes 589856 | tf_op jit(solution)/shard_map/ppermute | solution.py:381
  81.0 1.6 collective-permute-start.11
  82.6 1.4 collective-permute-start.12
  84.7 4.5 %collective-permute-done.11.refs_2_.refs_3_.refs_9_ = f32[5,32,256]{2,1,0:T(8,128)S(1)} collective-permute-done((f32[5,32,256]{2,1,0:T(8,128)}, f32[5,32,256]{2,1,0:T(8,128)S(1)}, u32[]{:S(2)}, u32[]{:S(2)}) %collective-permute-start.11) | collective-permute-done | bytes 163872 | tf_op jit(solution)/shard_map/ppermute | solution.py:381
  89.2 3.9 %collective-permute-done.12.refs_6_.refs_7_.refs_11_ = f32[6,32,256]{2,1,0:T(8,128)S(1)} collective-permute-done((f32[6,32,256]{2,1,0:T(8,128)}, f32[6,32,256]{2,1,0:T(8,128)S(1)}, u32[]{:S(2)}, u32[]{:S(2)}) %collective-permute-start.12) | collective-permute-done | bytes 196640 | tf_op jit(solution)/shard_map/ppermute | solution.py:381
  93.1 1.4 collective-permute-start.13
  94.5 2.1 %collective-permute-done.13 = f32[2,128]{1,0:T(2,128)S(1)} collective-permute-done((f32[2,128]{1,0:T(2,128)S(1)}, f32[2,128]{1,0:T(2,128)S(1)}, u32[]{:S(2)}, u32[]{:S(2)}) %collective-permute-start.13) | collective-permute-done | bytes 1056 | tf_op jit(solution)/shard_map/ppermute | solution.py:1079
  97.2 3.1 %collective-permute-done.14 = f32[4,128]{1,0:T(4,128)S(1)} collective-permute-done((f32[4,128]{1,0:T(4,128)S(1)}, f32[4,128]{1,0:T(4,128)S(1)}, u32[]{:S(2)}, u32[]{:S(2)}) %collective-permute-start.14) | collective-permute-done | bytes 2080 | tf_op jit(solution)/shard_map/ppermute | solution.py:1079
  100.5 2.4 %pack_rows.5 = (f32[10,40,256]{2,1,0:T(8,128)}, f32[10,40,256]{2,1,0:T(8,128)}) custom-call(f32[7]{0:T(128)} %stack.55.refs_0_.flags, f32[18,32,256]{2,1,0:T(8,128)} %copy-done.3, f32[18,32,256]{2,1,0:T(8,128)} %copy-done.3, f32[5,32,256]{2,1,0:T(8,128)} %copy-done.5, f32[5,32,256]{2,1,0:T(8,128)} %copy-done.5, f32[24,32,256]{2,1,0:T(8,128)} %copy-done, ...), custom_call_target="tpu_custom_call" | custom-call | bytes 1500000 | tf_op jit(solution)/shard_map/pack_rows/pallas_call | solution.py:366
  102.9 2.0 %collective-permute-start.17 = (f32[10,40,256]{2,1,0:T(8,128)}, f32[10,40,256]{2,1,0:T(8,128)S(1)}, u32[]{:S(2)}, u32[]{:S(2)}) collective-permute-start(f32[10,40,256]{2,1,0:T(8,128)} %get-tuple-element.65), channel_id=1, source_target_pairs={{0,2},{2,0},{4,6},{6,4},{1,3},{3,1},{5,7},{7,5},{8,10},{10,8},{12,... | collective-permute-start | bytes 1228808 | tf_op jit(solution)/shard_map/ppermute | solution.py:393
  104.8 1.6 collective-permute-start.18
  106.5 1.9 %collective-permute-start.16 = (f32[16,128]{1,0:T(8,128)S(1)}, f32[16,128]{1,0:T(8,128)S(1)}, u32[]{:S(2)}, u32[]{:S(2)}) collective-permute-start(f32[16,128]{1,0:T(8,128)S(1)} %pad_maximum_fusion.1), channel_id=1, source_target_pairs={{0,4},{2,6},{4,0},{6,2},{1,5},{3,7},{5,1},{7,3},{8,12},{10,14},{12... | collective-permute-start | bytes 24584 | tf_op jit(solution)/shard_map/ppermute | solution.py:1079
  108.4 6.9 %collective-permute-done.16 = f32[16,128]{1,0:T(8,128)S(1)} collective-permute-done((f32[16,128]{1,0:T(8,128)S(1)}, f32[16,128]{1,0:T(8,128)S(1)}, u32[]{:S(2)}, u32[]{:S(2)}) %collective-permute-start.16) | collective-permute-done | bytes 8224 | tf_op jit(solution)/shard_map/ppermute | solution.py:1079
  117.3 56.5 %step.1 = (f32[3,32,32,256]{3,2,1,0:T(8,128)}, f32[3,32,32,256]{3,2,1,0:T(8,128)}, f32[3,32,32,256]{3,2,1,0:T(8,128)}, f32[32,32,256]{2,1,0:T(8,128)}, f32[32,32,256]{2,1,0:T(8,128)}) custom-call(f32[7]{0:T(128)} %stack.55.refs_0_.flags, f32[32,128]{1,0:T(8,128)} %pad_maximum_fusion.refs_1_, f32[1,32,32,256]{3,2,1,0:T(8,128)} %bitcast.21, ...), custom_call_target="tpu_custom_call" | custom-call | bytes 3000000 | tf_op jit(solution)/shard_map/step/pallas_call | solution.py:1162
  (50 shorter events, 5.9 us)
Async XLA Ops:
  3.1 2.2 %collective-permute-start = (f32[32,32,128]{2,1,0:T(8,128)}, f32[32,32,128]{2,1,0:T(8,128)S(1)}, u32[]{:S(2)}, u32[]{:S(2)}) collective-permute-start(f32[32,32,128]{2,1,0:T(8,128)} %pack_lanes.2), channel_id=1, source_target_pairs={{0,1},{1,0},{2,3},{3,2},{4,5},{5,4},{6,7},{7,6},{8,9},{9,8},{10,11... | collective-permute-start | bytes 1572872 | tf_op jit(solution)/shard_map/ppermute | solution.py:169
  8.6 9.6 %collective-permute-start.1 = (f32[5,32,256]{2,1,0:T(8,128)}, f32[5,32,256]{2,1,0:T(8,128)S(1)}, u32[]{:S(2)}, u32[]{:S(2)}) collective-permute-start(f32[5,32,256]{2,1,0:T(8,128)} %get-tuple-element.36), channel_id=1, source_target_pairs={{0,8},{8,16},{16,24},{24,0},{1,9},{9,17},{17,25},{25,1},{2,10},{10... | collective-permute-start | bytes 491528 | tf_op jit(solution)/shard_map/ppermute | solution.py:381
  11.5 9.4 %collective-permute-start.2 = (f32[5,32,256]{2,1,0:T(8,128)}, f32[5,32,256]{2,1,0:T(8,128)S(1)}, u32[]{:S(2)}, u32[]{:S(2)}) collective-permute-start(f32[5,32,256]{2,1,0:T(8,128)} %get-tuple-element.37), channel_id=1, source_target_pairs={{0,24},{8,0},{16,8},{24,16},{1,25},{9,1},{17,9},{25,17},{2,26},{10... | collective-permute-start | bytes 491528 | tf_op jit(solution)/shard_map/ppermute | solution.py:381
  18.2 2.7 %copy-start.1 = (f32[5,32,256]{2,1,0:T(8,128)}, f32[5,32,256]{2,1,0:T(8,128)S(1)}, u32[]{:S(2)}) copy-start(f32[5,32,256]{2,1,0:T(8,128)S(1)} %collective-permute-done.1.refs_6_.refs_7_.refs_4_.refs_8_.refs_9_.refs_16_) | copy-start | bytes 491524
  20.9 0.7 copy-start.2
  20.9 6.4 %collective-permute-start.5 = (f32[32,32,128]{2,1,0:T(8,128)}, f32[32,32,128]{2,1,0:T(8,128)S(1)}, u32[]{:S(2)}, u32[]{:S(2)}) collective-permute-start(f32[32,32,128]{2,1,0:T(8,128)} %pack_lanes.3), channel_id=1, source_target_pairs={{0,1},{1,0},{2,3},{3,2},{4,5},{5,4},{6,7},{7,6},{8,9},{9,8},{10,11... | collective-permute-start | bytes 1572872 | tf_op jit(solution)/shard_map/ppermute | solution.py:169
  24.1 12.7 %collective-permute-start.3 = (f32[36,8,256]{2,1,0:T(8,128)}, f32[36,8,256]{2,1,0:T(8,128)S(1)}, u32[]{:S(2)}, u32[]{:S(2)}) collective-permute-start(f32[36,8,256]{2,1,0:T(8,128)} %get-tuple-element.40), channel_id=1, source_target_pairs={{0,2},{2,0},{4,6},{6,4},{1,3},{3,1},{5,7},{7,5},{8,10},{10,8},{12,... | collective-permute-start | bytes 884744 | tf_op jit(solution)/shard_map/ppermute | solution.py:393
  25.6 11.1 %collective-permute-start.4 = (f32[36,8,256]{2,1,0:T(8,128)}, f32[36,8,256]{2,1,0:T(8,128)S(1)}, u32[]{:S(2)}, u32[]{:S(2)}) collective-permute-start(f32[36,8,256]{2,1,0:T(8,128)} %get-tuple-element.41), channel_id=1, source_target_pairs={{0,0},{2,4},{4,2},{6,6},{1,1},{3,5},{5,3},{7,7},{8,8},{10,12},{12,... | collective-permute-start | bytes 884744 | tf_op jit(solution)/shard_map/ppermute | solution.py:393
  36.8 15.0 %copy-start.6 = (f32[36,8,256]{2,1,0:T(8,128)}, f32[36,8,256]{2,1,0:T(8,128)S(1)}, u32[]{:S(2)}) copy-start(f32[36,8,256]{2,1,0:T(8,128)S(1)} %collective-permute-done.3.refs_6_.refs_18_) | copy-start | bytes 884740
  36.8 15.0 %copy-start.7 = (f32[36,8,256]{2,1,0:T(8,128)}, f32[36,8,256]{2,1,0:T(8,128)S(1)}, u32[]{:S(2)}) copy-start(f32[36,8,256]{2,1,0:T(8,128)S(1)} %collective-permute-done.4.refs_7_.refs_19_) | copy-start | bytes 884740
  36.8 44.1 %collective-permute-start.6 = (f32[32,32,256]{2,1,0:T(8,128)}, f32[32,32,256]{2,1,0:T(8,128)}, u32[]{:S(2)}, u32[]{:S(2)}) collective-permute-start(f32[32,32,256]{2,1,0:T(8,128)} %get-tuple-element.51), channel_id=1, source_target_pairs={{0,2},{2,0},{4,6},{6,4},{1,3},{3,1},{5,7},{7,5},{8,10},{10,8},{12,... | collective-permute-start | bytes 3145736 | tf_op jit(solution)/shard_map/ppermute | solution.py:393
  40.3 40.7 %collective-permute-start.7 = (f32[32,32,256]{2,1,0:T(8,128)}, f32[32,32,256]{2,1,0:T(8,128)}, u32[]{:S(2)}, u32[]{:S(2)}) collective-permute-start(f32[32,32,256]{2,1,0:T(8,128)} %get-tuple-element.52), channel_id=1, source_target_pairs={{0,0},{2,4},{4,2},{6,6},{1,1},{3,5},{5,3},{7,7},{8,8},{10,12},{12,... | collective-permute-start | bytes 3145736 | tf_op jit(solution)/shard_map/ppermute | solution.py:393
  49.7 31.2 %collective-permute-start.9 = (f32[24,32,256]{2,1,0:T(8,128)}, f32[24,32,256]{2,1,0:T(8,128)S(1)}, u32[]{:S(2)}, u32[]{:S(2)}) collective-permute-start(f32[24,32,256]{2,1,0:T(8,128)} %get-tuple-element.54), channel_id=1, source_target_pairs={{0,24},{8,0},{16,8},{24,16},{1,25},{9,1},{17,9},{25,17},{2,26},{10... | collective-permute-start | bytes 2359304 | tf_op jit(solution)/shard_map/ppermute | solution.py:381
  51.2 29.8 %collective-permute-start.8 = (f32[18,32,256]{2,1,0:T(8,128)}, f32[18,32,256]{2,1,0:T(8,128)S(1)}, u32[]{:S(2)}, u32[]{:S(2)}) collective-permute-start(f32[18,32,256]{2,1,0:T(8,128)} %get-tuple-element.53), channel_id=1, source_target_pairs={{0,8},{8,16},{16,24},{24,0},{1,9},{9,17},{17,25},{25,1},{2,10},{10... | collective-permute-start | bytes 1769480 | tf_op jit(solution)/shard_map/ppermute | solution.py:381
  80.9 19.5 %copy-start.3 = (f32[18,32,256]{2,1,0:T(8,128)}, f32[18,32,256]{2,1,0:T(8,128)S(1)}, u32[]{:S(2)}) copy-start(f32[18,32,256]{2,1,0:T(8,128)S(1)} %collective-permute-done.8.refs_0_.refs_1_.refs_8_) | copy-start | bytes 1769476
  80.9 19.5 %copy-start = (f32[24,32,256]{2,1,0:T(8,128)}, f32[24,32,256]{2,1,0:T(8,128)S(1)}, u32[]{:S(2)}) copy-start(f32[24,32,256]{2,1,0:T(8,128)S(1)} %collective-permute-done.9.refs_4_.refs_5_.refs_10_) | copy-start | bytes 2359300
  81.0 3.1 %collective-permute-start.10 = (f32[1,128]{1,0:T(1,128)}, f32[1,128]{1,0:T(1,128)S(1)}, u32[]{:S(2)}, u32[]{:S(2)}) collective-permute-start(f32[1,128]{1,0:T(1,128)} %moments.1), channel_id=1, source_target_pairs={{0,1},{1,0},{2,3},{3,2},{4,5},{5,4},{6,7},{7,6},{8,9},{9,8},{10,11... | collective-permute-start | bytes 1544 | tf_op jit(solution)/shard_map/ppermute | solution.py:1079
  81.0 8.2 %collective-permute-start.11 = (f32[5,32,256]{2,1,0:T(8,128)}, f32[5,32,256]{2,1,0:T(8,128)S(1)}, u32[]{:S(2)}, u32[]{:S(2)}) collective-permute-start(f32[5,32,256]{2,1,0:T(8,128)} %get-tuple-element.56), channel_id=1, source_target_pairs={{0,8},{8,16},{16,24},{24,0},{1,9},{9,17},{17,25},{25,1},{2,10},{10... | collective-permute-start | bytes 491528 | tf_op jit(solution)/shard_map/ppermute | solution.py:381
  82.6 10.5 %collective-permute-start.12 = (f32[6,32,256]{2,1,0:T(8,128)}, f32[6,32,256]{2,1,0:T(8,128)S(1)}, u32[]{:S(2)}, u32[]{:S(2)}) collective-permute-start(f32[6,32,256]{2,1,0:T(8,128)} %get-tuple-element.57), channel_id=1, source_target_pairs={{0,24},{8,0},{16,8},{24,16},{1,25},{9,1},{17,9},{25,17},{2,26},{10... | collective-permute-start | bytes 589832 | tf_op jit(solution)/shard_map/ppermute | solution.py:381
  89.2 11.2 %copy-start.5 = (f32[5,32,256]{2,1,0:T(8,128)}, f32[5,32,256]{2,1,0:T(8,128)S(1)}, u32[]{:S(2)}) copy-start(f32[5,32,256]{2,1,0:T(8,128)S(1)} %collective-permute-done.11.refs_2_.refs_3_.refs_9_) | copy-start | bytes 491524
  93.1 7.4 %copy-start.4 = (f32[6,32,256]{2,1,0:T(8,128)}, f32[6,32,256]{2,1,0:T(8,128)S(1)}, u32[]{:S(2)}) copy-start(f32[6,32,256]{2,1,0:T(8,128)S(1)} %collective-permute-done.12.refs_6_.refs_7_.refs_11_) | copy-start | bytes 589828
  93.1 3.6 %collective-permute-start.13 = (f32[2,128]{1,0:T(2,128)S(1)}, f32[2,128]{1,0:T(2,128)S(1)}, u32[]{:S(2)}, u32[]{:S(2)}) collective-permute-start(f32[2,128]{1,0:T(2,128)S(1)} %pad_maximum_fusion.4), channel_id=1, source_target_pairs={{0,8},{8,0},{16,24},{24,16},{1,9},{9,1},{17,25},{25,17},{2,10},{10... | collective-permute-start | bytes 3080 | tf_op jit(solution)/shard_map/ppermute | solution.py:1079
  96.7 3.6 %collective-permute-start.14 = (f32[4,128]{1,0:T(4,128)S(1)}, f32[4,128]{1,0:T(4,128)S(1)}, u32[]{:S(2)}, u32[]{:S(2)}) collective-permute-start(f32[4,128]{1,0:T(4,128)S(1)} %pad_maximum_fusion.3), channel_id=1, source_target_pairs={{0,16},{8,24},{16,0},{24,8},{1,17},{9,25},{17,1},{25,9},{2,18},{10... | collective-permute-start | bytes 6152 | tf_op jit(solution)/shard_map/ppermute | solution.py:1079
  100.3 6.1 %collective-permute-start.15 = (f32[8,128]{1,0:T(8,128)S(1)}, f32[8,128]{1,0:T(8,128)S(1)}, u32[]{:S(2)}, u32[]{:S(2)}) collective-permute-start(f32[8,128]{1,0:T(8,128)S(1)} %pad_maximum_fusion.2), channel_id=1, source_target_pairs={{0,2},{2,0},{4,6},{6,4},{1,3},{3,1},{5,7},{7,5},{8,10},{10,8},{12,... | collective-permute-start | bytes 12296 | tf_op jit(solution)/shard_map/ppermute | solution.py:1079
  102.9 13.0 %collective-permute-start.17 = (f32[10,40,256]{2,1,0:T(8,128)}, f32[10,40,256]{2,1,0:T(8,128)S(1)}, u32[]{:S(2)}, u32[]{:S(2)}) collective-permute-start(f32[10,40,256]{2,1,0:T(8,128)} %get-tuple-element.65), channel_id=1, source_target_pairs={{0,2},{2,0},{4,6},{6,4},{1,3},{3,1},{5,7},{7,5},{8,10},{10,8},{12,... | collective-permute-start | bytes 1228808 | tf_op jit(solution)/shard_map/ppermute | solution.py:393
  104.8 11.0 %collective-permute-start.18 = (f32[10,40,256]{2,1,0:T(8,128)}, f32[10,40,256]{2,1,0:T(8,128)S(1)}, u32[]{:S(2)}, u32[]{:S(2)}) collective-permute-start(f32[10,40,256]{2,1,0:T(8,128)} %get-tuple-element.66), channel_id=1, source_target_pairs={{0,0},{2,4},{4,2},{6,6},{1,1},{3,5},{5,3},{7,7},{8,8},{10,12},{12,... | collective-permute-start | bytes 1228808 | tf_op jit(solution)/shard_map/ppermute | solution.py:393
  106.5 8.7 %collective-permute-start.16 = (f32[16,128]{1,0:T(8,128)S(1)}, f32[16,128]{1,0:T(8,128)S(1)}, u32[]{:S(2)}, u32[]{:S(2)}) collective-permute-start(f32[16,128]{1,0:T(8,128)S(1)} %pad_maximum_fusion.1), channel_id=1, source_target_pairs={{0,4},{2,6},{4,0},{6,2},{1,5},{3,7},{5,1},{7,3},{8,12},{10,14},{12... | collective-permute-start | bytes 24584 | tf_op jit(solution)/shard_map/ppermute | solution.py:1079
  115.8 0.8 copy-start.8
  116.6 0.7 copy-start.9

commit v7 on v6

--- a/solution.py
+++ b/solution.py
@@ -383,14 +383,15 @@
     ]
 
 
-def exchange_rows(pair):
+def exchange_rows(pair, to_self=True):
     count = lax.axis_size("by")
     got = []
     for parity, one in enumerate(pair):
         partner = list(range(count))
         for i in range(parity, count - 1, 2):
             partner[i], partner[i + 1] = i + 1, i
-        got.append(lax.ppermute(one, "by", list(enumerate(partner))))
+        pairs = [(i, j) for i, j in enumerate(partner) if to_self or i != j]
+        got.append(lax.ppermute(one, "by", pairs))
     return got
 
 
@@ -861,8 +862,8 @@
 
 def step_kernel(plan, *refs):
     flags, sums, density, energy, position, velocity, pinned = refs[:7]
-    messages, inner = refs[7:16], refs[16:20]
-    velocity_new, accel, relaxed, density_new, energy_new = refs[20:25]
+    messages, inner = refs[7:14], refs[14:18]
+    velocity_new, accel, relaxed, density_new, energy_new = refs[18:23]
     (
         density_ext,
         energy_ext,
@@ -876,7 +877,7 @@
         other,
         semaphores,
         out_semaphores,
-    ) = refs[25:]
+    ) = refs[23:]
     assemble(
         plan,
         flags,
@@ -1068,18 +1069,23 @@
         one.wait()
 
 
-def gather_lines(line, axes):
-    for axis in axes:
+def line_hops():
+    hops = []
+    for axis in ("bz", "by", "bx"):
+        step = 1
+        while step < lax.axis_size(axis):
+            hops.append((axis, step))
+            step *= 2
+    return hops
+
+
+def gather_lines(line, hops):
+    for axis, step in hops:
         count = lax.axis_size(axis)
-        if count & (count - 1):
-            line = lax.all_gather(line, axis, axis=0, tiled=True)
-            continue
-        step = 1
-        while step < count:
-            got = lax.ppermute(line, axis, [(i, i ^ step) for i in range(count)])
-            later = (lax.axis_index(axis) // step) % 2 == 1
-            line = jnp.concatenate([jnp.where(later, got, line), jnp.where(later, line, got)])
-            step *= 2
+        assert count & (count - 1) == 0
+        got = lax.ppermute(line, axis, [(i, i ^ step) for i in range(count)])
+        later = (lax.axis_index(axis) // step) % 2 == 1
+        line = jnp.concatenate([jnp.where(later, got, line), jnp.where(later, line, got)])
     return line
 
 
@@ -1113,7 +1119,7 @@
         (1, SWEEPS - 1, SWEEPS),
     ]
     narrow = Plan([(1, NARROW, NARROW)] * 2, shape)
-    wide = Plan(groups, shape, narrow, cut=8)
+    wide = Plan(groups, shape, narrow, cut=None)
     cells = arrays[:2]
 
     packed = exchange_lanes(narrow, pack_lanes(narrow, cells))
@@ -1123,14 +1129,11 @@
     wide_packed = exchange_lanes(wide, wide_lanes)
     rows = exchange_rows(pack_rows(narrow, flags, cells, packed, True, planes))
 
-    first_planes, last_planes = pack_planes(wide, flags, arrays, wide_packed)
+    (wide_planes,) = pack_planes(wide, flags, arrays, wide_packed)
     wide_rows = pack_rows(wide, flags, arrays, wide_packed, True)
-    rows, first_planes, last_planes, wide_rows = lax.optimization_barrier(
-        (rows, first_planes, last_planes, wide_rows)
-    )
-    first_planes = exchange_planes(first_planes)
-    last_planes = exchange_planes(last_planes)
-    wide_rows = exchange_rows(wide_rows)
+    rows, wide_planes, wide_rows = lax.optimization_barrier((rows, wide_planes, wide_rows))
+    wide_planes = exchange_planes(wide_planes)
+    wide_rows = exchange_rows(wide_rows, to_self=False)
 
     line = pl.pallas_call(
         functools.partial(moments_kernel, narrow),
@@ -1151,17 +1154,20 @@
         name="moments",
     )(flags, *cells, packed, *planes, *rows)
 
-    line, wide_rows, first_planes = lax.optimization_barrier((line, wide_rows, first_planes))
-    lines = gather_lines(line, ("bz",))
-    lines, last_planes = lax.optimization_barrier((lines, last_planes))
-    wide_planes = [pair[side] for side in range(2) for pair in (first_planes, last_planes)]
-    corners = exchange_rows(pack_rows(wide, flags, None, None, False, wide_planes, planes))
+    line, wide_rows = lax.optimization_barrier((line, wide_rows))
+    hops = line_hops()
+    early = len(hops) - 3
+    lines = gather_lines(line, hops[:early])
+    lines, wide_planes = lax.optimization_barrier((lines, wide_planes))
+    corners = pack_rows(wide, flags, None, None, False, wide_planes, planes)
+    lines, corners = lax.optimization_barrier((lines, corners))
+    corners = exchange_rows(corners)
     messages = [wide_packed, *wide_planes, *wide_rows, *corners]
     nodes = jax.ShapeDtypeStruct((3, *shape), jnp.float32)
     cell = jax.ShapeDtypeStruct(shape, jnp.float32)
     return pl.pallas_call(
         functools.partial(step_kernel, wide),
-        in_specs=[in_smem(), in_vmem()] + [any_space()] * 5 + message_specs(5, 4) + message_specs(2, 2),
+        in_specs=[in_smem(), in_vmem()] + [any_space()] * 5 + message_specs(3, 4) + message_specs(2, 2),
         out_specs=[any_space()] * 5,
         out_shape=[nodes, nodes, nodes, cell, cell],
         scratch_shapes=[
@@ -1181,7 +1187,7 @@
         compiler_params=pltpu.CompilerParams(vmem_limit_bytes=VMEM_BYTES),
         cost_estimate=cost(1),
         name="step",
-    )(flags, gather_lines(lines, ("bx", "by")), *arrays, *messages, *planes, *rows)
+    )(flags, gather_lines(lines, hops[early:]), *arrays, *messages, *planes, *rows)
 
 
 def solution(mesh):

time: 175 us -> 158 us (0.903)
  waiting for transfers between devices: 31.8 us -> 21.4 us
  starting transfers between devices: 33.1 us -> 25.2 us
  local copies, waits for them, and re-layouts: 2.8 us -> 4.71 us
    ppermute x6, starting transfers between devices: 19.7 us -> 11.2 us  [exchange_rows(): got.append(lax.ppermute(one, 'by', pairs))]
    ppermute x6 -> x4, waiting for transfers between devices: 18.5 us -> 12.3 us  [exchange_planes(): lax.ppermute(one, 'bx', [(i, (i + step) % count) for i in range(count)])]
    ppermute x5, waiting for transfers between devices: 12.1 us -> 7.07 us  [gather_lines(): got = lax.ppermute(line, axis, [(i, i ^ step) for i in range(count)])]
    ppermute x5, starting transfers between devices: 3.96 us -> 7.58 us  [gather_lines(): got = lax.ppermute(line, axis, [(i, i ^ step) for i in range(count)])]
    ppermute x6 -> x4, starting transfers between devices: 8.94 us -> 5.96 us  [exchange_planes(): lax.ppermute(one, 'bx', [(i, (i + step) % count) for i in range(count)])]
    unnamed x20 -> x16, local copies, waits for them, and re-layouts: 2.19 us -> 4.03 us
  transfers between devices with their start and end apart: 19 -> 17, of which waited for: 8 -> 8; matrix products, arithmetic and copies ran while one was open for 2% -> 2% of each run, Pallas kernels for 24% -> 24%
where the time goes in v7:
time: 158 us; the launch traced here: 157 us
  Pallas kernels  102 us (65%)
  starting transfers between devices  25.2 us (16%)
  waiting for transfers between devices  21.4 us (14%)
  local copies, waits for them, and re-layouts  4.71 us (3%)
  other arithmetic  3.04 us (2%)
    pallas_call x1, Pallas kernels, on_device(): pl.pallas_call(functools.partial(step_kernel, wide), in_specs=[in_smem(),...  56.5 us
    pallas_call x1, Pallas kernels, on_device(): pl.pallas_call(functools.partial(moments_kernel, narrow), in_specs=[in_sm...  21.7 us
    ppermute x4, waiting for transfers between devices, exchange_planes(): lax.ppermute(one, 'bx', [(i, (i + step) % count) for i in range(count)])  12.3 us
    ppermute x6, starting transfers between devices, exchange_rows(): got.append(lax.ppermute(one, 'by', pairs))  11.2 us
    pallas_call x3, Pallas kernels, pack_rows(): pl.pallas_call(kernel, grid=(1,), in_specs=specs, out_specs=[pl.BlockSpec...  9.68 us
    pallas_call x2, Pallas kernels, pack_lanes(): pl.pallas_call(kernel, grid=(plan.x // planes,), in_specs=specs, out_spec...  8.14 us
    ppermute x5, starting transfers between devices, gather_lines(): got = lax.ppermute(line, axis, [(i, i ^ step) for i in range(count)])  7.58 us
    ppermute x5, waiting for transfers between devices, gather_lines(): got = lax.ppermute(line, axis, [(i, i ^ step) for i in range(count)])  7.07 us
  transfers between devices with their start and end apart: 17, of which 8 were waited for; matrix products, arithmetic and copies ran while one was open for 2% of the time, Pallas kernels for 24%

profile of v7, /device:TPU:0, one launch (start us, length us, event | category | flops | bytes accessed | tf_op | source)
XLA Modules:
  0.0 157.5 jit_solution(7255239637888443360)
XLA Ops:
  0.6 2.4 %pack_lanes.2 = f32[32,32,128]{2,1,0:T(8,128)} custom-call(f32[1,32,32,256]{3,2,1,0:T(8,128)} %bitcast.10, f32[1,32,32,256]{3,2,1,0:T(8,128)} %bitcast.11, f32[1,32,32,256]{3,2,1,0:T(8,128)} %bitcast.22, f32[1,32,32,256]{3,2,1,0:T(8,128)} %bitcast.23), custom_call_target="tpu_custom_call" | custom-call | bytes 1500000 | tf_op jit(solution)/shard_map/pack_lanes/pallas_call | solution.py:149
  4.2 1.1 collective-permute-done
  6.1 2.5 %pack_planes.2 = (f32[5,32,256]{2,1,0:T(8,128)}, f32[5,32,256]{2,1,0:T(8,128)}) custom-call(f32[7]{0:T(128)} %stack.55.refs_0_.flags, f32[1,32,32,256]{3,2,1,0:T(8,128)} %bitcast.12, f32[1,32,32,256]{3,2,1,0:T(8,128)} %bitcast.24, f32[32,32,128]{2,1,0:T(8,128)} %broadcast_select_fusion.1.refs_3_.refs_4_.refs_5_), custom_call_target="tpu_custom_call" | custom-call | bytes 1500000 | tf_op jit(solution)/shard_map/pack_planes/pallas_call | solution.py:242
  8.6 2.9 %collective-permute-start.1 = (f32[5,32,256]{2,1,0:T(8,128)}, f32[5,32,256]{2,1,0:T(8,128)S(1)}, u32[]{:S(2)}, u32[]{:S(2)}) collective-permute-start(f32[5,32,256]{2,1,0:T(8,128)} %get-tuple-element.33), channel_id=1, source_target_pairs={{0,8},{8,16},{16,24},{24,0},{1,9},{9,17},{17,25},{25,1},{2,10},{10... | collective-permute-start | bytes 491528 | tf_op jit(solution)/shard_map/ppermute | solution.py:381
  11.5 1.0 collective-permute-start.2
  12.5 5.7 %pack_lanes.3 = f32[32,32,128]{2,1,0:T(8,128)} custom-call(f32[1,32,32,256]{3,2,1,0:T(8,128)} %bitcast.13, f32[1,32,32,256]{3,2,1,0:T(8,128)} %bitcast.14, f32[1,32,32,256]{3,2,1,0:T(8,128)} %bitcast.25, f32[1,32,32,256]{3,2,1,0:T(8,128)} %bitcast.26, f32[3,32,32,256]{3,2,1,0:T(8,128)} %refs_4_.7, f32[3,32,32,256]{3,2,1,0:T(8,128)} %refs_4_.7, ...), custom_call_target="tpu_custom_call" | custom-call | bytes 1500000 | tf_op jit(solution)/shard_map/pack_lanes/pallas_call | solution.py:149
  18.2 2.7 %collective-permute-done.2.refs_8_.refs_9_.refs_5_.refs_6_.refs_7_.refs_15_ = f32[5,32,256]{2,1,0:T(8,128)S(1)} collective-permute-done((f32[5,32,256]{2,1,0:T(8,128)}, f32[5,32,256]{2,1,0:T(8,128)S(1)}, u32[]{:S(2)}, u32[]{:S(2)}) %collective-permute-start.2) | collective-permute-done | bytes 163872 | tf_op jit(solution)/shard_map/ppermute | solution.py:381
  21.6 2.5 %pack_rows.3 = (f32[36,8,256]{2,1,0:T(8,128)}, f32[36,8,256]{2,1,0:T(8,128)}) custom-call(f32[7]{0:T(128)} %stack.55.refs_0_.flags, f32[1,32,32,256]{3,2,1,0:T(8,128)} %bitcast.15, f32[1,32,32,256]{3,2,1,0:T(8,128)} %bitcast.16, f32[1,32,32,256]{3,2,1,0:T(8,128)} %bitcast.27, f32[1,32,32,256]{3,2,1,0:T(8,128)} %bitcast.28, ...), custom_call_target="tpu_custom_call" | custom-call | bytes 1500000 | tf_op jit(solution)/shard_map/pack_rows/pallas_call | solution.py:366
  24.1 1.6 collective-permute-start.3
  25.6 1.6 %collective-permute-start.4 = (f32[36,8,256]{2,1,0:T(8,128)}, f32[36,8,256]{2,1,0:T(8,128)S(1)}, u32[]{:S(2)}, u32[]{:S(2)}) collective-permute-start(f32[36,8,256]{2,1,0:T(8,128)} %get-tuple-element.38), channel_id=1, source_target_pairs={{0,0},{2,4},{4,2},{6,6},{1,1},{3,5},{5,3},{7,7},{8,8},{10,12},{12,... | collective-permute-start | bytes 884744 | tf_op jit(solution)/shard_map/ppermute | solution.py:394
  28.1 3.9 %pack_planes.3 = (f32[23,32,256]{2,1,0:T(8,128)}, f32[30,32,256]{2,1,0:T(8,128)}) custom-call(f32[7]{0:T(128)} %stack.55.refs_0_.flags, f32[1,32,32,256]{3,2,1,0:T(8,128)} %bitcast.17, f32[1,32,32,256]{3,2,1,0:T(8,128)} %bitcast.29, f32[3,32,32,256]{3,2,1,0:T(8,128)} %refs_4_.7, f32[3,32,32,256]{3,2,1,0:T(8,128)} %refs_5_.5, s32[1,32,32,256]{3,2,1,0:T(8,128)} %bitcast.36, ...), custom_call_target="tpu_custom_call" | custom-call | bytes 1500000 | tf_op jit(solution)/shard_map/pack_planes/pallas_call | solution.py:242
  32.0 4.8 %pack_rows.4 = (f32[32,32,256]{2,1,0:T(8,128)}, f32[32,32,256]{2,1,0:T(8,128)}) custom-call(f32[7]{0:T(128)} %stack.55.refs_0_.flags, f32[1,32,32,256]{3,2,1,0:T(8,128)} %bitcast.18, f32[1,32,32,256]{3,2,1,0:T(8,128)} %bitcast.19, f32[1,32,32,256]{3,2,1,0:T(8,128)} %bitcast.30, f32[1,32,32,256]{3,2,1,0:T(8,128)} %bitcast.31, f32[3,32,32,256]{3,2,1,0:T(8,128)} %refs_4_.7, ...), custom_call_target="tpu_custom_call" | custom-call | bytes 1500000 | tf_op jit(solution)/shard_map/pack_rows/pallas_call | solution.py:366
  36.8 3.5 %collective-permute-start.6 = (f32[32,32,256]{2,1,0:T(8,128)}, f32[32,32,256]{2,1,0:T(8,128)}, u32[]{:S(2)}, u32[]{:S(2)}) collective-permute-start(f32[32,32,256]{2,1,0:T(8,128)} %get-tuple-element.46), channel_id=1, source_target_pairs={{0,2},{2,0},{4,6},{6,4},{1,3},{3,1},{5,7},{7,5},{8,10},{10,8},{12,... | collective-permute-start | bytes 3145736 | tf_op jit(solution)/shard_map/ppermute | solution.py:394
  40.3 1.6 %collective-permute-start.7 = (f32[32,32,256]{2,1,0:T(8,128)}, f32[32,32,256]{2,1,0:T(8,128)}, u32[]{:S(2)}, u32[]{:S(2)}) collective-permute-start(f32[32,32,256]{2,1,0:T(8,128)} %get-tuple-element.47), channel_id=1, source_target_pairs={{2,4},{4,2},{3,5},{5,3},{10,12},{12,10},{11,13},{13,11},{18,20},{2... | collective-permute-start | bytes 3145736 | tf_op jit(solution)/shard_map/ppermute | solution.py:394
  41.9 1.4 collective-permute-start.11
  43.9 21.7 %moments.1 = f32[1,128]{1,0:T(1,128)} custom-call(f32[7]{0:T(128)} %stack.55.refs_0_.flags, f32[1,32,32,256]{3,2,1,0:T(8,128)} %bitcast.20, f32[1,32,32,256]{3,2,1,0:T(8,128)} %bitcast.32, f32[32,32,128]{2,1,0:T(8,128)} %broadcast_select_fusion.1.refs_3_.refs_4_.refs_5_, f32[5,32,256]{2,1,0:T(8,128)} %copy-done.2, f32[5,32,256]{2,1,0:T(8,128)} %copy-done.3, ...), custom_call_target="tpu_custom_call" | custom-call | bytes 3000000 | tf_op jit(solution)/shard_map/moments/pallas_call | solution.py:1138
  65.7 1.2 collective-permute-done.8
  67.6 1.9 %collective-permute-start.9 = (f32[2,128]{1,0:T(2,128)S(1)}, f32[2,128]{1,0:T(2,128)S(1)}, u32[]{:S(2)}, u32[]{:S(2)}) collective-permute-start(f32[2,128]{1,0:T(2,128)S(1)} %pad_maximum_fusion.4), channel_id=1, source_target_pairs={{0,2},{2,0},{4,6},{6,4},{1,3},{3,1},{5,7},{7,5},{8,10},{10,8},{12,... | collective-permute-start | bytes 3080 | tf_op jit(solution)/shard_map/ppermute | solution.py:1086
  69.5 1.7 %collective-permute-done.9 = f32[2,128]{1,0:T(2,128)S(1)} collective-permute-done((f32[2,128]{1,0:T(2,128)S(1)}, f32[2,128]{1,0:T(2,128)S(1)}, u32[]{:S(2)}, u32[]{:S(2)}) %collective-permute-start.9) | collective-permute-done | bytes 1056 | tf_op jit(solution)/shard_map/ppermute | solution.py:1086
  71.2 9.6 %collective-permute-done.10.refs_0_.refs_1_.refs_8_ = f32[23,32,256]{2,1,0:T(8,128)S(1)} collective-permute-done((f32[23,32,256]{2,1,0:T(8,128)}, f32[23,32,256]{2,1,0:T(8,128)S(1)}, u32[]{:S(2)}, u32[]{:S(2)}) %collective-permute-start.10) | collective-permute-done | bytes 753696 | tf_op jit(solution)/shard_map/ppermute | solution.py:381
  80.8 0.9 copy-done.1
  81.7 1.0 copy-done
  82.7 2.4 %pack_rows.5 = (f32[10,40,256]{2,1,0:T(8,128)}, f32[10,40,256]{2,1,0:T(8,128)}) custom-call(f32[7]{0:T(128)} %stack.55.refs_0_.flags, f32[23,32,256]{2,1,0:T(8,128)} %copy-done.1, f32[23,32,256]{2,1,0:T(8,128)} %copy-done.1, f32[30,32,256]{2,1,0:T(8,128)} %copy-done, f32[30,32,256]{2,1,0:T(8,128)} %copy-done, f32[5,32,256]{2,1,0:T(8,128)} %copy-done.2, ...), custom_call_target="tpu_custom_call" | custom-call | bytes 1500000 | tf_op jit(solution)/shard_map/pack_rows/pallas_call | solution.py:366
  85.1 2.5 %collective-permute-start.12 = (f32[4,128]{1,0:T(4,128)S(1)}, f32[4,128]{1,0:T(4,128)S(1)}, u32[]{:S(2)}, u32[]{:S(2)}) collective-permute-start(f32[4,128]{1,0:T(4,128)S(1)} %pad_maximum_fusion.3), channel_id=1, source_target_pairs={{0,4},{2,6},{4,0},{6,2},{1,5},{3,7},{5,1},{7,3},{8,12},{10,14},{12... | collective-permute-start | bytes 6152 | tf_op jit(solution)/shard_map/ppermute | solution.py:1086
  87.5 2.0 %collective-permute-done.12 = f32[4,128]{1,0:T(4,128)S(1)} collective-permute-done((f32[4,128]{1,0:T(4,128)S(1)}, f32[4,128]{1,0:T(4,128)S(1)}, u32[]{:S(2)}, u32[]{:S(2)}) %collective-permute-start.12) | collective-permute-done | bytes 2080 | tf_op jit(solution)/shard_map/ppermute | solution.py:1086
  89.6 1.6 %collective-permute-start.13 = (f32[8,128]{1,0:T(8,128)S(1)}, f32[8,128]{1,0:T(8,128)S(1)}, u32[]{:S(2)}, u32[]{:S(2)}) collective-permute-start(f32[8,128]{1,0:T(8,128)S(1)} %pad_maximum_fusion.2), channel_id=1, source_target_pairs={{0,8},{8,0},{16,24},{24,16},{1,9},{9,1},{17,25},{25,17},{2,10},{10... | collective-permute-start | bytes 12296 | tf_op jit(solution)/shard_map/ppermute | solution.py:1086
  91.2 1.3 collective-permute-start.15
  92.5 1.6 %collective-permute-start.16 = (f32[10,40,256]{2,1,0:T(8,128)}, f32[10,40,256]{2,1,0:T(8,128)S(1)}, u32[]{:S(2)}, u32[]{:S(2)}) collective-permute-start(f32[10,40,256]{2,1,0:T(8,128)} %get-tuple-element.60), channel_id=1, source_target_pairs={{0,0},{2,4},{4,2},{6,6},{1,1},{3,5},{5,3},{7,7},{8,8},{10,12},{12,... | collective-permute-start | bytes 1228808 | tf_op jit(solution)/shard_map/ppermute | solution.py:394
  94.1 1.5 collective-permute-start.14
  95.7 2.2 %collective-permute-done.14 = f32[16,128]{1,0:T(8,128)S(1)} collective-permute-done((f32[16,128]{1,0:T(8,128)S(1)}, f32[16,128]{1,0:T(8,128)S(1)}, u32[]{:S(2)}, u32[]{:S(2)}) %collective-permute-start.14) | collective-permute-done | bytes 8224 | tf_op jit(solution)/shard_map/ppermute | solution.py:1086
  98.5 1.0 collective-permute-done.15.refs_12_
  101.0 56.5 %step.1 = (f32[3,32,32,256]{3,2,1,0:T(8,128)}, f32[3,32,32,256]{3,2,1,0:T(8,128)}, f32[3,32,32,256]{3,2,1,0:T(8,128)}, f32[32,32,256]{2,1,0:T(8,128)}, f32[32,32,256]{2,1,0:T(8,128)}) custom-call(f32[7]{0:T(128)} %stack.55.refs_0_.flags, f32[32,128]{1,0:T(8,128)} %pad_maximum_fusion.refs_1_, f32[1,32,32,256]{3,2,1,0:T(8,128)} %bitcast.21, ...), custom_call_target="tpu_custom_call" | custom-call | bytes 3000000 | tf_op jit(solution)/shard_map/step/pallas_call | solution.py:1168
  (42 shorter events, 7.1 us)
Async XLA Ops:
  3.1 2.2 %collective-permute-start = (f32[32,32,128]{2,1,0:T(8,128)}, f32[32,32,128]{2,1,0:T(8,128)S(1)}, u32[]{:S(2)}, u32[]{:S(2)}) collective-permute-start(f32[32,32,128]{2,1,0:T(8,128)} %pack_lanes.2), channel_id=1, source_target_pairs={{0,1},{1,0},{2,3},{3,2},{4,5},{5,4},{6,7},{7,6},{8,9},{9,8},{10,11... | collective-permute-start | bytes 1572872 | tf_op jit(solution)/shard_map/ppermute | solution.py:169
  8.6 9.6 %collective-permute-start.1 = (f32[5,32,256]{2,1,0:T(8,128)}, f32[5,32,256]{2,1,0:T(8,128)S(1)}, u32[]{:S(2)}, u32[]{:S(2)}) collective-permute-start(f32[5,32,256]{2,1,0:T(8,128)} %get-tuple-element.33), channel_id=1, source_target_pairs={{0,8},{8,16},{16,24},{24,0},{1,9},{9,17},{17,25},{25,1},{2,10},{10... | collective-permute-start | bytes 491528 | tf_op jit(solution)/shard_map/ppermute | solution.py:381
  11.5 9.4 %collective-permute-start.2 = (f32[5,32,256]{2,1,0:T(8,128)}, f32[5,32,256]{2,1,0:T(8,128)S(1)}, u32[]{:S(2)}, u32[]{:S(2)}) collective-permute-start(f32[5,32,256]{2,1,0:T(8,128)} %get-tuple-element.34), channel_id=1, source_target_pairs={{0,24},{8,0},{16,8},{24,16},{1,25},{9,1},{17,9},{25,17},{2,26},{10... | collective-permute-start | bytes 491528 | tf_op jit(solution)/shard_map/ppermute | solution.py:381
  18.2 2.7 %copy-start.2 = (f32[5,32,256]{2,1,0:T(8,128)}, f32[5,32,256]{2,1,0:T(8,128)S(1)}, u32[]{:S(2)}) copy-start(f32[5,32,256]{2,1,0:T(8,128)S(1)} %collective-permute-done.1.refs_6_.refs_7_.refs_4_.refs_5_.refs_14_) | copy-start | bytes 491524
  20.9 0.7 copy-start.3
  20.9 6.3 %collective-permute-start.5 = (f32[32,32,128]{2,1,0:T(8,128)}, f32[32,32,128]{2,1,0:T(8,128)S(1)}, u32[]{:S(2)}, u32[]{:S(2)}) collective-permute-start(f32[32,32,128]{2,1,0:T(8,128)} %pack_lanes.3), channel_id=1, source_target_pairs={{0,1},{1,0},{2,3},{3,2},{4,5},{5,4},{6,7},{7,6},{8,9},{9,8},{10,11... | collective-permute-start | bytes 1572872 | tf_op jit(solution)/shard_map/ppermute | solution.py:169
  24.1 12.7 %collective-permute-start.3 = (f32[36,8,256]{2,1,0:T(8,128)}, f32[36,8,256]{2,1,0:T(8,128)S(1)}, u32[]{:S(2)}, u32[]{:S(2)}) collective-permute-start(f32[36,8,256]{2,1,0:T(8,128)} %get-tuple-element.37), channel_id=1, source_target_pairs={{0,2},{2,0},{4,6},{6,4},{1,3},{3,1},{5,7},{7,5},{8,10},{10,8},{12,... | collective-permute-start | bytes 884744 | tf_op jit(solution)/shard_map/ppermute | solution.py:394
  25.6 11.2 %collective-permute-start.4 = (f32[36,8,256]{2,1,0:T(8,128)}, f32[36,8,256]{2,1,0:T(8,128)S(1)}, u32[]{:S(2)}, u32[]{:S(2)}) collective-permute-start(f32[36,8,256]{2,1,0:T(8,128)} %get-tuple-element.38), channel_id=1, source_target_pairs={{0,0},{2,4},{4,2},{6,6},{1,1},{3,5},{5,3},{7,7},{8,8},{10,12},{12,... | collective-permute-start | bytes 884744 | tf_op jit(solution)/shard_map/ppermute | solution.py:394
  36.8 7.2 %copy-start.4 = (f32[36,8,256]{2,1,0:T(8,128)}, f32[36,8,256]{2,1,0:T(8,128)S(1)}, u32[]{:S(2)}) copy-start(f32[36,8,256]{2,1,0:T(8,128)S(1)} %collective-permute-done.3.refs_6_.refs_16_) | copy-start | bytes 884740
  36.8 3.5 %copy-start.5 = (f32[36,8,256]{2,1,0:T(8,128)}, f32[36,8,256]{2,1,0:T(8,128)S(1)}, u32[]{:S(2)}) copy-start(f32[36,8,256]{2,1,0:T(8,128)S(1)} %collective-permute-done.4.refs_7_.refs_17_) | copy-start | bytes 884740
  36.8 28.8 %collective-permute-start.6 = (f32[32,32,256]{2,1,0:T(8,128)}, f32[32,32,256]{2,1,0:T(8,128)}, u32[]{:S(2)}, u32[]{:S(2)}) collective-permute-start(f32[32,32,256]{2,1,0:T(8,128)} %get-tuple-element.46), channel_id=1, source_target_pairs={{0,2},{2,0},{4,6},{6,4},{1,3},{3,1},{5,7},{7,5},{8,10},{10,8},{12,... | collective-permute-start | bytes 3145736 | tf_op jit(solution)/shard_map/ppermute | solution.py:394
  40.3 25.3 %collective-permute-start.7 = (f32[32,32,256]{2,1,0:T(8,128)}, f32[32,32,256]{2,1,0:T(8,128)}, u32[]{:S(2)}, u32[]{:S(2)}) collective-permute-start(f32[32,32,256]{2,1,0:T(8,128)} %get-tuple-element.47), channel_id=1, source_target_pairs={{2,4},{4,2},{3,5},{5,3},{10,12},{12,10},{11,13},{13,11},{18,20},{2... | collective-permute-start | bytes 3145736 | tf_op jit(solution)/shard_map/ppermute | solution.py:394
  41.9 38.9 %collective-permute-start.11 = (f32[30,32,256]{2,1,0:T(8,128)}, f32[30,32,256]{2,1,0:T(8,128)S(1)}, u32[]{:S(2)}, u32[]{:S(2)}) collective-permute-start(f32[30,32,256]{2,1,0:T(8,128)} %get-tuple-element.50), channel_id=1, source_target_pairs={{0,24},{8,0},{16,8},{24,16},{1,25},{9,1},{17,9},{25,17},{2,26},{10... | collective-permute-start | bytes 2949128 | tf_op jit(solution)/shard_map/ppermute | solution.py:381
  43.3 37.5 %collective-permute-start.10 = (f32[23,32,256]{2,1,0:T(8,128)}, f32[23,32,256]{2,1,0:T(8,128)S(1)}, u32[]{:S(2)}, u32[]{:S(2)}) collective-permute-start(f32[23,32,256]{2,1,0:T(8,128)} %get-tuple-element.49), channel_id=1, source_target_pairs={{0,8},{8,16},{16,24},{24,0},{1,9},{9,17},{17,25},{25,1},{2,10},{10... | collective-permute-start | bytes 2261000 | tf_op jit(solution)/shard_map/ppermute | solution.py:381
  65.6 1.2 collective-permute-start.8
  67.6 3.6 %collective-permute-start.9 = (f32[2,128]{1,0:T(2,128)S(1)}, f32[2,128]{1,0:T(2,128)S(1)}, u32[]{:S(2)}, u32[]{:S(2)}) collective-permute-start(f32[2,128]{1,0:T(2,128)S(1)} %pad_maximum_fusion.4), channel_id=1, source_target_pairs={{0,2},{2,0},{4,6},{6,4},{1,3},{3,1},{5,7},{7,5},{8,10},{10,8},{12,... | collective-permute-start | bytes 3080 | tf_op jit(solution)/shard_map/ppermute | solution.py:1086
  80.8 0.9 copy-start.1
  81.7 1.0 copy-start
  85.1 4.5 %collective-permute-start.12 = (f32[4,128]{1,0:T(4,128)S(1)}, f32[4,128]{1,0:T(4,128)S(1)}, u32[]{:S(2)}, u32[]{:S(2)}) collective-permute-start(f32[4,128]{1,0:T(4,128)S(1)} %pad_maximum_fusion.3), channel_id=1, source_target_pairs={{0,4},{2,6},{4,0},{6,2},{1,5},{3,7},{5,1},{7,3},{8,12},{10,14},{12... | collective-permute-start | bytes 6152 | tf_op jit(solution)/shard_map/ppermute | solution.py:1086
  89.6 4.5 %collective-permute-start.13 = (f32[8,128]{1,0:T(8,128)S(1)}, f32[8,128]{1,0:T(8,128)S(1)}, u32[]{:S(2)}, u32[]{:S(2)}) collective-permute-start(f32[8,128]{1,0:T(8,128)S(1)} %pad_maximum_fusion.2), channel_id=1, source_target_pairs={{0,8},{8,0},{16,24},{24,16},{1,9},{9,1},{17,25},{25,17},{2,10},{10... | collective-permute-start | bytes 12296 | tf_op jit(solution)/shard_map/ppermute | solution.py:1086
  91.2 8.3 %collective-permute-start.15 = (f32[10,40,256]{2,1,0:T(8,128)}, f32[10,40,256]{2,1,0:T(8,128)S(1)}, u32[]{:S(2)}, u32[]{:S(2)}) collective-permute-start(f32[10,40,256]{2,1,0:T(8,128)} %get-tuple-element.59), channel_id=1, source_target_pairs={{0,2},{2,0},{4,6},{6,4},{1,3},{3,1},{5,7},{7,5},{8,10},{10,8},{12,... | collective-permute-start | bytes 1228808 | tf_op jit(solution)/shard_map/ppermute | solution.py:394
  92.5 7.0 %collective-permute-start.16 = (f32[10,40,256]{2,1,0:T(8,128)}, f32[10,40,256]{2,1,0:T(8,128)S(1)}, u32[]{:S(2)}, u32[]{:S(2)}) collective-permute-start(f32[10,40,256]{2,1,0:T(8,128)} %get-tuple-element.60), channel_id=1, source_target_pairs={{0,0},{2,4},{4,2},{6,6},{1,1},{3,5},{5,3},{7,7},{8,8},{10,12},{12,... | collective-permute-start | bytes 1228808 | tf_op jit(solution)/shard_map/ppermute | solution.py:394
  94.1 3.7 %collective-permute-start.14 = (f32[16,128]{1,0:T(8,128)S(1)}, f32[16,128]{1,0:T(8,128)S(1)}, u32[]{:S(2)}, u32[]{:S(2)}) collective-permute-start(f32[16,128]{1,0:T(8,128)S(1)} %pad_maximum_fusion.1), channel_id=1, source_target_pairs={{0,16},{8,24},{16,0},{24,8},{1,17},{9,25},{17,1},{25,9},{2,18},{10... | collective-permute-start | bytes 24584 | tf_op jit(solution)/shard_map/ppermute | solution.py:1086
  99.4 0.8 copy-start.6
  100.2 0.8 copy-start.7

commit v8 on v7

--- a/solution.py
+++ b/solution.py
@@ -17,7 +17,8 @@
 LANES = 128
 ROWS = 8
 MOMENTS = 7
-UNROLL = 6
+MOMENTS_UNROLL = 12
+STEP_UNROLL = 3
 POSITION, VELOCITY, PINNED = 2, 3, 4
 NARROW = 2
 WIDE = SWEEPS + 2
@@ -112,6 +113,17 @@
     )
 
 
+def every_plane(count, body, together):
+    together = together if count % together == 0 else 1
+
+    def turn(j, _):
+        for k in range(together):
+            body(j * together + k)
+        return 0
+
+    lax.fori_loop(0, count // together, turn, 0)
+
+
 def lane_index(shape):
     return lax.broadcasted_iota(jnp.int32, shape, len(shape) - 1)
 
@@ -294,7 +306,7 @@
             del refs[: 2 * groups + 2]
             base = plan.x
 
-            def own_plane(x, _):
+            def own_plane(x):
                 for field in plan.fields:
                     first, last = [
                         plan.value(
@@ -305,9 +317,8 @@
                     ]
                     put(x, field, first, last)
                 put_packed(x, blocks[-2].at[x], blocks[-1].at[x], 0)
-                return 0
-
-            lax.fori_loop(0, plan.x, own_plane, 0)
+
+            every_plane(plan.x, own_plane, 4)
         if planes:
             count = len(plan.parts[0])
             pairs = [tuple(refs[2 * k : 2 * k + 2]) for k in range(2 * count + 2)]
@@ -494,23 +505,20 @@
         own, halo = ordered(own_messages), ordered(halo_messages)
         inner_rows = (None, None) if inner is None else ordered(inner[2:4])
 
-        def own_plane(x, _):
+        def own_plane(x):
             fill(plan.low + x, *own, *inner_rows, x, True)
-            return 0
-
-        def low_plane(k, _):
+
+        def low_plane(k):
             fill(k, *halo, None, None, halo_at + k, False)
-            return 0
-
-        def high_plane(k, _):
+
+        def high_plane(k):
             fill(plan.low + plan.x + k, *halo, None, None, halo_at + plan.low + k, False)
-            return 0
-
-        lax.fori_loop(0, plan.x, own_plane, 0)
-        lax.fori_loop(0, plan.low, low_plane, 0)
-        lax.fori_loop(0, plan.high, high_plane, 0)
-
-    def finish_plane(x, _):
+
+        every_plane(plan.x, own_plane, 2)
+        every_plane(plan.low, low_plane, 1)
+        every_plane(plan.high, high_plane, 1)
+
+    def finish_plane(x):
         i = plan.low + x
         for t in range(plan.tiles):
             at = (i, t, slice(ROWS, top))
@@ -522,14 +530,13 @@
 
             for group, component in [(POSITION, c) for c in range(3)] + [(PINNED, 0)]:
                 extended[group][(component, *at)] = plan.value(group, component, get)
-        return 0
 
     for parity in range(2):
         pl.when(flags[6] == parity)(functools.partial(fill_all, parity))
     for one in copies[:large]:
         one.wait()
     if pinned_own is not None:
-        lax.fori_loop(0, plan.x, finish_plane, 0)
+        every_plane(plan.x, finish_plane, 2)
 
 
 def assemble_copies(plan):
@@ -537,7 +544,7 @@
     return (3 * len(plan.fields) + 2 * skipping) * plan.tiles + 1 + plan.low + plan.high
 
 
-def plane_loop(ref, first, last, row, body, carried):
+def plane_loop(ref, first, last, row, body, carried, unroll):
     def turn(plane, carried, count):
         here = spot(ref, plane, row)
         pending = []
@@ -550,9 +557,9 @@
 
     count = last - first + 1
     carried = lax.fori_loop(
-        0, count // UNROLL, lambda j, c: turn(first + j * UNROLL, c, UNROLL), carried
+        0, count // unroll, lambda j, c: turn(first + j * unroll, c, unroll), carried
     )
-    rest = count % UNROLL
+    rest = count % unroll
     return turn(last + 1 - rest, carried, rest) if rest else carried
 
 
@@ -650,7 +657,7 @@
         )
 
 
-def force_pass(density, energy, force, mass, inside, planes, rows):
+def force_pass(density, energy, force, mass, inside, planes, rows, unroll):
     def chunk(row):
         keep = inside.tiles(row, 0.4 * 0.25)
 
@@ -681,7 +688,7 @@
             stores.append((mass, 0, at, result))
             return now, stores
 
-        plane_loop(density, *planes, row, plane, slab(spot(density, planes[0] - 1, row)))
+        plane_loop(density, *planes, row, plane, slab(spot(density, planes[0] - 1, row)), unroll)
 
     chunks(*rows, chunk)
 
@@ -692,7 +699,7 @@
     return add(total, sides)
 
 
-def stencil_pass(ref, planes, rows, setup, use):
+def stencil_pass(ref, planes, rows, setup, use, unroll):
     def chunk(row):
         given = setup(row)
 
@@ -708,7 +715,7 @@
         start = spot(ref, planes[0], row)
         first = [load(ref, component, start.at_plane(-1)) for component in range(3)]
         second = [load(ref, component, start) for component in range(3)]
-        plane_loop(ref, *planes, row, plane, (first, second))
+        plane_loop(ref, *planes, row, plane, (first, second), unroll)
 
     chunks(*rows, chunk)
 
@@ -742,6 +749,7 @@
         inside,
         (low - 1, low + x + 1),
         (ROWS - 1, ROWS + y + 1),
+        MOMENTS_UNROLL,
     )
 
     def multiply(at, here, sums, keep):
@@ -761,6 +769,7 @@
         (ROWS, ROWS + y),
         lambda row: inside.tiles(row, CONSISTENT),
         multiply,
+        MOMENTS_UNROLL,
     )
 
     own = range(plan.tiles)
@@ -779,7 +788,7 @@
                     sums[3 + component] = sums[3 + component] + f[t] * v[t]
             return tuple(sums), []
 
-        return plane_loop(force, low, low + x - 1, row, plane, sums)
+        return plane_loop(force, low, low + x - 1, row, plane, sums, MOMENTS_UNROLL)
 
     sums = lax.fori_loop(0, y // ROWS, first_chunk, (nothing,) * 6)
     sums = [whole_sum(one) for one in sums]
@@ -825,7 +834,7 @@
             return (ahead, tuple(sums)), []
 
         start = [pair(component, spot(force, low, row)) for component in range(3)]
-        return plane_loop(force, low, low + x - 1, row, plane, (start, sums))[1]
+        return plane_loop(force, low, low + x - 1, row, plane, (start, sums), MOMENTS_UNROLL)[1]
 
     rest = lax.fori_loop(0, y // ROWS, second_chunk, (nothing,) * 15)
     lane = lane_index((1, LANES))
@@ -901,6 +910,7 @@
         inside,
         (low - reach, low + x + reach),
         (ROWS - reach, ROWS + y + reach),
+        STEP_UNROLL,
     )
 
     def advance(at, here, sums, keep):
@@ -935,6 +945,7 @@
         (ROWS - reach, ROWS - reach + advanced - 1),
         lambda row: inside.tiles(row, CONSISTENT),
         advance,
+        STEP_UNROLL,
     )
 
     out_copies = []
@@ -979,7 +990,7 @@
             result = each(lambda d, e: d * e, load(density_ext, 0, at), lagged)
             return now, [(content, 0, at, result)]
 
-        plane_loop(speed, low - 1, low + x, row, plane, slab(spot(speed, low - 1, row)))
+        plane_loop(speed, low - 1, low + x, row, plane, slab(spot(speed, low - 1, row)), STEP_UNROLL)
 
     chunks(ROWS - 1, ROWS + y, content_chunk)
 
@@ -1008,6 +1019,7 @@
             (ROWS - reach, ROWS + y + reach),
             lambda row: None,
             relax,
+            STEP_UNROLL,
         )
         source, target = target, (force if target is other else other)
     settled, free_buffer = source, target
@@ -1060,7 +1072,7 @@
         first = spot(settled, low, row)
         start = slab(first)
         before = [load(one, 0, first.at_plane(-1)) for one in quantities]
-        plane_loop(settled, low, low + x - 1, row, plane, (start, x_flux(start[0], start[4], before)))
+        plane_loop(settled, low, low + x - 1, row, plane, (start, x_flux(start[0], start[4], before)), STEP_UNROLL)
 
     chunks(ROWS, ROWS + y - 1, remap_chunk)
     write(free_buffer, density_new, 0)

time: 158 us -> 171 us (1.082)
  Pallas kernels: 102 us -> 111 us
  starting transfers between devices: 25.2 us -> 27.6 us
  waiting for transfers between devices: 21.4 us -> 23.2 us
    pallas_call x1, Pallas kernels: 56.5 us -> 70 us  [on_device(): pl.pallas_call(functools.partial(step_kernel, wide), in_specs=[in_smem(),...]
    pallas_call x1, Pallas kernels: 21.7 us -> 17.6 us  [on_device(): pl.pallas_call(functools.partial(moments_kernel, narrow), in_specs=[in_sm...]
    ppermute x5, starting transfers between devices: 7.58 us -> 9.97 us  [gather_lines(): got = lax.ppermute(line, axis, [(i, i ^ step) for i in range(count)])]
    ppermute x6, waiting for transfers between devices: 0.98 us -> 2.7 us  [exchange_rows(): got.append(lax.ppermute(one, 'by', pairs))]
  transfers between devices with their start and end apart: 17 -> 17, of which waited for: 8 -> 9; matrix products, arithmetic and copies ran while one was open for 2% -> 2% of each run, Pallas kernels for 24% -> 20%
where the time goes in v8:
time: 171 us
  Pallas kernels  111 us (65%)
  starting transfers between devices  27.6 us (16%)
  waiting for transfers between devices  23.2 us (14%)
  local copies, waits for them, and re-layouts  4.71 us (3%)
  other arithmetic  3.04 us (2%)
    pallas_call x1, Pallas kernels, on_device(): pl.pallas_call(functools.partial(step_kernel, wide), in_specs=[in_smem(),...  70 us
    pallas_call x1, Pallas kernels, on_device(): pl.pallas_call(functools.partial(moments_kernel, narrow), in_specs=[in_sm...  17.6 us
    ppermute x4, waiting for transfers between devices, exchange_planes(): lax.ppermute(one, 'bx', [(i, (i + step) % count) for i in range(count)])  12.5 us
    ppermute x6, starting transfers between devices, exchange_rows(): got.append(lax.ppermute(one, 'by', pairs))  11.2 us
    ppermute x5, starting transfers between devices, gather_lines(): got = lax.ppermute(line, axis, [(i, i ^ step) for i in range(count)])  9.97 us
    pallas_call x3, Pallas kernels, pack_rows(): pl.pallas_call(kernel, grid=(1,), in_specs=specs, out_specs=[pl.BlockSpec...  9.39 us
    pallas_call x2, Pallas kernels, pack_lanes(): pl.pallas_call(kernel, grid=(plan.x // planes,), in_specs=specs, out_spec...  8.14 us
    ppermute x5, waiting for transfers between devices, gather_lines(): got = lax.ppermute(line, axis, [(i, i ^ step) for i in range(count)])  6.92 us
  transfers between devices with their start and end apart: 17, of which 9 were waited for; matrix products, arithmetic and copies ran while one was open for 2% of the time, Pallas kernels for 20%

profile of v8, /device:TPU:0, one launch (start us, length us, event | category | flops | bytes accessed | tf_op | source)
XLA Modules:
  0.0 170.6 jit_solution(8161484656644081928)
XLA Ops:
  0.6 2.4 %pack_lanes.2 = f32[32,32,128]{2,1,0:T(8,128)} custom-call(f32[1,32,32,256]{3,2,1,0:T(8,128)} %bitcast.10, f32[1,32,32,256]{3,2,1,0:T(8,128)} %bitcast.11, f32[1,32,32,256]{3,2,1,0:T(8,128)} %bitcast.22, f32[1,32,32,256]{3,2,1,0:T(8,128)} %bitcast.23), custom_call_target="tpu_custom_call" | custom-call | bytes 1500000 | tf_op jit(solution)/shard_map/pack_lanes/pallas_call | solution.py:161
  4.2 1.1 collective-permute-done
  6.1 2.5 %pack_planes.2 = (f32[5,32,256]{2,1,0:T(8,128)}, f32[5,32,256]{2,1,0:T(8,128)}) custom-call(f32[7]{0:T(128)} %stack.55.refs_0_.flags, f32[1,32,32,256]{3,2,1,0:T(8,128)} %bitcast.12, f32[1,32,32,256]{3,2,1,0:T(8,128)} %bitcast.24, f32[32,32,128]{2,1,0:T(8,128)} %broadcast_select_fusion.1.refs_3_.refs_4_.refs_5_), custom_call_target="tpu_custom_call" | custom-call | bytes 1500000 | tf_op jit(solution)/shard_map/pack_planes/pallas_call | solution.py:254
  8.6 2.9 %collective-permute-start.1 = (f32[5,32,256]{2,1,0:T(8,128)}, f32[5,32,256]{2,1,0:T(8,128)S(1)}, u32[]{:S(2)}, u32[]{:S(2)}) collective-permute-start(f32[5,32,256]{2,1,0:T(8,128)} %get-tuple-element.33), channel_id=1, source_target_pairs={{0,8},{8,16},{16,24},{24,0},{1,9},{9,17},{17,25},{25,1},{2,10},{10... | collective-permute-start | bytes 491528 | tf_op jit(solution)/shard_map/ppermute | solution.py:392
  11.5 1.0 collective-permute-start.2
  12.5 5.7 %pack_lanes.3 = f32[32,32,128]{2,1,0:T(8,128)} custom-call(f32[1,32,32,256]{3,2,1,0:T(8,128)} %bitcast.13, f32[1,32,32,256]{3,2,1,0:T(8,128)} %bitcast.14, f32[1,32,32,256]{3,2,1,0:T(8,128)} %bitcast.25, f32[1,32,32,256]{3,2,1,0:T(8,128)} %bitcast.26, f32[3,32,32,256]{3,2,1,0:T(8,128)} %refs_4_.7, f32[3,32,32,256]{3,2,1,0:T(8,128)} %refs_4_.7, ...), custom_call_target="tpu_custom_call" | custom-call | bytes 1500000 | tf_op jit(solution)/shard_map/pack_lanes/pallas_call | solution.py:161
  18.2 2.7 %collective-permute-done.2.refs_8_.refs_9_.refs_5_.refs_6_.refs_7_.refs_15_ = f32[5,32,256]{2,1,0:T(8,128)S(1)} collective-permute-done((f32[5,32,256]{2,1,0:T(8,128)}, f32[5,32,256]{2,1,0:T(8,128)S(1)}, u32[]{:S(2)}, u32[]{:S(2)}) %collective-permute-start.2) | collective-permute-done | bytes 163872 | tf_op jit(solution)/shard_map/ppermute | solution.py:392
  21.6 2.4 %pack_rows.3 = (f32[36,8,256]{2,1,0:T(8,128)}, f32[36,8,256]{2,1,0:T(8,128)}) custom-call(f32[7]{0:T(128)} %stack.55.refs_0_.flags, f32[1,32,32,256]{3,2,1,0:T(8,128)} %bitcast.15, f32[1,32,32,256]{3,2,1,0:T(8,128)} %bitcast.16, f32[1,32,32,256]{3,2,1,0:T(8,128)} %bitcast.27, f32[1,32,32,256]{3,2,1,0:T(8,128)} %bitcast.28, ...), custom_call_target="tpu_custom_call" | custom-call | bytes 1500000 | tf_op jit(solution)/shard_map/pack_rows/pallas_call | solution.py:377
  23.9 1.6 collective-permute-start.3
  25.5 1.6 collective-permute-start.4
  28.0 3.9 %pack_planes.3 = (f32[23,32,256]{2,1,0:T(8,128)}, f32[30,32,256]{2,1,0:T(8,128)}) custom-call(f32[7]{0:T(128)} %stack.55.refs_0_.flags, f32[1,32,32,256]{3,2,1,0:T(8,128)} %bitcast.17, f32[1,32,32,256]{3,2,1,0:T(8,128)} %bitcast.29, f32[3,32,32,256]{3,2,1,0:T(8,128)} %refs_4_.7, f32[3,32,32,256]{3,2,1,0:T(8,128)} %refs_5_.5, s32[1,32,32,256]{3,2,1,0:T(8,128)} %bitcast.36, ...), custom_call_target="tpu_custom_call" | custom-call | bytes 1500000 | tf_op jit(solution)/shard_map/pack_planes/pallas_call | solution.py:254
  31.9 4.6 %pack_rows.4 = (f32[32,32,256]{2,1,0:T(8,128)}, f32[32,32,256]{2,1,0:T(8,128)}) custom-call(f32[7]{0:T(128)} %stack.55.refs_0_.flags, f32[1,32,32,256]{3,2,1,0:T(8,128)} %bitcast.18, f32[1,32,32,256]{3,2,1,0:T(8,128)} %bitcast.19, f32[1,32,32,256]{3,2,1,0:T(8,128)} %bitcast.30, f32[1,32,32,256]{3,2,1,0:T(8,128)} %bitcast.31, f32[3,32,32,256]{3,2,1,0:T(8,128)} %refs_4_.7, ...), custom_call_target="tpu_custom_call" | custom-call | bytes 1500000 | tf_op jit(solution)/shard_map/pack_rows/pallas_call | solution.py:377
  36.5 3.5 %collective-permute-start.6 = (f32[32,32,256]{2,1,0:T(8,128)}, f32[32,32,256]{2,1,0:T(8,128)}, u32[]{:S(2)}, u32[]{:S(2)}) collective-permute-start(f32[32,32,256]{2,1,0:T(8,128)} %get-tuple-element.46), channel_id=1, source_target_pairs={{0,2},{2,0},{4,6},{6,4},{1,3},{3,1},{5,7},{7,5},{8,10},{10,8},{12,... | collective-permute-start | bytes 3145736 | tf_op jit(solution)/shard_map/ppermute | solution.py:405
  40.0 1.6 collective-permute-start.7
  41.6 1.4 collective-permute-start.11
  43.6 17.6 %moments.1 = f32[1,128]{1,0:T(1,128)} custom-call(f32[7]{0:T(128)} %stack.55.refs_0_.flags, f32[1,32,32,256]{3,2,1,0:T(8,128)} %bitcast.20, f32[1,32,32,256]{3,2,1,0:T(8,128)} %bitcast.32, f32[32,32,128]{2,1,0:T(8,128)} %broadcast_select_fusion.1.refs_3_.refs_4_.refs_5_, f32[5,32,256]{2,1,0:T(8,128)} %copy-done.2, f32[5,32,256]{2,1,0:T(8,128)} %copy-done.3, ...), custom_call_target="tpu_custom_call" | custom-call | bytes 3000000 | tf_op jit(solution)/shard_map/moments/pallas_call | solution.py:1150
  61.2 1.7 %collective-permute-done.6.refs_10_ = f32[32,32,256]{2,1,0:T(8,128)} collective-permute-done((f32[32,32,256]{2,1,0:T(8,128)}, f32[32,32,256]{2,1,0:T(8,128)}, u32[]{:S(2)}, u32[]{:S(2)}) %collective-permute-start.6) | collective-permute-done | bytes 1048608 | tf_op jit(solution)/shard_map/ppermute | solution.py:405
  62.9 1.2 collective-permute-done.8
  64.8 4.4 %collective-permute-start.9 = (f32[2,128]{1,0:T(2,128)S(1)}, f32[2,128]{1,0:T(2,128)S(1)}, u32[]{:S(2)}, u32[]{:S(2)}) collective-permute-start(f32[2,128]{1,0:T(2,128)S(1)} %pad_maximum_fusion.4), channel_id=1, source_target_pairs={{0,2},{2,0},{4,6},{6,4},{1,3},{3,1},{5,7},{7,5},{8,10},{10,8},{12,... | collective-permute-start | bytes 3080 | tf_op jit(solution)/shard_map/ppermute | solution.py:1098
  69.2 1.5 collective-permute-done.9
  70.7 9.8 %collective-permute-done.10.refs_0_.refs_1_.refs_8_ = f32[23,32,256]{2,1,0:T(8,128)S(1)} collective-permute-done((f32[23,32,256]{2,1,0:T(8,128)}, f32[23,32,256]{2,1,0:T(8,128)S(1)}, u32[]{:S(2)}, u32[]{:S(2)}) %collective-permute-start.10) | collective-permute-done | bytes 753696 | tf_op jit(solution)/shard_map/ppermute | solution.py:392
  81.4 1.0 copy-done
  82.4 2.4 %pack_rows.5 = (f32[10,40,256]{2,1,0:T(8,128)}, f32[10,40,256]{2,1,0:T(8,128)}) custom-call(f32[7]{0:T(128)} %stack.55.refs_0_.flags, f32[23,32,256]{2,1,0:T(8,128)} %copy-done.1, f32[23,32,256]{2,1,0:T(8,128)} %copy-done.1, f32[30,32,256]{2,1,0:T(8,128)} %copy-done, f32[30,32,256]{2,1,0:T(8,128)} %copy-done, f32[5,32,256]{2,1,0:T(8,128)} %copy-done.2, ...), custom_call_target="tpu_custom_call" | custom-call | bytes 1500000 | tf_op jit(solution)/shard_map/pack_rows/pallas_call | solution.py:377
  84.8 2.5 %collective-permute-start.12 = (f32[4,128]{1,0:T(4,128)S(1)}, f32[4,128]{1,0:T(4,128)S(1)}, u32[]{:S(2)}, u32[]{:S(2)}) collective-permute-start(f32[4,128]{1,0:T(4,128)S(1)} %pad_maximum_fusion.3), channel_id=1, source_target_pairs={{0,4},{2,6},{4,0},{6,2},{1,5},{3,7},{5,1},{7,3},{8,12},{10,14},{12... | collective-permute-start | bytes 6152 | tf_op jit(solution)/shard_map/ppermute | solution.py:1098
  87.2 2.0 %collective-permute-done.12 = f32[4,128]{1,0:T(4,128)S(1)} collective-permute-done((f32[4,128]{1,0:T(4,128)S(1)}, f32[4,128]{1,0:T(4,128)S(1)}, u32[]{:S(2)}, u32[]{:S(2)}) %collective-permute-start.12) | collective-permute-done | bytes 2080 | tf_op jit(solution)/shard_map/ppermute | solution.py:1098
  89.3 1.6 collective-permute-start.13
  90.9 1.3 collective-permute-start.15
  92.2 1.6 collective-permute-start.16
  93.8 1.5 collective-permute-start.14
  95.4 2.2 %collective-permute-done.14 = f32[16,128]{1,0:T(8,128)S(1)} collective-permute-done((f32[16,128]{1,0:T(8,128)S(1)}, f32[16,128]{1,0:T(8,128)S(1)}, u32[]{:S(2)}, u32[]{:S(2)}) %collective-permute-start.14) | collective-permute-done | bytes 8224 | tf_op jit(solution)/shard_map/ppermute | solution.py:1098
  98.2 1.0 collective-permute-done.15.refs_12_
  100.7 70.0 %step.1 = (f32[3,32,32,256]{3,2,1,0:T(8,128)}, f32[3,32,32,256]{3,2,1,0:T(8,128)}, f32[3,32,32,256]{3,2,1,0:T(8,128)}, f32[32,32,256]{2,1,0:T(8,128)}, f32[32,32,256]{2,1,0:T(8,128)}) custom-call(f32[7]{0:T(128)} %stack.55.refs_0_.flags, f32[32,128]{1,0:T(8,128)} %pad_maximum_fusion.refs_1_, f32[1,32,32,256]{3,2,1,0:T(8,128)} %bitcast.21, ...), custom_call_target="tpu_custom_call" | custom-call | bytes 3000000 | tf_op jit(solution)/shard_map/step/pallas_call | solution.py:1180
  (42 shorter events, 7.9 us)
Async XLA Ops:
  3.1 2.2 %collective-permute-start = (f32[32,32,128]{2,1,0:T(8,128)}, f32[32,32,128]{2,1,0:T(8,128)S(1)}, u32[]{:S(2)}, u32[]{:S(2)}) collective-permute-start(f32[32,32,128]{2,1,0:T(8,128)} %pack_lanes.2), channel_id=1, source_target_pairs={{0,1},{1,0},{2,3},{3,2},{4,5},{5,4},{6,7},{7,6},{8,9},{9,8},{10,11... | collective-permute-start | bytes 1572872 | tf_op jit(solution)/shard_map/ppermute | solution.py:181
  8.6 9.6 %collective-permute-start.1 = (f32[5,32,256]{2,1,0:T(8,128)}, f32[5,32,256]{2,1,0:T(8,128)S(1)}, u32[]{:S(2)}, u32[]{:S(2)}) collective-permute-start(f32[5,32,256]{2,1,0:T(8,128)} %get-tuple-element.33), channel_id=1, source_target_pairs={{0,8},{8,16},{16,24},{24,0},{1,9},{9,17},{17,25},{25,1},{2,10},{10... | collective-permute-start | bytes 491528 | tf_op jit(solution)/shard_map/ppermute | solution.py:392
  11.5 9.4 %collective-permute-start.2 = (f32[5,32,256]{2,1,0:T(8,128)}, f32[5,32,256]{2,1,0:T(8,128)S(1)}, u32[]{:S(2)}, u32[]{:S(2)}) collective-permute-start(f32[5,32,256]{2,1,0:T(8,128)} %get-tuple-element.34), channel_id=1, source_target_pairs={{0,24},{8,0},{16,8},{24,16},{1,25},{9,1},{17,9},{25,17},{2,26},{10... | collective-permute-start | bytes 491528 | tf_op jit(solution)/shard_map/ppermute | solution.py:392
  18.2 2.7 %copy-start.2 = (f32[5,32,256]{2,1,0:T(8,128)}, f32[5,32,256]{2,1,0:T(8,128)S(1)}, u32[]{:S(2)}) copy-start(f32[5,32,256]{2,1,0:T(8,128)S(1)} %collective-permute-done.1.refs_6_.refs_7_.refs_4_.refs_5_.refs_14_) | copy-start | bytes 491524
  20.9 0.7 copy-start.3
  20.9 6.2 %collective-permute-start.5 = (f32[32,32,128]{2,1,0:T(8,128)}, f32[32,32,128]{2,1,0:T(8,128)S(1)}, u32[]{:S(2)}, u32[]{:S(2)}) collective-permute-start(f32[32,32,128]{2,1,0:T(8,128)} %pack_lanes.3), channel_id=1, source_target_pairs={{0,1},{1,0},{2,3},{3,2},{4,5},{5,4},{6,7},{7,6},{8,9},{9,8},{10,11... | collective-permute-start | bytes 1572872 | tf_op jit(solution)/shard_map/ppermute | solution.py:181
  23.9 12.5 %collective-permute-start.3 = (f32[36,8,256]{2,1,0:T(8,128)}, f32[36,8,256]{2,1,0:T(8,128)S(1)}, u32[]{:S(2)}, u32[]{:S(2)}) collective-permute-start(f32[36,8,256]{2,1,0:T(8,128)} %get-tuple-element.37), channel_id=1, source_target_pairs={{0,2},{2,0},{4,6},{6,4},{1,3},{3,1},{5,7},{7,5},{8,10},{10,8},{12,... | collective-permute-start | bytes 884744 | tf_op jit(solution)/shard_map/ppermute | solution.py:405
  25.5 11.0 %collective-permute-start.4 = (f32[36,8,256]{2,1,0:T(8,128)}, f32[36,8,256]{2,1,0:T(8,128)S(1)}, u32[]{:S(2)}, u32[]{:S(2)}) collective-permute-start(f32[36,8,256]{2,1,0:T(8,128)} %get-tuple-element.38), channel_id=1, source_target_pairs={{0,0},{2,4},{4,2},{6,6},{1,1},{3,5},{5,3},{7,7},{8,8},{10,12},{12,... | collective-permute-start | bytes 884744 | tf_op jit(solution)/shard_map/ppermute | solution.py:405
  36.5 7.2 %copy-start.4 = (f32[36,8,256]{2,1,0:T(8,128)}, f32[36,8,256]{2,1,0:T(8,128)S(1)}, u32[]{:S(2)}) copy-start(f32[36,8,256]{2,1,0:T(8,128)S(1)} %collective-permute-done.3.refs_6_.refs_16_) | copy-start | bytes 884740
  36.5 3.5 %copy-start.5 = (f32[36,8,256]{2,1,0:T(8,128)}, f32[36,8,256]{2,1,0:T(8,128)S(1)}, u32[]{:S(2)}) copy-start(f32[36,8,256]{2,1,0:T(8,128)S(1)} %collective-permute-done.4.refs_7_.refs_17_) | copy-start | bytes 884740
  36.5 26.4 %collective-permute-start.6 = (f32[32,32,256]{2,1,0:T(8,128)}, f32[32,32,256]{2,1,0:T(8,128)}, u32[]{:S(2)}, u32[]{:S(2)}) collective-permute-start(f32[32,32,256]{2,1,0:T(8,128)} %get-tuple-element.46), channel_id=1, source_target_pairs={{0,2},{2,0},{4,6},{6,4},{1,3},{3,1},{5,7},{7,5},{8,10},{10,8},{12,... | collective-permute-start | bytes 3145736 | tf_op jit(solution)/shard_map/ppermute | solution.py:405
  40.0 22.9 %collective-permute-start.7 = (f32[32,32,256]{2,1,0:T(8,128)}, f32[32,32,256]{2,1,0:T(8,128)}, u32[]{:S(2)}, u32[]{:S(2)}) collective-permute-start(f32[32,32,256]{2,1,0:T(8,128)} %get-tuple-element.47), channel_id=1, source_target_pairs={{2,4},{4,2},{3,5},{5,3},{10,12},{12,10},{11,13},{13,11},{18,20},{2... | collective-permute-start | bytes 3145736 | tf_op jit(solution)/shard_map/ppermute | solution.py:405
  41.6 38.9 %collective-permute-start.11 = (f32[30,32,256]{2,1,0:T(8,128)}, f32[30,32,256]{2,1,0:T(8,128)S(1)}, u32[]{:S(2)}, u32[]{:S(2)}) collective-permute-start(f32[30,32,256]{2,1,0:T(8,128)} %get-tuple-element.50), channel_id=1, source_target_pairs={{0,24},{8,0},{16,8},{24,16},{1,25},{9,1},{17,9},{25,17},{2,26},{10... | collective-permute-start | bytes 2949128 | tf_op jit(solution)/shard_map/ppermute | solution.py:392
  43.0 37.5 %collective-permute-start.10 = (f32[23,32,256]{2,1,0:T(8,128)}, f32[23,32,256]{2,1,0:T(8,128)S(1)}, u32[]{:S(2)}, u32[]{:S(2)}) collective-permute-start(f32[23,32,256]{2,1,0:T(8,128)} %get-tuple-element.49), channel_id=1, source_target_pairs={{0,8},{8,16},{16,24},{24,0},{1,9},{9,17},{17,25},{25,1},{2,10},{10... | collective-permute-start | bytes 2261000 | tf_op jit(solution)/shard_map/ppermute | solution.py:392
  62.9 1.2 collective-permute-start.8
  64.8 5.9 %collective-permute-start.9 = (f32[2,128]{1,0:T(2,128)S(1)}, f32[2,128]{1,0:T(2,128)S(1)}, u32[]{:S(2)}, u32[]{:S(2)}) collective-permute-start(f32[2,128]{1,0:T(2,128)S(1)} %pad_maximum_fusion.4), channel_id=1, source_target_pairs={{0,2},{2,0},{4,6},{6,4},{1,3},{3,1},{5,7},{7,5},{8,10},{10,8},{12,... | collective-permute-start | bytes 3080 | tf_op jit(solution)/shard_map/ppermute | solution.py:1098
  80.5 0.9 copy-start.1
  81.4 1.0 copy-start
  84.8 4.5 %collective-permute-start.12 = (f32[4,128]{1,0:T(4,128)S(1)}, f32[4,128]{1,0:T(4,128)S(1)}, u32[]{:S(2)}, u32[]{:S(2)}) collective-permute-start(f32[4,128]{1,0:T(4,128)S(1)} %pad_maximum_fusion.3), channel_id=1, source_target_pairs={{0,4},{2,6},{4,0},{6,2},{1,5},{3,7},{5,1},{7,3},{8,12},{10,14},{12... | collective-permute-start | bytes 6152 | tf_op jit(solution)/shard_map/ppermute | solution.py:1098
  89.3 4.5 %collective-permute-start.13 = (f32[8,128]{1,0:T(8,128)S(1)}, f32[8,128]{1,0:T(8,128)S(1)}, u32[]{:S(2)}, u32[]{:S(2)}) collective-permute-start(f32[8,128]{1,0:T(8,128)S(1)} %pad_maximum_fusion.2), channel_id=1, source_target_pairs={{0,8},{8,0},{16,24},{24,16},{1,9},{9,1},{17,25},{25,17},{2,10},{10... | collective-permute-start | bytes 12296 | tf_op jit(solution)/shard_map/ppermute | solution.py:1098
  90.9 8.3 %collective-permute-start.15 = (f32[10,40,256]{2,1,0:T(8,128)}, f32[10,40,256]{2,1,0:T(8,128)S(1)}, u32[]{:S(2)}, u32[]{:S(2)}) collective-permute-start(f32[10,40,256]{2,1,0:T(8,128)} %get-tuple-element.59), channel_id=1, source_target_pairs={{0,2},{2,0},{4,6},{6,4},{1,3},{3,1},{5,7},{7,5},{8,10},{10,8},{12,... | collective-permute-start | bytes 1228808 | tf_op jit(solution)/shard_map/ppermute | solution.py:405
  92.2 7.0 %collective-permute-start.16 = (f32[10,40,256]{2,1,0:T(8,128)}, f32[10,40,256]{2,1,0:T(8,128)S(1)}, u32[]{:S(2)}, u32[]{:S(2)}) collective-permute-start(f32[10,40,256]{2,1,0:T(8,128)} %get-tuple-element.60), channel_id=1, source_target_pairs={{0,0},{2,4},{4,2},{6,6},{1,1},{3,5},{5,3},{7,7},{8,8},{10,12},{12,... | collective-permute-start | bytes 1228808 | tf_op jit(solution)/shard_map/ppermute | solution.py:405
  93.8 3.7 %collective-permute-start.14 = (f32[16,128]{1,0:T(8,128)S(1)}, f32[16,128]{1,0:T(8,128)S(1)}, u32[]{:S(2)}, u32[]{:S(2)}) collective-permute-start(f32[16,128]{1,0:T(8,128)S(1)} %pad_maximum_fusion.1), channel_id=1, source_target_pairs={{0,16},{8,24},{16,0},{24,8},{1,17},{9,25},{17,1},{25,9},{2,18},{10... | collective-permute-start | bytes 24584 | tf_op jit(solution)/shard_map/ppermute | solution.py:1098
  99.1 0.8 copy-start.6
  99.9 0.8 copy-start.7

commit v9 on v8

--- a/solution.py
+++ b/solution.py
@@ -17,8 +17,8 @@
 LANES = 128
 ROWS = 8
 MOMENTS = 7
-MOMENTS_UNROLL = 12
-STEP_UNROLL = 3
+MOMENTS_UNROLL = 18
+STEP_UNROLL = 13
 POSITION, VELOCITY, PINNED = 2, 3, 4
 NARROW = 2
 WIDE = SWEEPS + 2

time: 171 us -> 155 us (0.906)
  Pallas kernels: 111 us -> 93.4 us
  waiting for transfers between devices: 23.2 us -> 25.1 us
    pallas_call x1, Pallas kernels: 70 us -> 53.9 us  [on_device(): pl.pallas_call(functools.partial(step_kernel, wide), in_specs=[in_smem(),...]
    ppermute x6, waiting for transfers between devices: 2.7 us -> 4.63 us  [exchange_rows(): got.append(lax.ppermute(one, 'by', pairs))]
    pallas_call x1, Pallas kernels: 17.6 us -> 15.6 us  [on_device(): pl.pallas_call(functools.partial(moments_kernel, narrow), in_specs=[in_sm...]
  transfers between devices with their start and end apart: 17 -> 17, of which waited for: 9 -> 9; matrix products, arithmetic and copies ran while one was open for 2% -> 2% of each run, Pallas kernels for 20% -> 21%
where the time goes in v9:
time: 155 us
  Pallas kernels  93.4 us (60%)
  starting transfers between devices  27.6 us (18%)
  waiting for transfers between devices  25.1 us (16%)
  local copies, waits for them, and re-layouts  4.71 us (3%)
  other arithmetic  3.04 us (2%)
    pallas_call x1, Pallas kernels, on_device(): pl.pallas_call(functools.partial(step_kernel, wide), in_specs=[in_smem(),...  53.9 us
    pallas_call x1, Pallas kernels, on_device(): pl.pallas_call(functools.partial(moments_kernel, narrow), in_specs=[in_sm...  15.6 us
    ppermute x4, waiting for transfers between devices, exchange_planes(): lax.ppermute(one, 'bx', [(i, (i + step) % count) for i in range(count)])  12.5 us
    ppermute x6, starting transfers between devices, exchange_rows(): got.append(lax.ppermute(one, 'by', pairs))  11.2 us
    ppermute x5, starting transfers between devices, gather_lines(): got = lax.ppermute(line, axis, [(i, i ^ step) for i in range(count)])  9.97 us
    pallas_call x3, Pallas kernels, pack_rows(): pl.pallas_call(kernel, grid=(1,), in_specs=specs, out_specs=[pl.BlockSpec...  9.39 us
    pallas_call x2, Pallas kernels, pack_lanes(): pl.pallas_call(kernel, grid=(plan.x // planes,), in_specs=specs, out_spec...  8.14 us
    ppermute x5, waiting for transfers between devices, gather_lines(): got = lax.ppermute(line, axis, [(i, i ^ step) for i in range(count)])  6.92 us
  transfers between devices with their start and end apart: 17, of which 9 were waited for; matrix products, arithmetic and copies ran while one was open for 2% of the time, Pallas kernels for 21%

profile of v9, /device:TPU:0, one launch (start us, length us, event | category | flops | bytes accessed | tf_op | source)
XLA Modules:
  0.0 154.5 jit_solution(13315482577400632409)
XLA Ops:
  0.6 2.4 %pack_lanes.2 = f32[32,32,128]{2,1,0:T(8,128)} custom-call(f32[1,32,32,256]{3,2,1,0:T(8,128)} %bitcast.10, f32[1,32,32,256]{3,2,1,0:T(8,128)} %bitcast.11, f32[1,32,32,256]{3,2,1,0:T(8,128)} %bitcast.22, f32[1,32,32,256]{3,2,1,0:T(8,128)} %bitcast.23), custom_call_target="tpu_custom_call" | custom-call | bytes 1500000 | tf_op jit(solution)/shard_map/pack_lanes/pallas_call | solution.py:161
  4.2 1.1 collective-permute-done
  6.1 2.5 %pack_planes.2 = (f32[5,32,256]{2,1,0:T(8,128)}, f32[5,32,256]{2,1,0:T(8,128)}) custom-call(f32[7]{0:T(128)} %stack.55.refs_0_.flags, f32[1,32,32,256]{3,2,1,0:T(8,128)} %bitcast.12, f32[1,32,32,256]{3,2,1,0:T(8,128)} %bitcast.24, f32[32,32,128]{2,1,0:T(8,128)} %broadcast_select_fusion.1.refs_3_.refs_4_.refs_5_), custom_call_target="tpu_custom_call" | custom-call | bytes 1500000 | tf_op jit(solution)/shard_map/pack_planes/pallas_call | solution.py:254
  8.6 2.9 %collective-permute-start.1 = (f32[5,32,256]{2,1,0:T(8,128)}, f32[5,32,256]{2,1,0:T(8,128)S(1)}, u32[]{:S(2)}, u32[]{:S(2)}) collective-permute-start(f32[5,32,256]{2,1,0:T(8,128)} %get-tuple-element.33), channel_id=1, source_target_pairs={{0,8},{8,16},{16,24},{24,0},{1,9},{9,17},{17,25},{25,1},{2,10},{10... | collective-permute-start | bytes 491528 | tf_op jit(solution)/shard_map/ppermute | solution.py:392
  11.5 1.0 collective-permute-start.2
  12.5 5.7 %pack_lanes.3 = f32[32,32,128]{2,1,0:T(8,128)} custom-call(f32[1,32,32,256]{3,2,1,0:T(8,128)} %bitcast.13, f32[1,32,32,256]{3,2,1,0:T(8,128)} %bitcast.14, f32[1,32,32,256]{3,2,1,0:T(8,128)} %bitcast.25, f32[1,32,32,256]{3,2,1,0:T(8,128)} %bitcast.26, f32[3,32,32,256]{3,2,1,0:T(8,128)} %refs_4_.7, f32[3,32,32,256]{3,2,1,0:T(8,128)} %refs_4_.7, ...), custom_call_target="tpu_custom_call" | custom-call | bytes 1500000 | tf_op jit(solution)/shard_map/pack_lanes/pallas_call | solution.py:161
  18.2 2.7 %collective-permute-done.2.refs_8_.refs_9_.refs_5_.refs_6_.refs_7_.refs_15_ = f32[5,32,256]{2,1,0:T(8,128)S(1)} collective-permute-done((f32[5,32,256]{2,1,0:T(8,128)}, f32[5,32,256]{2,1,0:T(8,128)S(1)}, u32[]{:S(2)}, u32[]{:S(2)}) %collective-permute-start.2) | collective-permute-done | bytes 163872 | tf_op jit(solution)/shard_map/ppermute | solution.py:392
  21.6 2.4 %pack_rows.3 = (f32[36,8,256]{2,1,0:T(8,128)}, f32[36,8,256]{2,1,0:T(8,128)}) custom-call(f32[7]{0:T(128)} %stack.55.refs_0_.flags, f32[1,32,32,256]{3,2,1,0:T(8,128)} %bitcast.15, f32[1,32,32,256]{3,2,1,0:T(8,128)} %bitcast.16, f32[1,32,32,256]{3,2,1,0:T(8,128)} %bitcast.27, f32[1,32,32,256]{3,2,1,0:T(8,128)} %bitcast.28, ...), custom_call_target="tpu_custom_call" | custom-call | bytes 1500000 | tf_op jit(solution)/shard_map/pack_rows/pallas_call | solution.py:377
  23.9 1.6 %collective-permute-start.3 = (f32[36,8,256]{2,1,0:T(8,128)}, f32[36,8,256]{2,1,0:T(8,128)S(1)}, u32[]{:S(2)}, u32[]{:S(2)}) collective-permute-start(f32[36,8,256]{2,1,0:T(8,128)} %get-tuple-element.37), channel_id=1, source_target_pairs={{0,2},{2,0},{4,6},{6,4},{1,3},{3,1},{5,7},{7,5},{8,10},{10,8},{12,... | collective-permute-start | bytes 884744 | tf_op jit(solution)/shard_map/ppermute | solution.py:405
  25.5 1.6 %collective-permute-start.4 = (f32[36,8,256]{2,1,0:T(8,128)}, f32[36,8,256]{2,1,0:T(8,128)S(1)}, u32[]{:S(2)}, u32[]{:S(2)}) collective-permute-start(f32[36,8,256]{2,1,0:T(8,128)} %get-tuple-element.38), channel_id=1, source_target_pairs={{0,0},{2,4},{4,2},{6,6},{1,1},{3,5},{5,3},{7,7},{8,8},{10,12},{12,... | collective-permute-start | bytes 884744 | tf_op jit(solution)/shard_map/ppermute | solution.py:405
  28.0 3.9 %pack_planes.3 = (f32[23,32,256]{2,1,0:T(8,128)}, f32[30,32,256]{2,1,0:T(8,128)}) custom-call(f32[7]{0:T(128)} %stack.55.refs_0_.flags, f32[1,32,32,256]{3,2,1,0:T(8,128)} %bitcast.17, f32[1,32,32,256]{3,2,1,0:T(8,128)} %bitcast.29, f32[3,32,32,256]{3,2,1,0:T(8,128)} %refs_4_.7, f32[3,32,32,256]{3,2,1,0:T(8,128)} %refs_5_.5, s32[1,32,32,256]{3,2,1,0:T(8,128)} %bitcast.36, ...), custom_call_target="tpu_custom_call" | custom-call | bytes 1500000 | tf_op jit(solution)/shard_map/pack_planes/pallas_call | solution.py:254
  31.9 4.6 %pack_rows.4 = (f32[32,32,256]{2,1,0:T(8,128)}, f32[32,32,256]{2,1,0:T(8,128)}) custom-call(f32[7]{0:T(128)} %stack.55.refs_0_.flags, f32[1,32,32,256]{3,2,1,0:T(8,128)} %bitcast.18, f32[1,32,32,256]{3,2,1,0:T(8,128)} %bitcast.19, f32[1,32,32,256]{3,2,1,0:T(8,128)} %bitcast.30, f32[1,32,32,256]{3,2,1,0:T(8,128)} %bitcast.31, f32[3,32,32,256]{3,2,1,0:T(8,128)} %refs_4_.7, ...), custom_call_target="tpu_custom_call" | custom-call | bytes 1500000 | tf_op jit(solution)/shard_map/pack_rows/pallas_call | solution.py:377
  36.5 3.5 %collective-permute-start.6 = (f32[32,32,256]{2,1,0:T(8,128)}, f32[32,32,256]{2,1,0:T(8,128)}, u32[]{:S(2)}, u32[]{:S(2)}) collective-permute-start(f32[32,32,256]{2,1,0:T(8,128)} %get-tuple-element.46), channel_id=1, source_target_pairs={{0,2},{2,0},{4,6},{6,4},{1,3},{3,1},{5,7},{7,5},{8,10},{10,8},{12,... | collective-permute-start | bytes 3145736 | tf_op jit(solution)/shard_map/ppermute | solution.py:405
  40.0 1.6 %collective-permute-start.7 = (f32[32,32,256]{2,1,0:T(8,128)}, f32[32,32,256]{2,1,0:T(8,128)}, u32[]{:S(2)}, u32[]{:S(2)}) collective-permute-start(f32[32,32,256]{2,1,0:T(8,128)} %get-tuple-element.47), channel_id=1, source_target_pairs={{2,4},{4,2},{3,5},{5,3},{10,12},{12,10},{11,13},{13,11},{18,20},{2... | collective-permute-start | bytes 3145736 | tf_op jit(solution)/shard_map/ppermute | solution.py:405
  41.6 1.4 collective-permute-start.11
  43.6 15.6 %moments.1 = f32[1,128]{1,0:T(1,128)} custom-call(f32[7]{0:T(128)} %stack.55.refs_0_.flags, f32[1,32,32,256]{3,2,1,0:T(8,128)} %bitcast.20, f32[1,32,32,256]{3,2,1,0:T(8,128)} %bitcast.32, f32[32,32,128]{2,1,0:T(8,128)} %broadcast_select_fusion.1.refs_3_.refs_4_.refs_5_, f32[5,32,256]{2,1,0:T(8,128)} %copy-done.2, f32[5,32,256]{2,1,0:T(8,128)} %copy-done.3, ...), custom_call_target="tpu_custom_call" | custom-call | bytes 3000000 | tf_op jit(solution)/shard_map/moments/pallas_call | solution.py:1150
  59.3 3.7 %collective-permute-done.6.refs_10_ = f32[32,32,256]{2,1,0:T(8,128)} collective-permute-done((f32[32,32,256]{2,1,0:T(8,128)}, f32[32,32,256]{2,1,0:T(8,128)}, u32[]{:S(2)}, u32[]{:S(2)}) %collective-permute-start.6) | collective-permute-done | bytes 1048608 | tf_op jit(solution)/shard_map/ppermute | solution.py:405
  62.9 1.2 collective-permute-done.8
  64.8 4.4 %collective-permute-start.9 = (f32[2,128]{1,0:T(2,128)S(1)}, f32[2,128]{1,0:T(2,128)S(1)}, u32[]{:S(2)}, u32[]{:S(2)}) collective-permute-start(f32[2,128]{1,0:T(2,128)S(1)} %pad_maximum_fusion.4), channel_id=1, source_target_pairs={{0,2},{2,0},{4,6},{6,4},{1,3},{3,1},{5,7},{7,5},{8,10},{10,8},{12,... | collective-permute-start | bytes 3080 | tf_op jit(solution)/shard_map/ppermute | solution.py:1098
  69.2 1.5 %collective-permute-done.9 = f32[2,128]{1,0:T(2,128)S(1)} collective-permute-done((f32[2,128]{1,0:T(2,128)S(1)}, f32[2,128]{1,0:T(2,128)S(1)}, u32[]{:S(2)}, u32[]{:S(2)}) %collective-permute-start.9) | collective-permute-done | bytes 1056 | tf_op jit(solution)/shard_map/ppermute | solution.py:1098
  70.7 9.8 %collective-permute-done.10.refs_0_.refs_1_.refs_8_ = f32[23,32,256]{2,1,0:T(8,128)S(1)} collective-permute-done((f32[23,32,256]{2,1,0:T(8,128)}, f32[23,32,256]{2,1,0:T(8,128)S(1)}, u32[]{:S(2)}, u32[]{:S(2)}) %collective-permute-start.10) | collective-permute-done | bytes 753696 | tf_op jit(solution)/shard_map/ppermute | solution.py:392
  81.4 1.0 copy-done
  82.4 2.4 %pack_rows.5 = (f32[10,40,256]{2,1,0:T(8,128)}, f32[10,40,256]{2,1,0:T(8,128)}) custom-call(f32[7]{0:T(128)} %stack.55.refs_0_.flags, f32[23,32,256]{2,1,0:T(8,128)} %copy-done.1, f32[23,32,256]{2,1,0:T(8,128)} %copy-done.1, f32[30,32,256]{2,1,0:T(8,128)} %copy-done, f32[30,32,256]{2,1,0:T(8,128)} %copy-done, f32[5,32,256]{2,1,0:T(8,128)} %copy-done.2, ...), custom_call_target="tpu_custom_call" | custom-call | bytes 1500000 | tf_op jit(solution)/shard_map/pack_rows/pallas_call | solution.py:377
  84.8 2.5 %collective-permute-start.12 = (f32[4,128]{1,0:T(4,128)S(1)}, f32[4,128]{1,0:T(4,128)S(1)}, u32[]{:S(2)}, u32[]{:S(2)}) collective-permute-start(f32[4,128]{1,0:T(4,128)S(1)} %pad_maximum_fusion.3), channel_id=1, source_target_pairs={{0,4},{2,6},{4,0},{6,2},{1,5},{3,7},{5,1},{7,3},{8,12},{10,14},{12... | collective-permute-start | bytes 6152 | tf_op jit(solution)/shard_map/ppermute | solution.py:1098
  87.2 2.0 %collective-permute-done.12 = f32[4,128]{1,0:T(4,128)S(1)} collective-permute-done((f32[4,128]{1,0:T(4,128)S(1)}, f32[4,128]{1,0:T(4,128)S(1)}, u32[]{:S(2)}, u32[]{:S(2)}) %collective-permute-start.12) | collective-permute-done | bytes 2080 | tf_op jit(solution)/shard_map/ppermute | solution.py:1098
  89.3 1.6 %collective-permute-start.13 = (f32[8,128]{1,0:T(8,128)S(1)}, f32[8,128]{1,0:T(8,128)S(1)}, u32[]{:S(2)}, u32[]{:S(2)}) collective-permute-start(f32[8,128]{1,0:T(8,128)S(1)} %pad_maximum_fusion.2), channel_id=1, source_target_pairs={{0,8},{8,0},{16,24},{24,16},{1,9},{9,1},{17,25},{25,17},{2,10},{10... | collective-permute-start | bytes 12296 | tf_op jit(solution)/shard_map/ppermute | solution.py:1098
  90.9 1.3 collective-permute-start.15
  92.2 1.6 %collective-permute-start.16 = (f32[10,40,256]{2,1,0:T(8,128)}, f32[10,40,256]{2,1,0:T(8,128)S(1)}, u32[]{:S(2)}, u32[]{:S(2)}) collective-permute-start(f32[10,40,256]{2,1,0:T(8,128)} %get-tuple-element.60), channel_id=1, source_target_pairs={{0,0},{2,4},{4,2},{6,6},{1,1},{3,5},{5,3},{7,7},{8,8},{10,12},{12,... | collective-permute-start | bytes 1228808 | tf_op jit(solution)/shard_map/ppermute | solution.py:405
  93.8 1.5 %collective-permute-start.14 = (f32[16,128]{1,0:T(8,128)S(1)}, f32[16,128]{1,0:T(8,128)S(1)}, u32[]{:S(2)}, u32[]{:S(2)}) collective-permute-start(f32[16,128]{1,0:T(8,128)S(1)} %pad_maximum_fusion.1), channel_id=1, source_target_pairs={{0,16},{8,24},{16,0},{24,8},{1,17},{9,25},{17,1},{25,9},{2,18},{10... | collective-permute-start | bytes 24584 | tf_op jit(solution)/shard_map/ppermute | solution.py:1098
  95.4 2.2 %collective-permute-done.14 = f32[16,128]{1,0:T(8,128)S(1)} collective-permute-done((f32[16,128]{1,0:T(8,128)S(1)}, f32[16,128]{1,0:T(8,128)S(1)}, u32[]{:S(2)}, u32[]{:S(2)}) %collective-permute-start.14) | collective-permute-done | bytes 8224 | tf_op jit(solution)/shard_map/ppermute | solution.py:1098
  98.2 1.0 collective-permute-done.15.refs_12_
  100.7 53.9 %step.1 = (f32[3,32,32,256]{3,2,1,0:T(8,128)}, f32[3,32,32,256]{3,2,1,0:T(8,128)}, f32[3,32,32,256]{3,2,1,0:T(8,128)}, f32[32,32,256]{2,1,0:T(8,128)}, f32[32,32,256]{2,1,0:T(8,128)}) custom-call(f32[7]{0:T(128)} %stack.55.refs_0_.flags, f32[32,128]{1,0:T(8,128)} %pad_maximum_fusion.refs_1_, f32[1,32,32,256]{3,2,1,0:T(8,128)} %bitcast.21, ...), custom_call_target="tpu_custom_call" | custom-call | bytes 3000000 | tf_op jit(solution)/shard_map/step/pallas_call | solution.py:1180
  (42 shorter events, 7.9 us)
Async XLA Ops:
  3.1 2.2 %collective-permute-start = (f32[32,32,128]{2,1,0:T(8,128)}, f32[32,32,128]{2,1,0:T(8,128)S(1)}, u32[]{:S(2)}, u32[]{:S(2)}) collective-permute-start(f32[32,32,128]{2,1,0:T(8,128)} %pack_lanes.2), channel_id=1, source_target_pairs={{0,1},{1,0},{2,3},{3,2},{4,5},{5,4},{6,7},{7,6},{8,9},{9,8},{10,11... | collective-permute-start | bytes 1572872 | tf_op jit(solution)/shard_map/ppermute | solution.py:181
  8.6 9.6 %collective-permute-start.1 = (f32[5,32,256]{2,1,0:T(8,128)}, f32[5,32,256]{2,1,0:T(8,128)S(1)}, u32[]{:S(2)}, u32[]{:S(2)}) collective-permute-start(f32[5,32,256]{2,1,0:T(8,128)} %get-tuple-element.33), channel_id=1, source_target_pairs={{0,8},{8,16},{16,24},{24,0},{1,9},{9,17},{17,25},{25,1},{2,10},{10... | collective-permute-start | bytes 491528 | tf_op jit(solution)/shard_map/ppermute | solution.py:392
  11.5 9.4 %collective-permute-start.2 = (f32[5,32,256]{2,1,0:T(8,128)}, f32[5,32,256]{2,1,0:T(8,128)S(1)}, u32[]{:S(2)}, u32[]{:S(2)}) collective-permute-start(f32[5,32,256]{2,1,0:T(8,128)} %get-tuple-element.34), channel_id=1, source_target_pairs={{0,24},{8,0},{16,8},{24,16},{1,25},{9,1},{17,9},{25,17},{2,26},{10... | collective-permute-start | bytes 491528 | tf_op jit(solution)/shard_map/ppermute | solution.py:392
  18.2 2.7 %copy-start.2 = (f32[5,32,256]{2,1,0:T(8,128)}, f32[5,32,256]{2,1,0:T(8,128)S(1)}, u32[]{:S(2)}) copy-start(f32[5,32,256]{2,1,0:T(8,128)S(1)} %collective-permute-done.1.refs_6_.refs_7_.refs_4_.refs_5_.refs_14_) | copy-start | bytes 491524
  20.9 0.7 copy-start.3
  20.9 6.2 %collective-permute-start.5 = (f32[32,32,128]{2,1,0:T(8,128)}, f32[32,32,128]{2,1,0:T(8,128)S(1)}, u32[]{:S(2)}, u32[]{:S(2)}) collective-permute-start(f32[32,32,128]{2,1,0:T(8,128)} %pack_lanes.3), channel_id=1, source_target_pairs={{0,1},{1,0},{2,3},{3,2},{4,5},{5,4},{6,7},{7,6},{8,9},{9,8},{10,11... | collective-permute-start | bytes 1572872 | tf_op jit(solution)/shard_map/ppermute | solution.py:181
  23.9 12.5 %collective-permute-start.3 = (f32[36,8,256]{2,1,0:T(8,128)}, f32[36,8,256]{2,1,0:T(8,128)S(1)}, u32[]{:S(2)}, u32[]{:S(2)}) collective-permute-start(f32[36,8,256]{2,1,0:T(8,128)} %get-tuple-element.37), channel_id=1, source_target_pairs={{0,2},{2,0},{4,6},{6,4},{1,3},{3,1},{5,7},{7,5},{8,10},{10,8},{12,... | collective-permute-start | bytes 884744 | tf_op jit(solution)/shard_map/ppermute | solution.py:405
  25.5 11.0 %collective-permute-start.4 = (f32[36,8,256]{2,1,0:T(8,128)}, f32[36,8,256]{2,1,0:T(8,128)S(1)}, u32[]{:S(2)}, u32[]{:S(2)}) collective-permute-start(f32[36,8,256]{2,1,0:T(8,128)} %get-tuple-element.38), channel_id=1, source_target_pairs={{0,0},{2,4},{4,2},{6,6},{1,1},{3,5},{5,3},{7,7},{8,8},{10,12},{12,... | collective-permute-start | bytes 884744 | tf_op jit(solution)/shard_map/ppermute | solution.py:405
  36.5 7.2 %copy-start.4 = (f32[36,8,256]{2,1,0:T(8,128)}, f32[36,8,256]{2,1,0:T(8,128)S(1)}, u32[]{:S(2)}) copy-start(f32[36,8,256]{2,1,0:T(8,128)S(1)} %collective-permute-done.3.refs_6_.refs_16_) | copy-start | bytes 884740
  36.5 3.5 %copy-start.5 = (f32[36,8,256]{2,1,0:T(8,128)}, f32[36,8,256]{2,1,0:T(8,128)S(1)}, u32[]{:S(2)}) copy-start(f32[36,8,256]{2,1,0:T(8,128)S(1)} %collective-permute-done.4.refs_7_.refs_17_) | copy-start | bytes 884740
  36.5 26.4 %collective-permute-start.6 = (f32[32,32,256]{2,1,0:T(8,128)}, f32[32,32,256]{2,1,0:T(8,128)}, u32[]{:S(2)}, u32[]{:S(2)}) collective-permute-start(f32[32,32,256]{2,1,0:T(8,128)} %get-tuple-element.46), channel_id=1, source_target_pairs={{0,2},{2,0},{4,6},{6,4},{1,3},{3,1},{5,7},{7,5},{8,10},{10,8},{12,... | collective-permute-start | bytes 3145736 | tf_op jit(solution)/shard_map/ppermute | solution.py:405
  40.0 22.9 %collective-permute-start.7 = (f32[32,32,256]{2,1,0:T(8,128)}, f32[32,32,256]{2,1,0:T(8,128)}, u32[]{:S(2)}, u32[]{:S(2)}) collective-permute-start(f32[32,32,256]{2,1,0:T(8,128)} %get-tuple-element.47), channel_id=1, source_target_pairs={{2,4},{4,2},{3,5},{5,3},{10,12},{12,10},{11,13},{13,11},{18,20},{2... | collective-permute-start | bytes 3145736 | tf_op jit(solution)/shard_map/ppermute | solution.py:405
  41.6 38.9 %collective-permute-start.11 = (f32[30,32,256]{2,1,0:T(8,128)}, f32[30,32,256]{2,1,0:T(8,128)S(1)}, u32[]{:S(2)}, u32[]{:S(2)}) collective-permute-start(f32[30,32,256]{2,1,0:T(8,128)} %get-tuple-element.50), channel_id=1, source_target_pairs={{0,24},{8,0},{16,8},{24,16},{1,25},{9,1},{17,9},{25,17},{2,26},{10... | collective-permute-start | bytes 2949128 | tf_op jit(solution)/shard_map/ppermute | solution.py:392
  43.0 37.5 %collective-permute-start.10 = (f32[23,32,256]{2,1,0:T(8,128)}, f32[23,32,256]{2,1,0:T(8,128)S(1)}, u32[]{:S(2)}, u32[]{:S(2)}) collective-permute-start(f32[23,32,256]{2,1,0:T(8,128)} %get-tuple-element.49), channel_id=1, source_target_pairs={{0,8},{8,16},{16,24},{24,0},{1,9},{9,17},{17,25},{25,1},{2,10},{10... | collective-permute-start | bytes 2261000 | tf_op jit(solution)/shard_map/ppermute | solution.py:392
  62.9 1.2 collective-permute-start.8
  64.8 5.9 %collective-permute-start.9 = (f32[2,128]{1,0:T(2,128)S(1)}, f32[2,128]{1,0:T(2,128)S(1)}, u32[]{:S(2)}, u32[]{:S(2)}) collective-permute-start(f32[2,128]{1,0:T(2,128)S(1)} %pad_maximum_fusion.4), channel_id=1, source_target_pairs={{0,2},{2,0},{4,6},{6,4},{1,3},{3,1},{5,7},{7,5},{8,10},{10,8},{12,... | collective-permute-start | bytes 3080 | tf_op jit(solution)/shard_map/ppermute | solution.py:1098
  80.5 0.9 copy-start.1
  81.4 1.0 copy-start
  84.8 4.5 %collective-permute-start.12 = (f32[4,128]{1,0:T(4,128)S(1)}, f32[4,128]{1,0:T(4,128)S(1)}, u32[]{:S(2)}, u32[]{:S(2)}) collective-permute-start(f32[4,128]{1,0:T(4,128)S(1)} %pad_maximum_fusion.3), channel_id=1, source_target_pairs={{0,4},{2,6},{4,0},{6,2},{1,5},{3,7},{5,1},{7,3},{8,12},{10,14},{12... | collective-permute-start | bytes 6152 | tf_op jit(solution)/shard_map/ppermute | solution.py:1098
  89.3 4.5 %collective-permute-start.13 = (f32[8,128]{1,0:T(8,128)S(1)}, f32[8,128]{1,0:T(8,128)S(1)}, u32[]{:S(2)}, u32[]{:S(2)}) collective-permute-start(f32[8,128]{1,0:T(8,128)S(1)} %pad_maximum_fusion.2), channel_id=1, source_target_pairs={{0,8},{8,0},{16,24},{24,16},{1,9},{9,1},{17,25},{25,17},{2,10},{10... | collective-permute-start | bytes 12296 | tf_op jit(solution)/shard_map/ppermute | solution.py:1098
  90.9 8.3 %collective-permute-start.15 = (f32[10,40,256]{2,1,0:T(8,128)}, f32[10,40,256]{2,1,0:T(8,128)S(1)}, u32[]{:S(2)}, u32[]{:S(2)}) collective-permute-start(f32[10,40,256]{2,1,0:T(8,128)} %get-tuple-element.59), channel_id=1, source_target_pairs={{0,2},{2,0},{4,6},{6,4},{1,3},{3,1},{5,7},{7,5},{8,10},{10,8},{12,... | collective-permute-start | bytes 1228808 | tf_op jit(solution)/shard_map/ppermute | solution.py:405
  92.2 7.0 %collective-permute-start.16 = (f32[10,40,256]{2,1,0:T(8,128)}, f32[10,40,256]{2,1,0:T(8,128)S(1)}, u32[]{:S(2)}, u32[]{:S(2)}) collective-permute-start(f32[10,40,256]{2,1,0:T(8,128)} %get-tuple-element.60), channel_id=1, source_target_pairs={{0,0},{2,4},{4,2},{6,6},{1,1},{3,5},{5,3},{7,7},{8,8},{10,12},{12,... | collective-permute-start | bytes 1228808 | tf_op jit(solution)/shard_map/ppermute | solution.py:405
  93.8 3.7 %collective-permute-start.14 = (f32[16,128]{1,0:T(8,128)S(1)}, f32[16,128]{1,0:T(8,128)S(1)}, u32[]{:S(2)}, u32[]{:S(2)}) collective-permute-start(f32[16,128]{1,0:T(8,128)S(1)} %pad_maximum_fusion.1), channel_id=1, source_target_pairs={{0,16},{8,24},{16,0},{24,8},{1,17},{9,25},{17,1},{25,9},{2,18},{10... | collective-permute-start | bytes 24584 | tf_op jit(solution)/shard_map/ppermute | solution.py:1098
  99.1 0.8 copy-start.6
  99.9 0.8 copy-start.7
